TPU v7x, 32 devices: a whole 2x2x4 slice. The times are simulated.
32 devices in a mesh: seq: 8 (over z, core), mp: 4 (over y, x).
Axes of the slice: x: 2, y: 2, z: 4, core: 2. Of those that a mesh axis runs over, the one named last changes fastest.
Arguments:
- continued_prompt_entries: bfloat16 [1024, 4096], P('seq', 'mp'), may hold values from -6 to 6
- padded_prompt_entries: bfloat16 [1024, 4096], P('seq', 'mp'), may hold values from -6 to 6
- prompt_live_extents: int32 [16], P('seq'), may hold values from 8 to 64, as said below
- preceding_entry_line: bfloat16 [4096], P('mp'), may hold values from -6 to 6
- carried_memory: float32 [64, 64, 64], P('mp'), may hold values from -24 to 24
- token_mixing_ratios: float32 [5, 4096], replicated, may hold values from 0.05 to 0.95
- acceptance_transform: bfloat16 [4096, 4096], P('seq', 'mp'), may hold values from -0.09375 to 0.09375
- lookup_transform: bfloat16 [4096, 4096], P('seq', 'mp'), may hold values from -0.09375 to 0.09375
- payload_transform: bfloat16 [4096, 4096], P('seq', 'mp'), may hold values from -0.09375 to 0.09375
- gating_transform: bfloat16 [4096, 4096], P('seq', 'mp'), may hold values from -0.09375 to 0.09375
- fading_baseline: float32 [4096], P('mp'), may hold values from -10 to -3.5
- fading_left_factor: bfloat16 [4096, 128], replicated, may hold values from -0.09375 to 0.09375
- fading_right_factor: bfloat16 [128, 4096], P(None, 'mp'), may hold values from -0.5 to 0.5
- present_reward: float32 [64, 64], P('mp'), may hold values from -3 to 3
- group_layer_scaling: float32 [4096], P('mp'), may hold values from 0.5 to 1.5
- group_layer_shift_term: float32 [4096], P('mp'), may hold values from -1.8 to 1.8
- final_transform: bfloat16 [4096, 4096], P('mp', 'seq'), may hold values from -0.09375 to 0.09375
Outputs:
- mixed: bfloat16 [8, 256, 4096], P('seq', 'mp')
- span_states: float32 [8, 64, 64, 64], P('seq', 'mp')
- request_states: float32 [16, 64, 64, 64], P('seq', 'mp')
Inputs may be any that keep to these rules, and one draw needn't show every extreme that they name: `prompt_live_extents`: some request has all 64 rows live.
All inputs are finite; a program needn't handle non-finite values.
Results may differ from a plain program's by a relative error of at most 0.0076.
Values may be sent and summed in bfloat16 or wider, within the bound.
No kernel may reach another device: no remote copies, remote signals or barrier semaphores. Data moves between devices by JAX's collectives and lax.ppermute only.
A program may use at most 128 MiB of HBM per device.

v0:
```python
import jax
import jax.numpy as jnp
from jax import lax
from jax.sharding import PartitionSpec as P

BLK = 64


norm_eps = 0.00064
highest = lax.Precision.HIGHEST


def passed_along(x, axis, by):
    length = lax.axis_size(axis)
    pairs = [(i, i + by) for i in range(length) if 0 <= i + by < length]
    return lax.ppermute(x, axis, pairs)


def entering(value, axis, join, neutral):
    count, mine = (lax.axis_size(axis), lax.axis_index(axis))
    pieces = jax.tree.map(lambda part: lax.all_gather(part, axis), value)
    total = jax.tree.map(
        lambda part, zero: jnp.full_like(part, 0) + jnp.asarray(zero, part.dtype), value, neutral
    )

    def hop(position, total):
        longer = join(total, jax.tree.map(lambda part: part[position], pieces))
        return jax.tree.map(lambda new, old: jnp.where(position < mine, new, old), longer, total)

    return lax.fori_loop(0, count - 1, hop, total)


def mix_rows(current, previous, weight):
    here = current.astype(jnp.float32)
    return (here + weight[None, :] * (previous.astype(jnp.float32) - here)).astype(jnp.bfloat16)


def block_sweep(
    evolving_memory,
    acceptance_entries,
    lookup_entries,
    payload_entries,
    log_fading_amount,
    diagonal_reward,
):
    inclusive = jnp.cumsum(log_fading_amount, axis=0)
    exclusive = inclusive - log_fading_amount
    recept_scaled = acceptance_entries * jnp.exp(exclusive)
    keys_scaled = lookup_entries * jnp.exp(-inclusive)
    scores = jnp.einsum("ihc,jhc->hij", recept_scaled, keys_scaled, precision=highest)
    count = acceptance_entries.shape[0]
    row_index = lax.broadcasted_iota(jnp.int32, (count, count), 0)
    col_index = lax.broadcasted_iota(jnp.int32, (count, count), 1)
    scores = jnp.where((row_index > col_index)[None], scores, 0.0)
    diagonal_contribution = jnp.sum(
        acceptance_entries * diagonal_reward[None] * lookup_entries, axis=-1, keepdims=True
    )
    answer_lines = (
        jnp.einsum("hij,jhd->ihd", scores, payload_entries, precision=highest)
        + diagonal_contribution * payload_entries
    )
    answer_lines = answer_lines + jnp.einsum(
        "ihc,hcd->ihd", recept_scaled, evolving_memory, precision=highest
    )
    total = inclusive[-1]
    carried = lookup_entries * jnp.exp(total[None] - inclusive)
    new_state = jnp.exp(total)[:, :, None] * evolving_memory + jnp.einsum(
        "jhc,jhd->hcd", carried, payload_entries, precision=highest
    )
    return (new_state, answer_lines)


def continued_recurrence(
    acceptance_entries, lookup_entries, payload_entries, log_fading_amount, diagonal_reward
):
    length, per_group_view, embedding_dimension = acceptance_entries.shape
    blocks = length // BLK

    def step(evolving_memory, entry_lines):
        return block_sweep(
            evolving_memory,
            entry_lines[0],
            entry_lines[1],
            entry_lines[2],
            entry_lines[3],
            diagonal_reward,
        )

    shaped = tuple(
        (
            a.reshape(blocks, BLK, per_group_view, embedding_dimension)
            for a in (acceptance_entries, lookup_entries, payload_entries, log_fading_amount)
        )
    )
    evolving_memory, results = lax.scan(
        step,
        jnp.zeros((per_group_view, embedding_dimension, embedding_dimension), jnp.float32),
        shaped,
    )
    return (evolving_memory, results.reshape(length, per_group_view, embedding_dimension))


def combine(earlier, later):
    return (earlier[0] + later[0], jnp.exp(later[0])[:, :, None] * earlier[1] + later[1])


def shifted_rows(current, edge_row, long_rows, requests, slot_rows):
    feature_part = current.shape[1]
    long_prev = jnp.concatenate([edge_row, current[: long_rows - 1]], axis=0)
    short_view = current[long_rows:].reshape(requests, slot_rows, feature_part)
    short_prev = jnp.concatenate(
        [jnp.zeros((requests, 1, feature_part), current.dtype), short_view[:, :-1]], axis=1
    )
    short_prev = short_prev.reshape(requests * slot_rows, feature_part)
    return jnp.concatenate([long_prev, short_prev], axis=0)


def on_device(
    continued_prompt_entries,
    padded_prompt_entries,
    prompt_live_extents,
    preceding_entry_line,
    carried_memory,
    token_mixing_ratios,
    acceptance_transform,
    lookup_transform,
    payload_transform,
    gating_transform,
    fading_baseline,
    fading_left_factor,
    fading_right_factor,
    present_reward,
    group_layer_scaling,
    group_layer_shift_term,
    final_transform,
):
    long_rows = continued_prompt_entries.shape[0]
    requests = prompt_live_extents.shape[0]
    slot_rows = padded_prompt_entries.shape[0] // requests
    per_group_view, embedding_dimension = present_reward.shape
    arrived = passed_along(continued_prompt_entries[-1:], "seq", 1)
    first = lax.axis_index("seq") == 0
    edge_row = jnp.where(first, preceding_entry_line[None, :], arrived)
    current = jnp.concatenate([continued_prompt_entries, padded_prompt_entries], axis=0)
    current, edge_full = (
        lax.all_gather(current, "mp", axis=1, tiled=True),
        lax.all_gather(edge_row, "mp", axis=1, tiled=True),
    )
    previous = shifted_rows(current, edge_full, long_rows, requests, slot_rows)
    mixes = [mix_rows(current, previous, token_mixing_ratios[index]) for index in range(5)]
    total_rows = current.shape[0]
    columns = acceptance_transform.shape[1]
    pieces = (
        lax.all_gather(acceptance_transform, "seq", axis=0, tiled=True),
        lax.all_gather(lookup_transform, "seq", axis=0, tiled=True),
        lax.all_gather(payload_transform, "seq", axis=0, tiled=True),
        lax.all_gather(gating_transform, "seq", axis=0, tiled=True),
    )
    acceptance_entries, lookup_entries, payload_entries, gate = tuple(
        (
            jnp.dot(source, piece, preferred_element_type=jnp.float32)
            for source, piece in zip(mixes[:4], pieces)
        )
    )
    squeezed = jnp.tanh(
        jnp.dot(mixes[4], fading_left_factor, preferred_element_type=jnp.float32)
    ).astype(jnp.bfloat16)
    log_fading_amount = -jnp.exp(
        fading_baseline[None, :]
        + jnp.dot(squeezed, fading_right_factor, preferred_element_type=jnp.float32)
    )
    recept3, keys3, values3, decay3 = [
        a.reshape(total_rows, per_group_view, embedding_dimension)
        for a in (acceptance_entries, lookup_entries, payload_entries, log_fading_amount)
    ]
    local_state, long_out = continued_recurrence(
        recept3[:long_rows],
        keys3[:long_rows],
        values3[:long_rows],
        decay3[:long_rows],
        present_reward,
    )
    long_decay = decay3[:long_rows]
    group_total = jnp.sum(long_decay, axis=0)
    blank = (
        jnp.zeros((per_group_view, embedding_dimension), jnp.float32),
        jnp.zeros((per_group_view, embedding_dimension, embedding_dimension), jnp.float32),
    )
    prefix_total, prefix_state = entering((group_total, local_state), "seq", combine, blank)
    incoming = jnp.exp(prefix_total)[:, :, None] * carried_memory + prefix_state
    before_row = jnp.cumsum(long_decay, axis=0) - long_decay
    long_out = long_out + jnp.einsum(
        "ihc,hcd->ihd", recept3[:long_rows] * jnp.exp(before_row), incoming, precision=highest
    )
    span_end = jnp.exp(group_total)[:, :, None] * incoming + local_state
    live_rows = (
        lax.broadcasted_iota(jnp.int32, (requests, slot_rows), 1) < prompt_live_extents[:, None]
    )
    live_flat = live_rows.reshape(requests * slot_rows).astype(jnp.float32)[:, None, None]
    short_shape = (requests, slot_rows, per_group_view, embedding_dimension)
    short_recept = recept3[long_rows:].reshape(short_shape)
    short_keys = (keys3[long_rows:] * live_flat).reshape(short_shape)
    short_values = values3[long_rows:].reshape(short_shape)
    short_decay = (decay3[long_rows:] * live_flat).reshape(short_shape)
    zeroed_memory = jnp.zeros(
        (per_group_view, embedding_dimension, embedding_dimension), jnp.float32
    )

    def request_pass(acceptance_lines, lookup_table, payload_table, fading_table):
        return block_sweep(
            zeroed_memory,
            acceptance_lines,
            lookup_table,
            payload_table,
            fading_table,
            present_reward,
        )

    request_states, short_out = jax.vmap(request_pass)(
        short_recept, short_keys, short_values, short_decay
    )
    wkv = jnp.concatenate(
        [long_out, short_out.reshape(requests * slot_rows, per_group_view, embedding_dimension)],
        axis=0,
    )
    mean = jnp.mean(wkv, axis=-1, keepdims=True)
    centred = wkv - mean
    variance = jnp.mean(centred * centred, axis=-1, keepdims=True)
    normed = (centred * lax.rsqrt(variance + norm_eps)).reshape(
        total_rows, columns
    ) * group_layer_scaling[None, :] + group_layer_shift_term[None, :]
    row_live = jnp.concatenate(
        [jnp.ones((long_rows,), dtype=bool), live_rows.reshape(requests * slot_rows)], axis=0
    )
    hidden = jnp.where(row_live[:, None], normed * jax.nn.silu(gate), 0.0).astype(jnp.bfloat16)
    full_out = lax.all_gather(final_transform, "seq", axis=1, tiled=True)
    mixed_rows = lax.psum_scatter(
        jnp.dot(hidden, full_out, preferred_element_type=jnp.float32),
        "mp",
        scatter_dimension=0,
        tiled=True,
    )
    return (mixed_rows.astype(jnp.bfloat16)[None], span_end[None], request_states)


def solution(mesh):
    placed = (
        P("seq", "mp"),
        P("seq", "mp"),
        P("seq"),
        P("mp"),
        P("mp", None, None),
        P(),
        P("seq", "mp"),
        P("seq", "mp"),
        P("seq", "mp"),
        P("seq", "mp"),
        P("mp"),
        P(),
        P(None, "mp"),
        P("mp", None),
        P("mp"),
        P("mp"),
        P("mp", "seq"),
    )
    return jax.shard_map(
        on_device,
        mesh=mesh,
        in_specs=placed,
        out_specs=(P("seq", "mp", None), P("seq", "mp", None, None), P("seq", "mp", None, None)),
        check_vma=False,
    )
```

profile of v0, /device:TPU:0, one launch (start us, length us, event | category | flops | bytes accessed | tf_op | source)
XLA Modules:
  0.0 640.2 jit_solution(5540476954611894625)
XLA Ops:
  7.2 1.9 pad_maximum_fusion.2
  12.1 2.3 collective-permute-start
  15.2 9.0 %all_gather.34 = bf16[1,4096]{1,0:T(2,128)(2,1)S(1)} all-gather(bf16[1,1024]{1,0:T(2,128)(2,1)S(1)} %broadcast_select_fusion), channel_id=1, replica_groups=mesh['seq'=8,'mp'=4] {'mp'}, dimensions={1}, use_global_device_ids=true | all-gather | bytes 10240 | tf_op jit(solution)/shard_map/all_gather | solution.py:147
  24.3 24.3 %all-gather.9.cloned.1.call-done = bf16[256,4096]{1,0:T(8,128)(2,1)} async-done(((bf16[256,1024]{1,0:T(8,128)(2,1)}), bf16[256,4096]{1,0:T(8,128)(2,1)}) %all-gather.9.cloned.1.call-update) | async-done | bytes 2097168 | tf_op jit(solution)/shard_map/all_gather | solution.py:146
  48.5 1.5 slice.100
  50.4 1.1 slice.99
  51.6 4.3 fusion.43
  55.9 2.2 slice_reduce_fusion
  58.1 1.3 reshape.138
  59.4 72.8 %all-gather.15.cloned.1.call-done = bf16[4096,1024]{1,0:T(8,128)(2,1)} async-done(((bf16[512,1024]{1,0:T(8,128)(2,1)}), bf16[4096,1024]{1,0:T(8,128)(2,1)}) %all-gather.15.cloned.1.call-update) | async-done | bytes 8388624 | tf_op jit(solution)/shard_map/all_gather | solution.py:154
  132.2 6.7 %fusion.27 = f32[256,1024]{1,0:T(8,128)S(1)} fusion(bf16[4096,1024]{1,0:T(8,128)(2,1)} %all-gather.15.cloned.1.call-done, bf16[256,4096]{1,0:T(8,128)(2,1)} %all-gather.9.cloned.1.call-done, f32[4096]{0:T(1024)S(1)} %bitcast.142, bf16[128,4096]{1,0:T(8,128)(2,1)S(1)} %bitcast.135, bf16[127,4096]{1,0:T(8,128)(2,1)} %slice.99, bf16[1,4096]{1,0:T(2,128)(2,1)S(1)} %all_gather.34), kind=kOutput, calls=%fused_computation.48 | convolution fusion | flops 2159017984 | bytes 13647872 | tf_op jit(solution)/shard_map/dot_general | solution.py:161
  139.9 1.3 reshape.141
  141.1 73.3 %all-gather.11.cloned.1.call-done = bf16[4096,1024]{1,0:T(8,128)(2,1)} async-done(((bf16[512,1024]{1,0:T(8,128)(2,1)}), bf16[4096,1024]{1,0:T(8,128)(2,1)}) %all-gather.11.cloned.1.call-update) | async-done | bytes 8388624 | tf_op jit(solution)/shard_map/all_gather | solution.py:155
  214.5 6.7 %fusion.31 = f32[256,1024]{1,0:T(8,128)S(1)} fusion(bf16[4096,1024]{1,0:T(8,128)(2,1)} %all-gather.11.cloned.1.call-done, bf16[256,4096]{1,0:T(8,128)(2,1)} %all-gather.9.cloned.1.call-done, f32[4096]{0:T(1024)S(1)} %bitcast.141, bf16[128,4096]{1,0:T(8,128)(2,1)S(1)} %bitcast.136, bf16[127,4096]{1,0:T(8,128)(2,1)} %slice.99, bf16[1,4096]{1,0:T(2,128)(2,1)S(1)} %all_gather.34), kind=kOutput, calls=%fused_computation.50 | convolution fusion | flops 2159017984 | bytes 13647872 | tf_op jit(solution)/shard_map/dot_general | solution.py:161
  222.1 1.2 reshape.139
  223.3 73.2 %all-gather.13.cloned.1.call-done = bf16[4096,1024]{1,0:T(8,128)(2,1)} async-done(((bf16[512,1024]{1,0:T(8,128)(2,1)}), bf16[4096,1024]{1,0:T(8,128)(2,1)}) %all-gather.13.cloned.1.call-update) | async-done | bytes 8388624 | tf_op jit(solution)/shard_map/all_gather | solution.py:156
  296.5 6.7 %fusion.29 = f32[256,1024]{1,0:T(8,128)S(1)} fusion(bf16[4096,1024]{1,0:T(8,128)(2,1)} %all-gather.13.cloned.1.call-done, bf16[256,4096]{1,0:T(8,128)(2,1)} %all-gather.9.cloned.1.call-done, f32[4096]{0:T(1024)S(1)} %bitcast.140, bf16[128,4096]{1,0:T(8,128)(2,1)S(1)} %bitcast.137, bf16[127,4096]{1,0:T(8,128)(2,1)} %slice.99, bf16[1,4096]{1,0:T(2,128)(2,1)S(1)} %all_gather.34), kind=kOutput, calls=%fused_computation.49 | convolution fusion | flops 2159017984 | bytes 13647872 | tf_op jit(solution)/shard_map/dot_general | solution.py:161
  304.1 1.3 reshape.140
  305.4 47.9 %while.29 = (s32[]{:T(128)}, f32[16,64,64]{2,1,0:T(8,128)S(1)}, f32[2,64,16,64]{1,0,3,2:T(2,128)}, f32[2,64,16,64]{3,2,1,0:T(8,128)}, f32[2,64,16,64]{3,2,1,0:T(...) while((s32[]{:T(128)}, f32[16,64,64]{2,1,0:T(8,128)S(1)}, ...), condition=%wide.region_3.4_spmd.clone, body=%wide.region_0.3_spmd.clone.sunk | while | flops 206572544 | bytes 7918204 | solution.py:95
  305.6 1.1 fusion.119
  306.7 2.4 bitcast_multiply_fusion.5
  309.2 1.3 convolution_select_fusion.3
  313.7 13.4 %dynamic_update_slice.6 = f32[2,64,16,64]{1,0,3,2:T(2,128)} dynamic-update-slice(f32[2,64,16,64]{1,0,3,2:T(2,128)} %get-tuple-element.396, f32[1,64,16,64]{1,0,3,2:T(1,128)S(1)} %copy.144, s32[]{:T(128)} %get-tuple-element.394, s32[]{:T(128)} %constant.64.clone.1..sunk, s32[]{:T(128)} %constant.64.clone.1..sunk, s32[]{:T(128)} %constant.64.clone.1..sunk) | dynamic-update-slice | bytes 524292 | tf_op jit(solution)/shard_map/while/body/jit(dynamic_update_index_in_dim)/dynamic_update_slice | solution.py:95
  327.0 2.4 convolution_add_fusion.4
  330.6 2.4 bitcast_multiply_fusion.5
  333.0 1.3 convolution_select_fusion.3
  337.6 13.4 %dynamic_update_slice.6 = f32[2,64,16,64]{1,0,3,2:T(2,128)} dynamic-update-slice(f32[2,64,16,64]{1,0,3,2:T(2,128)} %get-tuple-element.396, f32[1,64,16,64]{1,0,3,2:T(1,128)S(1)} %copy.144, s32[]{:T(128)} %get-tuple-element.394, s32[]{:T(128)} %constant.64.clone.1..sunk, s32[]{:T(128)} %constant.64.clone.1..sunk, s32[]{:T(128)} %constant.64.clone.1..sunk) | dynamic-update-slice | bytes 524292 | tf_op jit(solution)/shard_map/while/body/jit(dynamic_update_index_in_dim)/dynamic_update_slice | solution.py:95
  350.9 2.4 convolution_add_fusion.4
  355.8 1.2 copy.72
  357.1 1.4 copy.73
  358.7 14.2 %all_gather.39 = f32[8,16,64]{2,1,0:T(8,128)S(1)} all-gather(f32[1,16,64]{2,1,0:T(8,128)S(1)} %all_gather.38), channel_id=1, replica_groups=mesh['seq'=8,'mp'=4] {'seq'}, dimensions={0}, use_global_device_ids=true | all-gather | bytes 36864 | tf_op jit(solution)/shard_map/all_gather | solution.py:21
  374.7 2.4 reshape.144
  377.1 2.3 slice.94
  379.4 3.8 exponential_multiply_fusion
  383.3 2.3 reshape.143
  385.6 1.6 copy.80
  387.3 3.2 convolution_bitcast_fusion.3
  390.4 3.6 convolution_select_fusion.1
  394.1 2.8 fusion.41
  396.9 3.0 copy.86
  399.9 2.7 copy.84
  402.6 2.6 reshape.142
  405.3 1.4 copy.75
  406.7 2.7 reshape.145
  409.4 2.5 concatenate.27
  411.9 2.5 exponential_multiply_fusion.3
  414.4 10.3 %while.30 = (s32[]{:T(128)}, f32[16,64]{1,0:T(8,128)S(1)}, f32[16,64,64]{2,1,0:T(8,128)S(1)}, s32[]{:T(128)}, f32[8,16,64]{2,1,0:T(8,128)S(1)}, /*index=5*/f32[8,16,64,64]{3,2,1,0:T(8,128)}, s32[]{:T(128)}, s32[]{:T(128)}) while((s32[]{:T(128)}, f32[16,64]{1,0:T(8,128)S(1)}, f32[16,64,64]{2,1,0:T(8,128)S(1)}, s32[]{:T(128)}, ...), condition=%wide.region_6.7_spmd.clone, body=%wide.region_5.6_spmd.clone.sunk | while | flops 265220 | bytes 807027 | solution.py:30
  414.6 1.4 fusion.123
  416.1 1.4 fusion.123
  417.5 1.4 fusion.123
  419.0 1.4 fusion.123
  420.4 1.4 fusion.123
  421.9 1.4 fusion.123
  423.3 1.4 fusion.123
  424.7 3.4 fusion.44
  429.5 2.5 copy.88
  433.1 2.5 copy.87
  435.8 47.0 %all-gather.17.cloned.1.call-done = bf16[4096,1024]{1,0:T(8,128)(2,1)} async-done(((bf16[512,1024]{1,0:T(8,128)(2,1)}), bf16[4096,1024]{1,0:T(8,128)(2,1)}) %all-gather.17.cloned.1.call-update) | async-done | bytes 8388624 | tf_op jit(solution)/shard_map/all_gather | solution.py:157
  482.9 82.2 %all-gather.19.cloned.1.call-done = bf16[1024,4096]{1,0:T(8,128)(2,1)} async-done(((bf16[1024,512]{1,0:T(8,128)(2,1)}), bf16[1024,4096]{1,0:T(8,128)(2,1)}) %all-gather.19.cloned.1.call-update) | async-done | bytes 8388624 | tf_op jit(solution)/shard_map/all_gather | solution.py:236
  565.1 14.4 %fusion.70 = f32[256,4096]{1,0:T(8,128)} fusion(bf16[1024,4096]{1,0:T(8,128)(2,1)} %all-gather.19.cloned.1.call-done, f32[256,1024]{1,0:T(8,128)} %copy.88, f32[256,1024]{1,0:T(8,128)} %copy.87, f32[128,1024]{1,0:T(8,128)S(1)} %copy-done.14, f32[128,1024]{1,0:T(8,128)S(1)} %copy.85, bf16[4096,1024]{1,0:T(8,128)(2,1)} %all-gather.17.cloned.1.call-done, ...), kind=kOutput, calls=%fused_computation.93 | convolution fusion | flops 4309647360 | bytes 28336384 | tf_op jit(solution)/shard_map/dot_general | solution.py:238
  580.4 4.4 convolution_add_fusion.1
  584.8 2.2 add_bitcast_fusion
  587.0 43.9 %reduce-scatter.2.cloned.1.call-done = f32[64,4096]{1,0:T(8,128)} async-done(((f32[256,4096]{1,0:T(8,128)}), f32[64,4096]{1,0:T(8,128)}) %reduce-scatter.2.cloned.1.call-update) | async-done | bytes 1048592 | tf_op jit(solution)/shard_map/reduce_scatter | solution.py:237
  630.9 2.1 convert_bitcast_fusion
  (120 shorter events, 22.4 us)
Async XLA Ops:
  7.2 44.4 %copy-start = (bf16[4096,128]{1,0:T(8,128)(2,1)S(1)}, bf16[4096,128]{1,0:T(8,128)(2,1)}, u32[]{:S(2)}) copy-start(bf16[4096,128]{1,0:T(8,128)(2,1)} %param.32) | copy-start | bytes 3145732
  7.2 7.2 %copy-start.16 = (f32[5,4096]{1,0:T(8,128)S(1)}, f32[5,4096]{1,0:T(8,128)}, u32[]{:S(2)}) copy-start(f32[5,4096]{1,0:T(8,128)} %param.26) | copy-start | bytes 245764
  7.2 8.0 %copy-start.17 = (bf16[1024]{0:T(1024)(128)(2,1)S(1)}, bf16[1024]{0:T(1024)(128)(2,1)}, u32[]{:S(2)}) copy-start(bf16[1024]{0:T(1024)(128)(2,1)} %param.24) | copy-start | bytes 6148
  7.2 41.3 %all-gather.9.cloned.1.call-start = ((), (), s32[]{:S(2)}) async-start(), calls=%async_computation.1 | async-start | bytes 2621440 | tf_op jit(solution)/shard_map/all_gather | solution.py:146
  9.2 123.0 %all-gather.15.cloned.1.call-start = ((), (), s32[]{:S(2)}) async-start(), calls=%async_computation.4 | async-start | bytes 9437184 | tf_op jit(solution)/shard_map/all_gather | solution.py:154
  10.0 41.6 %copy-start.19 = (bf16[128,1024]{1,0:T(8,128)(2,1)S(1)}, bf16[128,1024]{1,0:T(8,128)(2,1)}, u32[]{:S(2)}) copy-start(bf16[128,1024]{1,0:T(8,128)(2,1)} %param.33) | copy-start | bytes 786436
  10.0 41.6 %copy-start.20 = (f32[1024]{0:T(1024)S(1)}, f32[1024]{0:T(1024)}, u32[]{:S(2)}) copy-start(f32[1024]{0:T(1024)} %param.31) | copy-start | bytes 12292
  10.0 204.5 %all-gather.11.cloned.1.call-start = ((), (), s32[]{:S(2)}) async-start(), calls=%async_computation.2 | async-start | bytes 9437184 | tf_op jit(solution)/shard_map/all_gather | solution.py:155
  10.7 285.8 %all-gather.13.cloned.1.call-start = ((), (), s32[]{:S(2)}) async-start(), calls=%async_computation.3 | async-start | bytes 9437184 | tf_op jit(solution)/shard_map/all_gather | solution.py:156
  11.3 403.1 %all-gather.21.cloned.1.call-start = ((), (), s32[]{:S(2)}) async-start(), calls=%async_computation.8 | async-start | bytes 4718592 | tf_op jit(solution)/shard_map/all_gather | solution.py:21
  12.1 3.2 collective-permute-start
  48.5 1.9 copy-start.10
  50.4 246.1 %copy-start.13 = (bf16[2,64,4096]{2,1,0:T(8,128)(2,1)}, bf16[2,64,4096]{2,1,0:T(8,128)(2,1)S(1)}, u32[]{:S(2)}) copy-start(bf16[2,64,4096]{2,1,0:T(8,128)(2,1)S(1)} %concatenate.24) | copy-start | bytes 3145732
  58.1 74.1 %copy-start.8 = (f32[128,1024]{1,0:T(8,128)}, f32[128,1024]{1,0:T(8,128)S(1)}, u32[]{:S(2)}) copy-start(f32[128,1024]{1,0:T(8,128)S(1)} %get-tuple-element.272) | copy-start | bytes 1572868
  139.9 81.3 %copy-start.6 = (f32[128,1024]{1,0:T(8,128)}, f32[128,1024]{1,0:T(8,128)S(1)}, u32[]{:S(2)}) copy-start(f32[128,1024]{1,0:T(8,128)S(1)} %get-tuple-element.273) | copy-start | bytes 1572868
  296.5 8.9 %copy-start.15 = (f32[16,64]{1,0:T(8,128)S(1)}, f32[16,64]{1,0:T(8,128)}, u32[]{:S(2)}) copy-start(f32[16,64]{1,0:T(8,128)} %param.34) | copy-start | bytes 12292
  305.4 50.2 %copy-start.18 = (s32[2]{0:T(128)S(1)}, s32[2]{0:T(128)}, u32[]{:S(2)}) copy-start(s32[2]{0:T(128)} %param.23) | copy-start | bytes 28
  353.3 0.8 copy-start.2
  353.3 5.1 copy-start.11
  354.2 20.3 %copy-start.7 = (f32[128,1024]{1,0:T(8,128)S(1)}, f32[128,1024]{1,0:T(8,128)}, u32[]{:S(2)}) copy-start(f32[128,1024]{1,0:T(8,128)} %copy-done.6) | copy-start | bytes 1572868
  354.2 128.7 %all-gather.17.cloned.1.call-start = ((), (), s32[]{:S(2)}) async-start(), calls=%async_computation.5 | async-start | bytes 9437184 | tf_op jit(solution)/shard_map/all_gather | solution.py:157
  354.8 210.3 %all-gather.19.cloned.1.call-start = ((), (), s32[]{:S(2)}) async-start(), calls=%async_computation.6 | async-start | bytes 9437184 | tf_op jit(solution)/shard_map/all_gather | solution.py:236
  355.5 275.4 %reduce-scatter.2.cloned.1.call-start = ((), (), s32[]{:S(2)}) async-start(), calls=%async_computation.7 | async-start | bytes 5242880 | tf_op jit(solution)/shard_map/reduce_scatter | solution.py:237
  373.5 1.0 copy-start.9
  399.9 12.0 %copy-start.4 = (f32[128,16,64]{2,1,0:T(8,128)S(1)}, f32[128,16,64]{2,1,0:T(8,128)}, u32[]{:S(2)}) copy-start(f32[128,16,64]{2,1,0:T(8,128)} %copy.73) | copy-start | bytes 1572868
  414.4 10.3 %copy-start.12 = (f32[128,16,64]{0,2,1:T(8,128)S(1)}, f32[128,16,64]{0,2,1:T(8,128)}, u32[]{:S(2)}) copy-start(f32[128,16,64]{0,2,1:T(8,128)} %reshape.142) | copy-start | bytes 1572868
  414.4 13.8 %copy-start.5 = (f32[128,16,64]{0,2,1:T(8,128)S(1)}, f32[128,16,64]{0,2,1:T(8,128)}, u32[]{:S(2)}) copy-start(f32[128,16,64]{0,2,1:T(8,128)} %reshape.145) | copy-start | bytes 1572868
  428.3 136.8 %copy-start.14 = (f32[128,1024]{1,0:T(8,128)S(1)}, f32[128,1024]{1,0:T(8,128)}, u32[]{:S(2)}) copy-start(f32[128,1024]{1,0:T(8,128)} %concatenate.27) | copy-start | bytes 1572868
  428.3 136.8 %copy-start.21 = (f32[1024]{0:T(1024)S(1)}, f32[1024]{0:T(1024)}, u32[]{:S(2)}) copy-start(f32[1024]{0:T(1024)} %param.36) | copy-start | bytes 12292
  428.3 136.8 %copy-start.22 = (f32[1024]{0:T(1024)S(1)}, f32[1024]{0:T(1024)}, u32[]{:S(2)}) copy-start(f32[1024]{0:T(1024)} %param.35) | copy-start | bytes 12292
  579.5 5.3 copy-start.3
  579.5 53.5 %copy-start.1 = (bf16[4096,128]{1,0:T(8,128)(2,1)S(1)}, bf16[4096,128]{1,0:T(8,128)(2,1)}, u32[]{:S(2)}) copy-start(bf16[4096,128]{1,0:T(8,128)(2,1)} %param.32) | copy-start | bytes 3145732
Sparse Core Ops, SparseCore 0:
  10.5 38.0 all-gather.8
  50.1 82.0 all-gather.14
  133.8 80.5 all-gather.10
  215.9 80.5 all-gather.12
  354.3 46.1 all-gather.20
  401.9 80.8 all-gather.16
  484.5 80.5 all-gather.18
  579.6 51.2 reduce-scatter.1
where the time goes:
time: 651 us; the launch traced here: 640 us
  waiting for transfers between devices  421 us (65%)
  local copies, waits for them, and re-layouts  77.6 us (12%)
  matrix products  67.1 us (10%)
  other arithmetic  33.3 us (5%)
  blocking collectives  23.3 us (4%)
  between operations  15 us (2%)
    all_gather x1, waiting for transfers between devices, on_device(): full_out = lax.all_gather(final_transform, 'seq', axis=1, tiled=True)  82.2 us
    all_gather x1, waiting for transfers between devices, on_device(): lax.all_gather(lookup_transform, 'seq', axis=0, tiled=True)  73.3 us
    all_gather x1, waiting for transfers between devices, on_device(): lax.all_gather(payload_transform, 'seq', axis=0, tiled=True)  73.2 us
    all_gather x1, waiting for transfers between devices, on_device(): lax.all_gather(acceptance_transform, 'seq', axis=0, tiled=True)  72.8 us
    all_gather x1, waiting for transfers between devices, on_device(): lax.all_gather(gating_transform, 'seq', axis=0, tiled=True)  47 us
    reduce_scatter x1, waiting for transfers between devices, on_device(): lax.psum_scatter(jnp.dot(hidden, full_out, preferred_element_type=jnp.flo...  43.9 us
    dynamic_update_slice x4, local copies, waits for them, and re-layouts, continued_recurrence(): lax.scan(step, jnp.zeros((per_group_view, embedding_dimension, embedding_...  27.4 us
    all_gather x1, waiting for transfers between devices, on_device(): lax.all_gather(current, 'mp', axis=1, tiled=True)  24.3 us
  transfers between devices with their start and end apart: 9, of which 8 were waited for; matrix products, arithmetic and copies ran while one was open for 16% of the time, Pallas kernels for 0%

commit v1 on v0

--- a/solution.py
+++ b/solution.py
@@ -1,6 +1,10 @@
 import jax
 import jax.numpy as jnp
+import numpy as np
 from jax import lax
+from jax.experimental import pallas as pl
+from jax.experimental.pallas import tpu as pltpu
+from jax.sharding import Mesh
 from jax.sharding import PartitionSpec as P
 
 BLK = 64
@@ -243,7 +247,447 @@
     return (mixed_rows.astype(jnp.bfloat16)[None], span_end[None], request_states)
 
 
-def solution(mesh):
+f32 = jnp.float32
+bf16 = jnp.bfloat16
+VMEM_LIMIT = 56 * 1024 * 1024
+TILE = 256
+
+
+def in_vmem():
+    return pl.BlockSpec(memory_space=pltpu.VMEM)
+
+
+def in_smem():
+    return pl.BlockSpec(memory_space=pltpu.SMEM)
+
+
+def kernel_params():
+    return pltpu.CompilerParams(vmem_limit_bytes=VMEM_LIMIT)
+
+
+def previous_rows(x_ref, first_row, tile, start):
+    here = x_ref[pl.ds(pl.multiple_of(tile * TILE, TILE), TILE), :].astype(f32)
+    above_at = jnp.maximum(tile * TILE - 16, 0)
+    above = x_ref[pl.ds(pl.multiple_of(above_at, 16), 16), :].astype(f32)[15:16]
+    row = lax.broadcasted_iota(jnp.int32, here.shape, 0)
+    before = jnp.where(row == 0, above, pltpu.roll(here, 1, 0))
+    before = jnp.where(start, first_row, before)
+    return here, before - here
+
+
+def project_kernel(count, outs, finish, *refs):
+    place, period = refs[0], refs[1]
+    chunks = refs[2:10]
+    first, ratios, own, sibling = refs[10:14]
+    extra = refs[14:-outs]
+    results = refs[-outs:]
+    rows = chunks[0].shape[0]
+
+    @pl.loop(0, rows // TILE)
+    def _(tile):
+        row = lax.broadcasted_iota(jnp.int32, (TILE, 1), 0) + tile * TILE
+        start = (row & (period[0] - 1)) == 0
+        totals = [None] * count
+        for at, chunk in enumerate(chunks):
+            here, step = previous_rows(chunk, first[at : at + 1, :], tile, start)
+            held = own if at % 2 == 0 else sibling
+            for c in range(count):
+                mixed = (here + ratios[c, at : at + 1, :] * step).astype(bf16)
+                part = jnp.dot(mixed, held[place[at // 2], c], preferred_element_type=f32)
+                totals[c] = part if totals[c] is None else totals[c] + part
+        finish(tile, totals, extra, results)
+
+
+def store_tiles(tile, totals, extra, results):
+    at = pl.ds(pl.multiple_of(tile * TILE, TILE), TILE)
+    for total, result in zip(totals, results):
+        result[at, :] = total
+
+
+def store_decay(tile, totals, extra, results):
+    right, base = extra
+    at = pl.ds(pl.multiple_of(tile * TILE, TILE), TILE)
+    squeezed = jnp.tanh(totals[0]).astype(bf16)
+    grown = jnp.dot(squeezed, right[...], preferred_element_type=f32)
+    results[0][at, :] = -jnp.exp(base[...] + grown)
+
+
+def store_hidden(tile, totals, extra, results):
+    normed, live = extra
+    at = pl.ds(pl.multiple_of(tile * TILE, TILE), TILE)
+    gate = totals[0]
+    value = normed[at, :] * (gate * jax.nn.sigmoid(gate))
+    results[0][at, :] = jnp.where(live[at, :] > 0, value, 0.0).astype(bf16)
+
+
+def project(finish, out_shapes, place, period, chunks, first, ratios, own, sibling, *extra):
+    count = own.shape[1]
+    outs = len(out_shapes)
+    return pl.pallas_call(
+        lambda *refs: project_kernel(count, outs, finish, *refs),
+        out_shape=out_shapes,
+        in_specs=[in_smem(), in_smem()] + [in_vmem()] * (12 + len(extra)),
+        out_specs=[in_vmem()] * outs,
+        compiler_params=kernel_params(),
+    )(place, period, *chunks, first, ratios, own, sibling, *extra)
+
+
+def sweep_kernel(
+    lengths, carry, r_ref, k_ref, v_ref, w_ref, u_ref, s_ref, gain, bias, out_ref, state_ref, hold
+):
+    span, width = BLK, r_ref.shape[1]
+    heads = width // span
+    row = lax.broadcasted_iota(jnp.int32, (span, width), 0)
+    lane = lax.broadcasted_iota(jnp.int32, (span, width), 1)
+    col = lane % span
+    tall = lax.broadcasted_iota(jnp.int32, (width, width), 0) // span
+    wide = lax.broadcasted_iota(jnp.int32, (width, width), 1) // span
+    same_head = tall == wide
+    for h in range(heads):
+        hold[:, h * span : (h + 1) * span] = s_ref[h]
+
+    def spread(value):
+        stacked = jnp.concatenate([value.astype(bf16)] * heads, axis=0)
+        return jnp.where(same_head, stacked, jnp.zeros_like(stacked))
+
+    def against(a, b):
+        return lax.dot_general(a, b, (((1,), (1,)), ((), ())), preferred_element_type=f32)
+
+    @pl.loop(0, r_ref.shape[0] // span)
+    def _(n):
+        at = pl.ds(pl.multiple_of(n * span, span), span)
+        live = row < lengths[n]
+        r, v = r_ref[at, :], v_ref[at, :]
+        k = jnp.where(live, k_ref[at, :], 0.0)
+        total = jnp.where(live, w_ref[at, :], 0.0)
+        before = jnp.zeros_like(total)
+        after = jnp.zeros_like(total)
+        scores = against((r * u_ref[...]).astype(bf16), spread(k))
+        scores = jnp.where(row == col, scores, 0.0)
+        level = 0
+        while (1 << level) < span:
+            half = 1 << level
+            upper = (row & half) != 0
+            if level:
+                scale = jnp.exp(jnp.where(upper, before, after))
+                part = against((r * scale).astype(bf16), spread(k * scale))
+            else:
+                part = against(r.astype(bf16), spread(k))
+            pair = upper & (((row >> level) ^ (col >> level)) == 1)
+            scores = jnp.where(pair, part, scores)
+            across = jnp.where(
+                upper, pltpu.roll(total, half, 0), pltpu.roll(total, span - half, 0)
+            )
+            before = before + jnp.where(upper, across, 0.0)
+            after = after + jnp.where(upper, 0.0, across)
+            total = total + across
+            level += 1
+        entered = hold[...] * carry[0]
+        out = jnp.dot(scores.astype(bf16), spread(v), preferred_element_type=f32)
+        out = out + jnp.dot(
+            (r * jnp.exp(before)).astype(bf16), spread(entered), preferred_element_type=f32
+        )
+        out_ref[at, :] = out
+        added = lax.dot_general(
+            (k * jnp.exp(after)).astype(bf16),
+            v.astype(bf16),
+            (((0,), (0,)), ((), ())),
+            preferred_element_type=f32,
+        )
+        fresh = jnp.zeros((span, width), f32)
+        for h in range(heads):
+            fresh = jnp.where(lane // span == h, added[h * span : (h + 1) * span], fresh)
+        twice = jnp.concatenate([total] * 2, axis=0)
+        turned = []
+        for p in range(width // (2 * span)):
+            flipped = jnp.transpose(twice[:, p * 2 * span : (p + 1) * 2 * span])
+            turned.append(
+                jnp.where(lane[:, : 2 * span] < span, flipped[:span], flipped[span:])
+            )
+        fade = jnp.exp(jnp.concatenate(turned, axis=1))
+        state = fade * entered + fresh
+        hold[...] = state
+        for h in range(heads):
+            state_ref[n, h] = state[:, h * span : (h + 1) * span]
+
+    ones = jnp.where(same_head, 1.0, 0.0).astype(bf16)
+
+    def head_mean(value):
+        high = value.astype(bf16)
+        low = (value - high.astype(f32)).astype(bf16)
+        both = jnp.dot(high, ones, preferred_element_type=f32) + jnp.dot(
+            low, ones, preferred_element_type=f32
+        )
+        return both * (1.0 / span)
+
+    @pl.loop(0, r_ref.shape[0] // TILE)
+    def _(tile):
+        at = pl.ds(pl.multiple_of(tile * TILE, TILE), TILE)
+        value = out_ref[at, :]
+        centred = value - head_mean(value)
+        spread_of = head_mean(centred * centred)
+        out_ref[at, :] = centred * lax.rsqrt(spread_of + norm_eps) * gain[...] + bias[...]
+
+
+def sweep(lengths, carry, r, k, v, w, bonus, state, gain, bias):
+    rows, width = r.shape
+    heads = width // BLK
+    return pl.pallas_call(
+        sweep_kernel,
+        out_shape=[
+            jax.ShapeDtypeStruct((rows, width), f32),
+            jax.ShapeDtypeStruct((rows // BLK, heads, BLK, BLK), f32),
+        ],
+        in_specs=[in_smem(), in_smem()] + [in_vmem()] * 8,
+        out_specs=[in_vmem(), in_vmem()],
+        scratch_shapes=[pltpu.VMEM((BLK, width), f32)],
+        compiler_params=kernel_params(),
+    )(lengths, carry, r, k, v, w, bonus, state, gain, bias)
+
+
+def final_kernel(h0, h1, h2, h3, weight, out_ref):
+    @pl.loop(0, h0.shape[0] // TILE)
+    def _(tile):
+        at = pl.ds(pl.multiple_of(tile * TILE, TILE), TILE)
+        total = None
+        for k, piece in enumerate((h0, h1, h2, h3)):
+            part = jnp.dot(piece[at, :], weight[k], preferred_element_type=f32)
+            total = part if total is None else total + part
+        out_ref[at, :] = total.astype(bf16)
+
+
+def final_product(pieces, weight):
+    return pl.pallas_call(
+        final_kernel,
+        out_shape=jax.ShapeDtypeStruct((pieces[0].shape[0], weight.shape[2]), bf16),
+        in_specs=[in_vmem()] * 5,
+        out_specs=in_vmem(),
+        compiler_params=kernel_params(),
+    )(*pieces, weight)
+
+
+def turned(x, axis, by):
+    length = lax.axis_size(axis)
+    return lax.ppermute(x, axis, [(i, (i + by) % length) for i in range(length)])
+
+
+def flipped_core(x):
+    return lax.ppermute(x, "core", [(0, 1), (1, 0)])
+
+
+def over_x(x):
+    return lax.ppermute(x, "x", [(0, 1), (1, 0)])
+
+
+def over_y(x):
+    return lax.ppermute(x, "y", [(0, 1), (1, 0)])
+
+
+def dealt(blocks, z):
+    length = lax.axis_size("z")
+    return [blocks(z)] + [turned(blocks((z + k) % length), "z", k) for k in range(1, length)]
+
+
+def in_order(pieces, z):
+    length = len(pieces)
+    whole = jnp.zeros((length,) + pieces[0].shape, pieces[0].dtype)
+    for k, piece in enumerate(pieces):
+        whole = lax.dynamic_update_index_in_dim(whole, piece, (z - k) % length, 0)
+    return whole
+
+
+def on_core(
+    continued_prompt_entries,
+    padded_prompt_entries,
+    prompt_live_extents,
+    preceding_entry_line,
+    carried_memory,
+    token_mixing_ratios,
+    acceptance_transform,
+    lookup_transform,
+    payload_transform,
+    gating_transform,
+    fading_baseline,
+    fading_left_factor,
+    fading_right_factor,
+    present_reward,
+    group_layer_scaling,
+    group_layer_shift_term,
+    final_transform,
+):
+    z, core = lax.axis_index("z"), lax.axis_index("core")
+    y, x = lax.axis_index("y"), lax.axis_index("x")
+    mp = 2 * y + x
+    is_long = core == 0
+    lines = lax.axis_size("z")
+    group_rows, columns = continued_prompt_entries.shape
+    requests = prompt_live_extents.shape[0]
+    slot_rows = group_rows // requests
+    heads, span = present_reward.shape
+    heads = heads // lines
+    width = heads * span
+    depth = acceptance_transform.shape[0]
+    rows = 2 * lines * group_rows
+
+    kept = jnp.where(is_long, continued_prompt_entries, padded_prompt_entries)
+    given = jnp.where(is_long, padded_prompt_entries, continued_prompt_entries)
+    taken = flipped_core(given)
+    both = jnp.concatenate(
+        [jnp.where(is_long, kept, taken), jnp.where(is_long, taken, kept)], axis=0
+    )
+    half_at = jnp.stack([core * depth, (1 - core) * depth])
+    halves = []
+    for h in range(2):
+        mine = lax.dynamic_slice_in_dim(both, half_at[h], depth, 1)
+        gathered = in_order([mine] + [turned(mine, "z", k) for k in range(1, lines)], z)
+        halves.append(gathered.reshape(rows, depth))
+    a, b = halves
+    a_x, b_y = over_x(a), over_y(b)
+    a_y, b_x = over_y(a), over_x(b)
+    a_xy, b_xy = over_y(a_x), over_x(b_y)
+    chunks = [a, b, a_x, b_x, a_y, b_y, a_xy, b_xy]
+    edge = preceding_entry_line.reshape(2, depth)
+    edge_x, edge_y = over_x(edge), over_y(edge)
+    edge_xy = over_y(edge_x)
+    edges = jnp.stack([edge, edge_x, edge_y, edge_xy])
+    edges = jnp.where(is_long, edges, edges[:, ::-1])
+    first = jnp.where(is_long, edges.astype(f32), 0.0).reshape(8, depth)
+    place = jnp.stack([mp ^ rel for rel in range(4)]).astype(jnp.int32)
+    period = jnp.where(is_long, rows, slot_rows).astype(jnp.int32)[None]
+
+    def chunk_order(whole):
+        split = whole.reshape((4, 2, depth) + whole.shape[1:])
+        parts = []
+        for rel in range(4):
+            for h in range(2):
+                side = core if h == 0 else 1 - core
+                parts.append(split[mp ^ rel, side])
+        return jnp.stack(parts)
+
+    ratios = chunk_order(token_mixing_ratios.T).transpose(2, 0, 1)
+
+    def columns_of(weights):
+        stacked = jnp.stack(weights)
+
+        def block(j):
+            return lax.dynamic_slice_in_dim(stacked, j * width, width, 2)
+
+        pieces = dealt(block, z)
+        return in_order(pieces, z), in_order([flipped_core(piece) for piece in pieces], z)
+
+    own, sibling = columns_of([acceptance_transform, lookup_transform, payload_transform])
+    own_gate, sibling_gate = columns_of([gating_transform])
+    left = fading_left_factor.reshape(4, 2, 1, depth, fading_left_factor.shape[1])
+    left_own = jnp.where(is_long, left[:, 0], left[:, 1])
+    left_sibling = jnp.where(is_long, left[:, 1], left[:, 0])
+
+    def mine_of(vector):
+        return lax.dynamic_slice_in_dim(vector, z * width, width, 0)[None]
+
+    flat = jax.ShapeDtypeStruct((rows, width), f32)
+    (decay,) = project(
+        store_decay,
+        [flat],
+        place,
+        period,
+        chunks,
+        first,
+        ratios[4:5],
+        left_own,
+        left_sibling,
+        lax.dynamic_slice_in_dim(fading_right_factor, z * width, width, 1),
+        mine_of(fading_baseline),
+    )
+    recept, keys, values = project(
+        store_tiles, [flat] * 3, place, period, chunks, first, ratios[:3], own, sibling
+    )
+    extents = lax.all_gather(prompt_live_extents, ("z", "core"), axis=0, tiled=True)
+    extents = jnp.where(is_long, slot_rows, extents).astype(jnp.int32)
+    entered = lax.dynamic_slice_in_dim(carried_memory, z * heads, heads, 0)
+    bonus = lax.dynamic_slice_in_dim(present_reward, z * heads, heads, 0).reshape(1, width)
+    normed, states = sweep(
+        extents,
+        is_long.astype(f32)[None],
+        recept,
+        keys,
+        values,
+        decay,
+        bonus,
+        jnp.where(is_long, entered, 0.0),
+        mine_of(group_layer_scaling),
+        mine_of(group_layer_shift_term),
+    )
+    live = lax.broadcasted_iota(jnp.int32, (rows // slot_rows, slot_rows), 1) < extents[:, None]
+    live = live.reshape(rows, 1).astype(f32)
+    (hidden,) = project(
+        store_hidden,
+        [jax.ShapeDtypeStruct((rows, width), bf16)],
+        place,
+        period,
+        chunks,
+        first,
+        ratios[3:4],
+        own_gate,
+        sibling_gate,
+        normed,
+        live,
+    )
+
+    states = states.reshape(lines, 2, requests, heads, span, span)
+    passed = flipped_core(lax.dynamic_index_in_dim(states, 1 - core, 1, keepdims=False))
+    held = lax.dynamic_index_in_dim(states, core, 1, keepdims=False)
+    bundle = jnp.concatenate(
+        [jnp.where(is_long, held, passed)[:, -1:], jnp.where(is_long, passed, held)], axis=1
+    ).astype(bf16)
+    arrived = in_order(
+        dealt(lambda j: lax.dynamic_index_in_dim(bundle, j, 0, keepdims=False), z), z
+    ).astype(f32)
+    span_states = arrived[:, 0].reshape(1, lines * heads, span, span)
+    request_states = jnp.swapaxes(arrived[:, 1:], 0, 1).reshape(
+        requests, lines * heads, span, span
+    )
+
+    wide_out = 2 * final_transform.shape[1]
+    beside = flipped_core(final_transform)
+    out_weight = jnp.concatenate(
+        [
+            jnp.where(is_long, final_transform, beside),
+            jnp.where(is_long, beside, final_transform),
+        ],
+        axis=1,
+    ).reshape(lines, width, wide_out)
+    pieces = [hidden] + [turned(hidden, "z", k) for k in range(1, lines)]
+    out_weight = jnp.stack(
+        [
+            lax.dynamic_index_in_dim(out_weight, (z - k) % lines, 0, keepdims=False)
+            for k in range(lines)
+        ]
+    )
+    partial = final_product(pieces, out_weight)
+    partial = partial.reshape(2 * lines, 2, group_rows // 2, wide_out)
+    kept_half = lax.dynamic_index_in_dim(partial, x, 1, keepdims=False)
+    sent_half = lax.dynamic_index_in_dim(partial, 1 - x, 1, keepdims=False)
+    summed = kept_half.astype(f32) + over_x(sent_half).astype(f32)
+    summed = summed.reshape(lines, 2, group_rows // 2, wide_out)
+    same_core = lax.dynamic_index_in_dim(summed, core, 1, keepdims=False)
+    other_core = lax.dynamic_index_in_dim(summed, 1 - core, 1, keepdims=False).astype(bf16)
+    from_same = lax.ppermute(same_core.astype(bf16), ("core", "y"), [(1, 0), (2, 3)])
+    from_cross = lax.ppermute(other_core, ("core", "y"), [(1, 2), (2, 1)])
+    from_beside = lax.ppermute(other_core, ("core", "y"), [(0, 2), (3, 1)])
+    mixed_part = (
+        jnp.where(core == y, same_core, 0.0)
+        + from_same.astype(f32)
+        + from_cross.astype(f32)
+        + from_beside.astype(f32)
+    ).astype(bf16)
+    out_pieces = in_order(
+        dealt(lambda j: lax.dynamic_index_in_dim(mixed_part, j, 0, keepdims=False), z), z
+    )
+    mixed = jnp.swapaxes(out_pieces, 0, 1).reshape(1, group_rows // 2, lines * wide_out)
+    return mixed, span_states, request_states
+
+
+def rows_kept_solution(mesh):
     placed = (
         P("seq", "mp"),
         P("seq", "mp"),
@@ -270,3 +714,41 @@
         out_specs=(P("seq", "mp", None), P("seq", "mp", None, None), P("seq", "mp", None, None)),
         check_vma=False,
     )
+
+
+def heads_kept_solution(mesh):
+    seq, mp = mesh.shape["seq"], mesh.shape["mp"]
+    split = Mesh(mesh.devices.reshape(seq // 2, 2, 2, mp // 2), ("z", "core", "y", "x"))
+    s, m = ("z", "core"), ("y", "x")
+    placed = (
+        P(s, m),
+        P(s, m),
+        P(s),
+        P(m),
+        P(m, None, None),
+        P(),
+        P(s, m),
+        P(s, m),
+        P(s, m),
+        P(s, m),
+        P(m),
+        P(),
+        P(None, m),
+        P(m, None),
+        P(m),
+        P(m),
+        P(m, s),
+    )
+    return jax.shard_map(
+        on_core,
+        mesh=split,
+        in_specs=placed,
+        out_specs=(P(s, m, None), P(s, m, None, None), P(s, m, None, None)),
+        check_vma=False,
+    )
+
+
+def solution(mesh):
+    if mesh.shape["mp"] == 4 and mesh.shape["seq"] == 8:
+        return heads_kept_solution(mesh)
+    return rows_kept_solution(mesh)

time: 651 us -> 407 us (0.63); the launches traced: 640 us -> 406 us
  waiting for transfers between devices: 421 us -> 149 us
  starting transfers between devices: 2.66 us -> 127 us
  matrix products: 67.1 us -> 0 us
  Pallas kernels: 0 us -> 60.1 us
  local copies, waits for them, and re-layouts: 77.6 us -> 44.1 us
  other arithmetic: 33.3 us -> 15 us
  blocking collectives: 23.3 us -> 9.16 us
  between operations: 15 us -> 2.13 us
    all_gather x7 -> x0, waiting for transfers between devices: 373 us -> none  [the longest x1 82.2 us: on_device(): full_out = lax.all_gather(final_transform, 'seq', axis=1, tiled=True)]
    ppermute x1 -> x45, waiting for transfers between devices: 0.7 us -> 149 us  [the longest x21 94.3 us: turned(): lax.ppermute(x, axis, [(i, (i + by) % length) for i in range(length)])]
    ppermute x1 -> x45, starting transfers between devices: 2.34 us -> 127 us  [the longest x21 106 us: turned(): lax.ppermute(x, axis, [(i, (i + by) % length) for i in range(length)])]
    dot_general x18 -> x0, matrix products: 67.1 us -> none  [the longest x3 20.2 us: on_device(): jnp.dot(source, piece, preferred_element_type=jnp.float32)]
    pallas_call x0 -> x5, Pallas kernels: none -> 60.1 us  [the longest x3 36.9 us: project(): pl.pallas_call(lambda *refs: project_kernel(count, outs, finish, *refs),...]
    reduce_scatter x1 -> x0, waiting for transfers between devices: 43.9 us -> none  [on_device(): lax.psum_scatter(jnp.dot(hidden, full_out, preferred_element_type=jnp.flo...]
    all_gather x2 -> x0, blocking collectives: 23.3 us -> none  [the longest x1 14.2 us: entering(): pieces = jax.tree.map(lambda part: lax.all_gather(part, axis), value)]
    reshape x9 -> x5, local copies, waits for them, and re-layouts: 16.8 us -> 3.26 us  [the longest x1 1.17 us: on_core(): jnp.swapaxes(out_pieces, 0, 1).reshape(1, group_rows // 2, lines * wide_out)]
  transfers between devices with their start and end apart: 9 -> 45, of which waited for: 8 -> 16; matrix products, arithmetic and copies ran while one was open for 16% -> 11% of each run, Pallas kernels for 0% -> 13%
where the time goes in v1:
time: 407 us; the launch traced here: 406 us
  waiting for transfers between devices  149 us (37%)
  starting transfers between devices  127 us (31%)
  Pallas kernels  60.1 us (15%)
  local copies, waits for them, and re-layouts  44.1 us (11%)
  other arithmetic  15 us (4%)
  blocking collectives  9.16 us (2%)
    ppermute x21, starting transfers between devices, turned(): lax.ppermute(x, axis, [(i, (i + by) % length) for i in range(length)])  106 us
    ppermute x21, waiting for transfers between devices, turned(): lax.ppermute(x, axis, [(i, (i + by) % length) for i in range(length)])  94.3 us
    ppermute x5, waiting for transfers between devices, over_x(): return lax.ppermute(x, 'x', [(0, 1), (1, 0)])  50.6 us
    pallas_call x3, Pallas kernels, project(): pl.pallas_call(lambda *refs: project_kernel(count, outs, finish, *refs),...  36.9 us
    pallas_call x1, Pallas kernels, sweep(): pl.pallas_call(sweep_kernel, out_shape=[jax.ShapeDtypeStruct((rows, width...  16.7 us
    dynamic_update_slice x29, local copies, waits for them, and re-layouts, in_order(): whole = lax.dynamic_update_index_in_dim(whole, piece, (z - k) % length, 0)  14.8 us
    unnamed x1, blocking collectives  9.16 us
  transfers between devices with their start and end apart: 45, of which 16 were waited for; matrix products, arithmetic and copies ran while one was open for 11% of the time, Pallas kernels for 13%

profile of v1, /device:TPU:0, one launch (start us, length us, event | category | flops | bytes accessed | tf_op | source)
XLA Modules:
  0.0 406.2 jit_solution(10511461510683586832)
XLA Ops:
  1.4 2.9 collective-permute-start.13
  4.3 1.5 collective-permute-start.14
  5.8 1.7 broadcast_select_fusion.4
  7.5 2.2 pad_maximum_fusion
  9.7 1.9 broadcast.45.clone
  11.7 1.2 bitcast_dynamic-update-slice_fusion.7
  13.4 2.4 dynamic-slice_bitcast_fusion.6
  15.8 1.5 constant_dynamic-slice_fusion.7
  18.9 2.2 select_bitcast_fusion
  21.2 1.6 dynamic-slice_select_fusion.s_ref
  25.1 9.2 %all-reduce = s32[16]{0:T(128)S(1)} all-reduce(s32[16]{0:T(128)S(1)} %dynamic-update-slice), channel_id=1, replica_groups=mesh['z'=4,'core'=2,'y'=2,'x'=2] {'z','core'}, use_global_device_ids=true, to_apply=%add | all-reduce | flops 16 | bytes 128
  37.1 1.3 dynamic_slice.151
  38.4 1.3 dynamic_slice.154
  39.8 1.3 dynamic_slice.155
  41.8 1.3 reshape.151.refs_15_
  45.1 2.6 collective-permute-start.18
  50.7 3.5 collective-permute-done.16
  54.2 8.2 %collective-permute-start.5 = (bf16[256,512]{1,0:T(8,128)(2,1)S(1)}, bf16[256,512]{1,0:T(8,128)(2,1)S(1)}, u32[]{:S(2)}, u32[]{:S(2)}) collective-permute-start(bf16[256,512]{1,0:T(8,128)(2,1)S(1)} %get-tuple-element.18), channel_id=1, source_target_pairs={{0,16},{8,24},{16,0},{24,8},{1,17},{9,25},{17,1},{25,9},{2,18},{10... | collective-permute-start | bytes 786440 | tf_op jit(solution)/shard_map/ppermute | solution.py:471
  62.5 9.3 %collective-permute-done.17 = bf16[1,512,256]{2,1,0:T(8,128)(2,1)S(1)} collective-permute-done((bf16[1,512,256]{2,1,0:T(8,128)(2,1)S(1)}, bf16[1,512,256]{2,1,0:T(8,128)(2,1)S(1)}, u32[]{:S(2)}, u32[]{:S(2)}) %collective-permute-start.17) | collective-permute-done | bytes 262176 | tf_op jit(solution)/shard_map/ppermute | solution.py:471
  71.8 7.0 %collective-permute-start.6 = (bf16[256,512]{1,0:T(8,128)(2,1)S(1)}, bf16[256,512]{1,0:T(8,128)(2,1)S(1)}, u32[]{:S(2)}, u32[]{:S(2)}) collective-permute-start(bf16[256,512]{1,0:T(8,128)(2,1)S(1)} %get-tuple-element.18), channel_id=1, source_target_pairs={{0,24},{8,0},{16,8},{24,16},{1,25},{9,1},{17,9},{25,17},{2,26},{10... | collective-permute-start | bytes 786440 | tf_op jit(solution)/shard_map/ppermute | solution.py:471
  79.0 4.2 %collective-permute-start.1 = (bf16[256,512]{1,0:T(8,128)(2,1)S(1)}, bf16[256,512]{1,0:T(8,128)(2,1)S(1)}, u32[]{:S(2)}, u32[]{:S(2)}) collective-permute-start(bf16[256,512]{1,0:T(8,128)(2,1)S(1)} %get-tuple-element.20), channel_id=1, source_target_pairs={{0,8},{8,16},{16,24},{24,0},{1,9},{9,17},{17,25},{25,1},{2,10},{10... | collective-permute-start | bytes 786440 | tf_op jit(solution)/shard_map/ppermute | solution.py:471
  83.3 2.6 collective-permute-start.2
  85.8 10.9 %collective-permute-done.5 = bf16[256,512]{1,0:T(8,128)(2,1)S(1)} collective-permute-done((bf16[256,512]{1,0:T(8,128)(2,1)S(1)}, bf16[256,512]{1,0:T(8,128)(2,1)S(1)}, u32[]{:S(2)}, u32[]{:S(2)}) %collective-permute-start.5) | collective-permute-done | bytes 262176 | tf_op jit(solution)/shard_map/ppermute | solution.py:471
  96.7 1.8 collective-permute-start.3
  99.2 8.8 %collective-permute-done.2 = bf16[256,512]{1,0:T(8,128)(2,1)S(1)} collective-permute-done((bf16[256,512]{1,0:T(8,128)(2,1)S(1)}, bf16[256,512]{1,0:T(8,128)(2,1)S(1)}, u32[]{:S(2)}, u32[]{:S(2)}) %collective-permute-start.2) | collective-permute-done | bytes 262176 | tf_op jit(solution)/shard_map/ppermute | solution.py:471
  108.0 2.0 collective-permute-start.23
  110.1 19.5 %collective-permute-start.24 = (bf16[3,512,256]{2,1,0:T(8,128)(2,1)S(1)}, bf16[3,512,256]{2,1,0:T(8,128)(2,1)S(1)}, u32[]{:S(2)}, u32[]{:S(2)}) collective-permute-start(bf16[3,512,256]{2,1,0:T(8,128)(2,1)S(1)} %copy-done.18), channel_id=1, source_target_pairs={{0,16},{8,24},{16,0},{24,8},{1,17},{9,25},{17,1},{25,9},{2,18},{10... | collective-permute-start | bytes 2359304 | tf_op jit(solution)/shard_map/ppermute | solution.py:471
  129.6 3.4 collective-permute-start.25
  133.1 1.5 collective-permute-done.22
  134.5 1.5 collective-permute-start.10
  136.7 28.2 %collective-permute-done.24 = bf16[3,512,256]{2,1,0:T(8,128)(2,1)S(1)} collective-permute-done((bf16[3,512,256]{2,1,0:T(8,128)(2,1)S(1)}, bf16[3,512,256]{2,1,0:T(8,128)(2,1)S(1)}, u32[]{:S(2)}, u32[]{:S(2)}) %collective-permute-start.24) | collective-permute-done | bytes 786464 | tf_op jit(solution)/shard_map/ppermute | solution.py:471
  169.0 1.5 collective-permute-start.9
  170.5 1.5 collective-permute-start.12
  172.8 1.2 bitcast_dynamic-update-slice_fusion.3
  174.2 20.2 %collective-permute-done.8.refs_5_ = bf16[1024,512]{1,0:T(8,128)(2,1)S(1)} collective-permute-done((bf16[1024,512]{1,0:T(8,128)(2,1)S(1)}, bf16[1024,512]{1,0:T(8,128)(2,1)S(1)}, u32[]{:S(2)}, u32[]{:S(2)}) %collective-permute-start.8) | collective-permute-done | bytes 1048608 | tf_op jit(solution)/shard_map/ppermute | solution.py:479
  195.0 21.5 %collective-permute-done.12.refs_9_ = bf16[1024,512]{1,0:T(8,128)(2,1)S(1)} collective-permute-done((bf16[1024,512]{1,0:T(8,128)(2,1)S(1)}, bf16[1024,512]{1,0:T(8,128)(2,1)S(1)}, u32[]{:S(2)}, u32[]{:S(2)}) %collective-permute-start.12) | collective-permute-done | bytes 1048608 | tf_op jit(solution)/shard_map/ppermute | solution.py:479
  218.5 15.8 %shard_map.184 = (f32[1024,256]{1,0:T(8,128)}, f32[1024,256]{1,0:T(8,128)}, f32[1024,256]{1,0:T(8,128)}) custom-call(s32[4]{0:T(128)} %pad_add_fusion.refs_0_, s32[1]{0:T(128)} %bitcast.4.refs_1_, bf16[1024,512]{1,0:T(8,128)(2,1)} %bitcast.210, bf16[1024,512]{1,0:T(8,128)(2,1)} %bitcast.215, bf16[1024,512]{1,0:T(8,128)(2,1)} %copy-done.6, ...), custom_call_target="tpu_custom_call" | custom-call | tf_op jit(solution)/shard_map/pallas_call | solution.py:326
  234.3 10.8 %shard_map.185.w_ref = f32[1024,256]{1,0:T(8,128)} custom-call(s32[4]{0:T(128)} %pad_add_fusion.refs_0_, s32[1]{0:T(128)} %bitcast.4.refs_1_, bf16[1024,512]{1,0:T(8,128)(2,1)} %bitcast.211, bf16[1024,512]{1,0:T(8,128)(2,1)} %bitcast.216, bf16[1024,512]{1,0:T(8,128)(2,1)} %copy-done.6, bf16[1024,512]{1,0:T(8,128)(2,1)} %copy-done.7, ...), custom_call_target="tpu_custom_call" | custom-call | tf_op jit(solution)/shard_map/pallas_call | solution.py:326
  245.0 16.7 %shard_map.186 = (f32[1024,256]{1,0:T(8,128)}, f32[16,4,64,64]{3,2,1,0:T(8,128)}) custom-call(s32[16]{0:T(128)} %copy-done.28, f32[1]{0:T(128)} %bitcast.41.carry, f32[1024,256]{1,0:T(8,128)} %get-tuple-element.8.r_ref, f32[1024,256]{1,0:T(8,128)} %get-tuple-element.9.k_ref, f32[1024,256]{1,0:T(8,128)} %get-tuple-element.10.v_ref, ...), custom_call_target="tpu_custom_call" | custom-call | tf_op jit(solution)/shard_map/pallas_call | solution.py:435
  261.8 10.3 %shard_map.187.h0 = bf16[1024,256]{1,0:T(8,128)(2,1)} custom-call(s32[4]{0:T(128)} %pad_add_fusion.refs_0_, s32[1]{0:T(128)} %bitcast.4.refs_1_, bf16[1024,512]{1,0:T(8,128)(2,1)} %bitcast.212, bf16[1024,512]{1,0:T(8,128)(2,1)} %bitcast.217, bf16[1024,512]{1,0:T(8,128)(2,1)} %copy-done.6, bf16[1024,512]{1,0:T(8,128)(2,1)} %copy-done.7, ...), custom_call_target="tpu_custom_call" | custom-call | tf_op jit(solution)/shard_map/pallas_call | solution.py:326
  272.1 15.7 %collective-permute-start.30 = (bf16[1024,256]{1,0:T(8,128)(2,1)}, bf16[1024,256]{1,0:T(8,128)(2,1)S(1)}, u32[]{:S(2)}, u32[]{:S(2)}) collective-permute-start(bf16[1024,256]{1,0:T(8,128)(2,1)} %shard_map.187.h0), channel_id=1, source_target_pairs={{0,8},{8,16},{16,24},{24,0},{1,9},{9,17},{17,25},{25,1},{2,10},{10... | collective-permute-start | bytes 1572872 | tf_op jit(solution)/shard_map/ppermute | solution.py:471
  287.7 3.4 collective-permute-start.31
  291.8 1.6 pad_maximum_fusion.2.weight
  293.4 10.3 %collective-permute-done.30.h1 = bf16[1024,256]{1,0:T(8,128)(2,1)S(1)} collective-permute-done((bf16[1024,256]{1,0:T(8,128)(2,1)}, bf16[1024,256]{1,0:T(8,128)(2,1)S(1)}, u32[]{:S(2)}, u32[]{:S(2)}) %collective-permute-start.30) | collective-permute-done | bytes 524320 | tf_op jit(solution)/shard_map/ppermute | solution.py:471
  303.7 21.5 %collective-permute-done.31.h2 = bf16[1024,256]{1,0:T(8,128)(2,1)S(1)} collective-permute-done((bf16[1024,256]{1,0:T(8,128)(2,1)}, bf16[1024,256]{1,0:T(8,128)(2,1)S(1)}, u32[]{:S(2)}, u32[]{:S(2)}) %collective-permute-start.31) | collective-permute-done | bytes 524320 | tf_op jit(solution)/shard_map/ppermute | solution.py:471
  326.8 6.5 %shard_map.188 = bf16[1024,1024]{1,0:T(8,128)(2,1)} custom-call(bf16[1024,256]{1,0:T(8,128)(2,1)} %shard_map.187.h0, bf16[1024,256]{1,0:T(8,128)(2,1)} %copy-done.20, bf16[1024,256]{1,0:T(8,128)(2,1)} %copy-done.21, bf16[1024,256]{1,0:T(8,128)(2,1)} %copy-done.22, bf16[4,256,1024]{2,1,0:T(8,128)(2,1)} %pad_maximum_fusion.2.weight), custom_call_target="tpu_custom_call" | custom-call | tf_op jit(solution)/shard_map/pallas_call | solution.py:460
  333.2 2.3 dynamic-slice_bitcast_fusion.2
  336.0 1.4 dynamic-slice_bitcast_fusion
  337.5 1.9 collective-permute-done.41
  339.4 1.3 select_convert_fusion
  340.9 11.0 %collective-permute-start.42 = (bf16[3,4,64,64]{3,2,1,0:T(8,128)(2,1)S(1)}, bf16[3,4,64,64]{3,2,1,0:T(8,128)(2,1)S(1)}, u32[]{:S(2)}, u32[]{:S(2)}) collective-permute-start(bf16[3,4,64,64]{3,2,1,0:T(8,128)(2,1)S(1)} %get-tuple-element.39), channel_id=1, source_target_pairs={{0,8},{8,16},{16,24},{24,0},{1,9},{9,17},{17,25},{25,1},{2,10},{10... | collective-permute-start | bytes 294920 | tf_op jit(solution)/shard_map/ppermute | solution.py:471
  351.9 8.9 %collective-permute-done.34 = bf16[8,64,1024]{2,1,0:T(8,128)(2,1)} collective-permute-done((bf16[8,64,1024]{2,1,0:T(8,128)(2,1)}, bf16[8,64,1024]{2,1,0:T(8,128)(2,1)}, u32[]{:S(2)}, u32[]{:S(2)}) %collective-permute-start.34) | collective-permute-done | bytes 1048608 | tf_op jit(solution)/shard_map/ppermute | solution.py:479
  360.8 1.6 convert_add_fusion
  363.3 4.8 %collective-permute-start.37 = (bf16[4,64,1024]{2,1,0:T(8,128)(2,1)S(1)}, bf16[4,64,1024]{2,1,0:T(8,128)(2,1)S(1)}, u32[]{:S(2)}, u32[]{:S(2)}) collective-permute-start(bf16[4,64,1024]{2,1,0:T(8,128)(2,1)S(1)} %get-tuple-element.25), channel_id=1, source_target_pairs={{0,4},{6,2},{1,5},{7,3},{8,12},{14,10},{9,13},{15,11},{16,20},{22,... | collective-permute-start | bytes 1572872 | tf_op jit(solution)/shard_map/ppermute | solution.py:676
  368.1 1.3 collective-permute-start.35
  369.7 9.3 %collective-permute-start.44 = (bf16[3,4,64,64]{3,2,1,0:T(8,128)(2,1)S(1)}, bf16[3,4,64,64]{3,2,1,0:T(8,128)(2,1)S(1)}, u32[]{:S(2)}, u32[]{:S(2)}) collective-permute-start(bf16[3,4,64,64]{3,2,1,0:T(8,128)(2,1)S(1)} %get-tuple-element.38), channel_id=1, source_target_pairs={{0,24},{8,0},{16,8},{24,16},{1,25},{9,1},{17,9},{25,17},{2,26},{10... | collective-permute-start | bytes 294920 | tf_op jit(solution)/shard_map/ppermute | solution.py:471
  379.6 11.3 %collective-permute-start.38 = (bf16[64,1024]{1,0:T(8,128)(2,1)S(1)}, bf16[64,1024]{1,0:T(8,128)(2,1)S(1)}, u32[]{:S(2)}, u32[]{:S(2)}) collective-permute-start(bf16[64,1024]{1,0:T(8,128)(2,1)S(1)} %get-tuple-element.45), channel_id=1, source_target_pairs={{0,8},{8,16},{16,24},{24,0},{1,9},{9,17},{17,25},{25,1},{2,10},{10... | collective-permute-start | bytes 393224 | tf_op jit(solution)/shard_map/ppermute | solution.py:471
  390.9 2.4 collective-permute-start.40
  395.6 1.7 dynamic_update_slice.125
  397.6 1.8 collective-permute-done.39
  399.8 1.7 dynamic_update_slice.126
  401.6 1.7 dynamic_update_slice.127
  403.3 1.7 dynamic_update_slice.128
  405.1 1.2 reshape.140
  (185 shorter events, 29.7 us)
Async XLA Ops:
  1.4 34.6 %collective-permute-start.13 = (bf16[2,512]{1,0:T(2,128)(2,1)S(1)}, bf16[2,512]{1,0:T(2,128)(2,1)S(1)}, u32[]{:S(2)}, u32[]{:S(2)}) collective-permute-start(bf16[2,512]{1,0:T(2,128)(2,1)S(1)} %reshape.132), channel_id=1, source_target_pairs={{0,1},{1,0},{2,3},{3,2},{4,5},{5,4},{6,7},{7,6},{8,9},{9,8},{10,11... | collective-permute-start | bytes 6152 | tf_op jit(solution)/shard_map/ppermute | solution.py:479
  4.3 38.7 %collective-permute-start.14 = (bf16[2,512]{1,0:T(2,128)(2,1)S(1)}, bf16[2,512]{1,0:T(2,128)(2,1)S(1)}, u32[]{:S(2)}, u32[]{:S(2)}) collective-permute-start(bf16[2,512]{1,0:T(2,128)(2,1)S(1)} %reshape.132), channel_id=1, source_target_pairs={{0,2},{2,0},{1,3},{3,1},{4,6},{6,4},{5,7},{7,5},{8,10},{10,8},{9,1... | collective-permute-start | bytes 6152 | tf_op jit(solution)/shard_map/ppermute | solution.py:483
  7.5 37.6 %collective-permute-start = (bf16[128,1024]{1,0:T(8,128)(2,1)}, bf16[128,1024]{1,0:T(8,128)(2,1)}, u32[]{:S(2)}, u32[]{:S(2)}) collective-permute-start(bf16[128,1024]{1,0:T(8,128)(2,1)} %broadcast_select_fusion.4), channel_id=1, source_target_pairs={{0,4},{4,0},{1,5},{5,1},{2,6},{6,2},{3,7},{7,3},{8,12},{12,8},{9,1... | collective-permute-start | bytes 786440 | tf_op jit(solution)/shard_map/ppermute | solution.py:475
  12.9 123.1 %collective-permute-start.26 = (bf16[3,512,256]{2,1,0:T(8,128)(2,1)}, bf16[3,512,256]{2,1,0:T(8,128)(2,1)}, u32[]{:S(2)}, u32[]{:S(2)}) collective-permute-start(bf16[3,512,256]{2,1,0:T(8,128)(2,1)} %get-tuple-element.16), channel_id=1, source_target_pairs={{0,4},{4,0},{1,5},{5,1},{2,6},{6,2},{3,7},{7,3},{8,12},{12,8},{9,1... | collective-permute-start | bytes 2359304 | tf_op jit(solution)/shard_map/ppermute | solution.py:475
  15.8 33.1 %collective-permute-start.19 = (bf16[1,512,256]{2,1,0:T(8,128)(2,1)}, bf16[1,512,256]{2,1,0:T(8,128)(2,1)}, u32[]{:S(2)}, u32[]{:S(2)}) collective-permute-start(bf16[1,512,256]{2,1,0:T(8,128)(2,1)} %get-tuple-element.34), channel_id=1, source_target_pairs={{0,4},{4,0},{1,5},{5,1},{2,6},{6,2},{3,7},{7,3},{8,12},{12,8},{9,1... | collective-permute-start | bytes 786440 | tf_op jit(solution)/shard_map/ppermute | solution.py:475
  17.3 19.2 %copy-start.27 = (bf16[1024]{0:T(1024)(128)(2,1)S(1)}, bf16[1024]{0:T(1024)(128)(2,1)}, u32[]{:S(2)}) copy-start(bf16[1024]{0:T(1024)(128)(2,1)} %param.20) | copy-start | bytes 6148
  17.3 25.8 %copy-start.25 = (bf16[1,512,256]{2,1,0:T(8,128)(2,1)S(1)}, bf16[1,512,256]{2,1,0:T(8,128)(2,1)}, u32[]{:S(2)}) copy-start(bf16[1,512,256]{2,1,0:T(8,128)(2,1)} %get-tuple-element.35) | copy-start | bytes 786436
  17.3 26.6 %copy-start.24 = (bf16[1,512,256]{2,1,0:T(8,128)(2,1)S(1)}, bf16[1,512,256]{2,1,0:T(8,128)(2,1)}, u32[]{:S(2)}) copy-start(bf16[1,512,256]{2,1,0:T(8,128)(2,1)} %get-tuple-element.37) | copy-start | bytes 786436
  17.3 27.8 %copy-start.23 = (bf16[1,512,256]{2,1,0:T(8,128)(2,1)S(1)}, bf16[1,512,256]{2,1,0:T(8,128)(2,1)}, u32[]{:S(2)}) copy-start(bf16[1,512,256]{2,1,0:T(8,128)(2,1)} %get-tuple-element.36) | copy-start | bytes 786436
  17.3 30.4 %copy-start.15 = (bf16[128,1024]{1,0:T(8,128)(2,1)S(1)}, bf16[128,1024]{1,0:T(8,128)(2,1)}, u32[]{:S(2)}) copy-start(bf16[128,1024]{1,0:T(8,128)(2,1)} %param.18) | copy-start | bytes 786436
  17.3 30.4 %copy-start.16 = (bf16[128,1024]{1,0:T(8,128)(2,1)S(1)}, bf16[128,1024]{1,0:T(8,128)(2,1)}, u32[]{:S(2)}) copy-start(bf16[128,1024]{1,0:T(8,128)(2,1)} %param.17) | copy-start | bytes 786436
  35.9 8.0 %collective-permute-start.15 = (bf16[2,512]{1,0:T(2,128)(2,1)S(1)}, bf16[2,512]{1,0:T(2,128)(2,1)S(1)}, u32[]{:S(2)}, u32[]{:S(2)}) collective-permute-start(bf16[2,512]{1,0:T(2,128)(2,1)S(1)} %collective-permute-done.13), channel_id=1, source_target_pairs={{0,2},{2,0},{1,3},{3,1},{4,6},{6,4},{5,7},{7,5},{8,10},{10,8},{9,1... | collective-permute-start | bytes 6152 | tf_op jit(solution)/shard_map/ppermute | solution.py:483
  43.0 11.1 %collective-permute-start.16 = (bf16[1,512,256]{2,1,0:T(8,128)(2,1)S(1)}, bf16[1,512,256]{2,1,0:T(8,128)(2,1)S(1)}, u32[]{:S(2)}, u32[]{:S(2)}) collective-permute-start(bf16[1,512,256]{2,1,0:T(8,128)(2,1)S(1)} %copy-done.25), channel_id=1, source_target_pairs={{0,8},{8,16},{16,24},{24,0},{1,9},{9,17},{17,25},{25,1},{2,10},{10... | collective-permute-start | bytes 786440 | tf_op jit(solution)/shard_map/ppermute | solution.py:471
  43.9 27.9 %collective-permute-start.17 = (bf16[1,512,256]{2,1,0:T(8,128)(2,1)S(1)}, bf16[1,512,256]{2,1,0:T(8,128)(2,1)S(1)}, u32[]{:S(2)}, u32[]{:S(2)}) collective-permute-start(bf16[1,512,256]{2,1,0:T(8,128)(2,1)S(1)} %copy-done.24), channel_id=1, source_target_pairs={{0,16},{8,24},{16,0},{24,8},{1,17},{9,25},{17,1},{25,9},{2,18},{10... | collective-permute-start | bytes 786440 | tf_op jit(solution)/shard_map/ppermute | solution.py:471
  45.1 33.9 %collective-permute-start.18 = (bf16[1,512,256]{2,1,0:T(8,128)(2,1)S(1)}, bf16[1,512,256]{2,1,0:T(8,128)(2,1)S(1)}, u32[]{:S(2)}, u32[]{:S(2)}) collective-permute-start(bf16[1,512,256]{2,1,0:T(8,128)(2,1)S(1)} %copy-done.23), channel_id=1, source_target_pairs={{0,24},{8,0},{16,8},{24,16},{1,25},{9,1},{17,9},{25,17},{2,26},{10... | collective-permute-start | bytes 786440 | tf_op jit(solution)/shard_map/ppermute | solution.py:471
  48.9 34.4 %collective-permute-start.4 = (bf16[256,512]{1,0:T(8,128)(2,1)S(1)}, bf16[256,512]{1,0:T(8,128)(2,1)S(1)}, u32[]{:S(2)}, u32[]{:S(2)}) collective-permute-start(bf16[256,512]{1,0:T(8,128)(2,1)S(1)} %get-tuple-element.18), channel_id=1, source_target_pairs={{0,8},{8,16},{16,24},{24,0},{1,9},{9,17},{17,25},{25,1},{2,10},{10... | collective-permute-start | bytes 786440 | tf_op jit(solution)/shard_map/ppermute | solution.py:471
  49.6 58.4 %copy-start.19 = (bf16[3,512,256]{2,1,0:T(8,128)(2,1)S(1)}, bf16[3,512,256]{2,1,0:T(8,128)(2,1)}, u32[]{:S(2)}) copy-start(bf16[3,512,256]{2,1,0:T(8,128)(2,1)} %get-tuple-element.23) | copy-start | bytes 2359300
  50.6 59.4 %copy-start.18 = (bf16[3,512,256]{2,1,0:T(8,128)(2,1)S(1)}, bf16[3,512,256]{2,1,0:T(8,128)(2,1)}, u32[]{:S(2)}) copy-start(bf16[3,512,256]{2,1,0:T(8,128)(2,1)} %get-tuple-element.22) | copy-start | bytes 2359300
  50.7 78.9 %copy-start.17 = (bf16[3,512,256]{2,1,0:T(8,128)(2,1)S(1)}, bf16[3,512,256]{2,1,0:T(8,128)(2,1)}, u32[]{:S(2)}) copy-start(bf16[3,512,256]{2,1,0:T(8,128)(2,1)} %get-tuple-element.21) | copy-start | bytes 2359300
  54.2 42.5 %collective-permute-start.5 = (bf16[256,512]{1,0:T(8,128)(2,1)S(1)}, bf16[256,512]{1,0:T(8,128)(2,1)S(1)}, u32[]{:S(2)}, u32[]{:S(2)}) collective-permute-start(bf16[256,512]{1,0:T(8,128)(2,1)S(1)} %get-tuple-element.18), channel_id=1, source_target_pairs={{0,16},{8,24},{16,0},{24,8},{1,17},{9,25},{17,1},{25,9},{2,18},{10... | collective-permute-start | bytes 786440 | tf_op jit(solution)/shard_map/ppermute | solution.py:471
  71.8 26.7 %collective-permute-start.6 = (bf16[256,512]{1,0:T(8,128)(2,1)S(1)}, bf16[256,512]{1,0:T(8,128)(2,1)S(1)}, u32[]{:S(2)}, u32[]{:S(2)}) collective-permute-start(bf16[256,512]{1,0:T(8,128)(2,1)S(1)} %get-tuple-element.18), channel_id=1, source_target_pairs={{0,24},{8,0},{16,8},{24,16},{1,25},{9,1},{17,9},{25,17},{2,26},{10... | collective-permute-start | bytes 786440 | tf_op jit(solution)/shard_map/ppermute | solution.py:471
  79.0 19.6 %collective-permute-start.1 = (bf16[256,512]{1,0:T(8,128)(2,1)S(1)}, bf16[256,512]{1,0:T(8,128)(2,1)S(1)}, u32[]{:S(2)}, u32[]{:S(2)}) collective-permute-start(bf16[256,512]{1,0:T(8,128)(2,1)S(1)} %get-tuple-element.20), channel_id=1, source_target_pairs={{0,8},{8,16},{16,24},{24,0},{1,9},{9,17},{17,25},{25,1},{2,10},{10... | collective-permute-start | bytes 786440 | tf_op jit(solution)/shard_map/ppermute | solution.py:471
  83.2 51.3 %copy-start.13 = (bf16[4,1,512,256]{3,2,1,0:T(8,128)(2,1)}, bf16[4,1,512,256]{3,2,1,0:T(8,128)(2,1)S(1)}, u32[]{:S(2)}) copy-start(bf16[4,1,512,256]{3,2,1,0:T(8,128)(2,1)S(1)} %bitcast_dynamic-update-slice_fusion.12.refs_12_) | copy-start | bytes 3145732
  83.3 24.8 %collective-permute-start.2 = (bf16[256,512]{1,0:T(8,128)(2,1)S(1)}, bf16[256,512]{1,0:T(8,128)(2,1)S(1)}, u32[]{:S(2)}, u32[]{:S(2)}) collective-permute-start(bf16[256,512]{1,0:T(8,128)(2,1)S(1)} %get-tuple-element.20), channel_id=1, source_target_pairs={{0,16},{8,24},{16,0},{24,8},{1,17},{9,25},{17,1},{25,9},{2,18},{10... | collective-permute-start | bytes 786440 | tf_op jit(solution)/shard_map/ppermute | solution.py:471
  96.7 13.3 %collective-permute-start.3 = (bf16[256,512]{1,0:T(8,128)(2,1)S(1)}, bf16[256,512]{1,0:T(8,128)(2,1)S(1)}, u32[]{:S(2)}, u32[]{:S(2)}) collective-permute-start(bf16[256,512]{1,0:T(8,128)(2,1)S(1)} %get-tuple-element.20), channel_id=1, source_target_pairs={{0,24},{8,0},{16,8},{24,16},{1,25},{9,1},{17,9},{25,17},{2,26},{10... | collective-permute-start | bytes 786440 | tf_op jit(solution)/shard_map/ppermute | solution.py:471
  98.5 31.1 %collective-permute-start.20 = (bf16[1,512,256]{2,1,0:T(8,128)(2,1)S(1)}, bf16[1,512,256]{2,1,0:T(8,128)(2,1)S(1)}, u32[]{:S(2)}, u32[]{:S(2)}) collective-permute-start(bf16[1,512,256]{2,1,0:T(8,128)(2,1)S(1)} %collective-permute-done.16), channel_id=1, source_target_pairs={{0,4},{4,0},{1,5},{5,1},{2,6},{6,2},{3,7},{7,3},{8,12},{12,8},{9,1... | collective-permute-start | bytes 786440 | tf_op jit(solution)/shard_map/ppermute | solution.py:475
  98.6 69.7 %copy-start.3 = (bf16[4,256,512]{2,1,0:T(8,128)(2,1)}, bf16[4,256,512]{2,1,0:T(8,128)(2,1)S(1)}, u32[]{:S(2)}) copy-start(bf16[4,256,512]{2,1,0:T(8,128)(2,1)S(1)} %bitcast_dynamic-update-slice_fusion.16) | copy-start | bytes 3145732
  98.7 34.3 %collective-permute-start.21 = (bf16[1,512,256]{2,1,0:T(8,128)(2,1)S(1)}, bf16[1,512,256]{2,1,0:T(8,128)(2,1)S(1)}, u32[]{:S(2)}, u32[]{:S(2)}) collective-permute-start(bf16[1,512,256]{2,1,0:T(8,128)(2,1)S(1)} %collective-permute-done.17), channel_id=1, source_target_pairs={{0,4},{4,0},{1,5},{5,1},{2,6},{6,2},{3,7},{7,3},{8,12},{12,8},{9,1... | collective-permute-start | bytes 786440 | tf_op jit(solution)/shard_map/ppermute | solution.py:475
  108.0 28.6 %collective-permute-start.23 = (bf16[3,512,256]{2,1,0:T(8,128)(2,1)S(1)}, bf16[3,512,256]{2,1,0:T(8,128)(2,1)S(1)}, u32[]{:S(2)}, u32[]{:S(2)}) collective-permute-start(bf16[3,512,256]{2,1,0:T(8,128)(2,1)S(1)} %copy-done.19), channel_id=1, source_target_pairs={{0,8},{8,16},{16,24},{24,0},{1,9},{9,17},{17,25},{25,1},{2,10},{10... | collective-permute-start | bytes 2359304 | tf_op jit(solution)/shard_map/ppermute | solution.py:471
  110.1 54.9 %collective-permute-start.24 = (bf16[3,512,256]{2,1,0:T(8,128)(2,1)S(1)}, bf16[3,512,256]{2,1,0:T(8,128)(2,1)S(1)}, u32[]{:S(2)}, u32[]{:S(2)}) collective-permute-start(bf16[3,512,256]{2,1,0:T(8,128)(2,1)S(1)} %copy-done.18), channel_id=1, source_target_pairs={{0,16},{8,24},{16,0},{24,8},{1,17},{9,25},{17,1},{25,9},{2,18},{10... | collective-permute-start | bytes 2359304 | tf_op jit(solution)/shard_map/ppermute | solution.py:471
  129.6 35.3 %collective-permute-start.25 = (bf16[3,512,256]{2,1,0:T(8,128)(2,1)S(1)}, bf16[3,512,256]{2,1,0:T(8,128)(2,1)S(1)}, u32[]{:S(2)}, u32[]{:S(2)}) collective-permute-start(bf16[3,512,256]{2,1,0:T(8,128)(2,1)S(1)} %copy-done.17), channel_id=1, source_target_pairs={{0,24},{8,0},{16,8},{24,16},{1,25},{9,1},{17,9},{25,17},{2,26},{10... | collective-permute-start | bytes 2359304 | tf_op jit(solution)/shard_map/ppermute | solution.py:471
  133.0 1.5 collective-permute-start.22
  133.0 36.0 %copy-start.2 = (bf16[4,256,512]{2,1,0:T(8,128)(2,1)}, bf16[4,256,512]{2,1,0:T(8,128)(2,1)S(1)}, u32[]{:S(2)}) copy-start(bf16[4,256,512]{2,1,0:T(8,128)(2,1)S(1)} %bitcast_dynamic-update-slice_fusion.20) | copy-start | bytes 3145732
  133.0 35.3 %copy-start.14 = (bf16[1024,512]{1,0:T(8,128)(2,1)S(1)}, bf16[1024,512]{1,0:T(8,128)(2,1)}, u32[]{:S(2)}) copy-start(bf16[1024,512]{1,0:T(8,128)(2,1)} %param.33) | copy-start | bytes 3145732
  134.5 33.8 %collective-permute-start.10 = (bf16[1024,512]{1,0:T(8,128)(2,1)S(1)}, bf16[1024,512]{1,0:T(8,128)(2,1)S(1)}, u32[]{:S(2)}, u32[]{:S(2)}) collective-permute-start(bf16[1024,512]{1,0:T(8,128)(2,1)S(1)} %bitcast.213), channel_id=1, source_target_pairs={{0,2},{2,0},{1,3},{3,1},{4,6},{6,4},{5,7},{7,5},{8,10},{10,8},{9,1... | collective-permute-start | bytes 3145736 | tf_op jit(solution)/shard_map/ppermute | solution.py:483
  136.1 32.3 %collective-permute-start.7 = (bf16[1024,512]{1,0:T(8,128)(2,1)S(1)}, bf16[1024,512]{1,0:T(8,128)(2,1)S(1)}, u32[]{:S(2)}, u32[]{:S(2)}) collective-permute-start(bf16[1024,512]{1,0:T(8,128)(2,1)S(1)} %bitcast.208), channel_id=1, source_target_pairs={{0,1},{1,0},{2,3},{3,2},{4,5},{5,4},{6,7},{7,6},{8,9},{9,8},{10,11... | collective-permute-start | bytes 3145736 | tf_op jit(solution)/shard_map/ppermute | solution.py:479
  136.6 35.4 %copy-start.12 = (bf16[4,1,512,256]{3,2,1,0:T(8,128)(2,1)}, bf16[4,1,512,256]{3,2,1,0:T(8,128)(2,1)S(1)}, u32[]{:S(2)}) copy-start(bf16[4,1,512,256]{3,2,1,0:T(8,128)(2,1)S(1)} %bitcast_dynamic-update-slice_fusion.8.refs_13_) | copy-start | bytes 3145732
  136.7 32.3 %collective-permute-start.27 = (bf16[3,512,256]{2,1,0:T(8,128)(2,1)S(1)}, bf16[3,512,256]{2,1,0:T(8,128)(2,1)S(1)}, u32[]{:S(2)}, u32[]{:S(2)}) collective-permute-start(bf16[3,512,256]{2,1,0:T(8,128)(2,1)S(1)} %collective-permute-done.23), channel_id=1, source_target_pairs={{0,4},{4,0},{1,5},{5,1},{2,6},{6,2},{3,7},{7,3},{8,12},{12,8},{9,1... | collective-permute-start | bytes 2359304 | tf_op jit(solution)/shard_map/ppermute | solution.py:475
  164.9 5.6 %collective-permute-start.28 = (bf16[3,512,256]{2,1,0:T(8,128)(2,1)S(1)}, bf16[3,512,256]{2,1,0:T(8,128)(2,1)S(1)}, u32[]{:S(2)}, u32[]{:S(2)}) collective-permute-start(bf16[3,512,256]{2,1,0:T(8,128)(2,1)S(1)} %collective-permute-done.24), channel_id=1, source_target_pairs={{0,4},{4,0},{1,5},{5,1},{2,6},{6,2},{3,7},{7,3},{8,12},{12,8},{9,1... | collective-permute-start | bytes 2359304 | tf_op jit(solution)/shard_map/ppermute | solution.py:475
  164.9 7.1 %collective-permute-start.29 = (bf16[3,512,256]{2,1,0:T(8,128)(2,1)S(1)}, bf16[3,512,256]{2,1,0:T(8,128)(2,1)S(1)}, u32[]{:S(2)}, u32[]{:S(2)}) collective-permute-start(bf16[3,512,256]{2,1,0:T(8,128)(2,1)S(1)} %collective-permute-done.25), channel_id=1, source_target_pairs={{0,4},{4,0},{1,5},{5,1},{2,6},{6,2},{3,7},{7,3},{8,12},{12,8},{9,1... | collective-permute-start | bytes 2359304 | tf_op jit(solution)/shard_map/ppermute | solution.py:475
  168.3 122.9 %collective-permute-start.33 = (bf16[1024,512]{1,0:T(8,128)(2,1)S(1)}, bf16[1024,512]{1,0:T(8,128)(2,1)S(1)}, u32[]{:S(2)}, u32[]{:S(2)}) collective-permute-start(bf16[1024,512]{1,0:T(8,128)(2,1)S(1)} %copy-done.14), channel_id=1, source_target_pairs={{0,4},{4,0},{1,5},{5,1},{2,6},{6,2},{3,7},{7,3},{8,12},{12,8},{9,1... | collective-permute-start | bytes 3145736 | tf_op jit(solution)/shard_map/ppermute | solution.py:475
  168.4 26.0 %collective-permute-start.8 = (bf16[1024,512]{1,0:T(8,128)(2,1)S(1)}, bf16[1024,512]{1,0:T(8,128)(2,1)S(1)}, u32[]{:S(2)}, u32[]{:S(2)}) collective-permute-start(bf16[1024,512]{1,0:T(8,128)(2,1)S(1)} %bitcast.214), channel_id=1, source_target_pairs={{0,1},{1,0},{2,3},{3,2},{4,5},{5,4},{6,7},{7,6},{8,9},{9,8},{10,11... | collective-permute-start | bytes 3145736 | tf_op jit(solution)/shard_map/ppermute | solution.py:479
  169.0 26.0 %collective-permute-start.9 = (bf16[1024,512]{1,0:T(8,128)(2,1)S(1)}, bf16[1024,512]{1,0:T(8,128)(2,1)S(1)}, u32[]{:S(2)}, u32[]{:S(2)}) collective-permute-start(bf16[1024,512]{1,0:T(8,128)(2,1)S(1)} %bitcast.209), channel_id=1, source_target_pairs={{0,2},{2,0},{1,3},{3,1},{4,6},{6,4},{5,7},{7,5},{8,10},{10,8},{9,1... | collective-permute-start | bytes 3145736 | tf_op jit(solution)/shard_map/ppermute | solution.py:483
  170.5 45.9 %collective-permute-start.12 = (bf16[1024,512]{1,0:T(8,128)(2,1)S(1)}, bf16[1024,512]{1,0:T(8,128)(2,1)S(1)}, u32[]{:S(2)}, u32[]{:S(2)}) collective-permute-start(bf16[1024,512]{1,0:T(8,128)(2,1)S(1)} %collective-permute-done.10.refs_7_), channel_id=1, source_target_pairs={{0,1},{1,0},{2,3},{3,2},{4,5},{5,4},{6,7},{7,6},{8,9},{9,8},{10,11... | collective-permute-start | bytes 3145736 | tf_op jit(solution)/shard_map/ppermute | solution.py:479
  172.0 44.7 %collective-permute-start.11 = (bf16[1024,512]{1,0:T(8,128)(2,1)S(1)}, bf16[1024,512]{1,0:T(8,128)(2,1)S(1)}, u32[]{:S(2)}, u32[]{:S(2)}) collective-permute-start(bf16[1024,512]{1,0:T(8,128)(2,1)S(1)} %collective-permute-done.7.refs_4_), channel_id=1, source_target_pairs={{0,2},{2,0},{1,3},{3,1},{4,6},{6,4},{5,7},{7,5},{8,10},{10,8},{9,1... | collective-permute-start | bytes 3145736 | tf_op jit(solution)/shard_map/ppermute | solution.py:483
  174.2 44.2 %copy-start.4 = (bf16[4,3,512,256]{3,2,1,0:T(8,128)(2,1)}, bf16[4,3,512,256]{3,2,1,0:T(8,128)(2,1)S(1)}, u32[]{:S(2)}) copy-start(bf16[4,3,512,256]{3,2,1,0:T(8,128)(2,1)S(1)} %bitcast_dynamic-update-slice_fusion.refs_13_) | copy-start | bytes 9437188
  194.4 22.3 %copy-start.7 = (bf16[1024,512]{1,0:T(8,128)(2,1)}, bf16[1024,512]{1,0:T(8,128)(2,1)S(1)}, u32[]{:S(2)}) copy-start(bf16[1024,512]{1,0:T(8,128)(2,1)S(1)} %collective-permute-done.8.refs_5_) | copy-start | bytes 3145732
  195.0 21.7 %copy-start.8 = (bf16[1024,512]{1,0:T(8,128)(2,1)}, bf16[1024,512]{1,0:T(8,128)(2,1)S(1)}, u32[]{:S(2)}) copy-start(bf16[1024,512]{1,0:T(8,128)(2,1)S(1)} %collective-permute-done.9.refs_6_) | copy-start | bytes 3145732
  272.1 31.7 %collective-permute-start.30 = (bf16[1024,256]{1,0:T(8,128)(2,1)}, bf16[1024,256]{1,0:T(8,128)(2,1)S(1)}, u32[]{:S(2)}, u32[]{:S(2)}) collective-permute-start(bf16[1024,256]{1,0:T(8,128)(2,1)} %shard_map.187.h0), channel_id=1, source_target_pairs={{0,8},{8,16},{16,24},{24,0},{1,9},{9,17},{17,25},{25,1},{2,10},{10... | collective-permute-start | bytes 1572872 | tf_op jit(solution)/shard_map/ppermute | solution.py:471
  287.7 37.4 %collective-permute-start.31 = (bf16[1024,256]{1,0:T(8,128)(2,1)}, bf16[1024,256]{1,0:T(8,128)(2,1)S(1)}, u32[]{:S(2)}, u32[]{:S(2)}) collective-permute-start(bf16[1024,256]{1,0:T(8,128)(2,1)} %shard_map.187.h0), channel_id=1, source_target_pairs={{0,16},{8,24},{16,0},{24,8},{1,17},{9,25},{17,1},{25,9},{2,18},{10... | collective-permute-start | bytes 1572872 | tf_op jit(solution)/shard_map/ppermute | solution.py:471
  291.2 34.0 %collective-permute-start.32 = (bf16[1024,256]{1,0:T(8,128)(2,1)}, bf16[1024,256]{1,0:T(8,128)(2,1)S(1)}, u32[]{:S(2)}, u32[]{:S(2)}) collective-permute-start(bf16[1024,256]{1,0:T(8,128)(2,1)} %shard_map.187.h0), channel_id=1, source_target_pairs={{0,24},{8,0},{16,8},{24,16},{1,25},{9,1},{17,9},{25,17},{2,26},{10... | collective-permute-start | bytes 1572872 | tf_op jit(solution)/shard_map/ppermute | solution.py:471
  303.7 21.5 %copy-start.20 = (bf16[1024,256]{1,0:T(8,128)(2,1)}, bf16[1024,256]{1,0:T(8,128)(2,1)S(1)}, u32[]{:S(2)}) copy-start(bf16[1024,256]{1,0:T(8,128)(2,1)S(1)} %collective-permute-done.30.h1) | copy-start | bytes 1572868
  335.5 25.3 %copy-start.11 = (bf16[1024,1024]{1,0:T(8,128)(2,1)S(1)}, bf16[1024,1024]{1,0:T(8,128)(2,1)}, u32[]{:S(2)}) copy-start(bf16[1024,1024]{1,0:T(8,128)(2,1)} %shard_map.188) | copy-start | bytes 6291460
  335.5 25.3 %collective-permute-start.34 = (bf16[8,64,1024]{2,1,0:T(8,128)(2,1)}, bf16[8,64,1024]{2,1,0:T(8,128)(2,1)}, u32[]{:S(2)}, u32[]{:S(2)}) collective-permute-start(bf16[8,64,1024]{2,1,0:T(8,128)(2,1)} %dynamic-slice_bitcast_fusion.2), channel_id=1, source_target_pairs={{0,1},{1,0},{2,3},{3,2},{4,5},{5,4},{6,7},{7,6},{8,9},{9,8},{10,11... | collective-permute-start | bytes 3145736 | tf_op jit(solution)/shard_map/ppermute | solution.py:479
  337.4 2.0 collective-permute-start.41
  340.9 28.7 %collective-permute-start.42 = (bf16[3,4,64,64]{3,2,1,0:T(8,128)(2,1)S(1)}, bf16[3,4,64,64]{3,2,1,0:T(8,128)(2,1)S(1)}, u32[]{:S(2)}, u32[]{:S(2)}) collective-permute-start(bf16[3,4,64,64]{3,2,1,0:T(8,128)(2,1)S(1)} %get-tuple-element.39), channel_id=1, source_target_pairs={{0,8},{8,16},{16,24},{24,0},{1,9},{9,17},{17,25},{25,1},{2,10},{10... | collective-permute-start | bytes 294920 | tf_op jit(solution)/shard_map/ppermute | solution.py:471
  351.9 27.1 %collective-permute-start.43 = (bf16[3,4,64,64]{3,2,1,0:T(8,128)(2,1)S(1)}, bf16[3,4,64,64]{3,2,1,0:T(8,128)(2,1)S(1)}, u32[]{:S(2)}, u32[]{:S(2)}) collective-permute-start(bf16[3,4,64,64]{3,2,1,0:T(8,128)(2,1)S(1)} %get-tuple-element.40), channel_id=1, source_target_pairs={{0,16},{8,24},{16,0},{24,8},{1,17},{9,25},{17,1},{25,9},{2,18},{10... | collective-permute-start | bytes 294920 | tf_op jit(solution)/shard_map/ppermute | solution.py:471
  362.6 16.6 %collective-permute-start.36 = (bf16[4,64,1024]{2,1,0:T(8,128)(2,1)S(1)}, bf16[4,64,1024]{2,1,0:T(8,128)(2,1)S(1)}, u32[]{:S(2)}, u32[]{:S(2)}) collective-permute-start(bf16[4,64,1024]{2,1,0:T(8,128)(2,1)S(1)} %get-tuple-element.25), channel_id=1, source_target_pairs={{2,4},{4,2},{3,5},{5,3},{10,12},{12,10},{11,13},{13,11},{18,20},{2... | collective-permute-start | bytes 1572872 | tf_op jit(solution)/shard_map/ppermute | solution.py:675
  363.3 15.9 %collective-permute-start.37 = (bf16[4,64,1024]{2,1,0:T(8,128)(2,1)S(1)}, bf16[4,64,1024]{2,1,0:T(8,128)(2,1)S(1)}, u32[]{:S(2)}, u32[]{:S(2)}) collective-permute-start(bf16[4,64,1024]{2,1,0:T(8,128)(2,1)S(1)} %get-tuple-element.25), channel_id=1, source_target_pairs={{0,4},{6,2},{1,5},{7,3},{8,12},{14,10},{9,13},{15,11},{16,20},{22,... | collective-permute-start | bytes 1572872 | tf_op jit(solution)/shard_map/ppermute | solution.py:676
  368.1 11.1 %collective-permute-start.35 = (bf16[4,64,1024]{2,1,0:T(8,128)(2,1)S(1)}, bf16[4,64,1024]{2,1,0:T(8,128)(2,1)S(1)}, u32[]{:S(2)}, u32[]{:S(2)}) collective-permute-start(bf16[4,64,1024]{2,1,0:T(8,128)(2,1)S(1)} %get-tuple-element.24), channel_id=1, source_target_pairs={{2,0},{4,6},{3,1},{5,7},{10,8},{12,14},{11,9},{13,15},{18,16},{20,... | collective-permute-start | bytes 1572872 | tf_op jit(solution)/shard_map/ppermute | solution.py:674
  369.7 23.6 %collective-permute-start.44 = (bf16[3,4,64,64]{3,2,1,0:T(8,128)(2,1)S(1)}, bf16[3,4,64,64]{3,2,1,0:T(8,128)(2,1)S(1)}, u32[]{:S(2)}, u32[]{:S(2)}) collective-permute-start(bf16[3,4,64,64]{3,2,1,0:T(8,128)(2,1)S(1)} %get-tuple-element.38), channel_id=1, source_target_pairs={{0,24},{8,0},{16,8},{24,16},{1,25},{9,1},{17,9},{25,17},{2,26},{10... | collective-permute-start | bytes 294920 | tf_op jit(solution)/shard_map/ppermute | solution.py:471
  379.6 17.8 %collective-permute-start.38 = (bf16[64,1024]{1,0:T(8,128)(2,1)S(1)}, bf16[64,1024]{1,0:T(8,128)(2,1)S(1)}, u32[]{:S(2)}, u32[]{:S(2)}) collective-permute-start(bf16[64,1024]{1,0:T(8,128)(2,1)S(1)} %get-tuple-element.45), channel_id=1, source_target_pairs={{0,8},{8,16},{16,24},{24,0},{1,9},{9,17},{17,25},{25,1},{2,10},{10... | collective-permute-start | bytes 393224 | tf_op jit(solution)/shard_map/ppermute | solution.py:471
  390.9 8.5 %collective-permute-start.39 = (bf16[64,1024]{1,0:T(8,128)(2,1)S(1)}, bf16[64,1024]{1,0:T(8,128)(2,1)S(1)}, u32[]{:S(2)}, u32[]{:S(2)}) collective-permute-start(bf16[64,1024]{1,0:T(8,128)(2,1)S(1)} %get-tuple-element.44), channel_id=1, source_target_pairs={{0,16},{8,24},{16,0},{24,8},{1,17},{9,25},{17,1},{25,9},{2,18},{10... | collective-permute-start | bytes 393224 | tf_op jit(solution)/shard_map/ppermute | solution.py:471
  390.9 8.7 %collective-permute-start.40 = (bf16[64,1024]{1,0:T(8,128)(2,1)S(1)}, bf16[64,1024]{1,0:T(8,128)(2,1)S(1)}, u32[]{:S(2)}, u32[]{:S(2)}) collective-permute-start(bf16[64,1024]{1,0:T(8,128)(2,1)S(1)} %get-tuple-element.43), channel_id=1, source_target_pairs={{0,24},{8,0},{16,8},{24,16},{1,25},{9,1},{17,9},{25,17},{2,26},{10... | collective-permute-start | bytes 393224 | tf_op jit(solution)/shard_map/ppermute | solution.py:471
  (12 other events, 80.0 us)

commit v2 on v1

--- a/solution.py
+++ b/solution.py
@@ -275,61 +275,111 @@
     return here, before - here
 
 
-def project_kernel(count, outs, finish, *refs):
-    place, period = refs[0], refs[1]
-    chunks = refs[2:10]
-    first, ratios, own, sibling = refs[10:14]
-    extra = refs[14:-outs]
-    results = refs[-outs:]
-    rows = chunks[0].shape[0]
+def mixed_kernel(
+    place,
+    period,
+    c0,
+    c1,
+    c2,
+    c3,
+    c4,
+    c5,
+    c6,
+    c7,
+    first,
+    ratios,
+    own_pair,
+    sibling_pair,
+    own_value,
+    sibling_value,
+    own_left,
+    sibling_left,
+    right,
+    base,
+    recept_ref,
+    keys_ref,
+    values_ref,
+    decay_ref,
+    gate_mix,
+):
+    rows, depth = c0.shape
 
     @pl.loop(0, rows // TILE)
     def _(tile):
+        at = pl.ds(pl.multiple_of(tile * TILE, TILE), TILE)
         row = lax.broadcasted_iota(jnp.int32, (TILE, 1), 0) + tile * TILE
         start = (row & (period[0] - 1)) == 0
-        totals = [None] * count
-        for at, chunk in enumerate(chunks):
-            here, step = previous_rows(chunk, first[at : at + 1, :], tile, start)
-            held = own if at % 2 == 0 else sibling
-            for c in range(count):
-                mixed = (here + ratios[c, at : at + 1, :] * step).astype(bf16)
-                part = jnp.dot(mixed, held[place[at // 2], c], preferred_element_type=f32)
-                totals[c] = part if totals[c] is None else totals[c] + part
-        finish(tile, totals, extra, results)
-
-
-def store_tiles(tile, totals, extra, results):
-    at = pl.ds(pl.multiple_of(tile * TILE, TILE), TILE)
-    for total, result in zip(totals, results):
-        result[at, :] = total
-
-
-def store_decay(tile, totals, extra, results):
-    right, base = extra
-    at = pl.ds(pl.multiple_of(tile * TILE, TILE), TILE)
-    squeezed = jnp.tanh(totals[0]).astype(bf16)
-    grown = jnp.dot(squeezed, right[...], preferred_element_type=f32)
-    results[0][at, :] = -jnp.exp(base[...] + grown)
-
-
-def store_hidden(tile, totals, extra, results):
-    normed, live = extra
-    at = pl.ds(pl.multiple_of(tile * TILE, TILE), TILE)
-    gate = totals[0]
-    value = normed[at, :] * (gate * jax.nn.sigmoid(gate))
-    results[0][at, :] = jnp.where(live[at, :] > 0, value, 0.0).astype(bf16)
-
-
-def project(finish, out_shapes, place, period, chunks, first, ratios, own, sibling, *extra):
-    count = own.shape[1]
-    outs = len(out_shapes)
+        totals = [None] * 4
+        for c, chunk in enumerate((c0, c1, c2, c3, c4, c5, c6, c7)):
+            here, step = previous_rows(chunk, first[c : c + 1, :], tile, start)
+            from_z = place[c // 2]
+            pair, value, left = (
+                (own_pair, own_value, own_left)
+                if c % 2 == 0
+                else (sibling_pair, sibling_value, sibling_left)
+            )
+            weights = (pair[from_z, 0], pair[from_z, 1], value[from_z, 0], left[from_z, 0])
+            for which, weight in zip((0, 1, 2, 4), weights):
+                mixed = (here + ratios[which, c : c + 1, :] * step).astype(bf16)
+                part = jnp.dot(mixed, weight, preferred_element_type=f32)
+                slot = min(which, 3)
+                totals[slot] = part if totals[slot] is None else totals[slot] + part
+            gate_mix[at, c * depth : (c + 1) * depth] = (
+                here + ratios[3, c : c + 1, :] * step
+            ).astype(bf16)
+        recept_ref[at, :] = totals[0]
+        keys_ref[at, :] = totals[1]
+        values_ref[at, :] = totals[2]
+        squeezed = jnp.tanh(totals[3]).astype(bf16)
+        grown = jnp.dot(squeezed, right[...], preferred_element_type=f32)
+        decay_ref[at, :] = -jnp.exp(base[...] + grown)
+
+
+def mixed_products(place, period, chunks, *rest):
+    rows, depth = chunks[0].shape
+    width = rest[2].shape[3]
+    flat = jax.ShapeDtypeStruct((rows, width), f32)
     return pl.pallas_call(
-        lambda *refs: project_kernel(count, outs, finish, *refs),
-        out_shape=out_shapes,
-        in_specs=[in_smem(), in_smem()] + [in_vmem()] * (12 + len(extra)),
-        out_specs=[in_vmem()] * outs,
+        mixed_kernel,
+        out_shape=[flat] * 4 + [jax.ShapeDtypeStruct((rows, 8 * depth), bf16)],
+        in_specs=[in_smem(), in_smem()] + [in_vmem()] * (8 + len(rest)),
+        out_specs=[in_vmem()] * 5,
         compiler_params=kernel_params(),
-    )(place, period, *chunks, first, ratios, own, sibling, *extra)
+    )(place, period, *chunks, *rest)
+
+
+def gate_kernel(place, mix, own, sibling, normed, live, first_ref, second_ref):
+    rows = mix.shape[0]
+    depth, width = own.shape[2:]
+    part_rows = BLK // 2
+
+    @pl.loop(0, rows // TILE)
+    def _(tile):
+        at = pl.ds(pl.multiple_of(tile * TILE, TILE), TILE)
+        total = None
+        for c in range(8):
+            weight = (own if c % 2 == 0 else sibling)[place[c // 2], 0]
+            part = jnp.dot(
+                mix[at, c * depth : (c + 1) * depth], weight, preferred_element_type=f32
+            )
+            total = part if total is None else total + part
+        value = normed[at, :] * (total * jax.nn.sigmoid(total))
+        value = jnp.where(live[at, :] > 0, value, 0.0).astype(bf16)
+        value = value.reshape(TILE // part_rows // 2, 2, part_rows, width)
+        half_at = pl.ds(pl.multiple_of(tile * (TILE // 2), TILE // 2), TILE // 2)
+        first_ref[half_at, :] = value[:, 0].reshape(TILE // 2, width)
+        second_ref[half_at, :] = value[:, 1].reshape(TILE // 2, width)
+
+
+def gated(place, mix, own, sibling, normed, live):
+    rows, width = normed.shape
+    return pl.pallas_call(
+        gate_kernel,
+        out_shape=[jax.ShapeDtypeStruct((rows // 2, width), bf16)] * 2,
+        in_specs=[in_smem()] + [in_vmem()] * 5,
+        out_specs=[in_vmem()] * 2,
+        compiler_params=kernel_params(),
+    )(place, mix, own, sibling, normed, live)
 
 
 def sweep_kernel(
@@ -445,7 +495,10 @@
     )(lengths, carry, r, k, v, w, bonus, state, gain, bias)
 
 
-def final_kernel(h0, h1, h2, h3, weight, out_ref):
+def final_kernel(side, h0, h1, h2, h3, weight, kept_ref, sent_ref):
+    part_rows = BLK // 2
+    width = weight.shape[2]
+
     @pl.loop(0, h0.shape[0] // TILE)
     def _(tile):
         at = pl.ds(pl.multiple_of(tile * TILE, TILE), TILE)
@@ -453,17 +506,48 @@
         for k, piece in enumerate((h0, h1, h2, h3)):
             part = jnp.dot(piece[at, :], weight[k], preferred_element_type=f32)
             total = part if total is None else total + part
-        out_ref[at, :] = total.astype(bf16)
-
-
-def final_product(pieces, weight):
+        split = total.astype(bf16).reshape(TILE // part_rows // 2, 2, part_rows, width)
+        mine = side[0] == 0
+        low, high = split[:, 0], split[:, 1]
+        group = pl.ds(tile * (TILE // part_rows // 2), TILE // part_rows // 2)
+        kept_ref[group] = jnp.where(mine, low, high)
+        sent_ref[group] = jnp.where(mine, high, low)
+
+
+def final_product(side, pieces, weight):
+    rows, width = pieces[0].shape[0], weight.shape[2]
+    half = jax.ShapeDtypeStruct((rows // BLK, BLK // 2, width), bf16)
     return pl.pallas_call(
         final_kernel,
-        out_shape=jax.ShapeDtypeStruct((pieces[0].shape[0], weight.shape[2]), bf16),
-        in_specs=[in_vmem()] * 5,
+        out_shape=[half] * 2,
+        in_specs=[in_smem()] + [in_vmem()] * 5,
+        out_specs=[in_vmem()] * 2,
+        compiler_params=kernel_params(),
+    )(side, *pieces, weight)
+
+
+def lay_kernel(at, *refs):
+    pieces, out_ref = refs[:-1], refs[-1]
+    rows, width = pieces[0].shape
+    lines = out_ref.shape[1] // width
+    for n, piece in enumerate(pieces):
+        column = pl.multiple_of(at[n % lines] * width, width)
+        out_ref[n // lines * rows : (n // lines + 1) * rows, pl.ds(column, width)] = piece[...]
+
+
+def laid(at, pieces, lines):
+    rows, width = pieces[0].shape
+    return pl.pallas_call(
+        lay_kernel,
+        out_shape=jax.ShapeDtypeStruct((len(pieces) // lines * rows, lines * width), bf16),
+        in_specs=[in_smem()] + [in_vmem()] * len(pieces),
         out_specs=in_vmem(),
         compiler_params=kernel_params(),
-    )(*pieces, weight)
+    )(at, *pieces)
+
+
+def after(value, *others):
+    return lax.optimization_barrier((value,) + others)[0]
 
 
 def turned(x, axis, by):
@@ -486,6 +570,24 @@
 def dealt(blocks, z):
     length = lax.axis_size("z")
     return [blocks(z)] + [turned(blocks((z + k) % length), "z", k) for k in range(1, length)]
+
+
+def spread_along(piece, z):
+    one = lax.ppermute(piece, "z", [(0, 1), (1, 2), (2, 3)])
+    three = lax.ppermute(piece, "z", [(1, 0), (2, 1), (3, 2)])
+    two = turned(piece, "z", 2)
+    far = lax.ppermute(two, "z", [(1, 0), (2, 3)])
+    return piece, one, two, three, far
+
+
+def in_place(spread, z, at=0):
+    piece, one, two, three, far = spread
+    whole = jnp.zeros((4,) + piece.shape, piece.dtype)
+    for k, part in ((1, one), (2, two), (3, three)):
+        whole = lax.dynamic_update_index_in_dim(whole, part, (z - k) % 4, 0)
+    far_at = jnp.where(z == 0, 3, jnp.where(z == 3, 0, z))
+    whole = lax.dynamic_update_index_in_dim(whole, far, far_at, 0)
+    return lax.dynamic_update_index_in_dim(whole, piece, z, 0)
 
 
 def in_order(pieces, z):
@@ -535,13 +637,14 @@
     both = jnp.concatenate(
         [jnp.where(is_long, kept, taken), jnp.where(is_long, taken, kept)], axis=0
     )
-    half_at = jnp.stack([core * depth, (1 - core) * depth])
     halves = []
     for h in range(2):
-        mine = lax.dynamic_slice_in_dim(both, half_at[h], depth, 1)
-        gathered = in_order([mine] + [turned(mine, "z", k) for k in range(1, lines)], z)
-        halves.append(gathered.reshape(rows, depth))
-    a, b = halves
+        side = core if h == 0 else 1 - core
+        halves.append(lax.dynamic_slice_in_dim(both, side * depth, depth, 1))
+    first_half = spread_along(halves[0], z)
+    second_half = spread_along(halves[1], z)
+    a = in_place(first_half, z).reshape(rows, depth)
+    b = in_place(second_half, z).reshape(rows, depth)
     a_x, b_y = over_x(a), over_y(b)
     a_y, b_x = over_y(a), over_x(b)
     a_xy, b_xy = over_y(a_x), over_x(b_y)
@@ -566,17 +669,28 @@
 
     ratios = chunk_order(token_mixing_ratios.T).transpose(2, 0, 1)
 
-    def columns_of(weights):
+    def columns_of(weights, *ready):
         stacked = jnp.stack(weights)
 
         def block(j):
             return lax.dynamic_slice_in_dim(stacked, j * width, width, 2)
 
-        pieces = dealt(block, z)
+        blocks = [block((z + k) % lines) for k in range(lines)]
+        blocks = lax.optimization_barrier((tuple(blocks),) + ready)[0]
+        pieces = [blocks[0]] + [turned(blocks[k], "z", k) for k in range(1, lines)]
+        return pieces
+
+    def both_cores(pieces):
         return in_order(pieces, z), in_order([flipped_core(piece) for piece in pieces], z)
 
-    own, sibling = columns_of([acceptance_transform, lookup_transform, payload_transform])
-    own_gate, sibling_gate = columns_of([gating_transform])
+    pair_pieces = columns_of(
+        [acceptance_transform, lookup_transform], first_half[4], second_half[4]
+    )
+    value_pieces = columns_of([payload_transform], a_x, b_y)
+    gate_pieces = columns_of([gating_transform], value_pieces[2])
+    own_pair, sibling_pair = both_cores(pair_pieces)
+    own_value, sibling_value = both_cores(value_pieces)
+    own_gate, sibling_gate = both_cores(gate_pieces)
     left = fading_left_factor.reshape(4, 2, 1, depth, fading_left_factor.shape[1])
     left_own = jnp.where(is_long, left[:, 0], left[:, 1])
     left_sibling = jnp.where(is_long, left[:, 1], left[:, 0])
@@ -584,24 +698,31 @@
     def mine_of(vector):
         return lax.dynamic_slice_in_dim(vector, z * width, width, 0)[None]
 
-    flat = jax.ShapeDtypeStruct((rows, width), f32)
-    (decay,) = project(
-        store_decay,
-        [flat],
+    recept, keys, values, decay, gate_mix = mixed_products(
         place,
         period,
         chunks,
         first,
-        ratios[4:5],
+        ratios,
+        own_pair,
+        sibling_pair,
+        own_value,
+        sibling_value,
         left_own,
         left_sibling,
         lax.dynamic_slice_in_dim(fading_right_factor, z * width, width, 1),
         mine_of(fading_baseline),
     )
-    recept, keys, values = project(
-        store_tiles, [flat] * 3, place, period, chunks, first, ratios[:3], own, sibling
-    )
-    extents = lax.all_gather(prompt_live_extents, ("z", "core"), axis=0, tiled=True)
+    beside_extents = flipped_core(prompt_live_extents)
+    chip_extents = jnp.stack(
+        [
+            jnp.where(is_long, prompt_live_extents, beside_extents),
+            jnp.where(is_long, beside_extents, prompt_live_extents),
+        ]
+    )
+    extents = in_order(
+        [chip_extents] + [turned(chip_extents, "z", k) for k in range(1, lines)], z
+    ).reshape(2 * lines * requests)
     extents = jnp.where(is_long, slot_rows, extents).astype(jnp.int32)
     entered = lax.dynamic_slice_in_dim(carried_memory, z * heads, heads, 0)
     bonus = lax.dynamic_slice_in_dim(present_reward, z * heads, heads, 0).reshape(1, width)
@@ -619,19 +740,7 @@
     )
     live = lax.broadcasted_iota(jnp.int32, (rows // slot_rows, slot_rows), 1) < extents[:, None]
     live = live.reshape(rows, 1).astype(f32)
-    (hidden,) = project(
-        store_hidden,
-        [jax.ShapeDtypeStruct((rows, width), bf16)],
-        place,
-        period,
-        chunks,
-        first,
-        ratios[3:4],
-        own_gate,
-        sibling_gate,
-        normed,
-        live,
-    )
+    hidden = gated(place, gate_mix, own_gate, sibling_gate, normed, live)
 
     states = states.reshape(lines, 2, requests, heads, span, span)
     passed = flipped_core(lax.dynamic_index_in_dim(states, 1 - core, 1, keepdims=False))
@@ -656,34 +765,41 @@
         ],
         axis=1,
     ).reshape(lines, width, wide_out)
-    pieces = [hidden] + [turned(hidden, "z", k) for k in range(1, lines)]
     out_weight = jnp.stack(
         [
             lax.dynamic_index_in_dim(out_weight, (z - k) % lines, 0, keepdims=False)
             for k in range(lines)
         ]
     )
-    partial = final_product(pieces, out_weight)
-    partial = partial.reshape(2 * lines, 2, group_rows // 2, wide_out)
-    kept_half = lax.dynamic_index_in_dim(partial, x, 1, keepdims=False)
-    sent_half = lax.dynamic_index_in_dim(partial, 1 - x, 1, keepdims=False)
-    summed = kept_half.astype(f32) + over_x(sent_half).astype(f32)
-    summed = summed.reshape(lines, 2, group_rows // 2, wide_out)
-    same_core = lax.dynamic_index_in_dim(summed, core, 1, keepdims=False)
-    other_core = lax.dynamic_index_in_dim(summed, 1 - core, 1, keepdims=False).astype(bf16)
-    from_same = lax.ppermute(same_core.astype(bf16), ("core", "y"), [(1, 0), (2, 3)])
-    from_cross = lax.ppermute(other_core, ("core", "y"), [(1, 2), (2, 1)])
-    from_beside = lax.ppermute(other_core, ("core", "y"), [(0, 2), (3, 1)])
-    mixed_part = (
-        jnp.where(core == y, same_core, 0.0)
-        + from_same.astype(f32)
-        + from_cross.astype(f32)
-        + from_beside.astype(f32)
-    ).astype(bf16)
-    out_pieces = in_order(
-        dealt(lambda j: lax.dynamic_index_in_dim(mixed_part, j, 0, keepdims=False), z), z
-    )
-    mixed = jnp.swapaxes(out_pieces, 0, 1).reshape(1, group_rows // 2, lines * wide_out)
+    order = jnp.stack([(z - k) % lines for k in range(lines)]).astype(jnp.int32)
+    side = x.astype(jnp.int32)[None]
+    spreads = []
+    for n, part in enumerate(hidden):
+        if n:
+            part = after(part, spreads[0][2])
+        spreads.append(spread_along(part, z))
+    out_pieces = []
+    for piece, one, two, three, far in spreads:
+        one = jnp.where(z == 0, far, one)
+        three = jnp.where(z == 3, far, three)
+        kept_half, sent_half = final_product(side, (piece, one, two, three), out_weight)
+        summed = kept_half.astype(f32) + over_x(sent_half).astype(f32)
+        summed = summed.reshape(lines, 2, group_rows // 4, wide_out)
+        same_core = lax.dynamic_index_in_dim(summed, core, 1, keepdims=False)
+        other_core = lax.dynamic_index_in_dim(summed, 1 - core, 1, keepdims=False).astype(bf16)
+        from_same = lax.ppermute(same_core.astype(bf16), ("core", "y"), [(1, 0), (2, 3)])
+        from_cross = lax.ppermute(other_core, ("core", "y"), [(1, 2), (2, 1)])
+        from_beside = lax.ppermute(other_core, ("core", "y"), [(0, 2), (3, 1)])
+        mixed_part = (
+            jnp.where(core == y, same_core, 0.0)
+            + from_same.astype(f32)
+            + from_cross.astype(f32)
+            + from_beside.astype(f32)
+        ).astype(bf16)
+        out_pieces += dealt(
+            lambda j: lax.dynamic_index_in_dim(mixed_part, j, 0, keepdims=False), z
+        )
+    mixed = laid(order, out_pieces, lines)[None]
     return mixed, span_states, request_states
 
 

time: 407 us -> 378 us (0.929)
  local copies, waits for them, and re-layouts: 44.1 us -> 26 us
  starting transfers between devices: 127 us -> 114 us
  waiting for transfers between devices: 149 us -> 160 us
  blocking collectives: 9.16 us -> 0 us
    ppermute x21 -> x25, starting transfers between devices: 106 us -> 57.7 us  [turned(): lax.ppermute(x, axis, [(i, (i + by) % length) for i in range(length)])]
    ppermute x5 -> x6, waiting for transfers between devices: 50.6 us -> 6.02 us  [over_x(): return lax.ppermute(x, 'x', [(0, 1), (1, 0)])]
    ppermute x5, waiting for transfers between devices: 0.85 us -> 41 us  [over_y(): return lax.ppermute(x, 'y', [(0, 1), (1, 0)])]
    ppermute x0 -> x12, starting transfers between devices: none -> 35.8 us  [the longest x4 25.5 us: spread_along(): one = lax.ppermute(piece, 'z', [(0, 1), (1, 2), (2, 3)])]
    ppermute x0 -> x12, waiting for transfers between devices: none -> 24 us  [the longest x4 23.1 us: spread_along(): far = lax.ppermute(two, 'z', [(1, 0), (2, 3)])]
    dynamic_update_slice x29 -> x30, local copies, waits for them, and re-layouts: 14.8 us -> 0.78 us  [in_order(): whole = lax.dynamic_update_index_in_dim(whole, piece, (z - k) % length, 0)]
    unnamed x1 -> x0, blocking collectives: 9.16 us -> none
    ppermute x21 -> x25, waiting for transfers between devices: 94.3 us -> 85.8 us  [turned(): lax.ppermute(x, axis, [(i, (i + by) % length) for i in range(length)])]
  transfers between devices with their start and end apart: 45 -> 70, of which waited for: 16 -> 26; matrix products, arithmetic and copies ran while one was open for 11% -> 10% of each run, Pallas kernels for 13% -> 2%
where the time goes in v2:
time: 378 us; the launch traced here: 377 us
  waiting for transfers between devices  160 us (42%)
  starting transfers between devices  114 us (30%)
  Pallas kernels  59.2 us (16%)
  local copies, waits for them, and re-layouts  26 us (7%)
  other arithmetic  16.1 us (4%)
    ppermute x25, waiting for transfers between devices, turned(): lax.ppermute(x, axis, [(i, (i + by) % length) for i in range(length)])  85.8 us
    ppermute x25, starting transfers between devices, turned(): lax.ppermute(x, axis, [(i, (i + by) % length) for i in range(length)])  57.7 us
    ppermute x5, waiting for transfers between devices, over_y(): return lax.ppermute(x, 'y', [(0, 1), (1, 0)])  41 us
    ppermute x4, starting transfers between devices, spread_along(): one = lax.ppermute(piece, 'z', [(0, 1), (1, 2), (2, 3)])  25.5 us
    pallas_call x1, Pallas kernels, mixed_products(): pl.pallas_call(mixed_kernel, out_shape=[flat] * 4 + [jax.ShapeDtypeStruct...  23.6 us
    ppermute x4, waiting for transfers between devices, spread_along(): far = lax.ppermute(two, 'z', [(1, 0), (2, 3)])  23.1 us
    pallas_call x1, Pallas kernels, sweep(): pl.pallas_call(sweep_kernel, out_shape=[jax.ShapeDtypeStruct((rows, width...  16.8 us
    pallas_call x2, Pallas kernels, final_product(): pl.pallas_call(final_kernel, out_shape=[half] * 2, in_specs=[in_smem()] +...  8.69 us
  transfers between devices with their start and end apart: 70, of which 26 were waited for; matrix products, arithmetic and copies ran while one was open for 10% of the time, Pallas kernels for 2%

profile of v2, /device:TPU:0, one launch (start us, length us, event | category | flops | bytes accessed | tf_op | source)
XLA Modules:
  0.0 377.2 jit_solution(11693240502364398718)
XLA Ops:
  1.5 2.9 collective-permute-start.15
  4.4 1.5 collective-permute-start.16
  5.9 1.7 broadcast_select_fusion.8
  9.8 2.2 select_bitcast_fusion
  12.7 1.4 dynamic_slice.174
  15.1 2.1 dynamic-slice_bitcast_fusion.2
  18.6 1.6 dynamic-slice_select_fusion.s_ref
  20.1 1.3 dynamic_slice.181
  21.5 1.3 dynamic_slice.182
  22.8 2.8 fusion
  27.7 1.6 collective-permute-start.40
  29.4 3.8 %collective-permute-done.40 = s32[2,2]{1,0:T(2,128)S(1)} collective-permute-done((s32[2,2]{1,0:T(2,128)S(1)}, s32[2,2]{1,0:T(2,128)S(1)}, u32[]{:S(2)}, u32[]{:S(2)}) %collective-permute-start.40) | collective-permute-done | bytes 48 | tf_op jit(solution)/shard_map/ppermute | solution.py:555
  33.9 3.7 collective-permute-done.41
  37.6 1.8 collective-permute-start.42
  39.4 1.8 collective-permute-done.42
  44.9 2.4 collective-permute-start.5
  47.5 3.8 collective-permute-start.6
  53.2 4.6 %collective-permute-start.1 = (bf16[256,512]{1,0:T(8,128)(2,1)}, bf16[256,512]{1,0:T(8,128)(2,1)S(1)}, u32[]{:S(2)}, u32[]{:S(2)}) collective-permute-start(bf16[256,512]{1,0:T(8,128)(2,1)} %get-tuple-element.87), channel_id=1, source_target_pairs={{0,8},{8,16},{16,24},{1,9},{9,17},{17,25},{2,10},{10,18},{18,26},{... | collective-permute-start | bytes 786440 | tf_op jit(solution)/shard_map/ppermute | solution.py:576
  57.8 5.1 %collective-permute-start.2 = (bf16[256,512]{1,0:T(8,128)(2,1)}, bf16[256,512]{1,0:T(8,128)(2,1)S(1)}, u32[]{:S(2)}, u32[]{:S(2)}) collective-permute-start(bf16[256,512]{1,0:T(8,128)(2,1)} %get-tuple-element.87), channel_id=1, source_target_pairs={{0,16},{8,24},{16,0},{24,8},{1,17},{9,25},{17,1},{25,9},{2,18},{10... | collective-permute-start | bytes 786440 | tf_op jit(solution)/shard_map/ppermute | solution.py:555
  66.3 1.3 collective-permute-start.8
  67.6 10.4 %collective-permute-done.2 = bf16[256,512]{1,0:T(8,128)(2,1)S(1)} collective-permute-done((bf16[256,512]{1,0:T(8,128)(2,1)}, bf16[256,512]{1,0:T(8,128)(2,1)S(1)}, u32[]{:S(2)}, u32[]{:S(2)}) %collective-permute-start.2) | collective-permute-done | bytes 262176 | tf_op jit(solution)/shard_map/ppermute | solution.py:555
  80.3 4.8 %collective-permute-done.8 = bf16[256,512]{1,0:T(8,128)(2,1)S(1)} collective-permute-done((bf16[256,512]{1,0:T(8,128)(2,1)}, bf16[256,512]{1,0:T(8,128)(2,1)S(1)}, u32[]{:S(2)}, u32[]{:S(2)}) %collective-permute-start.8) | collective-permute-done | bytes 262176 | tf_op jit(solution)/shard_map/ppermute | solution.py:579
  85.1 2.8 collective-permute-done.4
  89.7 1.6 collective-permute-start.12
  91.3 2.8 collective-permute-start.19
  95.8 12.2 %collective-permute-done.18 = bf16[2,512,256]{2,1,0:T(8,128)(2,1)S(1)} collective-permute-done((bf16[2,512,256]{2,1,0:T(8,128)(2,1)S(1)}, bf16[2,512,256]{2,1,0:T(8,128)(2,1)S(1)}, u32[]{:S(2)}, u32[]{:S(2)}) %collective-permute-start.18) | collective-permute-done | bytes 524320 | tf_op jit(solution)/shard_map/ppermute | solution.py:555
  108.1 17.5 %collective-permute-done.19 = bf16[2,512,256]{2,1,0:T(8,128)(2,1)S(1)} collective-permute-done((bf16[2,512,256]{2,1,0:T(8,128)(2,1)S(1)}, bf16[2,512,256]{2,1,0:T(8,128)(2,1)S(1)}, u32[]{:S(2)}, u32[]{:S(2)}) %collective-permute-start.19) | collective-permute-done | bytes 524320 | tf_op jit(solution)/shard_map/ppermute | solution.py:555
  126.6 1.6 collective-permute-start.10
  128.2 10.7 %collective-permute-start.25 = (bf16[1,512,256]{2,1,0:T(8,128)(2,1)S(1)}, bf16[1,512,256]{2,1,0:T(8,128)(2,1)S(1)}, u32[]{:S(2)}, u32[]{:S(2)}) collective-permute-start(bf16[1,512,256]{2,1,0:T(8,128)(2,1)S(1)} %copy-done.33), channel_id=1, source_target_pairs={{0,8},{8,16},{16,24},{24,0},{1,9},{9,17},{17,25},{25,1},{2,10},{10... | collective-permute-start | bytes 786440 | tf_op jit(solution)/shard_map/ppermute | solution.py:555
  140.1 2.3 collective-permute-start.27
  142.3 14.2 %collective-permute-done.26 = bf16[1,512,256]{2,1,0:T(8,128)(2,1)S(1)} collective-permute-done((bf16[1,512,256]{2,1,0:T(8,128)(2,1)S(1)}, bf16[1,512,256]{2,1,0:T(8,128)(2,1)S(1)}, u32[]{:S(2)}, u32[]{:S(2)}) %collective-permute-start.26) | collective-permute-done | bytes 262176 | tf_op jit(solution)/shard_map/ppermute | solution.py:555
  156.7 5.0 %collective-permute-start.32 = (bf16[1,512,256]{2,1,0:T(8,128)(2,1)S(1)}, bf16[1,512,256]{2,1,0:T(8,128)(2,1)S(1)}, u32[]{:S(2)}, u32[]{:S(2)}) collective-permute-start(bf16[1,512,256]{2,1,0:T(8,128)(2,1)S(1)} %copy-done.31), channel_id=1, source_target_pairs={{0,8},{8,16},{16,24},{24,0},{1,9},{9,17},{17,25},{25,1},{2,10},{10... | collective-permute-start | bytes 786440 | tf_op jit(solution)/shard_map/ppermute | solution.py:555
  163.4 3.4 collective-permute-start.33
  166.9 4.9 %collective-permute-done.32 = bf16[1,512,256]{2,1,0:T(8,128)(2,1)S(1)} collective-permute-done((bf16[1,512,256]{2,1,0:T(8,128)(2,1)S(1)}, bf16[1,512,256]{2,1,0:T(8,128)(2,1)S(1)}, u32[]{:S(2)}, u32[]{:S(2)}) %collective-permute-start.32) | collective-permute-done | bytes 262176 | tf_op jit(solution)/shard_map/ppermute | solution.py:555
  171.8 2.7 collective-permute-start.34
  174.7 8.2 %collective-permute-done.33 = bf16[1,512,256]{2,1,0:T(8,128)(2,1)S(1)} collective-permute-done((bf16[1,512,256]{2,1,0:T(8,128)(2,1)S(1)}, bf16[1,512,256]{2,1,0:T(8,128)(2,1)S(1)}, u32[]{:S(2)}, u32[]{:S(2)}) %collective-permute-start.33) | collective-permute-done | bytes 262176 | tf_op jit(solution)/shard_map/ppermute | solution.py:555
  183.4 1.8 collective-permute-done.34
  186.4 1.4 collective-permute-done.37
  188.0 1.3 collective-permute-done.38
  189.4 19.5 %collective-permute-done.11.c4 = bf16[1024,512]{1,0:T(8,128)(2,1)S(1)} collective-permute-done((bf16[1024,512]{1,0:T(8,128)(2,1)S(1)}, bf16[1024,512]{1,0:T(8,128)(2,1)S(1)}, u32[]{:S(2)}, u32[]{:S(2)}) %collective-permute-start.11) | collective-permute-done | bytes 1048608 | tf_op jit(solution)/shard_map/ppermute | solution.py:567
  208.9 21.5 %collective-permute-done.13.c6 = bf16[1024,512]{1,0:T(8,128)(2,1)S(1)} collective-permute-done((bf16[1024,512]{1,0:T(8,128)(2,1)S(1)}, bf16[1024,512]{1,0:T(8,128)(2,1)S(1)}, u32[]{:S(2)}, u32[]{:S(2)}) %collective-permute-start.13) | collective-permute-done | bytes 1048608 | tf_op jit(solution)/shard_map/ppermute | solution.py:567
  231.8 23.6 %shard_map.184 = (f32[1024,256]{1,0:T(8,128)}, f32[1024,256]{1,0:T(8,128)}, f32[1024,256]{1,0:T(8,128)}, f32[1024,256]{1,0:T(8,128)}, bf16[1024,4096]{1,0:T(8,128)(2,1)}) custom-call(s32[4]{0:T(128)} %pad_add_fusion.2.place, s32[1]{0:T(128)} %bitcast.9.period, bf16[1024,512]{1,0:T(8,128)(2,1)} %bitcast.294, bf16[1024,512]{1,0:T(8,128)(2,1)} %bitcast.291, ...), custom_call_target="tpu_custom_call" | custom-call | tf_op jit(solution)/shard_map/pallas_call | solution.py:342
  255.4 16.8 %shard_map.185 = (f32[1024,256]{1,0:T(8,128)}, f32[16,4,64,64]{3,2,1,0:T(8,128)}) custom-call(s32[16]{0:T(128)} %copy-done.45, f32[1]{0:T(128)} %bitcast.80.carry, f32[1024,256]{1,0:T(8,128)} %get-tuple-element.42.r_ref, f32[1024,256]{1,0:T(8,128)} %get-tuple-element.43.k_ref, f32[1024,256]{1,0:T(8,128)} %get-tuple-element.44.v_ref, ...), custom_call_target="tpu_custom_call" | custom-call | tf_op jit(solution)/shard_map/pallas_call | solution.py:485
  272.2 8.2 %shard_map.186 = (bf16[512,256]{1,0:T(8,128)(2,1)}, bf16[512,256]{1,0:T(8,128)(2,1)}) custom-call(s32[4]{0:T(128)} %pad_add_fusion.2.place, bf16[1024,4096]{1,0:T(8,128)(2,1)} %get-tuple-element.37.mix, bf16[4,1,512,256]{3,2,1,0:T(8,128)(2,1)} %copy-done.9, bf16[4,1,512,256]{3,2,1,0:T(8,128)(2,1)} %copy-done.7, f32[1024,256]{1,0:T(8,128)} %get-tuple-element.46.normed, ...), custom_call_target="tpu_custom_call" | custom-call | tf_op jit(solution)/shard_map/pallas_call | solution.py:376
  280.8 1.6 pad_maximum_fusion.1.weight
  283.7 8.1 %collective-permute-start.45 = (bf16[512,256]{1,0:T(8,128)(2,1)S(1)}, bf16[512,256]{1,0:T(8,128)(2,1)S(1)}, u32[]{:S(2)}, u32[]{:S(2)}) collective-permute-start(bf16[512,256]{1,0:T(8,128)(2,1)S(1)} %copy-done.36), channel_id=1, source_target_pairs={{0,8},{8,16},{16,24},{1,9},{9,17},{17,25},{2,10},{10,18},{18,26},{... | collective-permute-start | bytes 786440 | tf_op jit(solution)/shard_map/ppermute | solution.py:576
  291.8 4.6 %collective-permute-done.43.h2 = bf16[512,256]{1,0:T(8,128)(2,1)S(1)} collective-permute-done((bf16[512,256]{1,0:T(8,128)(2,1)}, bf16[512,256]{1,0:T(8,128)(2,1)S(1)}, u32[]{:S(2)}, u32[]{:S(2)}) %collective-permute-start.43) | collective-permute-done | bytes 262176 | tf_op jit(solution)/shard_map/ppermute | solution.py:555
  296.4 1.3 collective-permute-start.58
  297.7 1.3 collective-permute-start.44
  299.7 10.5 %collective-permute-start.57 = (bf16[512,256]{1,0:T(8,128)(2,1)S(1)}, bf16[512,256]{1,0:T(8,128)(2,1)S(1)}, u32[]{:S(2)}, u32[]{:S(2)}) collective-permute-start(bf16[512,256]{1,0:T(8,128)(2,1)S(1)} %copy-done.35), channel_id=1, source_target_pairs={{0,8},{8,16},{16,24},{1,9},{9,17},{17,25},{2,10},{10,18},{18,26},{... | collective-permute-start | bytes 786440 | tf_op jit(solution)/shard_map/ppermute | solution.py:576
  310.2 10.4 %collective-permute-done.44 = bf16[512,256]{1,0:T(8,128)(2,1)S(1)} collective-permute-done((bf16[512,256]{1,0:T(8,128)(2,1)S(1)}, bf16[512,256]{1,0:T(8,128)(2,1)S(1)}, u32[]{:S(2)}, u32[]{:S(2)}) %collective-permute-start.44) | collective-permute-done | bytes 262176 | tf_op jit(solution)/shard_map/ppermute | solution.py:579
  322.8 4.3 %shard_map.187 = (bf16[8,32,1024]{2,1,0:T(8,128)(2,1)}, bf16[8,32,1024]{2,1,0:T(8,128)(2,1)}) custom-call(s32[1]{0:T(128)} %bitcast.4.side, bf16[512,256]{1,0:T(8,128)(2,1)} %get-tuple-element.47.h0, bf16[512,256]{1,0:T(8,128)(2,1)} %get-tuple-element.99.h1, bf16[512,256]{1,0:T(8,128)(2,1)} %copy-done.38, bf16[512,256]{1,0:T(8,128)(2,1)} %get-tuple-element.98.h3, ...), custom_call_target="tpu_custom_call" | custom-call | tf_op jit(solution)/shard_map/pallas_call | solution.py:520
  327.7 1.9 collective-permute-start.69
  329.7 5.1 %collective-permute-done.56 = bf16[512,256]{1,0:T(8,128)(2,1)S(1)} collective-permute-done((bf16[512,256]{1,0:T(8,128)(2,1)S(1)}, bf16[512,256]{1,0:T(8,128)(2,1)S(1)}, u32[]{:S(2)}, u32[]{:S(2)}) %collective-permute-start.56) | collective-permute-done | bytes 262176 | tf_op jit(solution)/shard_map/ppermute | solution.py:579
  335.6 4.4 %shard_map.188 = (bf16[8,32,1024]{2,1,0:T(8,128)(2,1)}, bf16[8,32,1024]{2,1,0:T(8,128)(2,1)}) custom-call(s32[1]{0:T(128)} %bitcast.4.side, bf16[512,256]{1,0:T(8,128)(2,1)} %get-tuple-element.51.h0, bf16[512,256]{1,0:T(8,128)(2,1)} %get-tuple-element.93.h1, bf16[512,256]{1,0:T(8,128)(2,1)} %copy-done.37, bf16[512,256]{1,0:T(8,128)(2,1)} %get-tuple-element.92.h3, ...), custom_call_target="tpu_custom_call" | custom-call | tf_op jit(solution)/shard_map/pallas_call | solution.py:520
  340.9 1.3 collective-permute-start.51
  344.2 6.0 %collective-permute-done.59 = bf16[8,32,1024]{2,1,0:T(8,128)(2,1)S(1)} collective-permute-done((bf16[8,32,1024]{2,1,0:T(8,128)(2,1)}, bf16[8,32,1024]{2,1,0:T(8,128)(2,1)S(1)}, u32[]{:S(2)}, u32[]{:S(2)}) %collective-permute-start.59) | collective-permute-done | bytes 524320 | tf_op jit(solution)/shard_map/ppermute | solution.py:563
  350.4 1.3 collective-permute-start.62
  354.6 2.4 collective-permute-start.52
  357.0 5.1 %collective-permute-start.53 = (bf16[32,1024]{1,0:T(8,128)(2,1)S(1)}, bf16[32,1024]{1,0:T(8,128)(2,1)S(1)}, u32[]{:S(2)}, u32[]{:S(2)}) collective-permute-start(bf16[32,1024]{1,0:T(8,128)(2,1)S(1)} %get-tuple-element.95), channel_id=1, source_target_pairs={{0,16},{8,24},{16,0},{24,8},{1,17},{9,25},{17,1},{25,9},{2,18},{10... | collective-permute-start | bytes 196616 | tf_op jit(solution)/shard_map/ppermute | solution.py:555
  363.2 1.7 collective-permute-start.63
  364.9 4.7 %collective-permute-start.64 = (bf16[32,1024]{1,0:T(8,128)(2,1)S(1)}, bf16[32,1024]{1,0:T(8,128)(2,1)S(1)}, u32[]{:S(2)}, u32[]{:S(2)}) collective-permute-start(bf16[32,1024]{1,0:T(8,128)(2,1)S(1)} %get-tuple-element.89), channel_id=1, source_target_pairs={{0,16},{8,24},{16,0},{24,8},{1,17},{9,25},{17,1},{25,9},{2,18},{10... | collective-permute-start | bytes 196616 | tf_op jit(solution)/shard_map/ppermute | solution.py:555
  372.1 2.5 collective-permute-done.64.refs_6_
  375.3 1.9 shard_map.189
  (278 shorter events, 47.3 us)
Async XLA Ops:
  1.5 41.2 %collective-permute-start.15 = (bf16[2,512]{1,0:T(2,128)(2,1)S(1)}, bf16[2,512]{1,0:T(2,128)(2,1)S(1)}, u32[]{:S(2)}, u32[]{:S(2)}) collective-permute-start(bf16[2,512]{1,0:T(2,128)(2,1)S(1)} %reshape.143), channel_id=1, source_target_pairs={{0,1},{1,0},{2,3},{3,2},{4,5},{5,4},{6,7},{7,6},{8,9},{9,8},{10,11... | collective-permute-start | bytes 6152 | tf_op jit(solution)/shard_map/ppermute | solution.py:563
  4.4 42.9 %collective-permute-start.16 = (bf16[2,512]{1,0:T(2,128)(2,1)S(1)}, bf16[2,512]{1,0:T(2,128)(2,1)S(1)}, u32[]{:S(2)}, u32[]{:S(2)}) collective-permute-start(bf16[2,512]{1,0:T(2,128)(2,1)S(1)} %reshape.143), channel_id=1, source_target_pairs={{0,2},{2,0},{1,3},{3,1},{4,6},{6,4},{5,7},{7,5},{8,10},{10,8},{9,1... | collective-permute-start | bytes 6152 | tf_op jit(solution)/shard_map/ppermute | solution.py:567
  7.6 35.6 %collective-permute-start = (bf16[128,1024]{1,0:T(8,128)(2,1)}, bf16[128,1024]{1,0:T(8,128)(2,1)}, u32[]{:S(2)}, u32[]{:S(2)}) collective-permute-start(bf16[128,1024]{1,0:T(8,128)(2,1)} %broadcast_select_fusion.8), channel_id=1, source_target_pairs={{0,4},{4,0},{1,5},{5,1},{2,6},{6,2},{3,7},{7,3},{8,12},{12,8},{9,1... | collective-permute-start | bytes 786440 | tf_op jit(solution)/shard_map/ppermute | solution.py:559
  7.6 20.1 %collective-permute-start.39 = (s32[2]{0:T(128)}, s32[2]{0:T(128)S(1)}, u32[]{:S(2)}, u32[]{:S(2)}) collective-permute-start(s32[2]{0:T(128)} %param.19), channel_id=1, source_target_pairs={{0,4},{4,0},{1,5},{5,1},{2,6},{6,2},{3,7},{7,3},{8,12},{12,8},{9,1... | collective-permute-start | bytes 32 | tf_op jit(solution)/shard_map/ppermute | solution.py:559
  8.1 86.2 %collective-permute-start.47 = (bf16[1024,512]{1,0:T(8,128)(2,1)}, bf16[1024,512]{1,0:T(8,128)(2,1)S(1)}, u32[]{:S(2)}, u32[]{:S(2)}) collective-permute-start(bf16[1024,512]{1,0:T(8,128)(2,1)} %param.33), channel_id=1, source_target_pairs={{0,4},{4,0},{1,5},{5,1},{2,6},{6,2},{3,7},{7,3},{8,12},{12,8},{9,1... | collective-permute-start | bytes 3145736 | tf_op jit(solution)/shard_map/ppermute | solution.py:559
  27.7 5.4 %collective-permute-start.40 = (s32[2,2]{1,0:T(2,128)S(1)}, s32[2,2]{1,0:T(2,128)S(1)}, u32[]{:S(2)}, u32[]{:S(2)}) collective-permute-start(s32[2,2]{1,0:T(2,128)S(1)} %pad_add_fusion), channel_id=1, source_target_pairs={{0,8},{8,16},{16,24},{24,0},{1,9},{9,17},{17,25},{25,1},{2,10},{10... | collective-permute-start | bytes 56 | tf_op jit(solution)/shard_map/ppermute | solution.py:555
  44.9 12.9 %collective-permute-start.5 = (bf16[256,512]{1,0:T(8,128)(2,1)S(1)}, bf16[256,512]{1,0:T(8,128)(2,1)}, u32[]{:S(2)}, u32[]{:S(2)}) collective-permute-start(bf16[256,512]{1,0:T(8,128)(2,1)S(1)} %get-tuple-element.86), channel_id=1, source_target_pairs={{0,8},{8,16},{16,24},{1,9},{9,17},{17,25},{2,10},{10,18},{18,26},{... | collective-permute-start | bytes 786440 | tf_op jit(solution)/shard_map/ppermute | solution.py:576
  47.5 16.5 %collective-permute-start.6 = (bf16[256,512]{1,0:T(8,128)(2,1)S(1)}, bf16[256,512]{1,0:T(8,128)(2,1)}, u32[]{:S(2)}, u32[]{:S(2)}) collective-permute-start(bf16[256,512]{1,0:T(8,128)(2,1)S(1)} %get-tuple-element.86), channel_id=1, source_target_pairs={{0,16},{8,24},{16,0},{24,8},{1,17},{9,25},{17,1},{25,9},{2,18},{10... | collective-permute-start | bytes 786440 | tf_op jit(solution)/shard_map/ppermute | solution.py:555
  51.9 27.5 %collective-permute-start.7 = (bf16[256,512]{1,0:T(8,128)(2,1)S(1)}, bf16[256,512]{1,0:T(8,128)(2,1)S(1)}, u32[]{:S(2)}, u32[]{:S(2)}) collective-permute-start(bf16[256,512]{1,0:T(8,128)(2,1)S(1)} %get-tuple-element.86), channel_id=1, source_target_pairs={{8,0},{16,8},{24,16},{9,1},{17,9},{25,17},{10,2},{18,10},{26,18},{... | collective-permute-start | bytes 786440 | tf_op jit(solution)/shard_map/ppermute | solution.py:577
  53.2 13.1 %collective-permute-start.1 = (bf16[256,512]{1,0:T(8,128)(2,1)}, bf16[256,512]{1,0:T(8,128)(2,1)S(1)}, u32[]{:S(2)}, u32[]{:S(2)}) collective-permute-start(bf16[256,512]{1,0:T(8,128)(2,1)} %get-tuple-element.87), channel_id=1, source_target_pairs={{0,8},{8,16},{16,24},{1,9},{9,17},{17,25},{2,10},{10,18},{18,26},{... | collective-permute-start | bytes 786440 | tf_op jit(solution)/shard_map/ppermute | solution.py:576
  57.8 20.2 %collective-permute-start.2 = (bf16[256,512]{1,0:T(8,128)(2,1)}, bf16[256,512]{1,0:T(8,128)(2,1)S(1)}, u32[]{:S(2)}, u32[]{:S(2)}) collective-permute-start(bf16[256,512]{1,0:T(8,128)(2,1)} %get-tuple-element.87), channel_id=1, source_target_pairs={{0,16},{8,24},{16,0},{24,8},{1,17},{9,25},{17,1},{25,9},{2,18},{10... | collective-permute-start | bytes 786440 | tf_op jit(solution)/shard_map/ppermute | solution.py:555
  64.0 16.3 %collective-permute-start.3 = (bf16[256,512]{1,0:T(8,128)(2,1)}, bf16[256,512]{1,0:T(8,128)(2,1)S(1)}, u32[]{:S(2)}, u32[]{:S(2)}) collective-permute-start(bf16[256,512]{1,0:T(8,128)(2,1)} %get-tuple-element.87), channel_id=1, source_target_pairs={{8,0},{16,8},{24,16},{9,1},{17,9},{25,17},{10,2},{18,10},{26,18},{... | collective-permute-start | bytes 786440 | tf_op jit(solution)/shard_map/ppermute | solution.py:577
  66.3 18.9 %collective-permute-start.8 = (bf16[256,512]{1,0:T(8,128)(2,1)}, bf16[256,512]{1,0:T(8,128)(2,1)S(1)}, u32[]{:S(2)}, u32[]{:S(2)}) collective-permute-start(bf16[256,512]{1,0:T(8,128)(2,1)} %collective-permute-done.6), channel_id=1, source_target_pairs={{8,0},{16,24},{9,1},{17,25},{10,2},{18,26},{11,3},{19,27},{12,4},{... | collective-permute-start | bytes 786440 | tf_op jit(solution)/shard_map/ppermute | solution.py:579
  78.0 10.0 %collective-permute-start.4 = (bf16[256,512]{1,0:T(8,128)(2,1)S(1)}, bf16[256,512]{1,0:T(8,128)(2,1)S(1)}, u32[]{:S(2)}, u32[]{:S(2)}) collective-permute-start(bf16[256,512]{1,0:T(8,128)(2,1)S(1)} %collective-permute-done.2), channel_id=1, source_target_pairs={{8,0},{16,24},{9,1},{17,25},{10,2},{18,26},{11,3},{19,27},{12,4},{... | collective-permute-start | bytes 786440 | tf_op jit(solution)/shard_map/ppermute | solution.py:579
  89.1 37.5 %collective-permute-start.9 = (bf16[1024,512]{1,0:T(8,128)(2,1)S(1)}, bf16[1024,512]{1,0:T(8,128)(2,1)S(1)}, u32[]{:S(2)}, u32[]{:S(2)}) collective-permute-start(bf16[1024,512]{1,0:T(8,128)(2,1)S(1)} %bitcast.292), channel_id=1, source_target_pairs={{0,1},{1,0},{2,3},{3,2},{4,5},{5,4},{6,7},{7,6},{8,9},{9,8},{10,11... | collective-permute-start | bytes 3145736 | tf_op jit(solution)/shard_map/ppermute | solution.py:563
  89.7 38.4 %collective-permute-start.12 = (bf16[1024,512]{1,0:T(8,128)(2,1)S(1)}, bf16[1024,512]{1,0:T(8,128)(2,1)S(1)}, u32[]{:S(2)}, u32[]{:S(2)}) collective-permute-start(bf16[1024,512]{1,0:T(8,128)(2,1)S(1)} %bitcast.289), channel_id=1, source_target_pairs={{0,2},{2,0},{1,3},{3,1},{4,6},{6,4},{5,7},{7,5},{8,10},{10,8},{9,1... | collective-permute-start | bytes 3145736 | tf_op jit(solution)/shard_map/ppermute | solution.py:567
  91.3 16.7 %collective-permute-start.18 = (bf16[2,512,256]{2,1,0:T(8,128)(2,1)S(1)}, bf16[2,512,256]{2,1,0:T(8,128)(2,1)S(1)}, u32[]{:S(2)}, u32[]{:S(2)}) collective-permute-start(bf16[2,512,256]{2,1,0:T(8,128)(2,1)S(1)} %copy-done.28), channel_id=1, source_target_pairs={{0,8},{8,16},{16,24},{24,0},{1,9},{9,17},{17,25},{25,1},{2,10},{10... | collective-permute-start | bytes 1572872 | tf_op jit(solution)/shard_map/ppermute | solution.py:555
  91.3 34.3 %collective-permute-start.19 = (bf16[2,512,256]{2,1,0:T(8,128)(2,1)S(1)}, bf16[2,512,256]{2,1,0:T(8,128)(2,1)S(1)}, u32[]{:S(2)}, u32[]{:S(2)}) collective-permute-start(bf16[2,512,256]{2,1,0:T(8,128)(2,1)S(1)} %copy-done.27), channel_id=1, source_target_pairs={{0,16},{8,24},{16,0},{24,8},{1,17},{9,25},{17,1},{25,9},{2,18},{10... | collective-permute-start | bytes 1572872 | tf_op jit(solution)/shard_map/ppermute | solution.py:555
  94.3 31.4 %collective-permute-start.20 = (bf16[2,512,256]{2,1,0:T(8,128)(2,1)S(1)}, bf16[2,512,256]{2,1,0:T(8,128)(2,1)S(1)}, u32[]{:S(2)}, u32[]{:S(2)}) collective-permute-start(bf16[2,512,256]{2,1,0:T(8,128)(2,1)S(1)} %copy-done.26), channel_id=1, source_target_pairs={{0,24},{8,0},{16,8},{24,16},{1,25},{9,1},{17,9},{25,17},{2,26},{10... | collective-permute-start | bytes 1572872 | tf_op jit(solution)/shard_map/ppermute | solution.py:555
  108.0 18.3 %collective-permute-start.21 = (bf16[2,512,256]{2,1,0:T(8,128)(2,1)S(1)}, bf16[2,512,256]{2,1,0:T(8,128)(2,1)S(1)}, u32[]{:S(2)}, u32[]{:S(2)}) collective-permute-start(bf16[2,512,256]{2,1,0:T(8,128)(2,1)S(1)} %get-tuple-element.29), channel_id=1, source_target_pairs={{0,4},{4,0},{1,5},{5,1},{2,6},{6,2},{3,7},{7,3},{8,12},{12,8},{9,1... | collective-permute-start | bytes 1572872 | tf_op jit(solution)/shard_map/ppermute | solution.py:559
  125.6 13.3 %collective-permute-start.22 = (bf16[2,512,256]{2,1,0:T(8,128)(2,1)S(1)}, bf16[2,512,256]{2,1,0:T(8,128)(2,1)S(1)}, u32[]{:S(2)}, u32[]{:S(2)}) collective-permute-start(bf16[2,512,256]{2,1,0:T(8,128)(2,1)S(1)} %collective-permute-done.18), channel_id=1, source_target_pairs={{0,4},{4,0},{1,5},{5,1},{2,6},{6,2},{3,7},{7,3},{8,12},{12,8},{9,1... | collective-permute-start | bytes 1572872 | tf_op jit(solution)/shard_map/ppermute | solution.py:559
  125.7 13.5 %collective-permute-start.23 = (bf16[2,512,256]{2,1,0:T(8,128)(2,1)S(1)}, bf16[2,512,256]{2,1,0:T(8,128)(2,1)S(1)}, u32[]{:S(2)}, u32[]{:S(2)}) collective-permute-start(bf16[2,512,256]{2,1,0:T(8,128)(2,1)S(1)} %collective-permute-done.19), channel_id=1, source_target_pairs={{0,4},{4,0},{1,5},{5,1},{2,6},{6,2},{3,7},{7,3},{8,12},{12,8},{9,1... | collective-permute-start | bytes 1572872 | tf_op jit(solution)/shard_map/ppermute | solution.py:559
  126.3 13.0 %collective-permute-start.24 = (bf16[2,512,256]{2,1,0:T(8,128)(2,1)S(1)}, bf16[2,512,256]{2,1,0:T(8,128)(2,1)S(1)}, u32[]{:S(2)}, u32[]{:S(2)}) collective-permute-start(bf16[2,512,256]{2,1,0:T(8,128)(2,1)S(1)} %collective-permute-done.20), channel_id=1, source_target_pairs={{0,4},{4,0},{1,5},{5,1},{2,6},{6,2},{3,7},{7,3},{8,12},{12,8},{9,1... | collective-permute-start | bytes 1572872 | tf_op jit(solution)/shard_map/ppermute | solution.py:559
  126.6 62.8 %collective-permute-start.10 = (bf16[1024,512]{1,0:T(8,128)(2,1)S(1)}, bf16[1024,512]{1,0:T(8,128)(2,1)S(1)}, u32[]{:S(2)}, u32[]{:S(2)}) collective-permute-start(bf16[1024,512]{1,0:T(8,128)(2,1)S(1)} %bitcast.290), channel_id=1, source_target_pairs={{0,1},{1,0},{2,3},{3,2},{4,5},{5,4},{6,7},{7,6},{8,9},{9,8},{10,11... | collective-permute-start | bytes 3145736 | tf_op jit(solution)/shard_map/ppermute | solution.py:563
  128.2 28.5 %collective-permute-start.25 = (bf16[1,512,256]{2,1,0:T(8,128)(2,1)S(1)}, bf16[1,512,256]{2,1,0:T(8,128)(2,1)S(1)}, u32[]{:S(2)}, u32[]{:S(2)}) collective-permute-start(bf16[1,512,256]{2,1,0:T(8,128)(2,1)S(1)} %copy-done.33), channel_id=1, source_target_pairs={{0,8},{8,16},{16,24},{24,0},{1,9},{9,17},{17,25},{25,1},{2,10},{10... | collective-permute-start | bytes 786440 | tf_op jit(solution)/shard_map/ppermute | solution.py:555
  138.9 17.6 %collective-permute-start.26 = (bf16[1,512,256]{2,1,0:T(8,128)(2,1)S(1)}, bf16[1,512,256]{2,1,0:T(8,128)(2,1)S(1)}, u32[]{:S(2)}, u32[]{:S(2)}) collective-permute-start(bf16[1,512,256]{2,1,0:T(8,128)(2,1)S(1)} %copy-done.34), channel_id=1, source_target_pairs={{0,16},{8,24},{16,0},{24,8},{1,17},{9,25},{17,1},{25,9},{2,18},{10... | collective-permute-start | bytes 786440 | tf_op jit(solution)/shard_map/ppermute | solution.py:555
  139.1 23.0 %collective-permute-start.28 = (bf16[1,512,256]{2,1,0:T(8,128)(2,1)S(1)}, bf16[1,512,256]{2,1,0:T(8,128)(2,1)S(1)}, u32[]{:S(2)}, u32[]{:S(2)}) collective-permute-start(bf16[1,512,256]{2,1,0:T(8,128)(2,1)S(1)} %copy-done.17), channel_id=1, source_target_pairs={{0,4},{4,0},{1,5},{5,1},{2,6},{6,2},{3,7},{7,3},{8,12},{12,8},{9,1... | collective-permute-start | bytes 786440 | tf_op jit(solution)/shard_map/ppermute | solution.py:559
  140.1 21.7 %collective-permute-start.27 = (bf16[1,512,256]{2,1,0:T(8,128)(2,1)S(1)}, bf16[1,512,256]{2,1,0:T(8,128)(2,1)S(1)}, u32[]{:S(2)}, u32[]{:S(2)}) collective-permute-start(bf16[1,512,256]{2,1,0:T(8,128)(2,1)S(1)} %copy-done.32), channel_id=1, source_target_pairs={{0,24},{8,0},{16,8},{24,16},{1,25},{9,1},{17,9},{25,17},{2,26},{10... | collective-permute-start | bytes 786440 | tf_op jit(solution)/shard_map/ppermute | solution.py:555
  156.5 29.2 %collective-permute-start.35 = (bf16[1,512,256]{2,1,0:T(8,128)(2,1)S(1)}, bf16[1,512,256]{2,1,0:T(8,128)(2,1)S(1)}, u32[]{:S(2)}, u32[]{:S(2)}) collective-permute-start(bf16[1,512,256]{2,1,0:T(8,128)(2,1)S(1)} %get-tuple-element.38), channel_id=1, source_target_pairs={{0,4},{4,0},{1,5},{5,1},{2,6},{6,2},{3,7},{7,3},{8,12},{12,8},{9,1... | collective-permute-start | bytes 786440 | tf_op jit(solution)/shard_map/ppermute | solution.py:559
  156.7 15.1 %collective-permute-start.32 = (bf16[1,512,256]{2,1,0:T(8,128)(2,1)S(1)}, bf16[1,512,256]{2,1,0:T(8,128)(2,1)S(1)}, u32[]{:S(2)}, u32[]{:S(2)}) collective-permute-start(bf16[1,512,256]{2,1,0:T(8,128)(2,1)S(1)} %copy-done.31), channel_id=1, source_target_pairs={{0,8},{8,16},{16,24},{24,0},{1,9},{9,17},{17,25},{25,1},{2,10},{10... | collective-permute-start | bytes 786440 | tf_op jit(solution)/shard_map/ppermute | solution.py:555
  162.1 4.7 %collective-permute-start.30 = (bf16[1,512,256]{2,1,0:T(8,128)(2,1)S(1)}, bf16[1,512,256]{2,1,0:T(8,128)(2,1)S(1)}, u32[]{:S(2)}, u32[]{:S(2)}) collective-permute-start(bf16[1,512,256]{2,1,0:T(8,128)(2,1)S(1)} %collective-permute-done.26), channel_id=1, source_target_pairs={{0,4},{4,0},{1,5},{5,1},{2,6},{6,2},{3,7},{7,3},{8,12},{12,8},{9,1... | collective-permute-start | bytes 786440 | tf_op jit(solution)/shard_map/ppermute | solution.py:559
  163.4 19.5 %collective-permute-start.33 = (bf16[1,512,256]{2,1,0:T(8,128)(2,1)S(1)}, bf16[1,512,256]{2,1,0:T(8,128)(2,1)S(1)}, u32[]{:S(2)}, u32[]{:S(2)}) collective-permute-start(bf16[1,512,256]{2,1,0:T(8,128)(2,1)S(1)} %copy-done.30), channel_id=1, source_target_pairs={{0,16},{8,24},{16,0},{24,8},{1,17},{9,25},{17,1},{25,9},{2,18},{10... | collective-permute-start | bytes 786440 | tf_op jit(solution)/shard_map/ppermute | solution.py:555
  166.8 7.7 %collective-permute-start.31 = (bf16[1,512,256]{2,1,0:T(8,128)(2,1)S(1)}, bf16[1,512,256]{2,1,0:T(8,128)(2,1)S(1)}, u32[]{:S(2)}, u32[]{:S(2)}) collective-permute-start(bf16[1,512,256]{2,1,0:T(8,128)(2,1)S(1)} %collective-permute-done.27), channel_id=1, source_target_pairs={{0,4},{4,0},{1,5},{5,1},{2,6},{6,2},{3,7},{7,3},{8,12},{12,8},{9,1... | collective-permute-start | bytes 786440 | tf_op jit(solution)/shard_map/ppermute | solution.py:559
  171.8 13.4 %collective-permute-start.34 = (bf16[1,512,256]{2,1,0:T(8,128)(2,1)S(1)}, bf16[1,512,256]{2,1,0:T(8,128)(2,1)S(1)}, u32[]{:S(2)}, u32[]{:S(2)}) collective-permute-start(bf16[1,512,256]{2,1,0:T(8,128)(2,1)S(1)} %copy-done.29), channel_id=1, source_target_pairs={{0,24},{8,0},{16,8},{24,16},{1,25},{9,1},{17,9},{25,17},{2,26},{10... | collective-permute-start | bytes 786440 | tf_op jit(solution)/shard_map/ppermute | solution.py:555
  174.5 11.7 %collective-permute-start.36 = (bf16[1,512,256]{2,1,0:T(8,128)(2,1)S(1)}, bf16[1,512,256]{2,1,0:T(8,128)(2,1)S(1)}, u32[]{:S(2)}, u32[]{:S(2)}) collective-permute-start(bf16[1,512,256]{2,1,0:T(8,128)(2,1)S(1)} %collective-permute-done.32), channel_id=1, source_target_pairs={{0,4},{4,0},{1,5},{5,1},{2,6},{6,2},{3,7},{7,3},{8,12},{12,8},{9,1... | collective-permute-start | bytes 786440 | tf_op jit(solution)/shard_map/ppermute | solution.py:559
  182.8 26.0 %collective-permute-start.11 = (bf16[1024,512]{1,0:T(8,128)(2,1)S(1)}, bf16[1024,512]{1,0:T(8,128)(2,1)S(1)}, u32[]{:S(2)}, u32[]{:S(2)}) collective-permute-start(bf16[1024,512]{1,0:T(8,128)(2,1)S(1)} %bitcast.293), channel_id=1, source_target_pairs={{0,2},{2,0},{1,3},{3,1},{4,6},{6,4},{5,7},{7,5},{8,10},{10,8},{9,1... | collective-permute-start | bytes 3145736 | tf_op jit(solution)/shard_map/ppermute | solution.py:567
  185.2 45.2 %collective-permute-start.13 = (bf16[1024,512]{1,0:T(8,128)(2,1)S(1)}, bf16[1024,512]{1,0:T(8,128)(2,1)S(1)}, u32[]{:S(2)}, u32[]{:S(2)}) collective-permute-start(bf16[1024,512]{1,0:T(8,128)(2,1)S(1)} %collective-permute-done.9.c2), channel_id=1, source_target_pairs={{0,2},{2,0},{1,3},{3,1},{4,6},{6,4},{5,7},{7,5},{8,10},{10,8},{9,1... | collective-permute-start | bytes 3145736 | tf_op jit(solution)/shard_map/ppermute | solution.py:567
  185.7 44.7 %collective-permute-start.14 = (bf16[1024,512]{1,0:T(8,128)(2,1)S(1)}, bf16[1024,512]{1,0:T(8,128)(2,1)S(1)}, u32[]{:S(2)}, u32[]{:S(2)}) collective-permute-start(bf16[1024,512]{1,0:T(8,128)(2,1)S(1)} %collective-permute-done.12.c5), channel_id=1, source_target_pairs={{0,1},{1,0},{2,3},{3,2},{4,5},{5,4},{6,7},{7,6},{8,9},{9,8},{10,11... | collective-permute-start | bytes 3145736 | tf_op jit(solution)/shard_map/ppermute | solution.py:563
  280.4 16.0 %collective-permute-start.43 = (bf16[512,256]{1,0:T(8,128)(2,1)}, bf16[512,256]{1,0:T(8,128)(2,1)S(1)}, u32[]{:S(2)}, u32[]{:S(2)}) collective-permute-start(bf16[512,256]{1,0:T(8,128)(2,1)} %get-tuple-element.47.h0), channel_id=1, source_target_pairs={{0,16},{8,24},{16,0},{24,8},{1,17},{9,25},{17,1},{25,9},{2,18},{10... | collective-permute-start | bytes 786440 | tf_op jit(solution)/shard_map/ppermute | solution.py:555
  280.5 17.2 %collective-permute-start.66 = (bf16[4,2,4,64,64]{4,3,2,1,0:T(8,128)(2,1)S(1)}, bf16[4,2,4,64,64]{4,3,2,1,0:T(8,128)(2,1)S(1)}, u32[]{:S(2)}, u32[]{:S(2)}) collective-permute-start(bf16[4,2,4,64,64]{4,3,2,1,0:T(8,128)(2,1)S(1)} %dynamic-slice_bitcast_fusion), channel_id=1, source_target_pairs={{0,4},{4,0},{1,5},{5,1},{2,6},{6,2},{3,7},{7,3},{8,12},{12,8},{9,1... | collective-permute-start | bytes 786440 | tf_op jit(solution)/shard_map/ppermute | solution.py:559
  282.4 17.2 %collective-permute-start.46 = (bf16[512,256]{1,0:T(8,128)(2,1)S(1)}, bf16[512,256]{1,0:T(8,128)(2,1)S(1)}, u32[]{:S(2)}, u32[]{:S(2)}) collective-permute-start(bf16[512,256]{1,0:T(8,128)(2,1)S(1)} %copy-done.36), channel_id=1, source_target_pairs={{8,0},{16,8},{24,16},{9,1},{17,9},{25,17},{10,2},{18,10},{26,18},{... | collective-permute-start | bytes 786440 | tf_op jit(solution)/shard_map/ppermute | solution.py:577
  283.7 26.4 %collective-permute-start.45 = (bf16[512,256]{1,0:T(8,128)(2,1)S(1)}, bf16[512,256]{1,0:T(8,128)(2,1)S(1)}, u32[]{:S(2)}, u32[]{:S(2)}) collective-permute-start(bf16[512,256]{1,0:T(8,128)(2,1)S(1)} %copy-done.36), channel_id=1, source_target_pairs={{0,8},{8,16},{16,24},{1,9},{9,17},{17,25},{2,10},{10,18},{18,26},{... | collective-permute-start | bytes 786440 | tf_op jit(solution)/shard_map/ppermute | solution.py:576
  296.4 24.2 %collective-permute-start.55 = (bf16[512,256]{1,0:T(8,128)(2,1)S(1)}, bf16[512,256]{1,0:T(8,128)(2,1)S(1)}, u32[]{:S(2)}, u32[]{:S(2)}) collective-permute-start(bf16[512,256]{1,0:T(8,128)(2,1)S(1)} %copy-done.35), channel_id=1, source_target_pairs={{0,16},{8,24},{16,0},{24,8},{1,17},{9,25},{17,1},{25,9},{2,18},{10... | collective-permute-start | bytes 786440 | tf_op jit(solution)/shard_map/ppermute | solution.py:555
  296.4 31.3 %collective-permute-start.58 = (bf16[512,256]{1,0:T(8,128)(2,1)S(1)}, bf16[512,256]{1,0:T(8,128)(2,1)S(1)}, u32[]{:S(2)}, u32[]{:S(2)}) collective-permute-start(bf16[512,256]{1,0:T(8,128)(2,1)S(1)} %copy-done.35), channel_id=1, source_target_pairs={{8,0},{16,8},{24,16},{9,1},{17,9},{25,17},{10,2},{18,10},{26,18},{... | collective-permute-start | bytes 786440 | tf_op jit(solution)/shard_map/ppermute | solution.py:577
  297.7 22.9 %collective-permute-start.44 = (bf16[512,256]{1,0:T(8,128)(2,1)S(1)}, bf16[512,256]{1,0:T(8,128)(2,1)S(1)}, u32[]{:S(2)}, u32[]{:S(2)}) collective-permute-start(bf16[512,256]{1,0:T(8,128)(2,1)S(1)} %collective-permute-done.43.h2), channel_id=1, source_target_pairs={{8,0},{16,24},{9,1},{17,25},{10,2},{18,26},{11,3},{19,27},{12,4},{... | collective-permute-start | bytes 786440 | tf_op jit(solution)/shard_map/ppermute | solution.py:579
  299.7 30.0 %collective-permute-start.57 = (bf16[512,256]{1,0:T(8,128)(2,1)S(1)}, bf16[512,256]{1,0:T(8,128)(2,1)S(1)}, u32[]{:S(2)}, u32[]{:S(2)}) collective-permute-start(bf16[512,256]{1,0:T(8,128)(2,1)S(1)} %copy-done.35), channel_id=1, source_target_pairs={{0,8},{8,16},{16,24},{1,9},{9,17},{17,25},{2,10},{10,18},{18,26},{... | collective-permute-start | bytes 786440 | tf_op jit(solution)/shard_map/ppermute | solution.py:576
  310.1 17.0 %collective-permute-start.67 = (bf16[3,4,64,64]{3,2,1,0:T(8,128)(2,1)S(1)}, bf16[3,4,64,64]{3,2,1,0:T(8,128)(2,1)S(1)}, u32[]{:S(2)}, u32[]{:S(2)}) collective-permute-start(bf16[3,4,64,64]{3,2,1,0:T(8,128)(2,1)S(1)} %get-tuple-element.82), channel_id=1, source_target_pairs={{0,8},{8,16},{16,24},{24,0},{1,9},{9,17},{17,25},{25,1},{2,10},{10... | collective-permute-start | bytes 294920 | tf_op jit(solution)/shard_map/ppermute | solution.py:555
  320.6 19.9 %collective-permute-start.68 = (bf16[3,4,64,64]{3,2,1,0:T(8,128)(2,1)S(1)}, bf16[3,4,64,64]{3,2,1,0:T(8,128)(2,1)S(1)}, u32[]{:S(2)}, u32[]{:S(2)}) collective-permute-start(bf16[3,4,64,64]{3,2,1,0:T(8,128)(2,1)S(1)} %get-tuple-element.83), channel_id=1, source_target_pairs={{0,16},{8,24},{16,0},{24,8},{1,17},{9,25},{17,1},{25,9},{2,18},{10... | collective-permute-start | bytes 294920 | tf_op jit(solution)/shard_map/ppermute | solution.py:555
  320.6 14.1 %collective-permute-start.56 = (bf16[512,256]{1,0:T(8,128)(2,1)S(1)}, bf16[512,256]{1,0:T(8,128)(2,1)S(1)}, u32[]{:S(2)}, u32[]{:S(2)}) collective-permute-start(bf16[512,256]{1,0:T(8,128)(2,1)S(1)} %collective-permute-done.55.h2), channel_id=1, source_target_pairs={{8,0},{16,24},{9,1},{17,25},{10,2},{18,26},{11,3},{19,27},{12,4},{... | collective-permute-start | bytes 786440 | tf_op jit(solution)/shard_map/ppermute | solution.py:579
  327.1 13.5 %collective-permute-start.48 = (bf16[8,32,1024]{2,1,0:T(8,128)(2,1)}, bf16[8,32,1024]{2,1,0:T(8,128)(2,1)S(1)}, u32[]{:S(2)}, u32[]{:S(2)}) collective-permute-start(bf16[8,32,1024]{2,1,0:T(8,128)(2,1)} %get-tuple-element.49), channel_id=1, source_target_pairs={{0,1},{1,0},{2,3},{3,2},{4,5},{5,4},{6,7},{7,6},{8,9},{9,8},{10,11... | collective-permute-start | bytes 1572872 | tf_op jit(solution)/shard_map/ppermute | solution.py:563
  327.7 37.2 %collective-permute-start.69 = (bf16[3,4,64,64]{3,2,1,0:T(8,128)(2,1)S(1)}, bf16[3,4,64,64]{3,2,1,0:T(8,128)(2,1)S(1)}, u32[]{:S(2)}, u32[]{:S(2)}) collective-permute-start(bf16[3,4,64,64]{3,2,1,0:T(8,128)(2,1)S(1)} %get-tuple-element.81), channel_id=1, source_target_pairs={{0,24},{8,0},{16,8},{24,16},{1,25},{9,1},{17,9},{25,17},{2,26},{10... | collective-permute-start | bytes 294920 | tf_op jit(solution)/shard_map/ppermute | solution.py:555
  340.0 10.2 %collective-permute-start.59 = (bf16[8,32,1024]{2,1,0:T(8,128)(2,1)}, bf16[8,32,1024]{2,1,0:T(8,128)(2,1)S(1)}, u32[]{:S(2)}, u32[]{:S(2)}) collective-permute-start(bf16[8,32,1024]{2,1,0:T(8,128)(2,1)} %get-tuple-element.53), channel_id=1, source_target_pairs={{0,1},{1,0},{2,3},{3,2},{4,5},{5,4},{6,7},{7,6},{8,9},{9,8},{10,11... | collective-permute-start | bytes 1572872 | tf_op jit(solution)/shard_map/ppermute | solution.py:563
  340.9 10.9 %collective-permute-start.51 = (bf16[4,32,1024]{2,1,0:T(8,128)(2,1)S(1)}, bf16[4,32,1024]{2,1,0:T(8,128)(2,1)S(1)}, u32[]{:S(2)}, u32[]{:S(2)}) collective-permute-start(bf16[4,32,1024]{2,1,0:T(8,128)(2,1)S(1)} %get-tuple-element.70), channel_id=1, source_target_pairs={{0,4},{6,2},{1,5},{7,3},{8,12},{14,10},{9,13},{15,11},{16,20},{22,... | collective-permute-start | bytes 786440 | tf_op jit(solution)/shard_map/ppermute | solution.py:792
  342.2 10.3 %collective-permute-start.50 = (bf16[4,32,1024]{2,1,0:T(8,128)(2,1)S(1)}, bf16[4,32,1024]{2,1,0:T(8,128)(2,1)S(1)}, u32[]{:S(2)}, u32[]{:S(2)}) collective-permute-start(bf16[4,32,1024]{2,1,0:T(8,128)(2,1)S(1)} %get-tuple-element.70), channel_id=1, source_target_pairs={{2,4},{4,2},{3,5},{5,3},{10,12},{12,10},{11,13},{13,11},{18,20},{2... | collective-permute-start | bytes 786440 | tf_op jit(solution)/shard_map/ppermute | solution.py:791
  342.9 10.9 %collective-permute-start.49 = (bf16[4,32,1024]{2,1,0:T(8,128)(2,1)S(1)}, bf16[4,32,1024]{2,1,0:T(8,128)(2,1)S(1)}, u32[]{:S(2)}, u32[]{:S(2)}) collective-permute-start(bf16[4,32,1024]{2,1,0:T(8,128)(2,1)S(1)} %get-tuple-element.69), channel_id=1, source_target_pairs={{2,0},{4,6},{3,1},{5,7},{10,8},{12,14},{11,9},{13,15},{18,16},{20,... | collective-permute-start | bytes 786440 | tf_op jit(solution)/shard_map/ppermute | solution.py:790
  350.4 6.5 %collective-permute-start.62 = (bf16[4,32,1024]{2,1,0:T(8,128)(2,1)S(1)}, bf16[4,32,1024]{2,1,0:T(8,128)(2,1)S(1)}, u32[]{:S(2)}, u32[]{:S(2)}) collective-permute-start(bf16[4,32,1024]{2,1,0:T(8,128)(2,1)S(1)} %get-tuple-element.68), channel_id=1, source_target_pairs={{0,4},{6,2},{1,5},{7,3},{8,12},{14,10},{9,13},{15,11},{16,20},{22,... | collective-permute-start | bytes 786440 | tf_op jit(solution)/shard_map/ppermute | solution.py:792
  351.8 10.3 %collective-permute-start.61 = (bf16[4,32,1024]{2,1,0:T(8,128)(2,1)S(1)}, bf16[4,32,1024]{2,1,0:T(8,128)(2,1)S(1)}, u32[]{:S(2)}, u32[]{:S(2)}) collective-permute-start(bf16[4,32,1024]{2,1,0:T(8,128)(2,1)S(1)} %get-tuple-element.68), channel_id=1, source_target_pairs={{2,4},{4,2},{3,5},{5,3},{10,12},{12,10},{11,13},{13,11},{18,20},{2... | collective-permute-start | bytes 786440 | tf_op jit(solution)/shard_map/ppermute | solution.py:791
  352.5 9.9 %collective-permute-start.60 = (bf16[4,32,1024]{2,1,0:T(8,128)(2,1)S(1)}, bf16[4,32,1024]{2,1,0:T(8,128)(2,1)S(1)}, u32[]{:S(2)}, u32[]{:S(2)}) collective-permute-start(bf16[4,32,1024]{2,1,0:T(8,128)(2,1)S(1)} %get-tuple-element.67), channel_id=1, source_target_pairs={{2,0},{4,6},{3,1},{5,7},{10,8},{12,14},{11,9},{13,15},{18,16},{20,... | collective-permute-start | bytes 786440 | tf_op jit(solution)/shard_map/ppermute | solution.py:790
  354.6 15.1 %collective-permute-start.52 = (bf16[32,1024]{1,0:T(8,128)(2,1)S(1)}, bf16[32,1024]{1,0:T(8,128)(2,1)S(1)}, u32[]{:S(2)}, u32[]{:S(2)}) collective-permute-start(bf16[32,1024]{1,0:T(8,128)(2,1)S(1)} %get-tuple-element.96), channel_id=1, source_target_pairs={{0,8},{8,16},{16,24},{24,0},{1,9},{9,17},{17,25},{25,1},{2,10},{10... | collective-permute-start | bytes 196616 | tf_op jit(solution)/shard_map/ppermute | solution.py:555
  357.0 14.9 %collective-permute-start.53 = (bf16[32,1024]{1,0:T(8,128)(2,1)S(1)}, bf16[32,1024]{1,0:T(8,128)(2,1)S(1)}, u32[]{:S(2)}, u32[]{:S(2)}) collective-permute-start(bf16[32,1024]{1,0:T(8,128)(2,1)S(1)} %get-tuple-element.95), channel_id=1, source_target_pairs={{0,16},{8,24},{16,0},{24,8},{1,17},{9,25},{17,1},{25,9},{2,18},{10... | collective-permute-start | bytes 196616 | tf_op jit(solution)/shard_map/ppermute | solution.py:555
  362.1 9.8 %collective-permute-start.54 = (bf16[32,1024]{1,0:T(8,128)(2,1)S(1)}, bf16[32,1024]{1,0:T(8,128)(2,1)S(1)}, u32[]{:S(2)}, u32[]{:S(2)}) collective-permute-start(bf16[32,1024]{1,0:T(8,128)(2,1)S(1)} %get-tuple-element.94), channel_id=1, source_target_pairs={{0,24},{8,0},{16,8},{24,16},{1,25},{9,1},{17,9},{25,17},{2,26},{10... | collective-permute-start | bytes 196616 | tf_op jit(solution)/shard_map/ppermute | solution.py:555
  363.2 8.9 %collective-permute-start.63 = (bf16[32,1024]{1,0:T(8,128)(2,1)S(1)}, bf16[32,1024]{1,0:T(8,128)(2,1)S(1)}, u32[]{:S(2)}, u32[]{:S(2)}) collective-permute-start(bf16[32,1024]{1,0:T(8,128)(2,1)S(1)} %get-tuple-element.90), channel_id=1, source_target_pairs={{0,8},{8,16},{16,24},{24,0},{1,9},{9,17},{17,25},{25,1},{2,10},{10... | collective-permute-start | bytes 196616 | tf_op jit(solution)/shard_map/ppermute | solution.py:555
  364.9 9.7 %collective-permute-start.64 = (bf16[32,1024]{1,0:T(8,128)(2,1)S(1)}, bf16[32,1024]{1,0:T(8,128)(2,1)S(1)}, u32[]{:S(2)}, u32[]{:S(2)}) collective-permute-start(bf16[32,1024]{1,0:T(8,128)(2,1)S(1)} %get-tuple-element.89), channel_id=1, source_target_pairs={{0,16},{8,24},{16,0},{24,8},{1,17},{9,25},{17,1},{25,9},{2,18},{10... | collective-permute-start | bytes 196616 | tf_op jit(solution)/shard_map/ppermute | solution.py:555
  369.6 5.0 %collective-permute-start.65 = (bf16[32,1024]{1,0:T(8,128)(2,1)S(1)}, bf16[32,1024]{1,0:T(8,128)(2,1)S(1)}, u32[]{:S(2)}, u32[]{:S(2)}) collective-permute-start(bf16[32,1024]{1,0:T(8,128)(2,1)S(1)} %get-tuple-element.88), channel_id=1, source_target_pairs={{0,24},{8,0},{16,8},{24,16},{1,25},{9,1},{17,9},{25,17},{2,26},{10... | collective-permute-start | bytes 196616 | tf_op jit(solution)/shard_map/ppermute | solution.py:555
  (53 other events, 851.7 us)

commit v3 on v2

--- a/solution.py
+++ b/solution.py
@@ -265,35 +265,189 @@
     return pltpu.CompilerParams(vmem_limit_bytes=VMEM_LIMIT)
 
 
-def previous_rows(x_ref, first_row, tile, start):
-    here = x_ref[pl.ds(pl.multiple_of(tile * TILE, TILE), TILE), :].astype(f32)
-    above_at = jnp.maximum(tile * TILE - 16, 0)
-    above = x_ref[pl.ds(pl.multiple_of(above_at, 16), 16), :].astype(f32)[15:16]
+EXTRA = 16
+
+
+def here_and_step(x_ref, is_long, period, tile):
+    rows = x_ref.shape[1] - EXTRA
+    here = x_ref[tile, 0:rows, :].astype(f32)
+    above = x_ref[jnp.maximum(tile - 1, 0), rows - 16 : rows, :].astype(f32)[15:16]
+    first = jnp.where(is_long == 1, x_ref[0, rows : rows + 16, :].astype(f32)[0:1], 0.0)
     row = lax.broadcasted_iota(jnp.int32, here.shape, 0)
     before = jnp.where(row == 0, above, pltpu.roll(here, 1, 0))
-    before = jnp.where(start, first_row, before)
+    start = ((row + tile * rows) & (period - 1)) == 0
+    before = jnp.where(start, first, before)
     return here, before - here
 
 
-def mixed_kernel(
-    place,
-    period,
-    c0,
-    c1,
-    c2,
-    c3,
-    c4,
-    c5,
-    c6,
-    c7,
-    first,
+def given_kernel(kind, extents, long_ref, short_ref, out_ref):
+    rows = long_ref.shape[0]
+    is_long = kind[0] == 1
+    out_ref[0:rows, :] = jnp.where(is_long, short_ref[...], long_ref[...])
+    lane = lax.broadcasted_iota(jnp.int32, (EXTRA, out_ref.shape[1]), 1)
+    line = jnp.zeros(lane.shape, f32)
+    for n in range(extents.shape[0]):
+        line = jnp.where(lane == n, extents[n].astype(f32), line)
+    out_ref[rows : rows + EXTRA, :] = line.astype(bf16)
+
+
+def given_to_other_core(kind, extents, long_rows, short_rows):
+    rows, columns = long_rows.shape
+    return pl.pallas_call(
+        given_kernel,
+        out_shape=jax.ShapeDtypeStruct((rows + EXTRA, columns), bf16),
+        in_specs=[in_smem()] * 2 + [in_vmem()] * 2,
+        out_specs=in_vmem(),
+        compiler_params=kernel_params(),
+    )(kind, extents, long_rows, short_rows)
+
+
+def block_kernel(kind, extents, long_ref, short_ref, taken, edge, out_ref):
+    rows = long_ref.shape[0]
+    depth = out_ref.shape[2]
+    is_long = kind[0] == 1
+    count = extents.shape[0]
+    row = lax.broadcasted_iota(jnp.int32, (EXTRA, depth), 0)
+    lane = lax.broadcasted_iota(jnp.int32, (EXTRA, depth), 1)
+    other = taken[rows : rows + EXTRA, 0:depth].astype(f32)
+    line = jnp.where(is_long, pltpu.roll(other, count, 1), other)
+    own_at = jnp.where(is_long, 0, count)
+    for n in range(count):
+        line = jnp.where(lane == own_at + n, extents[n].astype(f32), line)
+    for half in range(2):
+        start = jnp.where(is_long, half, 1 - half) * depth
+        at = pl.ds(pl.multiple_of(start, depth), depth)
+        got = taken[0:rows, at]
+        out_ref[half, 0:rows, :] = jnp.where(is_long, long_ref[:, at], got)
+        out_ref[half, rows : 2 * rows, :] = jnp.where(is_long, got, short_ref[:, at])
+        first = edge[:, at].astype(f32)
+        out_ref[half, 2 * rows :, :] = jnp.where(row == 0, first, line).astype(bf16)
+
+
+def block_of_chip(kind, extents, long_rows, short_rows, taken, edge):
+    rows, columns = long_rows.shape
+    return pl.pallas_call(
+        block_kernel,
+        out_shape=jax.ShapeDtypeStruct((2, 2 * rows + EXTRA, columns // 2), bf16),
+        in_specs=[in_smem()] * 2 + [in_vmem()] * 4,
+        out_specs=in_vmem(),
+        compiler_params=kernel_params(),
+    )(kind, extents, long_rows, short_rows, taken, edge)
+
+
+def half_block(shape):
+    return pl.BlockSpec((1,) + shape[1:], lambda i: (i,) + (0,) * (len(shape) - 1))
+
+
+def mix_kernel(kind, chunk, ratios, left, pair_mix, value_mix, gate_mix, squeezed):
+    @pl.loop(0, chunk.shape[1])
+    def _(tile):
+        here, step = here_and_step(chunk.at[0], kind[0], kind[1], tile)
+        at = pl.ds(pl.multiple_of(tile * TILE, TILE), TILE)
+
+        def mix(which):
+            return (here + ratios[0, which : which + 1, :] * step).astype(bf16)
+
+        pair_mix[0, 0, at, :] = mix(0)
+        pair_mix[0, 1, at, :] = mix(1)
+        value_mix[0, at, :] = mix(2)
+        gate_mix[0, at, :] = mix(3)
+        squeezed[0, at, :] = jnp.dot(mix(4), left[0], preferred_element_type=f32)
+
+
+def mixes_of(kind, pair, ratios, left):
+    lines, rows, depth = pair.shape[1], pair.shape[2] - EXTRA, pair.shape[3]
+    whole = lines * rows
+    outs = [
+        jax.ShapeDtypeStruct((2, 2, whole, depth), bf16),
+        jax.ShapeDtypeStruct((2, whole, depth), bf16),
+        jax.ShapeDtypeStruct((2, whole, depth), bf16),
+        jax.ShapeDtypeStruct((2, whole, left.shape[2]), f32),
+    ]
+    return pl.pallas_call(
+        mix_kernel,
+        grid=(2,),
+        out_shape=outs,
+        in_specs=[in_smem()] + [half_block(a.shape) for a in (pair, ratios, left)],
+        out_specs=[half_block(out.shape) for out in outs],
+        compiler_params=kernel_params(),
+    )(kind, pair, ratios, left)
+
+
+def mix_project_kernel(rel, ready, kind, chunk, ratios, left, own, sibling, *refs):
+    earlier, refs = refs[:ready], refs[ready:]
+    value_mix, gate_mix, squeezed, recept_ref, keys_ref = refs
+    half = pl.program_id(0)
+
+    @pl.loop(0, chunk.shape[1])
+    def _(tile):
+        here, step = here_and_step(chunk.at[0], kind[0], kind[1], tile)
+        at = pl.ds(pl.multiple_of(tile * TILE, TILE), TILE)
+
+        def mix(which):
+            return (here + ratios[0, which : which + 1, :] * step).astype(bf16)
+
+        value_mix[0, at, :] = mix(2)
+        gate_mix[0, at, :] = mix(3)
+        squeezed[0, at, :] = jnp.dot(mix(4), left[0], preferred_element_type=f32)
+        for which, out in enumerate((recept_ref, keys_ref)):
+            weight = jnp.where(
+                half == 0, own[kind[2 + rel], which], sibling[kind[2 + rel], which]
+            )
+            part = jnp.dot(mix(which), weight, preferred_element_type=f32)
+            if ready == 1:
+                weight = jnp.where(half == 0, own[kind[2], which], sibling[kind[2], which])
+                part = part + jnp.dot(
+                    earlier[0][0, which, at, :], weight, preferred_element_type=f32
+                )
+                before = jnp.zeros_like(part)
+            else:
+                before = earlier[which][at, :]
+            out[at, :] = part + jnp.where(half == 0, before, out[at, :])
+
+
+def mix_and_project(rel, kind, pair, ratios, left, own, sibling, *earlier):
+    lines, rows, depth = pair.shape[1], pair.shape[2] - EXTRA, pair.shape[3]
+    whole, width = lines * rows, own.shape[3]
+    outs = [
+        jax.ShapeDtypeStruct((2, whole, depth), bf16),
+        jax.ShapeDtypeStruct((2, whole, depth), bf16),
+        jax.ShapeDtypeStruct((2, whole, left.shape[2]), f32),
+    ]
+    flat = jax.ShapeDtypeStruct((whole, width), f32)
+    ready = len(earlier)
+    return pl.pallas_call(
+        lambda *refs: mix_project_kernel(rel, ready, *refs),
+        grid=(2,),
+        out_shape=outs + [flat] * 2,
+        in_specs=[in_smem()]
+        + [half_block(a.shape) for a in (pair, ratios, left)]
+        + [in_vmem()] * 2
+        + ([half_block(earlier[0].shape)] if ready == 1 else [in_vmem()] * 2),
+        out_specs=[half_block(out.shape) for out in outs]
+        + [pl.BlockSpec((whole, width), lambda i: (0, 0))] * 2,
+        compiler_params=kernel_params(),
+    )(kind, pair, ratios, left, own, sibling, *earlier)
+
+
+def project_kernel(
+    kind,
+    mix0,
+    mix1,
+    mix2,
+    low0,
+    low1,
+    low2,
+    recept_part,
+    keys_part,
+    last0,
+    last1,
     ratios,
-    own_pair,
-    sibling_pair,
+    left,
+    own,
+    sibling,
     own_value,
     sibling_value,
-    own_left,
-    sibling_left,
     right,
     base,
     recept_ref,
@@ -302,99 +456,176 @@
     decay_ref,
     gate_mix,
 ):
-    rows, depth = c0.shape
-
-    @pl.loop(0, rows // TILE)
-    def _(tile):
-        at = pl.ds(pl.multiple_of(tile * TILE, TILE), TILE)
-        row = lax.broadcasted_iota(jnp.int32, (TILE, 1), 0) + tile * TILE
-        start = (row & (period[0] - 1)) == 0
-        totals = [None] * 4
-        for c, chunk in enumerate((c0, c1, c2, c3, c4, c5, c6, c7)):
-            here, step = previous_rows(chunk, first[c : c + 1, :], tile, start)
-            from_z = place[c // 2]
-            pair, value, left = (
-                (own_pair, own_value, own_left)
-                if c % 2 == 0
-                else (sibling_pair, sibling_value, sibling_left)
-            )
-            weights = (pair[from_z, 0], pair[from_z, 1], value[from_z, 0], left[from_z, 0])
-            for which, weight in zip((0, 1, 2, 4), weights):
-                mixed = (here + ratios[which, c : c + 1, :] * step).astype(bf16)
-                part = jnp.dot(mixed, weight, preferred_element_type=f32)
-                slot = min(which, 3)
-                totals[slot] = part if totals[slot] is None else totals[slot] + part
-            gate_mix[at, c * depth : (c + 1) * depth] = (
-                here + ratios[3, c : c + 1, :] * step
-            ).astype(bf16)
-        recept_ref[at, :] = totals[0]
-        keys_ref[at, :] = totals[1]
-        values_ref[at, :] = totals[2]
-        squeezed = jnp.tanh(totals[3]).astype(bf16)
-        grown = jnp.dot(squeezed, right[...], preferred_element_type=f32)
-        decay_ref[at, :] = -jnp.exp(base[...] + grown)
-
-
-def mixed_products(place, period, chunks, *rest):
-    rows, depth = chunks[0].shape
-    width = rest[2].shape[3]
+    tile = pl.program_id(0)
+    totals = [recept_part[...], keys_part[...], None]
+    squeezed = low0[0] + low0[1] + low1[0] + low1[1] + low2[0] + low2[1]
+    for half, chunk in enumerate((last0, last1)):
+        here, step = here_and_step(chunk, kind[0], kind[1], tile)
+
+        def mix(which):
+            return (here + ratios[half, which : which + 1, :] * step).astype(bf16)
+
+        for which in range(2):
+            weight = (own, sibling)[half][kind[5], which]
+            totals[which] += jnp.dot(mix(which), weight, preferred_element_type=f32)
+        weight = (own_value, sibling_value)[half][kind[5], 0]
+        part = jnp.dot(mix(2), weight, preferred_element_type=f32)
+        totals[2] = part if totals[2] is None else totals[2] + part
+        gate_mix[half] = mix(3)
+        squeezed = squeezed + jnp.dot(mix(4), left[half], preferred_element_type=f32)
+    for rel, mixes in enumerate((mix0, mix1, mix2)):
+        for half in range(2):
+            weight = (own_value, sibling_value)[half][kind[2 + rel], 0]
+            totals[2] += jnp.dot(mixes[half], weight, preferred_element_type=f32)
+    recept_ref[...] = totals[0]
+    keys_ref[...] = totals[1]
+    values_ref[...] = totals[2]
+    squeezed = jnp.tanh(squeezed).astype(bf16)
+    grown = jnp.dot(squeezed, right[...], preferred_element_type=f32)
+    decay_ref[...] = -jnp.exp(base[...] + grown)
+
+
+def projected(kind, mixes, lows, parts, last, *rest):
+    rows, depth = mixes[0].shape[1:]
+    width, rank = parts[0].shape[1], lows[0].shape[2]
     flat = jax.ShapeDtypeStruct((rows, width), f32)
+    tile_of = pl.BlockSpec((TILE, width), lambda i: (i, 0))
     return pl.pallas_call(
-        mixed_kernel,
-        out_shape=[flat] * 4 + [jax.ShapeDtypeStruct((rows, 8 * depth), bf16)],
-        in_specs=[in_smem(), in_smem()] + [in_vmem()] * (8 + len(rest)),
-        out_specs=[in_vmem()] * 5,
+        project_kernel,
+        grid=(rows // TILE,),
+        out_shape=[flat] * 4 + [jax.ShapeDtypeStruct((2, rows, depth), bf16)],
+        in_specs=[in_smem()]
+        + [pl.BlockSpec((2, TILE, depth), lambda i: (0, i, 0))] * 3
+        + [pl.BlockSpec((2, TILE, rank), lambda i: (0, i, 0))] * 3
+        + [tile_of] * 2
+        + [in_vmem()] * (2 + len(rest)),
+        out_specs=[tile_of] * 4 + [pl.BlockSpec((2, TILE, depth), lambda i: (0, i, 0))],
         compiler_params=kernel_params(),
-    )(place, period, *chunks, *rest)
-
-
-def gate_kernel(place, mix, own, sibling, normed, live, first_ref, second_ref):
-    rows = mix.shape[0]
-    depth, width = own.shape[2:]
-    part_rows = BLK // 2
-
-    @pl.loop(0, rows // TILE)
-    def _(tile):
-        at = pl.ds(pl.multiple_of(tile * TILE, TILE), TILE)
-        total = None
-        for c in range(8):
-            weight = (own if c % 2 == 0 else sibling)[place[c // 2], 0]
-            part = jnp.dot(
-                mix[at, c * depth : (c + 1) * depth], weight, preferred_element_type=f32
-            )
-            total = part if total is None else total + part
-        value = normed[at, :] * (total * jax.nn.sigmoid(total))
-        value = jnp.where(live[at, :] > 0, value, 0.0).astype(bf16)
-        value = value.reshape(TILE // part_rows // 2, 2, part_rows, width)
-        half_at = pl.ds(pl.multiple_of(tile * (TILE // 2), TILE // 2), TILE // 2)
-        first_ref[half_at, :] = value[:, 0].reshape(TILE // 2, width)
-        second_ref[half_at, :] = value[:, 1].reshape(TILE // 2, width)
-
-
-def gated(place, mix, own, sibling, normed, live):
+    )(kind, *mixes, *lows, *parts, *last, *rest)
+
+
+def gate_kernel(
+    kind, mix0, mix1, mix2, mix3, own, sibling, normed, live, kept0, sent0, kept1, sent1, total
+):
+    half = pl.program_id(0)
+    part = None
+    for rel, mixes in enumerate((mix0, mix1, mix2, mix3)):
+        weight = jnp.where(half == 0, own[kind[2 + rel], 0], sibling[kind[2 + rel], 0])
+        new = jnp.dot(mixes[0], weight, preferred_element_type=f32)
+        part = new if part is None else part + new
+
+    @pl.when(half == 0)
+    def _():
+        total[...] = part
+
+    @pl.when(half == 1)
+    def _():
+        gate = total[...] + part
+        value = normed[...] * (gate * jax.nn.sigmoid(gate))
+        value = jnp.where(live[...] > 0, value, 0.0).astype(bf16)
+        lines = kept0.shape[1]
+        value = value.reshape(lines, 2, 2, 2, BLK // 2, value.shape[1])
+        is_long = kind[0] == 1
+        for block in range(2):
+            for at, kept, sent in ((0, kept0, sent0), (1, kept1, sent1)):
+                even, odd = value[:, 0, block, at], value[:, 1, block, at]
+                kept[block] = jnp.where(is_long, even, odd)
+                sent[block] = jnp.where(is_long, odd, even)
+
+
+def gated(kind, mixes, own, sibling, normed, live):
     rows, width = normed.shape
+    quarter = jax.ShapeDtypeStruct((2, rows // TILE, BLK // 2, width), bf16)
     return pl.pallas_call(
         gate_kernel,
-        out_shape=[jax.ShapeDtypeStruct((rows // 2, width), bf16)] * 2,
-        in_specs=[in_smem()] + [in_vmem()] * 5,
+        grid=(2,),
+        out_shape=[quarter] * 4,
+        in_specs=[in_smem()] + [half_block(mix.shape) for mix in mixes] + [in_vmem()] * 4,
+        out_specs=[pl.BlockSpec(quarter.shape, lambda i: (0, 0, 0, 0))] * 4,
+        scratch_shapes=[pltpu.VMEM((rows, width), f32)],
+        compiler_params=kernel_params(),
+    )(kind, *mixes, own, sibling, normed, live)
+
+
+def head_blocks(heads):
+    width = heads * BLK
+    tall = lax.broadcasted_iota(jnp.int32, (width, width), 0) // BLK
+    wide = lax.broadcasted_iota(jnp.int32, (width, width), 1) // BLK
+    return tall == wide
+
+
+def state_kernel(lengths, carry, k_ref, v_ref, w_ref, s_ref, state_ref, entered_ref, hold):
+    span, width = BLK, k_ref.shape[1]
+    heads = width // span
+    row = lax.broadcasted_iota(jnp.int32, (span, width), 0)
+    lane = lax.broadcasted_iota(jnp.int32, (span, width), 1)
+    for h in range(heads):
+        hold[:, h * span : (h + 1) * span] = s_ref[h]
+
+    @pl.loop(0, k_ref.shape[0] // span)
+    def _(n):
+        at = pl.ds(pl.multiple_of(n * span, span), span)
+        live = row < lengths[n]
+        k = jnp.where(live, k_ref[at, :], 0.0)
+        total = jnp.where(live, w_ref[at, :], 0.0)
+        after_row = jnp.zeros_like(total)
+        half = 1
+        while half < span:
+            upper = (row & half) != 0
+            across = jnp.where(
+                upper, pltpu.roll(total, half, 0), pltpu.roll(total, span - half, 0)
+            )
+            after_row = after_row + jnp.where(upper, 0.0, across)
+            total = total + across
+            half *= 2
+        added = lax.dot_general(
+            (k * jnp.exp(after_row)).astype(bf16),
+            v_ref[at, :].astype(bf16),
+            (((0,), (0,)), ((), ())),
+            preferred_element_type=f32,
+        )
+        fresh = jnp.zeros((span, width), f32)
+        for h in range(heads):
+            fresh = jnp.where(lane // span == h, added[h * span : (h + 1) * span], fresh)
+        twice = jnp.concatenate([total] * 2, axis=0)
+        turned_parts = []
+        for p in range(width // (2 * span)):
+            flipped = jnp.transpose(twice[:, p * 2 * span : (p + 1) * 2 * span])
+            turned_parts.append(
+                jnp.where(lane[:, : 2 * span] < span, flipped[:span], flipped[span:])
+            )
+        fade = jnp.exp(jnp.concatenate(turned_parts, axis=1))
+        entered = hold[...] * carry[0]
+        entered_ref[n] = entered.astype(bf16)
+        state = fade * entered + fresh
+        hold[...] = state
+        for h in range(heads):
+            state_ref[n, h] = state[:, h * span : (h + 1) * span]
+
+
+def states_of(lengths, carry, k, v, w, state):
+    rows, width = k.shape
+    heads = width // BLK
+    return pl.pallas_call(
+        state_kernel,
+        out_shape=[
+            jax.ShapeDtypeStruct((rows // BLK, heads, BLK, BLK), f32),
+            jax.ShapeDtypeStruct((rows // BLK, BLK, width), bf16),
+        ],
+        in_specs=[in_smem()] * 2 + [in_vmem()] * 4,
         out_specs=[in_vmem()] * 2,
+        scratch_shapes=[pltpu.VMEM((BLK, width), f32)],
         compiler_params=kernel_params(),
-    )(place, mix, own, sibling, normed, live)
-
-
-def sweep_kernel(
-    lengths, carry, r_ref, k_ref, v_ref, w_ref, u_ref, s_ref, gain, bias, out_ref, state_ref, hold
-):
+    )(lengths, carry, k, v, w, state)
+
+
+def sweep_kernel(lengths, r_ref, k_ref, v_ref, w_ref, entered_ref, u_ref, gain, bias, out_ref):
     span, width = BLK, r_ref.shape[1]
     heads = width // span
     row = lax.broadcasted_iota(jnp.int32, (span, width), 0)
     lane = lax.broadcasted_iota(jnp.int32, (span, width), 1)
     col = lane % span
-    tall = lax.broadcasted_iota(jnp.int32, (width, width), 0) // span
-    wide = lax.broadcasted_iota(jnp.int32, (width, width), 1) // span
-    same_head = tall == wide
-    for h in range(heads):
-        hold[:, h * span : (h + 1) * span] = s_ref[h]
+    same_head = head_blocks(heads)
 
     def spread(value):
         stacked = jnp.concatenate([value.astype(bf16)] * heads, axis=0)
@@ -411,7 +642,7 @@
         k = jnp.where(live, k_ref[at, :], 0.0)
         total = jnp.where(live, w_ref[at, :], 0.0)
         before = jnp.zeros_like(total)
-        after = jnp.zeros_like(total)
+        after_row = jnp.zeros_like(total)
         scores = against((r * u_ref[...]).astype(bf16), spread(k))
         scores = jnp.where(row == col, scores, 0.0)
         level = 0
@@ -419,7 +650,7 @@
             half = 1 << level
             upper = (row & half) != 0
             if level:
-                scale = jnp.exp(jnp.where(upper, before, after))
+                scale = jnp.exp(jnp.where(upper, before, after_row))
                 part = against((r * scale).astype(bf16), spread(k * scale))
             else:
                 part = against(r.astype(bf16), spread(k))
@@ -429,36 +660,16 @@
                 upper, pltpu.roll(total, half, 0), pltpu.roll(total, span - half, 0)
             )
             before = before + jnp.where(upper, across, 0.0)
-            after = after + jnp.where(upper, 0.0, across)
+            after_row = after_row + jnp.where(upper, 0.0, across)
             total = total + across
             level += 1
-        entered = hold[...] * carry[0]
         out = jnp.dot(scores.astype(bf16), spread(v), preferred_element_type=f32)
         out = out + jnp.dot(
-            (r * jnp.exp(before)).astype(bf16), spread(entered), preferred_element_type=f32
+            (r * jnp.exp(before)).astype(bf16),
+            spread(entered_ref[n]),
+            preferred_element_type=f32,
         )
         out_ref[at, :] = out
-        added = lax.dot_general(
-            (k * jnp.exp(after)).astype(bf16),
-            v.astype(bf16),
-            (((0,), (0,)), ((), ())),
-            preferred_element_type=f32,
-        )
-        fresh = jnp.zeros((span, width), f32)
-        for h in range(heads):
-            fresh = jnp.where(lane // span == h, added[h * span : (h + 1) * span], fresh)
-        twice = jnp.concatenate([total] * 2, axis=0)
-        turned = []
-        for p in range(width // (2 * span)):
-            flipped = jnp.transpose(twice[:, p * 2 * span : (p + 1) * 2 * span])
-            turned.append(
-                jnp.where(lane[:, : 2 * span] < span, flipped[:span], flipped[span:])
-            )
-        fade = jnp.exp(jnp.concatenate(turned, axis=1))
-        state = fade * entered + fresh
-        hold[...] = state
-        for h in range(heads):
-            state_ref[n, h] = state[:, h * span : (h + 1) * span]
 
     ones = jnp.where(same_head, 1.0, 0.0).astype(bf16)
 
@@ -479,51 +690,43 @@
         out_ref[at, :] = centred * lax.rsqrt(spread_of + norm_eps) * gain[...] + bias[...]
 
 
-def sweep(lengths, carry, r, k, v, w, bonus, state, gain, bias):
-    rows, width = r.shape
-    heads = width // BLK
+def sweep(lengths, r, k, v, w, entered, bonus, gain, bias):
     return pl.pallas_call(
         sweep_kernel,
-        out_shape=[
-            jax.ShapeDtypeStruct((rows, width), f32),
-            jax.ShapeDtypeStruct((rows // BLK, heads, BLK, BLK), f32),
-        ],
-        in_specs=[in_smem(), in_smem()] + [in_vmem()] * 8,
-        out_specs=[in_vmem(), in_vmem()],
-        scratch_shapes=[pltpu.VMEM((BLK, width), f32)],
+        out_shape=jax.ShapeDtypeStruct(r.shape, f32),
+        in_specs=[in_smem()] + [in_vmem()] * 8,
+        out_specs=in_vmem(),
         compiler_params=kernel_params(),
-    )(lengths, carry, r, k, v, w, bonus, state, gain, bias)
-
-
-def final_kernel(side, h0, h1, h2, h3, weight, kept_ref, sent_ref):
-    part_rows = BLK // 2
-    width = weight.shape[2]
-
-    @pl.loop(0, h0.shape[0] // TILE)
+    )(lengths, r, k, v, w, entered, bonus, gain, bias)
+
+
+def final_kernel(block_of, h0, h1, h2, h3, weight, o0, o1, o2, o3, hold):
+    @pl.loop(0, hold.shape[1] // TILE)
     def _(tile):
         at = pl.ds(pl.multiple_of(tile * TILE, TILE), TILE)
         total = None
         for k, piece in enumerate((h0, h1, h2, h3)):
-            part = jnp.dot(piece[at, :], weight[k], preferred_element_type=f32)
+            part = jnp.dot(piece[...], weight[k, :, at], preferred_element_type=f32)
             total = part if total is None else total + part
-        split = total.astype(bf16).reshape(TILE // part_rows // 2, 2, part_rows, width)
-        mine = side[0] == 0
-        low, high = split[:, 0], split[:, 1]
-        group = pl.ds(tile * (TILE // part_rows // 2), TILE // part_rows // 2)
-        kept_ref[group] = jnp.where(mine, low, high)
-        sent_ref[group] = jnp.where(mine, high, low)
-
-
-def final_product(side, pieces, weight):
+        hold[:, at] = total.astype(bf16)
+
+    block = hold.shape[0] // 4
+    for rel, out in enumerate((o0, o1, o2, o3)):
+        at = pl.ds(pl.multiple_of(block_of[rel] * block, block), block)
+        out[...] = hold[at, :].reshape(out.shape)
+
+
+def final_product(block_of, pieces, weight, lines):
     rows, width = pieces[0].shape[0], weight.shape[2]
-    half = jax.ShapeDtypeStruct((rows // BLK, BLK // 2, width), bf16)
+    out = jax.ShapeDtypeStruct((lines, rows // 4 // lines, width), bf16)
     return pl.pallas_call(
         final_kernel,
-        out_shape=[half] * 2,
+        out_shape=[out] * 4,
         in_specs=[in_smem()] + [in_vmem()] * 5,
-        out_specs=[in_vmem()] * 2,
+        out_specs=[in_vmem()] * 4,
+        scratch_shapes=[pltpu.VMEM((rows, width), bf16)],
         compiler_params=kernel_params(),
-    )(side, *pieces, weight)
+    )(block_of, *pieces, weight)
 
 
 def lay_kernel(at, *refs):
@@ -631,43 +834,64 @@
     depth = acceptance_transform.shape[0]
     rows = 2 * lines * group_rows
 
-    kept = jnp.where(is_long, continued_prompt_entries, padded_prompt_entries)
-    given = jnp.where(is_long, padded_prompt_entries, continued_prompt_entries)
+    kind = jnp.stack(
+        [is_long.astype(jnp.int32), jnp.where(is_long, rows, slot_rows).astype(jnp.int32)]
+        + [(mp ^ rel).astype(jnp.int32) for rel in range(4)]
+    )
+    given = given_to_other_core(
+        kind, prompt_live_extents, continued_prompt_entries, padded_prompt_entries
+    )
     taken = flipped_core(given)
-    both = jnp.concatenate(
-        [jnp.where(is_long, kept, taken), jnp.where(is_long, taken, kept)], axis=0
-    )
-    halves = []
-    for h in range(2):
-        side = core if h == 0 else 1 - core
-        halves.append(lax.dynamic_slice_in_dim(both, side * depth, depth, 1))
-    first_half = spread_along(halves[0], z)
-    second_half = spread_along(halves[1], z)
-    a = in_place(first_half, z).reshape(rows, depth)
-    b = in_place(second_half, z).reshape(rows, depth)
-    a_x, b_y = over_x(a), over_y(b)
-    a_y, b_x = over_y(a), over_x(b)
-    a_xy, b_xy = over_y(a_x), over_x(b_y)
-    chunks = [a, b, a_x, b_x, a_y, b_y, a_xy, b_xy]
-    edge = preceding_entry_line.reshape(2, depth)
-    edge_x, edge_y = over_x(edge), over_y(edge)
-    edge_xy = over_y(edge_x)
-    edges = jnp.stack([edge, edge_x, edge_y, edge_xy])
-    edges = jnp.where(is_long, edges, edges[:, ::-1])
-    first = jnp.where(is_long, edges.astype(f32), 0.0).reshape(8, depth)
-    place = jnp.stack([mp ^ rel for rel in range(4)]).astype(jnp.int32)
-    period = jnp.where(is_long, rows, slot_rows).astype(jnp.int32)[None]
+    block = block_of_chip(
+        kind,
+        prompt_live_extents,
+        continued_prompt_entries,
+        padded_prompt_entries,
+        taken,
+        preceding_entry_line[None],
+    )
+    (
+        block,
+        acceptance_transform,
+        lookup_transform,
+        payload_transform,
+        gating_transform,
+        final_transform,
+        token_mixing_ratios,
+        fading_left_factor,
+        fading_right_factor,
+        carried_memory,
+    ) = lax.optimization_barrier(
+        (
+            block,
+            acceptance_transform,
+            lookup_transform,
+            payload_transform,
+            gating_transform,
+            final_transform,
+            token_mixing_ratios,
+            fading_left_factor,
+            fading_right_factor,
+            carried_memory,
+        )
+    )
+    spread = spread_along(block, z)
+    pair = jnp.swapaxes(in_place(spread, z), 0, 1)
+    pair_x, pair_y = over_x(pair), over_y(pair)
+    a_xy, b_xy = over_y(pair_x[0]), over_x(pair_y[1])
+    extents = pair[0, :, 2 * group_rows + 1, : 2 * requests].reshape(2 * lines * requests)
+    extents = jnp.where(is_long, slot_rows, extents.astype(jnp.int32)).astype(jnp.int32)
 
     def chunk_order(whole):
         split = whole.reshape((4, 2, depth) + whole.shape[1:])
         parts = []
         for rel in range(4):
-            for h in range(2):
-                side = core if h == 0 else 1 - core
-                parts.append(split[mp ^ rel, side])
-        return jnp.stack(parts)
-
-    ratios = chunk_order(token_mixing_ratios.T).transpose(2, 0, 1)
+            both = split[mp ^ rel]
+            parts.append(jnp.where(is_long, both, both[::-1]))
+        return parts
+
+    ratios = [part.transpose(0, 2, 1) for part in chunk_order(token_mixing_ratios.T)]
+    left = chunk_order(fading_left_factor)
 
     def columns_of(weights, *ready):
         stacked = jnp.stack(weights)
@@ -683,64 +907,69 @@
     def both_cores(pieces):
         return in_order(pieces, z), in_order([flipped_core(piece) for piece in pieces], z)
 
-    pair_pieces = columns_of(
-        [acceptance_transform, lookup_transform], first_half[4], second_half[4]
-    )
-    value_pieces = columns_of([payload_transform], a_x, b_y)
+    pieces = columns_of([acceptance_transform, lookup_transform], pair)
+    value_pieces = columns_of([payload_transform], pair_x, pair_y)
     gate_pieces = columns_of([gating_transform], value_pieces[2])
-    own_pair, sibling_pair = both_cores(pair_pieces)
+    own, sibling = both_cores(pieces)
     own_value, sibling_value = both_cores(value_pieces)
     own_gate, sibling_gate = both_cores(gate_pieces)
-    left = fading_left_factor.reshape(4, 2, 1, depth, fading_left_factor.shape[1])
-    left_own = jnp.where(is_long, left[:, 0], left[:, 1])
-    left_sibling = jnp.where(is_long, left[:, 1], left[:, 0])
 
     def mine_of(vector):
         return lax.dynamic_slice_in_dim(vector, z * width, width, 0)[None]
 
-    recept, keys, values, decay, gate_mix = mixed_products(
-        place,
-        period,
-        chunks,
-        first,
-        ratios,
-        own_pair,
-        sibling_pair,
+    pair_mix, value0, gate0, low0 = mixes_of(kind, pair, ratios[0], left[0])
+    value1, gate1, low1, recept, keys = mix_and_project(
+        1, kind, pair_x, ratios[1], left[1], own, sibling, pair_mix
+    )
+    value2, gate2, low2, recept, keys = mix_and_project(
+        2, kind, pair_y, ratios[2], left[2], own, sibling, recept, keys
+    )
+    recept, keys, values, decay, gate3 = projected(
+        kind,
+        (value0, value1, value2),
+        (low0, low1, low2),
+        (recept, keys),
+        (a_xy, b_xy),
+        ratios[3],
+        left[3],
+        own,
+        sibling,
         own_value,
         sibling_value,
-        left_own,
-        left_sibling,
         lax.dynamic_slice_in_dim(fading_right_factor, z * width, width, 1),
         mine_of(fading_baseline),
     )
-    beside_extents = flipped_core(prompt_live_extents)
-    chip_extents = jnp.stack(
-        [
-            jnp.where(is_long, prompt_live_extents, beside_extents),
-            jnp.where(is_long, beside_extents, prompt_live_extents),
-        ]
-    )
-    extents = in_order(
-        [chip_extents] + [turned(chip_extents, "z", k) for k in range(1, lines)], z
-    ).reshape(2 * lines * requests)
-    extents = jnp.where(is_long, slot_rows, extents).astype(jnp.int32)
     entered = lax.dynamic_slice_in_dim(carried_memory, z * heads, heads, 0)
     bonus = lax.dynamic_slice_in_dim(present_reward, z * heads, heads, 0).reshape(1, width)
-    normed, states = sweep(
+    states, states_in = states_of(
         extents,
         is_long.astype(f32)[None],
+        keys,
+        values,
+        decay,
+        jnp.where(is_long, entered, 0.0),
+    )
+    normed = sweep(
+        extents,
         recept,
         keys,
         values,
         decay,
+        states_in,
         bonus,
-        jnp.where(is_long, entered, 0.0),
         mine_of(group_layer_scaling),
         mine_of(group_layer_shift_term),
     )
     live = lax.broadcasted_iota(jnp.int32, (rows // slot_rows, slot_rows), 1) < extents[:, None]
     live = live.reshape(rows, 1).astype(f32)
-    hidden = gated(place, gate_mix, own_gate, sibling_gate, normed, live)
+    kept0, sent0, kept1, sent1 = gated(
+        kind,
+        (gate0, gate1, gate2, gate3),
+        own_gate,
+        sibling_gate,
+        normed,
+        live,
+    )
 
     states = states.reshape(lines, 2, requests, heads, span, span)
     passed = flipped_core(lax.dynamic_index_in_dim(states, 1 - core, 1, keepdims=False))
@@ -772,29 +1001,29 @@
         ]
     )
     order = jnp.stack([(z - k) % lines for k in range(lines)]).astype(jnp.int32)
-    side = x.astype(jnp.int32)[None]
+    block_of = jnp.stack(
+        [(((y ^ (rel >> 1)) ^ core) * 2 + (x ^ (rel & 1))).astype(jnp.int32) for rel in range(4)]
+    )
     spreads = []
-    for n, part in enumerate(hidden):
-        if n:
+    for kept, sent in ((kept0, sent0), (kept1, sent1)):
+        part = jnp.concatenate([kept, flipped_core(sent)], axis=0)
+        part = part.reshape(2 * rows // 4, width)
+        if spreads:
             part = after(part, spreads[0][2])
         spreads.append(spread_along(part, z))
     out_pieces = []
     for piece, one, two, three, far in spreads:
         one = jnp.where(z == 0, far, one)
         three = jnp.where(z == 3, far, three)
-        kept_half, sent_half = final_product(side, (piece, one, two, three), out_weight)
-        summed = kept_half.astype(f32) + over_x(sent_half).astype(f32)
-        summed = summed.reshape(lines, 2, group_rows // 4, wide_out)
-        same_core = lax.dynamic_index_in_dim(summed, core, 1, keepdims=False)
-        other_core = lax.dynamic_index_in_dim(summed, 1 - core, 1, keepdims=False).astype(bf16)
-        from_same = lax.ppermute(same_core.astype(bf16), ("core", "y"), [(1, 0), (2, 3)])
-        from_cross = lax.ppermute(other_core, ("core", "y"), [(1, 2), (2, 1)])
-        from_beside = lax.ppermute(other_core, ("core", "y"), [(0, 2), (3, 1)])
+        here, to_x, to_y, to_xy = final_product(
+            block_of, (piece, one, two, three), out_weight, lines
+        )
+        across = lax.ppermute(to_xy, ("y", "x"), [(i, 3 - i) for i in range(4)])
         mixed_part = (
-            jnp.where(core == y, same_core, 0.0)
-            + from_same.astype(f32)
-            + from_cross.astype(f32)
-            + from_beside.astype(f32)
+            here.astype(f32)
+            + over_x(to_x).astype(f32)
+            + over_y(to_y).astype(f32)
+            + across.astype(f32)
         ).astype(bf16)
         out_pieces += dealt(
             lambda j: lax.dynamic_index_in_dim(mixed_part, j, 0, keepdims=False), z

time: 378 us -> 328 us (0.87)
  waiting for transfers between devices: 160 us -> 105 us
  starting transfers between devices: 114 us -> 83.8 us
  Pallas kernels: 59.2 us -> 86.3 us
  local copies, waits for them, and re-layouts: 26 us -> 34.7 us
    ppermute x5 -> x4, waiting for transfers between devices: 41 us -> 1.81 us  [over_y(): return lax.ppermute(x, 'y', [(0, 1), (1, 0)])]
    pallas_call x5 -> x11, Pallas kernels: 57.3 us -> 84.4 us  [the longest x2 20.9 us: mix_and_project(): pl.pallas_call(lambda *refs: mix_project_kernel(rel, ready, *refs), grid=...]
    ppermute x25 -> x21, starting transfers between devices: 57.7 us -> 45.1 us  [turned(): lax.ppermute(x, axis, [(i, (i + by) % length) for i in range(length)])]
    ppermute x4 -> x3, starting transfers between devices: 25.5 us -> 13 us  [spread_along(): one = lax.ppermute(piece, 'z', [(0, 1), (1, 2), (2, 3)])]
    ppermute x25 -> x21, waiting for transfers between devices: 85.8 us -> 75.6 us  [turned(): lax.ppermute(x, axis, [(i, (i + by) % length) for i in range(length)])]
    ppermute x4 -> x3, waiting for transfers between devices: 23.1 us -> 16.3 us  [spread_along(): far = lax.ppermute(two, 'z', [(1, 0), (2, 3)])]
    dynamic_update_slice x30 -> x27, local copies, waits for them, and re-layouts: 0.78 us -> 5.76 us  [in_order(): whole = lax.dynamic_update_index_in_dim(whole, piece, (z - k) % length, 0)]
    ppermute x6 -> x2, waiting for transfers between devices: 0.02 us -> 4.53 us  [on_core(): across = lax.ppermute(to_xy, ('y', 'x'), [(i, 3 - i) for i in range(4)])]
  transfers between devices with their start and end apart: 70 -> 57, of which waited for: 26 -> 20; matrix products, arithmetic and copies ran while one was open for 10% -> 13% of each run, Pallas kernels for 2% -> 11%
where the time goes in v3:
time: 328 us; the launch traced here: 327 us
  waiting for transfers between devices  105 us (32%)
  Pallas kernels  86.3 us (26%)
  starting transfers between devices  83.8 us (26%)
  local copies, waits for them, and re-layouts  34.7 us (11%)
  other arithmetic  15.6 us (5%)
    ppermute x21, waiting for transfers between devices, turned(): lax.ppermute(x, axis, [(i, (i + by) % length) for i in range(length)])  75.6 us
    ppermute x21, starting transfers between devices, turned(): lax.ppermute(x, axis, [(i, (i + by) % length) for i in range(length)])  45.1 us
    pallas_call x2, Pallas kernels, mix_and_project(): pl.pallas_call(lambda *refs: mix_project_kernel(rel, ready, *refs), grid=...  20.9 us
    ppermute x3, waiting for transfers between devices, spread_along(): far = lax.ppermute(two, 'z', [(1, 0), (2, 3)])  16.3 us
    pallas_call x1, Pallas kernels, sweep(): pl.pallas_call(sweep_kernel, out_shape=jax.ShapeDtypeStruct(r.shape, f32)...  14.8 us
    ppermute x3, starting transfers between devices, spread_along(): one = lax.ppermute(piece, 'z', [(0, 1), (1, 2), (2, 3)])  13 us
    pallas_call x1, Pallas kernels, projected(): pl.pallas_call(project_kernel, grid=(rows // TILE,), out_shape=[flat] * 4...  11.8 us
    pallas_call x2, Pallas kernels, final_product(): pl.pallas_call(final_kernel, out_shape=[out] * 4, in_specs=[in_smem()] +...  9.6 us
  transfers between devices with their start and end apart: 57, of which 20 were waited for; matrix products, arithmetic and copies ran while one was open for 13% of the time, Pallas kernels for 11%

profile of v3, /device:TPU:0, one launch (start us, length us, event | category | flops | bytes accessed | tf_op | source)
XLA Modules:
  0.0 326.9 jit_solution(16276298349339935905)
XLA Ops:
  1.3 1.8 shard_map.184
  3.6 1.3 broadcast_in_dim.135.edge
  6.1 1.3 dynamic_slice.153
  7.4 1.3 dynamic_slice.160
  8.8 1.3 dynamic_slice.161
  12.0 2.0 shard_map.185
  14.0 4.5 %collective-permute-start.1 = (bf16[2,272,512]{2,1,0:T(8,128)(2,1)}, bf16[2,272,512]{2,1,0:T(8,128)(2,1)S(1)}, u32[]{:S(2)}, u32[]{:S(2)}) collective-permute-start(bf16[2,272,512]{2,1,0:T(8,128)(2,1)} %shard_map.185), channel_id=1, source_target_pairs={{0,8},{8,16},{16,24},{1,9},{9,17},{17,25},{2,10},{10,18},{18,26},{... | collective-permute-start | bytes 1671176 | tf_op jit(solution)/shard_map/ppermute | solution.py:779
  18.5 2.6 collective-permute-start.2
  21.1 1.3 collective-permute-start.3
  30.1 1.6 dynamic-slice_select_fusion.s_ref
  31.6 1.2 fusion
  33.5 13.6 %collective-permute-done.2 = bf16[2,272,512]{2,1,0:T(8,128)(2,1)S(1)} collective-permute-done((bf16[2,272,512]{2,1,0:T(8,128)(2,1)}, bf16[2,272,512]{2,1,0:T(8,128)(2,1)S(1)}, u32[]{:S(2)}, u32[]{:S(2)}) %collective-permute-start.2) | collective-permute-done | bytes 557088 | tf_op jit(solution)/shard_map/ppermute | solution.py:758
  47.1 1.3 collective-permute-start.4
  48.4 1.6 broadcast_in_dim.134
  53.0 1.3 constant_dynamic-slice_fusion.3
  54.3 16.3 %collective-permute-done.4 = bf16[2,272,512]{2,1,0:T(8,128)(2,1)S(1)} collective-permute-done((bf16[2,272,512]{2,1,0:T(8,128)(2,1)S(1)}, bf16[2,272,512]{2,1,0:T(8,128)(2,1)S(1)}, u32[]{:S(2)}, u32[]{:S(2)}) %collective-permute-start.4) | collective-permute-done | bytes 557088 | tf_op jit(solution)/shard_map/ppermute | solution.py:782
  72.2 1.5 collective-permute-start.5
  73.7 1.5 collective-permute-start.13
  75.3 5.6 %collective-permute-start.7 = (bf16[2,512,256]{2,1,0:T(8,128)(2,1)}, bf16[2,512,256]{2,1,0:T(8,128)(2,1)}, u32[]{:S(2)}, u32[]{:S(2)}) collective-permute-start(bf16[2,512,256]{2,1,0:T(8,128)(2,1)} %get-tuple-element.67), channel_id=1, source_target_pairs={{0,16},{8,24},{16,0},{24,8},{1,17},{9,25},{17,1},{25,9},{2,18},{10... | collective-permute-start | bytes 1572872 | tf_op jit(solution)/shard_map/ppermute | solution.py:758
  82.4 1.3 reshape.87.live
  83.7 7.0 %shard_map.186 = (bf16[2,2,1024,512]{3,2,1,0:T(8,128)(2,1)}, bf16[2,1024,512]{2,1,0:T(8,128)(2,1)}, bf16[2,1024,512]{2,1,0:T(8,128)(2,1)}, f32[2,1024,128]{2,1,0:T(8,128)}) custom-call(s32[6]{0:T(128)} %stack.89.kind.refs_0_, bf16[2,4,272,512]{3,2,1,0:T(8,128)(2,1)} %bitcast.20.chunk, f32[2,5,512]{2,1,0:T(8,128)} %fusion.14.ratios, ...), custom_call_target="tpu_custom_call" | custom-call | tf_op jit(solution)/shard_map/pallas_call | solution.py:367
  90.7 2.9 collective-permute-done.6
  94.7 18.9 %collective-permute-done.7 = bf16[2,512,256]{2,1,0:T(8,128)(2,1)} collective-permute-done((bf16[2,512,256]{2,1,0:T(8,128)(2,1)}, bf16[2,512,256]{2,1,0:T(8,128)(2,1)}, u32[]{:S(2)}, u32[]{:S(2)}) %collective-permute-start.7) | collective-permute-done | bytes 524320 | tf_op jit(solution)/shard_map/ppermute | solution.py:758
  118.6 3.4 %collective-permute-done.5.refs_1_ = bf16[2,4,272,512]{3,2,1,0:T(8,128)(2,1)} collective-permute-done((bf16[2,4,272,512]{3,2,1,0:T(8,128)(2,1)}, bf16[2,4,272,512]{3,2,1,0:T(8,128)(2,1)}, u32[]{:S(2)}, u32[]{:S(2)}) %collective-permute-start.5) | collective-permute-done | bytes 2228256 | tf_op jit(solution)/shard_map/ppermute | solution.py:766
  122.1 1.3 slice_bitcast_fusion.1
  123.4 1.6 collective-permute-start.14
  125.0 5.5 %collective-permute-start.17 = (bf16[1,512,256]{2,1,0:T(8,128)(2,1)}, bf16[1,512,256]{2,1,0:T(8,128)(2,1)S(1)}, u32[]{:S(2)}, u32[]{:S(2)}) collective-permute-start(bf16[1,512,256]{2,1,0:T(8,128)(2,1)} %get-tuple-element.85), channel_id=1, source_target_pairs={{0,16},{8,24},{16,0},{24,8},{1,17},{9,25},{17,1},{25,9},{2,18},{10... | collective-permute-start | bytes 786440 | tf_op jit(solution)/shard_map/ppermute | solution.py:758
  130.5 1.3 slice_bitcast_fusion
  132.4 3.2 collective-permute-start.16
  135.7 11.0 %shard_map.187 = (bf16[2,1024,512]{2,1,0:T(8,128)(2,1)}, bf16[2,1024,512]{2,1,0:T(8,128)(2,1)}, f32[2,1024,128]{2,1,0:T(8,128)}, f32[1024,256]{1,0:T(8,128)}, f32[1024,256]{1,0:T(8,128)}) custom-call(s32[6]{0:T(128)} %stack.89.kind.refs_0_, bf16[2,4,272,512]{3,2,1,0:T(8,128)(2,1)} %collective-permute-done.5.refs_1_, f32[2,5,512]{2,1,0:T(8,128)} %fusion.15.refs_2_, ...), custom_call_target="tpu_custom_call" | custom-call | tf_op jit(solution)/shard_map/pallas_call | solution.py:419
  146.7 9.9 %shard_map.188 = (bf16[2,1024,512]{2,1,0:T(8,128)(2,1)}, bf16[2,1024,512]{2,1,0:T(8,128)(2,1)}, f32[2,1024,128]{2,1,0:T(8,128)}, f32[1024,256]{1,0:T(8,128)}, f32[1024,256]{1,0:T(8,128)}) custom-call(s32[6]{0:T(128)} %stack.89.kind.refs_0_, bf16[2,4,272,512]{3,2,1,0:T(8,128)(2,1)} %collective-permute-done.13.refs_1_, f32[2,5,512]{2,1,0:T(8,128)} %fusion.16.refs_2_, ...), custom_call_target="tpu_custom_call" | custom-call | tf_op jit(solution)/shard_map/pallas_call | solution.py:419
  159.1 6.3 %collective-permute-done.18 = bf16[1,512,256]{2,1,0:T(8,128)(2,1)S(1)} collective-permute-done((bf16[1,512,256]{2,1,0:T(8,128)(2,1)S(1)}, bf16[1,512,256]{2,1,0:T(8,128)(2,1)S(1)}, u32[]{:S(2)}, u32[]{:S(2)}) %collective-permute-start.18) | collective-permute-done | bytes 262176 | tf_op jit(solution)/shard_map/ppermute | solution.py:758
  168.7 1.9 collective-permute-start.24
  170.6 7.9 %collective-permute-done.23 = bf16[1,512,256]{2,1,0:T(8,128)(2,1)S(1)} collective-permute-done((bf16[1,512,256]{2,1,0:T(8,128)(2,1)S(1)}, bf16[1,512,256]{2,1,0:T(8,128)(2,1)S(1)}, u32[]{:S(2)}, u32[]{:S(2)}) %collective-permute-start.23) | collective-permute-done | bytes 262176 | tf_op jit(solution)/shard_map/ppermute | solution.py:758
  179.0 10.1 %collective-permute-done.24 = bf16[1,512,256]{2,1,0:T(8,128)(2,1)S(1)} collective-permute-done((bf16[1,512,256]{2,1,0:T(8,128)(2,1)S(1)}, bf16[1,512,256]{2,1,0:T(8,128)(2,1)S(1)}, u32[]{:S(2)}, u32[]{:S(2)}) %collective-permute-start.24) | collective-permute-done | bytes 262176 | tf_op jit(solution)/shard_map/ppermute | solution.py:758
  189.2 1.9 collective-permute-done.25
  194.4 11.8 %shard_map.189 = (f32[1024,256]{1,0:T(8,128)}, f32[1024,256]{1,0:T(8,128)}, f32[1024,256]{1,0:T(8,128)}, f32[1024,256]{1,0:T(8,128)}, bf16[2,1024,512]{2,1,0:T(8,128)(2,1)}) custom-call(s32[6]{0:T(128)} %stack.89.kind.refs_0_, bf16[2,1024,512]{2,1,0:T(8,128)(2,1)} %get-tuple-element.74.mix0, bf16[2,1024,512]{2,1,0:T(8,128)(2,1)} %get-tuple-element.75.mix1, ...), custom_call_target="tpu_custom_call" | custom-call | tf_op jit(solution)/shard_map/pallas_call | solution.py:493
  206.3 9.0 %shard_map.190 = (f32[16,4,64,64]{3,2,1,0:T(8,128)}, bf16[16,64,256]{2,1,0:T(8,128)(2,1)}) custom-call(s32[16]{0:T(128)} %copy-done.45, f32[1]{0:T(128)} %bitcast.74.carry, f32[1024,256]{1,0:T(8,128)} %get-tuple-element.95.k_ref, f32[1024,256]{1,0:T(8,128)} %get-tuple-element.96.v_ref, f32[1024,256]{1,0:T(8,128)} %get-tuple-element.97.w_ref, ...), custom_call_target="tpu_custom_call" | custom-call | tf_op jit(solution)/shard_map/pallas_call | solution.py:609
  215.3 14.8 %shard_map.191.normed = f32[1024,256]{1,0:T(8,128)} custom-call(s32[16]{0:T(128)} %copy-done.45, f32[1024,256]{1,0:T(8,128)} %get-tuple-element.94.r_ref, f32[1024,256]{1,0:T(8,128)} %get-tuple-element.95.k_ref, f32[1024,256]{1,0:T(8,128)} %get-tuple-element.96.v_ref, f32[1024,256]{1,0:T(8,128)} %get-tuple-element.97.w_ref, ...), custom_call_target="tpu_custom_call" | custom-call | tf_op jit(solution)/shard_map/pallas_call | solution.py:694
  230.1 7.4 %shard_map.192 = (bf16[2,4,32,256]{3,2,1,0:T(8,128)(2,1)}, bf16[2,4,32,256]{3,2,1,0:T(8,128)(2,1)}, bf16[2,4,32,256]{3,2,1,0:T(8,128)(2,1)}, bf16[2,4,32,256]{3,2,1,0:T(8,128)(2,1)}) custom-call(s32[6]{0:T(128)} %stack.89.kind.refs_0_, bf16[2,1024,512]{2,1,0:T(8,128)(2,1)} %get-tuple-element.62.mix0, bf16[2,1024,512]{2,1,0:T(8,128)(2,1)} %get-tuple-element.70.mix1, ...), custom_call_target="tpu_custom_call" | custom-call | tf_op jit(solution)/shard_map/pallas_call | solution.py:539
  238.5 1.6 pad_maximum_fusion.1.weight
  240.1 4.0 %collective-permute-start.31 = (bf16[512,256]{1,0:T(8,128)(2,1)S(1)}, bf16[512,256]{1,0:T(8,128)(2,1)S(1)}, u32[]{:S(2)}, u32[]{:S(2)}) collective-permute-start(bf16[512,256]{1,0:T(8,128)(2,1)S(1)} %bitcast.188), channel_id=1, source_target_pairs={{0,16},{8,24},{16,0},{24,8},{1,17},{9,25},{17,1},{25,9},{2,18},{10... | collective-permute-start | bytes 786440 | tf_op jit(solution)/shard_map/ppermute | solution.py:758
  244.1 1.3 collective-permute-start.34
  245.4 4.6 %collective-permute-start.33 = (bf16[512,256]{1,0:T(8,128)(2,1)S(1)}, bf16[512,256]{1,0:T(8,128)(2,1)S(1)}, u32[]{:S(2)}, u32[]{:S(2)}) collective-permute-start(bf16[512,256]{1,0:T(8,128)(2,1)S(1)} %bitcast.190), channel_id=1, source_target_pairs={{0,8},{8,16},{16,24},{1,9},{9,17},{17,25},{2,10},{10,18},{18,26},{... | collective-permute-start | bytes 786440 | tf_op jit(solution)/shard_map/ppermute | solution.py:779
  250.8 6.0 %collective-permute-done.31.h2 = bf16[512,256]{1,0:T(8,128)(2,1)S(1)} collective-permute-done((bf16[512,256]{1,0:T(8,128)(2,1)S(1)}, bf16[512,256]{1,0:T(8,128)(2,1)S(1)}, u32[]{:S(2)}, u32[]{:S(2)}) %collective-permute-start.31) | collective-permute-done | bytes 262176 | tf_op jit(solution)/shard_map/ppermute | solution.py:758
  256.9 1.3 collective-permute-start.32
  258.4 5.4 %collective-permute-done.54 = bf16[3,4,64,64]{3,2,1,0:T(8,128)(2,1)S(1)} collective-permute-done((bf16[3,4,64,64]{3,2,1,0:T(8,128)(2,1)S(1)}, bf16[3,4,64,64]{3,2,1,0:T(8,128)(2,1)S(1)}, u32[]{:S(2)}, u32[]{:S(2)}) %collective-permute-start.54) | collective-permute-done | bytes 98336 | tf_op jit(solution)/shard_map/ppermute | solution.py:758
  263.8 1.3 collective-permute-start.46
  265.2 11.1 %collective-permute-start.55 = (bf16[3,4,64,64]{3,2,1,0:T(8,128)(2,1)S(1)}, bf16[3,4,64,64]{3,2,1,0:T(8,128)(2,1)S(1)}, u32[]{:S(2)}, u32[]{:S(2)}) collective-permute-start(bf16[3,4,64,64]{3,2,1,0:T(8,128)(2,1)S(1)} %get-tuple-element.141), channel_id=1, source_target_pairs={{0,16},{8,24},{16,0},{24,8},{1,17},{9,25},{17,1},{25,9},{2,18},{10... | collective-permute-start | bytes 294920 | tf_op jit(solution)/shard_map/ppermute | solution.py:758
  276.3 3.9 %collective-permute-start.45 = (bf16[512,256]{1,0:T(8,128)(2,1)S(1)}, bf16[512,256]{1,0:T(8,128)(2,1)S(1)}, u32[]{:S(2)}, u32[]{:S(2)}) collective-permute-start(bf16[512,256]{1,0:T(8,128)(2,1)S(1)} %bitcast.186), channel_id=1, source_target_pairs={{0,8},{8,16},{16,24},{1,9},{9,17},{17,25},{2,10},{10,18},{18,26},{... | collective-permute-start | bytes 786440 | tf_op jit(solution)/shard_map/ppermute | solution.py:779
  280.2 1.3 collective-permute-start.44
  282.4 4.8 %shard_map.193 = (bf16[4,32,1024]{2,1,0:T(8,128)(2,1)}, bf16[4,32,1024]{2,1,0:T(8,128)(2,1)}, bf16[4,32,1024]{2,1,0:T(8,128)(2,1)}, bf16[4,32,1024]{2,1,0:T(8,128)(2,1)}) custom-call(s32[4]{0:T(128)} %pad_add_fusion.1.block_of, bf16[512,256]{1,0:T(8,128)(2,1)} %bitcast.191, bf16[512,256]{1,0:T(8,128)(2,1)} %get-tuple-element.153.h1, ...), custom_call_target="tpu_custom_call" | custom-call | tf_op jit(solution)/shard_map/pallas_call | solution.py:722
  287.2 2.5 collective-permute-start.38
  289.7 2.1 collective-permute-done.55
  291.8 1.5 collective-permute-start.37
  293.3 1.5 collective-permute-start.36
  296.3 4.8 %shard_map.194 = (bf16[4,32,1024]{2,1,0:T(8,128)(2,1)}, bf16[4,32,1024]{2,1,0:T(8,128)(2,1)}, bf16[4,32,1024]{2,1,0:T(8,128)(2,1)}, bf16[4,32,1024]{2,1,0:T(8,128)(2,1)}) custom-call(s32[4]{0:T(128)} %pad_add_fusion.1.block_of, bf16[512,256]{1,0:T(8,128)(2,1)} %bitcast.187, bf16[512,256]{1,0:T(8,128)(2,1)} %get-tuple-element.147.h1, ...), custom_call_target="tpu_custom_call" | custom-call | tf_op jit(solution)/shard_map/pallas_call | solution.py:722
  301.1 2.5 collective-permute-start.49
  305.4 1.5 collective-permute-start.39
  306.9 4.5 %collective-permute-done.49 = bf16[4,32,1024]{2,1,0:T(8,128)(2,1)S(1)} collective-permute-done((bf16[4,32,1024]{2,1,0:T(8,128)(2,1)}, bf16[4,32,1024]{2,1,0:T(8,128)(2,1)S(1)}, u32[]{:S(2)}, u32[]{:S(2)}) %collective-permute-start.49) | collective-permute-done | bytes 262176 | tf_op jit(solution)/shard_map/ppermute | solution.py:1021
  312.1 1.8 collective-permute-done.48
  313.9 1.4 collective-permute-start.41
  318.9 2.9 collective-permute-start.52
  324.9 1.9 shard_map.195
  (243 shorter events, 48.4 us)
Async XLA Ops:
  0.6 32.2 %copy-start = (bf16[128,1024]{1,0:T(8,128)(2,1)S(1)}, bf16[128,1024]{1,0:T(8,128)(2,1)}, u32[]{:S(2)}) copy-start(bf16[128,1024]{1,0:T(8,128)(2,1)} %param.29) | copy-start | bytes 786436
  0.7 22.4 %copy-start.17 = (bf16[4096,128]{1,0:T(8,128)(2,1)S(1)}, bf16[4096,128]{1,0:T(8,128)(2,1)}, u32[]{:S(2)}) copy-start(bf16[4096,128]{1,0:T(8,128)(2,1)} %param.28) | copy-start | bytes 3145732
  3.1 8.1 %collective-permute-start = (bf16[144,1024]{1,0:T(8,128)(2,1)}, bf16[144,1024]{1,0:T(8,128)(2,1)S(1)}, u32[]{:S(2)}, u32[]{:S(2)}) collective-permute-start(bf16[144,1024]{1,0:T(8,128)(2,1)} %shard_map.184), channel_id=1, source_target_pairs={{0,4},{4,0},{1,5},{5,1},{2,6},{6,2},{3,7},{7,3},{8,12},{12,8},{9,1... | collective-permute-start | bytes 884744 | tf_op jit(solution)/shard_map/ppermute | solution.py:762
  14.0 34.4 %collective-permute-start.1 = (bf16[2,272,512]{2,1,0:T(8,128)(2,1)}, bf16[2,272,512]{2,1,0:T(8,128)(2,1)S(1)}, u32[]{:S(2)}, u32[]{:S(2)}) collective-permute-start(bf16[2,272,512]{2,1,0:T(8,128)(2,1)} %shard_map.185), channel_id=1, source_target_pairs={{0,8},{8,16},{16,24},{1,9},{9,17},{17,25},{2,10},{10,18},{18,26},{... | collective-permute-start | bytes 1671176 | tf_op jit(solution)/shard_map/ppermute | solution.py:779
  18.5 28.6 %collective-permute-start.2 = (bf16[2,272,512]{2,1,0:T(8,128)(2,1)}, bf16[2,272,512]{2,1,0:T(8,128)(2,1)S(1)}, u32[]{:S(2)}, u32[]{:S(2)}) collective-permute-start(bf16[2,272,512]{2,1,0:T(8,128)(2,1)} %shard_map.185), channel_id=1, source_target_pairs={{0,16},{8,24},{16,0},{24,8},{1,17},{9,25},{17,1},{25,9},{2,18},{10... | collective-permute-start | bytes 1671176 | tf_op jit(solution)/shard_map/ppermute | solution.py:758
  21.1 30.6 %collective-permute-start.3 = (bf16[2,272,512]{2,1,0:T(8,128)(2,1)}, bf16[2,272,512]{2,1,0:T(8,128)(2,1)S(1)}, u32[]{:S(2)}, u32[]{:S(2)}) collective-permute-start(bf16[2,272,512]{2,1,0:T(8,128)(2,1)} %shard_map.185), channel_id=1, source_target_pairs={{8,0},{16,8},{24,16},{9,1},{17,9},{25,17},{10,2},{18,10},{26,18},{... | collective-permute-start | bytes 1671176 | tf_op jit(solution)/shard_map/ppermute | solution.py:780
  28.0 24.5 %collective-permute-start.35 = (bf16[1024,512]{1,0:T(8,128)(2,1)S(1)}, bf16[1024,512]{1,0:T(8,128)(2,1)S(1)}, u32[]{:S(2)}, u32[]{:S(2)}) collective-permute-start(bf16[1024,512]{1,0:T(8,128)(2,1)S(1)} %copy-done.14), channel_id=1, source_target_pairs={{0,4},{4,0},{1,5},{5,1},{2,6},{6,2},{3,7},{7,3},{8,12},{12,8},{9,1... | collective-permute-start | bytes 3145736 | tf_op jit(solution)/shard_map/ppermute | solution.py:762
  47.1 23.4 %collective-permute-start.4 = (bf16[2,272,512]{2,1,0:T(8,128)(2,1)S(1)}, bf16[2,272,512]{2,1,0:T(8,128)(2,1)S(1)}, u32[]{:S(2)}, u32[]{:S(2)}) collective-permute-start(bf16[2,272,512]{2,1,0:T(8,128)(2,1)S(1)} %collective-permute-done.2), channel_id=1, source_target_pairs={{8,0},{16,24},{9,1},{17,25},{10,2},{18,26},{11,3},{19,27},{12,4},{... | collective-permute-start | bytes 1671176 | tf_op jit(solution)/shard_map/ppermute | solution.py:782
  72.2 49.8 %collective-permute-start.5 = (bf16[2,4,272,512]{3,2,1,0:T(8,128)(2,1)}, bf16[2,4,272,512]{3,2,1,0:T(8,128)(2,1)}, u32[]{:S(2)}, u32[]{:S(2)}) collective-permute-start(bf16[2,4,272,512]{3,2,1,0:T(8,128)(2,1)} %bitcast.20.chunk), channel_id=1, source_target_pairs={{0,1},{1,0},{2,3},{3,2},{4,5},{5,4},{6,7},{7,6},{8,9},{9,8},{10,11... | collective-permute-start | bytes 6684680 | tf_op jit(solution)/shard_map/ppermute | solution.py:766
  73.7 51.2 %collective-permute-start.13 = (bf16[2,4,272,512]{3,2,1,0:T(8,128)(2,1)}, bf16[2,4,272,512]{3,2,1,0:T(8,128)(2,1)}, u32[]{:S(2)}, u32[]{:S(2)}) collective-permute-start(bf16[2,4,272,512]{3,2,1,0:T(8,128)(2,1)} %bitcast.20.chunk), channel_id=1, source_target_pairs={{0,2},{2,0},{1,3},{3,1},{4,6},{6,4},{5,7},{7,5},{8,10},{10,8},{9,1... | collective-permute-start | bytes 6684680 | tf_op jit(solution)/shard_map/ppermute | solution.py:770
  75.3 18.3 %collective-permute-start.6 = (bf16[2,512,256]{2,1,0:T(8,128)(2,1)}, bf16[2,512,256]{2,1,0:T(8,128)(2,1)}, u32[]{:S(2)}, u32[]{:S(2)}) collective-permute-start(bf16[2,512,256]{2,1,0:T(8,128)(2,1)} %get-tuple-element.66), channel_id=1, source_target_pairs={{0,8},{8,16},{16,24},{24,0},{1,9},{9,17},{17,25},{25,1},{2,10},{10... | collective-permute-start | bytes 1572872 | tf_op jit(solution)/shard_map/ppermute | solution.py:758
  75.3 38.4 %collective-permute-start.7 = (bf16[2,512,256]{2,1,0:T(8,128)(2,1)}, bf16[2,512,256]{2,1,0:T(8,128)(2,1)}, u32[]{:S(2)}, u32[]{:S(2)}) collective-permute-start(bf16[2,512,256]{2,1,0:T(8,128)(2,1)} %get-tuple-element.67), channel_id=1, source_target_pairs={{0,16},{8,24},{16,0},{24,8},{1,17},{9,25},{17,1},{25,9},{2,18},{10... | collective-permute-start | bytes 1572872 | tf_op jit(solution)/shard_map/ppermute | solution.py:758
  80.9 33.8 %collective-permute-start.8 = (bf16[2,512,256]{2,1,0:T(8,128)(2,1)}, bf16[2,512,256]{2,1,0:T(8,128)(2,1)}, u32[]{:S(2)}, u32[]{:S(2)}) collective-permute-start(bf16[2,512,256]{2,1,0:T(8,128)(2,1)} %get-tuple-element.68), channel_id=1, source_target_pairs={{0,24},{8,0},{16,8},{24,16},{1,25},{9,1},{17,9},{25,17},{2,26},{10... | collective-permute-start | bytes 1572872 | tf_op jit(solution)/shard_map/ppermute | solution.py:758
  82.3 32.4 %copy-start.45 = (s32[16]{0:T(128)}, s32[16]{0:T(128)S(1)}, u32[]{:S(2)}) copy-start(s32[16]{0:T(128)S(1)} %select_n.416.lengths) | copy-start | bytes 196
  93.6 22.8 %collective-permute-start.9 = (bf16[2,512,256]{2,1,0:T(8,128)(2,1)S(1)}, bf16[2,512,256]{2,1,0:T(8,128)(2,1)S(1)}, u32[]{:S(2)}, u32[]{:S(2)}) collective-permute-start(bf16[2,512,256]{2,1,0:T(8,128)(2,1)S(1)} %get-tuple-element.65), channel_id=1, source_target_pairs={{0,4},{4,0},{1,5},{5,1},{2,6},{6,2},{3,7},{7,3},{8,12},{12,8},{9,1... | collective-permute-start | bytes 1572872 | tf_op jit(solution)/shard_map/ppermute | solution.py:762
  113.6 3.1 collective-permute-start.10
  114.7 3.0 collective-permute-start.11
  116.4 2.2 collective-permute-start.12
  123.4 69.6 %collective-permute-start.14 = (bf16[4,272,512]{2,1,0:T(8,128)(2,1)S(1)}, bf16[4,272,512]{2,1,0:T(8,128)(2,1)S(1)}, u32[]{:S(2)}, u32[]{:S(2)}) collective-permute-start(bf16[4,272,512]{2,1,0:T(8,128)(2,1)S(1)} %slice_bitcast_fusion.1), channel_id=1, source_target_pairs={{0,2},{2,0},{1,3},{3,1},{4,6},{6,4},{5,7},{7,5},{8,10},{10,8},{9,1... | collective-permute-start | bytes 3342344 | tf_op jit(solution)/shard_map/ppermute | solution.py:770
  125.0 31.7 %collective-permute-start.17 = (bf16[1,512,256]{2,1,0:T(8,128)(2,1)}, bf16[1,512,256]{2,1,0:T(8,128)(2,1)S(1)}, u32[]{:S(2)}, u32[]{:S(2)}) collective-permute-start(bf16[1,512,256]{2,1,0:T(8,128)(2,1)} %get-tuple-element.85), channel_id=1, source_target_pairs={{0,16},{8,24},{16,0},{24,8},{1,17},{9,25},{17,1},{25,9},{2,18},{10... | collective-permute-start | bytes 786440 | tf_op jit(solution)/shard_map/ppermute | solution.py:758
  131.8 61.2 %collective-permute-start.15 = (bf16[4,272,512]{2,1,0:T(8,128)(2,1)S(1)}, bf16[4,272,512]{2,1,0:T(8,128)(2,1)S(1)}, u32[]{:S(2)}, u32[]{:S(2)}) collective-permute-start(bf16[4,272,512]{2,1,0:T(8,128)(2,1)S(1)} %slice_bitcast_fusion), channel_id=1, source_target_pairs={{0,1},{1,0},{2,3},{3,2},{4,5},{5,4},{6,7},{7,6},{8,9},{9,8},{10,11... | collective-permute-start | bytes 3342344 | tf_op jit(solution)/shard_map/ppermute | solution.py:766
  132.4 25.1 %collective-permute-start.16 = (bf16[1,512,256]{2,1,0:T(8,128)(2,1)S(1)}, bf16[1,512,256]{2,1,0:T(8,128)(2,1)}, u32[]{:S(2)}, u32[]{:S(2)}) collective-permute-start(bf16[1,512,256]{2,1,0:T(8,128)(2,1)S(1)} %copy-done.30), channel_id=1, source_target_pairs={{0,8},{8,16},{16,24},{24,0},{1,9},{9,17},{17,25},{25,1},{2,10},{10... | collective-permute-start | bytes 786440 | tf_op jit(solution)/shard_map/ppermute | solution.py:758
  135.6 29.8 %collective-permute-start.19 = (bf16[1,512,256]{2,1,0:T(8,128)(2,1)S(1)}, bf16[1,512,256]{2,1,0:T(8,128)(2,1)}, u32[]{:S(2)}, u32[]{:S(2)}) collective-permute-start(bf16[1,512,256]{2,1,0:T(8,128)(2,1)S(1)} %copy-done.16), channel_id=1, source_target_pairs={{0,4},{4,0},{1,5},{5,1},{2,6},{6,2},{3,7},{7,3},{8,12},{12,8},{9,1... | collective-permute-start | bytes 786440 | tf_op jit(solution)/shard_map/ppermute | solution.py:762
  156.7 8.7 %collective-permute-start.18 = (bf16[1,512,256]{2,1,0:T(8,128)(2,1)S(1)}, bf16[1,512,256]{2,1,0:T(8,128)(2,1)S(1)}, u32[]{:S(2)}, u32[]{:S(2)}) collective-permute-start(bf16[1,512,256]{2,1,0:T(8,128)(2,1)S(1)} %copy-done.29), channel_id=1, source_target_pairs={{0,24},{8,0},{16,8},{24,16},{1,25},{9,1},{17,9},{25,17},{2,26},{10... | collective-permute-start | bytes 786440 | tf_op jit(solution)/shard_map/ppermute | solution.py:758
  157.5 33.6 %collective-permute-start.26 = (bf16[1,512,256]{2,1,0:T(8,128)(2,1)S(1)}, bf16[1,512,256]{2,1,0:T(8,128)(2,1)S(1)}, u32[]{:S(2)}, u32[]{:S(2)}) collective-permute-start(bf16[1,512,256]{2,1,0:T(8,128)(2,1)S(1)} %copy-done.15), channel_id=1, source_target_pairs={{0,4},{4,0},{1,5},{5,1},{2,6},{6,2},{3,7},{7,3},{8,12},{12,8},{9,1... | collective-permute-start | bytes 786440 | tf_op jit(solution)/shard_map/ppermute | solution.py:762
  165.4 1.7 collective-permute-start.20
  165.4 23.7 %copy-start.6 = (bf16[4,1,512,256]{3,2,1,0:T(8,128)(2,1)}, bf16[4,1,512,256]{3,2,1,0:T(8,128)(2,1)S(1)}, u32[]{:S(2)}) copy-start(bf16[4,1,512,256]{3,2,1,0:T(8,128)(2,1)S(1)} %bitcast_dynamic-update-slice_fusion.25.own_value) | copy-start | bytes 3145732
  165.5 1.9 collective-permute-start.21
  167.2 1.5 collective-permute-start.22
  167.4 11.1 %collective-permute-start.23 = (bf16[1,512,256]{2,1,0:T(8,128)(2,1)S(1)}, bf16[1,512,256]{2,1,0:T(8,128)(2,1)S(1)}, u32[]{:S(2)}, u32[]{:S(2)}) collective-permute-start(bf16[1,512,256]{2,1,0:T(8,128)(2,1)S(1)} %copy-done.28), channel_id=1, source_target_pairs={{0,8},{8,16},{16,24},{24,0},{1,9},{9,17},{17,25},{25,1},{2,10},{10... | collective-permute-start | bytes 786440 | tf_op jit(solution)/shard_map/ppermute | solution.py:758
  168.7 20.4 %collective-permute-start.24 = (bf16[1,512,256]{2,1,0:T(8,128)(2,1)S(1)}, bf16[1,512,256]{2,1,0:T(8,128)(2,1)S(1)}, u32[]{:S(2)}, u32[]{:S(2)}) collective-permute-start(bf16[1,512,256]{2,1,0:T(8,128)(2,1)S(1)} %copy-done.27), channel_id=1, source_target_pairs={{0,16},{8,24},{16,0},{24,8},{1,17},{9,25},{17,1},{25,9},{2,18},{10... | collective-permute-start | bytes 786440 | tf_op jit(solution)/shard_map/ppermute | solution.py:758
  170.6 22.0 %copy-start.4 = (bf16[4,1,512,256]{3,2,1,0:T(8,128)(2,1)}, bf16[4,1,512,256]{3,2,1,0:T(8,128)(2,1)S(1)}, u32[]{:S(2)}) copy-start(bf16[4,1,512,256]{3,2,1,0:T(8,128)(2,1)S(1)} %bitcast_dynamic-update-slice_fusion.21.sibling_value) | copy-start | bytes 3145732
  178.5 12.5 %collective-permute-start.25 = (bf16[1,512,256]{2,1,0:T(8,128)(2,1)S(1)}, bf16[1,512,256]{2,1,0:T(8,128)(2,1)S(1)}, u32[]{:S(2)}, u32[]{:S(2)}) collective-permute-start(bf16[1,512,256]{2,1,0:T(8,128)(2,1)S(1)} %copy-done.26), channel_id=1, source_target_pairs={{0,24},{8,0},{16,8},{24,16},{1,25},{9,1},{17,9},{25,17},{2,26},{10... | collective-permute-start | bytes 786440 | tf_op jit(solution)/shard_map/ppermute | solution.py:758
  189.1 2.6 collective-permute-start.27
  191.0 1.5 collective-permute-start.28
  191.1 1.9 collective-permute-start.29
  237.5 2.5 collective-permute-start.30
  237.8 12.2 %collective-permute-start.42 = (bf16[2,4,32,256]{3,2,1,0:T(8,128)(2,1)}, bf16[2,4,32,256]{3,2,1,0:T(8,128)(2,1)S(1)}, u32[]{:S(2)}, u32[]{:S(2)}) collective-permute-start(bf16[2,4,32,256]{3,2,1,0:T(8,128)(2,1)} %get-tuple-element.108), channel_id=1, source_target_pairs={{0,4},{4,0},{1,5},{5,1},{2,6},{6,2},{3,7},{7,3},{8,12},{12,8},{9,1... | collective-permute-start | bytes 393224 | tf_op jit(solution)/shard_map/ppermute | solution.py:762
  238.1 11.9 %collective-permute-start.53 = (bf16[4,2,4,64,64]{4,3,2,1,0:T(8,128)(2,1)S(1)}, bf16[4,2,4,64,64]{4,3,2,1,0:T(8,128)(2,1)S(1)}, u32[]{:S(2)}, u32[]{:S(2)}) collective-permute-start(bf16[4,2,4,64,64]{4,3,2,1,0:T(8,128)(2,1)S(1)} %dynamic-slice_bitcast_fusion), channel_id=1, source_target_pairs={{0,4},{4,0},{1,5},{5,1},{2,6},{6,2},{3,7},{7,3},{8,12},{12,8},{9,1... | collective-permute-start | bytes 786440 | tf_op jit(solution)/shard_map/ppermute | solution.py:762
  240.1 16.7 %collective-permute-start.31 = (bf16[512,256]{1,0:T(8,128)(2,1)S(1)}, bf16[512,256]{1,0:T(8,128)(2,1)S(1)}, u32[]{:S(2)}, u32[]{:S(2)}) collective-permute-start(bf16[512,256]{1,0:T(8,128)(2,1)S(1)} %bitcast.188), channel_id=1, source_target_pairs={{0,16},{8,24},{16,0},{24,8},{1,17},{9,25},{17,1},{25,9},{2,18},{10... | collective-permute-start | bytes 786440 | tf_op jit(solution)/shard_map/ppermute | solution.py:758
  244.1 21.0 %collective-permute-start.34 = (bf16[512,256]{1,0:T(8,128)(2,1)S(1)}, bf16[512,256]{1,0:T(8,128)(2,1)S(1)}, u32[]{:S(2)}, u32[]{:S(2)}) collective-permute-start(bf16[512,256]{1,0:T(8,128)(2,1)S(1)} %bitcast.189), channel_id=1, source_target_pairs={{8,0},{16,8},{24,16},{9,1},{17,9},{25,17},{10,2},{18,10},{26,18},{... | collective-permute-start | bytes 786440 | tf_op jit(solution)/shard_map/ppermute | solution.py:780
  245.4 30.9 %collective-permute-start.33 = (bf16[512,256]{1,0:T(8,128)(2,1)S(1)}, bf16[512,256]{1,0:T(8,128)(2,1)S(1)}, u32[]{:S(2)}, u32[]{:S(2)}) collective-permute-start(bf16[512,256]{1,0:T(8,128)(2,1)S(1)} %bitcast.190), channel_id=1, source_target_pairs={{0,8},{8,16},{16,24},{1,9},{9,17},{17,25},{2,10},{10,18},{18,26},{... | collective-permute-start | bytes 786440 | tf_op jit(solution)/shard_map/ppermute | solution.py:779
  250.0 26.3 %copy-start.22 = (bf16[4,4,32,256]{3,2,1,0:T(8,128)(2,1)}, bf16[4,4,32,256]{3,2,1,0:T(8,128)(2,1)S(1)}, u32[]{:S(2)}) copy-start(bf16[4,4,32,256]{3,2,1,0:T(8,128)(2,1)S(1)} %pad_maximum_fusion.3) | copy-start | bytes 786436
  250.3 13.5 %collective-permute-start.54 = (bf16[3,4,64,64]{3,2,1,0:T(8,128)(2,1)S(1)}, bf16[3,4,64,64]{3,2,1,0:T(8,128)(2,1)S(1)}, u32[]{:S(2)}, u32[]{:S(2)}) collective-permute-start(bf16[3,4,64,64]{3,2,1,0:T(8,128)(2,1)S(1)} %get-tuple-element.140), channel_id=1, source_target_pairs={{0,8},{8,16},{16,24},{24,0},{1,9},{9,17},{17,25},{25,1},{2,10},{10... | collective-permute-start | bytes 294920 | tf_op jit(solution)/shard_map/ppermute | solution.py:758
  256.8 25.5 %copy-start.35 = (bf16[512,256]{1,0:T(8,128)(2,1)}, bf16[512,256]{1,0:T(8,128)(2,1)S(1)}, u32[]{:S(2)}) copy-start(bf16[512,256]{1,0:T(8,128)(2,1)S(1)} %collective-permute-done.31.h2) | copy-start | bytes 786436
  256.8 23.4 %collective-permute-start.43 = (bf16[512,256]{1,0:T(8,128)(2,1)S(1)}, bf16[512,256]{1,0:T(8,128)(2,1)S(1)}, u32[]{:S(2)}, u32[]{:S(2)}) collective-permute-start(bf16[512,256]{1,0:T(8,128)(2,1)S(1)} %bitcast.184), channel_id=1, source_target_pairs={{0,16},{8,24},{16,0},{24,8},{1,17},{9,25},{17,1},{25,9},{2,18},{10... | collective-permute-start | bytes 786440 | tf_op jit(solution)/shard_map/ppermute | solution.py:758
  256.9 24.7 %collective-permute-start.32 = (bf16[512,256]{1,0:T(8,128)(2,1)S(1)}, bf16[512,256]{1,0:T(8,128)(2,1)S(1)}, u32[]{:S(2)}, u32[]{:S(2)}) collective-permute-start(bf16[512,256]{1,0:T(8,128)(2,1)S(1)} %collective-permute-done.31.h2), channel_id=1, source_target_pairs={{8,0},{16,24},{9,1},{17,25},{10,2},{18,26},{11,3},{19,27},{12,4},{... | collective-permute-start | bytes 786440 | tf_op jit(solution)/shard_map/ppermute | solution.py:782
  263.8 29.5 %collective-permute-start.46 = (bf16[512,256]{1,0:T(8,128)(2,1)S(1)}, bf16[512,256]{1,0:T(8,128)(2,1)S(1)}, u32[]{:S(2)}, u32[]{:S(2)}) collective-permute-start(bf16[512,256]{1,0:T(8,128)(2,1)S(1)} %bitcast.185), channel_id=1, source_target_pairs={{8,0},{16,8},{24,16},{9,1},{17,9},{25,17},{10,2},{18,10},{26,18},{... | collective-permute-start | bytes 786440 | tf_op jit(solution)/shard_map/ppermute | solution.py:780
  265.2 26.6 %collective-permute-start.55 = (bf16[3,4,64,64]{3,2,1,0:T(8,128)(2,1)S(1)}, bf16[3,4,64,64]{3,2,1,0:T(8,128)(2,1)S(1)}, u32[]{:S(2)}, u32[]{:S(2)}) collective-permute-start(bf16[3,4,64,64]{3,2,1,0:T(8,128)(2,1)S(1)} %get-tuple-element.141), channel_id=1, source_target_pairs={{0,16},{8,24},{16,0},{24,8},{1,17},{9,25},{17,1},{25,9},{2,18},{10... | collective-permute-start | bytes 294920 | tf_op jit(solution)/shard_map/ppermute | solution.py:758
  276.3 18.6 %collective-permute-start.45 = (bf16[512,256]{1,0:T(8,128)(2,1)S(1)}, bf16[512,256]{1,0:T(8,128)(2,1)S(1)}, u32[]{:S(2)}, u32[]{:S(2)}) collective-permute-start(bf16[512,256]{1,0:T(8,128)(2,1)S(1)} %bitcast.186), channel_id=1, source_target_pairs={{0,8},{8,16},{16,24},{1,9},{9,17},{17,25},{2,10},{10,18},{18,26},{... | collective-permute-start | bytes 786440 | tf_op jit(solution)/shard_map/ppermute | solution.py:779
  280.2 15.2 %collective-permute-start.44 = (bf16[512,256]{1,0:T(8,128)(2,1)S(1)}, bf16[512,256]{1,0:T(8,128)(2,1)S(1)}, u32[]{:S(2)}, u32[]{:S(2)}) collective-permute-start(bf16[512,256]{1,0:T(8,128)(2,1)S(1)} %collective-permute-done.43.h2), channel_id=1, source_target_pairs={{8,0},{16,24},{9,1},{17,25},{10,2},{18,26},{11,3},{19,27},{12,4},{... | collective-permute-start | bytes 786440 | tf_op jit(solution)/shard_map/ppermute | solution.py:782
  287.2 16.3 %collective-permute-start.38 = (bf16[4,32,1024]{2,1,0:T(8,128)(2,1)}, bf16[4,32,1024]{2,1,0:T(8,128)(2,1)S(1)}, u32[]{:S(2)}, u32[]{:S(2)}) collective-permute-start(bf16[4,32,1024]{2,1,0:T(8,128)(2,1)} %get-tuple-element.106), channel_id=1, source_target_pairs={{0,3},{1,2},{2,1},{3,0},{4,7},{5,6},{6,5},{7,4},{8,11},{9,10},{10,... | collective-permute-start | bytes 786440 | tf_op jit(solution)/shard_map/ppermute | solution.py:1021
  291.8 12.3 %collective-permute-start.37 = (bf16[4,32,1024]{2,1,0:T(8,128)(2,1)}, bf16[4,32,1024]{2,1,0:T(8,128)(2,1)S(1)}, u32[]{:S(2)}, u32[]{:S(2)}) collective-permute-start(bf16[4,32,1024]{2,1,0:T(8,128)(2,1)} %get-tuple-element.105), channel_id=1, source_target_pairs={{0,2},{2,0},{1,3},{3,1},{4,6},{6,4},{5,7},{7,5},{8,10},{10,8},{9,1... | collective-permute-start | bytes 786440 | tf_op jit(solution)/shard_map/ppermute | solution.py:770
  293.3 11.3 %collective-permute-start.36 = (bf16[4,32,1024]{2,1,0:T(8,128)(2,1)}, bf16[4,32,1024]{2,1,0:T(8,128)(2,1)S(1)}, u32[]{:S(2)}, u32[]{:S(2)}) collective-permute-start(bf16[4,32,1024]{2,1,0:T(8,128)(2,1)} %get-tuple-element.104), channel_id=1, source_target_pairs={{0,1},{1,0},{2,3},{3,2},{4,5},{5,4},{6,7},{7,6},{8,9},{9,8},{10,11... | collective-permute-start | bytes 786440 | tf_op jit(solution)/shard_map/ppermute | solution.py:766
  294.8 22.9 %collective-permute-start.56 = (bf16[3,4,64,64]{3,2,1,0:T(8,128)(2,1)S(1)}, bf16[3,4,64,64]{3,2,1,0:T(8,128)(2,1)S(1)}, u32[]{:S(2)}, u32[]{:S(2)}) collective-permute-start(bf16[3,4,64,64]{3,2,1,0:T(8,128)(2,1)S(1)} %get-tuple-element.139), channel_id=1, source_target_pairs={{0,24},{8,0},{16,8},{24,16},{1,25},{9,1},{17,9},{25,17},{2,26},{10... | collective-permute-start | bytes 294920 | tf_op jit(solution)/shard_map/ppermute | solution.py:758
  301.1 10.4 %collective-permute-start.49 = (bf16[4,32,1024]{2,1,0:T(8,128)(2,1)}, bf16[4,32,1024]{2,1,0:T(8,128)(2,1)S(1)}, u32[]{:S(2)}, u32[]{:S(2)}) collective-permute-start(bf16[4,32,1024]{2,1,0:T(8,128)(2,1)} %get-tuple-element.113), channel_id=1, source_target_pairs={{0,3},{1,2},{2,1},{3,0},{4,7},{5,6},{6,5},{7,4},{8,11},{9,10},{10,... | collective-permute-start | bytes 786440 | tf_op jit(solution)/shard_map/ppermute | solution.py:1021
  303.5 10.4 %collective-permute-start.48 = (bf16[4,32,1024]{2,1,0:T(8,128)(2,1)}, bf16[4,32,1024]{2,1,0:T(8,128)(2,1)S(1)}, u32[]{:S(2)}, u32[]{:S(2)}) collective-permute-start(bf16[4,32,1024]{2,1,0:T(8,128)(2,1)} %get-tuple-element.112), channel_id=1, source_target_pairs={{0,2},{2,0},{1,3},{3,1},{4,6},{6,4},{5,7},{7,5},{8,10},{10,8},{9,1... | collective-permute-start | bytes 786440 | tf_op jit(solution)/shard_map/ppermute | solution.py:770
  304.0 11.3 %collective-permute-start.47 = (bf16[4,32,1024]{2,1,0:T(8,128)(2,1)}, bf16[4,32,1024]{2,1,0:T(8,128)(2,1)S(1)}, u32[]{:S(2)}, u32[]{:S(2)}) collective-permute-start(bf16[4,32,1024]{2,1,0:T(8,128)(2,1)} %get-tuple-element.111), channel_id=1, source_target_pairs={{0,1},{1,0},{2,3},{3,2},{4,5},{5,4},{6,7},{7,6},{8,9},{9,8},{10,11... | collective-permute-start | bytes 786440 | tf_op jit(solution)/shard_map/ppermute | solution.py:766
  305.4 13.5 %collective-permute-start.39 = (bf16[32,1024]{1,0:T(8,128)(2,1)S(1)}, bf16[32,1024]{1,0:T(8,128)(2,1)S(1)}, u32[]{:S(2)}, u32[]{:S(2)}) collective-permute-start(bf16[32,1024]{1,0:T(8,128)(2,1)S(1)} %get-tuple-element.150), channel_id=1, source_target_pairs={{0,8},{8,16},{16,24},{24,0},{1,9},{9,17},{17,25},{25,1},{2,10},{10... | collective-permute-start | bytes 196616 | tf_op jit(solution)/shard_map/ppermute | solution.py:758
  311.4 12.4 %collective-permute-start.40 = (bf16[32,1024]{1,0:T(8,128)(2,1)S(1)}, bf16[32,1024]{1,0:T(8,128)(2,1)S(1)}, u32[]{:S(2)}, u32[]{:S(2)}) collective-permute-start(bf16[32,1024]{1,0:T(8,128)(2,1)S(1)} %get-tuple-element.149), channel_id=1, source_target_pairs={{0,16},{8,24},{16,0},{24,8},{1,17},{9,25},{17,1},{25,9},{2,18},{10... | collective-permute-start | bytes 196616 | tf_op jit(solution)/shard_map/ppermute | solution.py:758
  313.9 9.9 %collective-permute-start.41 = (bf16[32,1024]{1,0:T(8,128)(2,1)S(1)}, bf16[32,1024]{1,0:T(8,128)(2,1)S(1)}, u32[]{:S(2)}, u32[]{:S(2)}) collective-permute-start(bf16[32,1024]{1,0:T(8,128)(2,1)S(1)} %get-tuple-element.148), channel_id=1, source_target_pairs={{0,24},{8,0},{16,8},{24,16},{1,25},{9,1},{17,9},{25,17},{2,26},{10... | collective-permute-start | bytes 196616 | tf_op jit(solution)/shard_map/ppermute | solution.py:758
  317.1 6.7 %collective-permute-start.50 = (bf16[32,1024]{1,0:T(8,128)(2,1)S(1)}, bf16[32,1024]{1,0:T(8,128)(2,1)S(1)}, u32[]{:S(2)}, u32[]{:S(2)}) collective-permute-start(bf16[32,1024]{1,0:T(8,128)(2,1)S(1)} %get-tuple-element.144), channel_id=1, source_target_pairs={{0,8},{8,16},{16,24},{24,0},{1,9},{9,17},{17,25},{25,1},{2,10},{10... | collective-permute-start | bytes 196616 | tf_op jit(solution)/shard_map/ppermute | solution.py:758
  317.7 6.6 %collective-permute-start.51 = (bf16[32,1024]{1,0:T(8,128)(2,1)S(1)}, bf16[32,1024]{1,0:T(8,128)(2,1)S(1)}, u32[]{:S(2)}, u32[]{:S(2)}) collective-permute-start(bf16[32,1024]{1,0:T(8,128)(2,1)S(1)} %get-tuple-element.143), channel_id=1, source_target_pairs={{0,16},{8,24},{16,0},{24,8},{1,17},{9,25},{17,1},{25,9},{2,18},{10... | collective-permute-start | bytes 196616 | tf_op jit(solution)/shard_map/ppermute | solution.py:758
  318.9 5.4 %collective-permute-start.52 = (bf16[32,1024]{1,0:T(8,128)(2,1)S(1)}, bf16[32,1024]{1,0:T(8,128)(2,1)S(1)}, u32[]{:S(2)}, u32[]{:S(2)}) collective-permute-start(bf16[32,1024]{1,0:T(8,128)(2,1)S(1)} %get-tuple-element.142), channel_id=1, source_target_pairs={{0,24},{8,0},{16,8},{24,16},{1,25},{9,1},{17,9},{25,17},{2,26},{10... | collective-permute-start | bytes 196616 | tf_op jit(solution)/shard_map/ppermute | solution.py:758
  (39 other events, 290.8 us)

commit v4 on v3

--- a/solution.py
+++ b/solution.py
@@ -261,6 +261,12 @@
     return pl.BlockSpec(memory_space=pltpu.SMEM)
 
 
+def takes(us):
+    return pl.CostEstimate(
+        flops=int(us * 1.15e9), bytes_accessed=int(us * 3.0e6), transcendentals=0
+    )
+
+
 def kernel_params():
     return pltpu.CompilerParams(vmem_limit_bytes=VMEM_LIMIT)
 
@@ -299,6 +305,7 @@
         in_specs=[in_smem()] * 2 + [in_vmem()] * 2,
         out_specs=in_vmem(),
         compiler_params=kernel_params(),
+        cost_estimate=takes(1.5),
     )(kind, extents, long_rows, short_rows)
 
 
@@ -332,6 +339,7 @@
         in_specs=[in_smem()] * 2 + [in_vmem()] * 4,
         out_specs=in_vmem(),
         compiler_params=kernel_params(),
+        cost_estimate=takes(1.5),
     )(kind, extents, long_rows, short_rows, taken, edge)
 
 
@@ -339,24 +347,33 @@
     return pl.BlockSpec((1,) + shape[1:], lambda i: (i,) + (0,) * (len(shape) - 1))
 
 
-def mix_kernel(kind, chunk, ratios, left, pair_mix, value_mix, gate_mix, squeezed):
-    @pl.loop(0, chunk.shape[1])
+def gather_blocks(kind, own, rest, held):
+    held[kind[6]] = own[...]
+    for k in range(3):
+        held[kind[7 + k]] = rest[k]
+
+
+def mix_kernel(kind, own, rest, ratios, left, kv_mix, r_mix, gate_mix, squeezed, held):
+    gather_blocks(kind, own.at[0], rest.at[0], held)
+
+    @pl.loop(0, held.shape[0], unroll=2)
     def _(tile):
-        here, step = here_and_step(chunk.at[0], kind[0], kind[1], tile)
+        here, step = here_and_step(held, kind[0], kind[1], tile)
         at = pl.ds(pl.multiple_of(tile * TILE, TILE), TILE)
 
         def mix(which):
             return (here + ratios[0, which : which + 1, :] * step).astype(bf16)
 
-        pair_mix[0, 0, at, :] = mix(0)
-        pair_mix[0, 1, at, :] = mix(1)
-        value_mix[0, at, :] = mix(2)
+        r_mix[0, at, :] = mix(0)
+        kv_mix[0, 0, at, :] = mix(1)
+        kv_mix[0, 1, at, :] = mix(2)
         gate_mix[0, at, :] = mix(3)
         squeezed[0, at, :] = jnp.dot(mix(4), left[0], preferred_element_type=f32)
 
 
-def mixes_of(kind, pair, ratios, left):
-    lines, rows, depth = pair.shape[1], pair.shape[2] - EXTRA, pair.shape[3]
+def mixes_of(kind, own, rest, ratios, left):
+    rows, depth = own.shape[1] - EXTRA, own.shape[2]
+    lines = rest.shape[1] + 1
     whole = lines * rows
     outs = [
         jax.ShapeDtypeStruct((2, 2, whole, depth), bf16),
@@ -368,66 +385,12 @@
         mix_kernel,
         grid=(2,),
         out_shape=outs,
-        in_specs=[in_smem()] + [half_block(a.shape) for a in (pair, ratios, left)],
+        in_specs=[in_smem()] + [half_block(a.shape) for a in (own, rest, ratios, left)],
         out_specs=[half_block(out.shape) for out in outs],
+        scratch_shapes=[pltpu.VMEM((lines, rows + EXTRA, depth), bf16)],
         compiler_params=kernel_params(),
-    )(kind, pair, ratios, left)
-
-
-def mix_project_kernel(rel, ready, kind, chunk, ratios, left, own, sibling, *refs):
-    earlier, refs = refs[:ready], refs[ready:]
-    value_mix, gate_mix, squeezed, recept_ref, keys_ref = refs
-    half = pl.program_id(0)
-
-    @pl.loop(0, chunk.shape[1])
-    def _(tile):
-        here, step = here_and_step(chunk.at[0], kind[0], kind[1], tile)
-        at = pl.ds(pl.multiple_of(tile * TILE, TILE), TILE)
-
-        def mix(which):
-            return (here + ratios[0, which : which + 1, :] * step).astype(bf16)
-
-        value_mix[0, at, :] = mix(2)
-        gate_mix[0, at, :] = mix(3)
-        squeezed[0, at, :] = jnp.dot(mix(4), left[0], preferred_element_type=f32)
-        for which, out in enumerate((recept_ref, keys_ref)):
-            weight = jnp.where(
-                half == 0, own[kind[2 + rel], which], sibling[kind[2 + rel], which]
-            )
-            part = jnp.dot(mix(which), weight, preferred_element_type=f32)
-            if ready == 1:
-                weight = jnp.where(half == 0, own[kind[2], which], sibling[kind[2], which])
-                part = part + jnp.dot(
-                    earlier[0][0, which, at, :], weight, preferred_element_type=f32
-                )
-                before = jnp.zeros_like(part)
-            else:
-                before = earlier[which][at, :]
-            out[at, :] = part + jnp.where(half == 0, before, out[at, :])
-
-
-def mix_and_project(rel, kind, pair, ratios, left, own, sibling, *earlier):
-    lines, rows, depth = pair.shape[1], pair.shape[2] - EXTRA, pair.shape[3]
-    whole, width = lines * rows, own.shape[3]
-    outs = [
-        jax.ShapeDtypeStruct((2, whole, depth), bf16),
-        jax.ShapeDtypeStruct((2, whole, depth), bf16),
-        jax.ShapeDtypeStruct((2, whole, left.shape[2]), f32),
-    ]
-    flat = jax.ShapeDtypeStruct((whole, width), f32)
-    ready = len(earlier)
-    return pl.pallas_call(
-        lambda *refs: mix_project_kernel(rel, ready, *refs),
-        grid=(2,),
-        out_shape=outs + [flat] * 2,
-        in_specs=[in_smem()]
-        + [half_block(a.shape) for a in (pair, ratios, left)]
-        + [in_vmem()] * 2
-        + ([half_block(earlier[0].shape)] if ready == 1 else [in_vmem()] * 2),
-        out_specs=[half_block(out.shape) for out in outs]
-        + [pl.BlockSpec((whole, width), lambda i: (0, 0))] * 2,
-        compiler_params=kernel_params(),
-    )(kind, pair, ratios, left, own, sibling, *earlier)
+        cost_estimate=takes(7),
+    )(kind, own, rest, ratios, left)
 
 
 def project_kernel(
@@ -438,74 +401,128 @@
     low0,
     low1,
     low2,
-    recept_part,
-    keys_part,
-    last0,
-    last1,
+    own0,
+    own1,
+    rest0,
+    rest1,
     ratios,
     left,
-    own,
-    sibling,
-    own_value,
-    sibling_value,
+    own_weight,
+    sibling_weight,
     right,
     base,
-    recept_ref,
     keys_ref,
     values_ref,
     decay_ref,
+    r_mix,
     gate_mix,
+    held,
 ):
     tile = pl.program_id(0)
-    totals = [recept_part[...], keys_part[...], None]
+
+    @pl.when(tile == 0)
+    def _():
+        for half, (own, rest) in enumerate(((own0, rest0), (own1, rest1))):
+            gather_blocks(kind, own, rest, held.at[half])
+
+    totals = [None] * 2
+
+    def add(which, rel, half, mixed):
+        weight = (own_weight, sibling_weight)[half][kind[2 + rel], which]
+        part = jnp.dot(mixed, weight, preferred_element_type=f32)
+        totals[which] = part if totals[which] is None else totals[which] + part
+
     squeezed = low0[0] + low0[1] + low1[0] + low1[1] + low2[0] + low2[1]
-    for half, chunk in enumerate((last0, last1)):
-        here, step = here_and_step(chunk, kind[0], kind[1], tile)
+    for half in range(2):
+        here, step = here_and_step(held.at[half], kind[0], kind[1], tile)
 
         def mix(which):
             return (here + ratios[half, which : which + 1, :] * step).astype(bf16)
 
-        for which in range(2):
-            weight = (own, sibling)[half][kind[5], which]
-            totals[which] += jnp.dot(mix(which), weight, preferred_element_type=f32)
-        weight = (own_value, sibling_value)[half][kind[5], 0]
-        part = jnp.dot(mix(2), weight, preferred_element_type=f32)
-        totals[2] = part if totals[2] is None else totals[2] + part
+        r_mix[half] = mix(0)
+        add(0, 3, half, mix(1))
+        add(1, 3, half, mix(2))
         gate_mix[half] = mix(3)
         squeezed = squeezed + jnp.dot(mix(4), left[half], preferred_element_type=f32)
     for rel, mixes in enumerate((mix0, mix1, mix2)):
         for half in range(2):
-            weight = (own_value, sibling_value)[half][kind[2 + rel], 0]
-            totals[2] += jnp.dot(mixes[half], weight, preferred_element_type=f32)
-    recept_ref[...] = totals[0]
-    keys_ref[...] = totals[1]
-    values_ref[...] = totals[2]
+            for which in range(2):
+                add(which, rel, half, mixes[half, which])
+    keys_ref[...] = totals[0]
+    values_ref[...] = totals[1]
     squeezed = jnp.tanh(squeezed).astype(bf16)
     grown = jnp.dot(squeezed, right[...], preferred_element_type=f32)
     decay_ref[...] = -jnp.exp(base[...] + grown)
 
 
-def projected(kind, mixes, lows, parts, last, *rest):
-    rows, depth = mixes[0].shape[1:]
-    width, rank = parts[0].shape[1], lows[0].shape[2]
+def projected(kind, mixes, lows, owns, rests, *rest):
+    rows, depth = mixes[0].shape[2:]
+    own_weight = rest[2]
+    width, rank = own_weight.shape[3], lows[0].shape[2]
     flat = jax.ShapeDtypeStruct((rows, width), f32)
+    wide = jax.ShapeDtypeStruct((2, rows, depth), bf16)
     tile_of = pl.BlockSpec((TILE, width), lambda i: (i, 0))
+    wide_of = pl.BlockSpec((2, TILE, depth), lambda i: (0, i, 0))
     return pl.pallas_call(
         project_kernel,
         grid=(rows // TILE,),
-        out_shape=[flat] * 4 + [jax.ShapeDtypeStruct((2, rows, depth), bf16)],
+        out_shape=[flat] * 3 + [wide] * 2,
         in_specs=[in_smem()]
-        + [pl.BlockSpec((2, TILE, depth), lambda i: (0, i, 0))] * 3
+        + [pl.BlockSpec((2, 2, TILE, depth), lambda i: (0, 0, i, 0))] * 3
         + [pl.BlockSpec((2, TILE, rank), lambda i: (0, i, 0))] * 3
-        + [tile_of] * 2
-        + [in_vmem()] * (2 + len(rest)),
-        out_specs=[tile_of] * 4 + [pl.BlockSpec((2, TILE, depth), lambda i: (0, i, 0))],
+        + [in_vmem()] * (4 + len(rest)),
+        out_specs=[tile_of] * 3 + [wide_of] * 2,
+        scratch_shapes=[pltpu.VMEM((2, rests[0].shape[0] + 1) + owns[0].shape, bf16)],
         compiler_params=kernel_params(),
-    )(kind, *mixes, *lows, *parts, *last, *rest)
+        cost_estimate=takes(12),
+    )(kind, *mixes, *lows, *owns, *rests, *rest)
+
+
+def plain_kernel(kind, mix0, mix1, mix2, mix3, own, sibling, out_ref):
+    half = pl.program_id(0)
+    part = None
+    for rel, mixes in enumerate((mix0, mix1, mix2, mix3)):
+        weight = jnp.where(half == 0, own[kind[2 + rel], 0], sibling[kind[2 + rel], 0])
+        new = jnp.dot(mixes[0], weight, preferred_element_type=f32)
+        part = new if part is None else part + new
+
+    @pl.when(half == 0)
+    def _():
+        out_ref[...] = part
+
+    @pl.when(half == 1)
+    def _():
+        out_ref[...] += part
+
+
+def plain_product(kind, mixes, own, sibling):
+    rows, width = mixes[0].shape[1], own.shape[3]
+    return pl.pallas_call(
+        plain_kernel,
+        grid=(2,),
+        out_shape=jax.ShapeDtypeStruct((rows, width), f32),
+        in_specs=[in_smem()] + [half_block(mix.shape) for mix in mixes] + [in_vmem()] * 2,
+        out_specs=pl.BlockSpec((rows, width), lambda i: (0, 0)),
+        compiler_params=kernel_params(),
+        cost_estimate=takes(6),
+    )(kind, *mixes, own, sibling)
 
 
 def gate_kernel(
-    kind, mix0, mix1, mix2, mix3, own, sibling, normed, live, kept0, sent0, kept1, sent1, total
+    kind,
+    lengths,
+    mix0,
+    mix1,
+    mix2,
+    mix3,
+    own,
+    sibling,
+    normed,
+    kept0,
+    sent0,
+    kept1,
+    sent1,
+    total,
 ):
     half = pl.program_id(0)
     part = None
@@ -522,29 +539,38 @@
     def _():
         gate = total[...] + part
         value = normed[...] * (gate * jax.nn.sigmoid(gate))
-        value = jnp.where(live[...] > 0, value, 0.0).astype(bf16)
-        lines = kept0.shape[1]
-        value = value.reshape(lines, 2, 2, 2, BLK // 2, value.shape[1])
+        row = lax.broadcasted_iota(jnp.int32, (BLK, value.shape[1]), 0)
         is_long = kind[0] == 1
-        for block in range(2):
-            for at, kept, sent in ((0, kept0, sent0), (1, kept1, sent1)):
-                even, odd = value[:, 0, block, at], value[:, 1, block, at]
-                kept[block] = jnp.where(is_long, even, odd)
-                sent[block] = jnp.where(is_long, odd, even)
-
-
-def gated(kind, mixes, own, sibling, normed, live):
+        half_rows = BLK // 2
+
+        def lived(n):
+            block = value[n * BLK : (n + 1) * BLK]
+            return jnp.where(row < lengths[n], block, 0.0).astype(bf16)
+
+        for line in range(kept0.shape[1]):
+            for block in range(2):
+                even, odd = lived(4 * line + block), lived(4 * line + 2 + block)
+                kept = jnp.where(is_long, even, odd)
+                sent = jnp.where(is_long, odd, even)
+                kept0[block, line] = kept[:half_rows]
+                kept1[block, line] = kept[half_rows:]
+                sent0[block, line] = sent[:half_rows]
+                sent1[block, line] = sent[half_rows:]
+
+
+def gated(kind, lengths, mixes, own, sibling, normed):
     rows, width = normed.shape
     quarter = jax.ShapeDtypeStruct((2, rows // TILE, BLK // 2, width), bf16)
     return pl.pallas_call(
         gate_kernel,
         grid=(2,),
         out_shape=[quarter] * 4,
-        in_specs=[in_smem()] + [half_block(mix.shape) for mix in mixes] + [in_vmem()] * 4,
+        in_specs=[in_smem()] * 2 + [half_block(mix.shape) for mix in mixes] + [in_vmem()] * 3,
         out_specs=[pl.BlockSpec(quarter.shape, lambda i: (0, 0, 0, 0))] * 4,
         scratch_shapes=[pltpu.VMEM((rows, width), f32)],
         compiler_params=kernel_params(),
-    )(kind, *mixes, own, sibling, normed, live)
+        cost_estimate=takes(7),
+    )(kind, lengths, *mixes, own, sibling, normed)
 
 
 def head_blocks(heads):
@@ -562,7 +588,7 @@
     for h in range(heads):
         hold[:, h * span : (h + 1) * span] = s_ref[h]
 
-    @pl.loop(0, k_ref.shape[0] // span)
+    @pl.loop(0, k_ref.shape[0] // span, unroll=8)
     def _(n):
         at = pl.ds(pl.multiple_of(n * span, span), span)
         live = row < lengths[n]
@@ -616,6 +642,7 @@
         out_specs=[in_vmem()] * 2,
         scratch_shapes=[pltpu.VMEM((BLK, width), f32)],
         compiler_params=kernel_params(),
+        cost_estimate=takes(7),
     )(lengths, carry, k, v, w, state)
 
 
@@ -634,7 +661,7 @@
     def against(a, b):
         return lax.dot_general(a, b, (((1,), (1,)), ((), ())), preferred_element_type=f32)
 
-    @pl.loop(0, r_ref.shape[0] // span)
+    @pl.loop(0, r_ref.shape[0] // span, unroll=4)
     def _(n):
         at = pl.ds(pl.multiple_of(n * span, span), span)
         live = row < lengths[n]
@@ -681,7 +708,7 @@
         )
         return both * (1.0 / span)
 
-    @pl.loop(0, r_ref.shape[0] // TILE)
+    @pl.loop(0, r_ref.shape[0] // TILE, unroll=2)
     def _(tile):
         at = pl.ds(pl.multiple_of(tile * TILE, TILE), TILE)
         value = out_ref[at, :]
@@ -697,11 +724,12 @@
         in_specs=[in_smem()] + [in_vmem()] * 8,
         out_specs=in_vmem(),
         compiler_params=kernel_params(),
+        cost_estimate=takes(12),
     )(lengths, r, k, v, w, entered, bonus, gain, bias)
 
 
 def final_kernel(block_of, h0, h1, h2, h3, weight, o0, o1, o2, o3, hold):
-    @pl.loop(0, hold.shape[1] // TILE)
+    @pl.loop(0, hold.shape[1] // TILE, unroll=2)
     def _(tile):
         at = pl.ds(pl.multiple_of(tile * TILE, TILE), TILE)
         total = None
@@ -726,6 +754,7 @@
         out_specs=[in_vmem()] * 4,
         scratch_shapes=[pltpu.VMEM((rows, width), bf16)],
         compiler_params=kernel_params(),
+        cost_estimate=takes(4.5),
     )(block_of, *pieces, weight)
 
 
@@ -746,6 +775,7 @@
         in_specs=[in_smem()] + [in_vmem()] * len(pieces),
         out_specs=in_vmem(),
         compiler_params=kernel_params(),
+        cost_estimate=takes(2),
     )(at, *pieces)
 
 
@@ -837,6 +867,7 @@
     kind = jnp.stack(
         [is_long.astype(jnp.int32), jnp.where(is_long, rows, slot_rows).astype(jnp.int32)]
         + [(mp ^ rel).astype(jnp.int32) for rel in range(4)]
+        + [((z - k) % lines).astype(jnp.int32) for k in range(4)]
     )
     given = given_to_other_core(
         kind, prompt_live_extents, continued_prompt_entries, padded_prompt_entries
@@ -860,6 +891,10 @@
         token_mixing_ratios,
         fading_left_factor,
         fading_right_factor,
+        fading_baseline,
+        present_reward,
+        group_layer_scaling,
+        group_layer_shift_term,
         carried_memory,
     ) = lax.optimization_barrier(
         (
@@ -872,14 +907,23 @@
             token_mixing_ratios,
             fading_left_factor,
             fading_right_factor,
+            fading_baseline,
+            present_reward,
+            group_layer_scaling,
+            group_layer_shift_term,
             carried_memory,
         )
     )
     spread = spread_along(block, z)
-    pair = jnp.swapaxes(in_place(spread, z), 0, 1)
-    pair_x, pair_y = over_x(pair), over_y(pair)
-    a_xy, b_xy = over_y(pair_x[0]), over_x(pair_y[1])
-    extents = pair[0, :, 2 * group_rows + 1, : 2 * requests].reshape(2 * lines * requests)
+    _, one, two, three, far = spread
+    own_x, own_y = over_x(block), over_y(block)
+    own_xy = (over_y(own_x[0]), over_x(own_y[1]))
+    rest = jnp.stack([jnp.where(z == 0, far, one), two, jnp.where(z == 3, far, three)], axis=1)
+    rest_x, rest_y = over_x(rest), over_y(rest)
+    rest_xy = (over_y(rest_x[0]), over_x(rest_y[1]))
+    extents = in_order(
+        [part[2 * group_rows + 1, : 2 * requests] for part in (block[0],) + tuple(rest[0])], z
+    ).reshape(2 * lines * requests)
     extents = jnp.where(is_long, slot_rows, extents.astype(jnp.int32)).astype(jnp.int32)
 
     def chunk_order(whole):
@@ -907,38 +951,32 @@
     def both_cores(pieces):
         return in_order(pieces, z), in_order([flipped_core(piece) for piece in pieces], z)
 
-    pieces = columns_of([acceptance_transform, lookup_transform], pair)
-    value_pieces = columns_of([payload_transform], pair_x, pair_y)
-    gate_pieces = columns_of([gating_transform], value_pieces[2])
-    own, sibling = both_cores(pieces)
-    own_value, sibling_value = both_cores(value_pieces)
-    own_gate, sibling_gate = both_cores(gate_pieces)
+    kv_pieces = columns_of([lookup_transform, payload_transform], rest)
+    r_pieces = columns_of([acceptance_transform], kv_pieces[2])
+    gate_pieces = columns_of([gating_transform], r_pieces[2])
+    own_kv, sibling_kv = both_cores(after(tuple(kv_pieces), rest_x, rest_y))
 
     def mine_of(vector):
         return lax.dynamic_slice_in_dim(vector, z * width, width, 0)[None]
 
-    pair_mix, value0, gate0, low0 = mixes_of(kind, pair, ratios[0], left[0])
-    value1, gate1, low1, recept, keys = mix_and_project(
-        1, kind, pair_x, ratios[1], left[1], own, sibling, pair_mix
-    )
-    value2, gate2, low2, recept, keys = mix_and_project(
-        2, kind, pair_y, ratios[2], left[2], own, sibling, recept, keys
-    )
-    recept, keys, values, decay, gate3 = projected(
+    kv0, r0, gate0, low0 = mixes_of(kind, block, rest, ratios[0], left[0])
+    kv1, r1, gate1, low1 = mixes_of(kind, own_x, rest_x, ratios[1], left[1])
+    kv2, r2, gate2, low2 = mixes_of(kind, own_y, rest_y, ratios[2], left[2])
+    keys, values, decay, r3, gate3 = projected(
         kind,
-        (value0, value1, value2),
+        (kv0, kv1, kv2),
         (low0, low1, low2),
-        (recept, keys),
-        (a_xy, b_xy),
+        own_xy,
+        rest_xy,
         ratios[3],
         left[3],
-        own,
-        sibling,
-        own_value,
-        sibling_value,
+        own_kv,
+        sibling_kv,
         lax.dynamic_slice_in_dim(fading_right_factor, z * width, width, 1),
         mine_of(fading_baseline),
     )
+    own_r, sibling_r = both_cores(after(tuple(r_pieces), decay))
+    recept = plain_product(kind, (r0, r1, r2, r3), own_r, sibling_r)
     entered = lax.dynamic_slice_in_dim(carried_memory, z * heads, heads, 0)
     bonus = lax.dynamic_slice_in_dim(present_reward, z * heads, heads, 0).reshape(1, width)
     states, states_in = states_of(
@@ -960,15 +998,9 @@
         mine_of(group_layer_scaling),
         mine_of(group_layer_shift_term),
     )
-    live = lax.broadcasted_iota(jnp.int32, (rows // slot_rows, slot_rows), 1) < extents[:, None]
-    live = live.reshape(rows, 1).astype(f32)
+    own_gate, sibling_gate = both_cores(after(tuple(gate_pieces), states))
     kept0, sent0, kept1, sent1 = gated(
-        kind,
-        (gate0, gate1, gate2, gate3),
-        own_gate,
-        sibling_gate,
-        normed,
-        live,
+        kind, extents, (gate0, gate1, gate2, gate3), own_gate, sibling_gate, normed
     )
 
     states = states.reshape(lines, 2, requests, heads, span, span)
@@ -977,6 +1009,7 @@
     bundle = jnp.concatenate(
         [jnp.where(is_long, held, passed)[:, -1:], jnp.where(is_long, passed, held)], axis=1
     ).astype(bf16)
+    bundle = after(bundle, gate_pieces[2])
     arrived = in_order(
         dealt(lambda j: lax.dynamic_index_in_dim(bundle, j, 0, keepdims=False), z), z
     ).astype(f32)

time: 328 us -> 340 us (1.037)
  starting transfers between devices: 83.8 us -> 93 us
  waiting for transfers between devices: 105 us -> 111 us
  Pallas kernels: 86.3 us -> 80.9 us
    pallas_call x1 -> x3, Pallas kernels: 7.05 us -> 20.8 us  [mixes_of(): pl.pallas_call(mix_kernel, grid=(2,), out_shape=outs, in_specs=[in_smem()...]
    pallas_call x3 -> x2, Pallas kernels: 32.7 us -> 20.7 us  [the longest x1 13.8 us: projected(): pl.pallas_call(project_kernel, grid=(rows // TILE,), out_shape=[flat] * 3...]
    ppermute x3, waiting for transfers between devices: 16.3 us -> 5.29 us  [spread_along(): far = lax.ppermute(two, 'z', [(1, 0), (2, 3)])]
    ppermute x4 -> x6, waiting for transfers between devices: 3.42 us -> 13.7 us  [over_x(): return lax.ppermute(x, 'x', [(0, 1), (1, 0)])]
    ppermute x3, waiting for transfers between devices: 0.01 us -> 6.27 us  [spread_along(): one = lax.ppermute(piece, 'z', [(0, 1), (1, 2), (2, 3)])]
    ppermute x4 -> x6, waiting for transfers between devices: 1.81 us -> 7.64 us  [over_y(): return lax.ppermute(x, 'y', [(0, 1), (1, 0)])]
    squeeze x2 -> x6, local copies, waits for them, and re-layouts: 2.64 us -> 7.73 us  [the longest x2 3.38 us: on_core(): own_xy = (over_y(own_x[0]), over_x(own_y[1]))]
    ppermute x2, waiting for transfers between devices: 4.53 us -> 0.2 us  [on_core(): across = lax.ppermute(to_xy, ('y', 'x'), [(i, 3 - i) for i in range(4)])]
  transfers between devices with their start and end apart: 57 -> 61, of which waited for: 20 -> 17; matrix products, arithmetic and copies ran while one was open for 13% -> 13% of each run, Pallas kernels for 11% -> 22%
where the time goes in v4:
time: 340 us; the launch traced here: 338 us
  waiting for transfers between devices  111 us (33%)
  starting transfers between devices  93 us (27%)
  Pallas kernels  80.9 us (24%)
  local copies, waits for them, and re-layouts  34 us (10%)
  other arithmetic  17.7 us (5%)
    ppermute x21, waiting for transfers between devices, turned(): lax.ppermute(x, axis, [(i, (i + by) % length) for i in range(length)])  76 us
    ppermute x21, starting transfers between devices, turned(): lax.ppermute(x, axis, [(i, (i + by) % length) for i in range(length)])  48.6 us
    pallas_call x3, Pallas kernels, mixes_of(): pl.pallas_call(mix_kernel, grid=(2,), out_shape=outs, in_specs=[in_smem()...  20.8 us
    ppermute x3, starting transfers between devices, spread_along(): one = lax.ppermute(piece, 'z', [(0, 1), (1, 2), (2, 3)])  14.6 us
    pallas_call x1, Pallas kernels, projected(): pl.pallas_call(project_kernel, grid=(rows // TILE,), out_shape=[flat] * 3...  13.8 us
    ppermute x6, waiting for transfers between devices, over_x(): return lax.ppermute(x, 'x', [(0, 1), (1, 0)])  13.7 us
    pallas_call x1, Pallas kernels, sweep(): pl.pallas_call(sweep_kernel, out_shape=jax.ShapeDtypeStruct(r.shape, f32)...  11.9 us
    pallas_call x2, Pallas kernels, final_product(): pl.pallas_call(final_kernel, out_shape=[out] * 4, in_specs=[in_smem()] +...  9 us
  transfers between devices with their start and end apart: 61, of which 17 were waited for; matrix products, arithmetic and copies ran while one was open for 13% of the time, Pallas kernels for 22%

profile of v4, /device:TPU:0, one launch (start us, length us, event | category | flops | bytes accessed | tf_op | source)
XLA Modules:
  0.0 338.4 jit_solution(18342362673541760290)
XLA Ops:
  1.4 1.8 shard_map.184
  6.1 2.0 shard_map.185.own
  9.1 3.7 %collective-permute-start.1 = (bf16[2,272,512]{2,1,0:T(8,128)(2,1)}, bf16[2,272,512]{2,1,0:T(8,128)(2,1)S(1)}, u32[]{:S(2)}, u32[]{:S(2)}) collective-permute-start(bf16[2,272,512]{2,1,0:T(8,128)(2,1)} %shard_map.185.own), channel_id=1, source_target_pairs={{0,16},{8,24},{16,0},{24,8},{1,17},{9,25},{17,1},{25,9},{2,18},{10... | collective-permute-start | bytes 1671176 | tf_op jit(solution)/shard_map/ppermute | solution.py:788
  12.7 1.3 collective-permute-start.4
  14.0 1.6 collective-permute-start.5
  15.6 1.5 collective-permute-start.7
  23.4 1.6 dynamic-slice_select_fusion.s_ref
  26.3 1.3 dynamic_slice.149
  27.6 1.3 dynamic_slice.160
  28.9 1.4 dynamic_slice.161
  30.3 2.7 fusion
  34.9 3.5 %collective-permute-done.1 = bf16[2,272,512]{2,1,0:T(8,128)(2,1)S(1)} collective-permute-done((bf16[2,272,512]{2,1,0:T(8,128)(2,1)}, bf16[2,272,512]{2,1,0:T(8,128)(2,1)S(1)}, u32[]{:S(2)}, u32[]{:S(2)}) %collective-permute-start.1) | collective-permute-done | bytes 557088 | tf_op jit(solution)/shard_map/ppermute | solution.py:788
  38.4 2.5 collective-permute-start.3
  41.0 1.3 collective-permute-start.2
  42.3 1.7 slice_bitcast_fusion.3
  44.0 1.7 slice_bitcast_fusion.2
  45.7 1.4 broadcast_select_fusion.1
  47.0 6.3 %collective-permute-done.3 = bf16[2,272,512]{2,1,0:T(8,128)(2,1)S(1)} collective-permute-done((bf16[2,272,512]{2,1,0:T(8,128)(2,1)}, bf16[2,272,512]{2,1,0:T(8,128)(2,1)S(1)}, u32[]{:S(2)}, u32[]{:S(2)}) %collective-permute-start.3) | collective-permute-done | bytes 557088 | tf_op jit(solution)/shard_map/ppermute | solution.py:809
  53.3 3.9 %collective-permute-done.2 = bf16[2,272,512]{2,1,0:T(8,128)(2,1)S(1)} collective-permute-done((bf16[2,272,512]{2,1,0:T(8,128)(2,1)S(1)}, bf16[2,272,512]{2,1,0:T(8,128)(2,1)S(1)}, u32[]{:S(2)}, u32[]{:S(2)}) %collective-permute-start.2) | collective-permute-done | bytes 557088 | tf_op jit(solution)/shard_map/ppermute | solution.py:812
  57.5 1.6 collective-permute-start.6
  59.5 1.6 collective-permute-start.8
  61.1 1.6 pad_maximum_fusion.1.weight
  62.7 13.7 %collective-permute-start.14 = (bf16[2,512,256]{2,1,0:T(8,128)(2,1)S(1)}, bf16[2,512,256]{2,1,0:T(8,128)(2,1)}, u32[]{:S(2)}, u32[]{:S(2)}) collective-permute-start(bf16[2,512,256]{2,1,0:T(8,128)(2,1)S(1)} %copy-done.16), channel_id=1, source_target_pairs={{0,16},{8,24},{16,0},{24,8},{1,17},{9,25},{17,1},{25,9},{2,18},{10... | collective-permute-start | bytes 1572872 | tf_op jit(solution)/shard_map/ppermute | solution.py:788
  76.8 6.8 %shard_map.186 = (bf16[2,2,1024,512]{3,2,1,0:T(8,128)(2,1)}, bf16[2,1024,512]{2,1,0:T(8,128)(2,1)}, bf16[2,1024,512]{2,1,0:T(8,128)(2,1)}, f32[2,1024,128]{2,1,0:T(8,128)}) custom-call(s32[10]{0:T(128)} %stack.105.kind, bf16[2,272,512]{2,1,0:T(8,128)(2,1)} %shard_map.185.own, bf16[2,3,272,512]{3,2,1,0:T(8,128)(2,1)} %copy-done.4, ...), custom_call_target="tpu_custom_call" | custom-call | flops 8049999872 | bytes 21000000 | tf_op jit(solution)/shard_map/pallas_call | solution.py:384
  83.6 25.9 %collective-permute-done.14 = bf16[2,512,256]{2,1,0:T(8,128)(2,1)} collective-permute-done((bf16[2,512,256]{2,1,0:T(8,128)(2,1)S(1)}, bf16[2,512,256]{2,1,0:T(8,128)(2,1)}, u32[]{:S(2)}, u32[]{:S(2)}) %collective-permute-start.14) | collective-permute-done | bytes 524320 | tf_op jit(solution)/shard_map/ppermute | solution.py:788
  110.3 21.5 %collective-permute-done.20 = bf16[1,512,256]{2,1,0:T(8,128)(2,1)} collective-permute-done((bf16[1,512,256]{2,1,0:T(8,128)(2,1)S(1)}, bf16[1,512,256]{2,1,0:T(8,128)(2,1)}, u32[]{:S(2)}, u32[]{:S(2)}) %collective-permute-start.20) | collective-permute-done | bytes 262176 | tf_op jit(solution)/shard_map/ppermute | solution.py:788
  131.9 2.1 slice_bitcast_fusion.1
  135.9 1.2 slice_bitcast_fusion
  137.1 7.0 %shard_map.187 = (bf16[2,2,1024,512]{3,2,1,0:T(8,128)(2,1)}, bf16[2,1024,512]{2,1,0:T(8,128)(2,1)}, bf16[2,1024,512]{2,1,0:T(8,128)(2,1)}, f32[2,1024,128]{2,1,0:T(8,128)}) custom-call(s32[10]{0:T(128)} %stack.105.kind, bf16[2,272,512]{2,1,0:T(8,128)(2,1)} %collective-permute-done.5.own, bf16[2,3,272,512]{3,2,1,0:T(8,128)(2,1)} %collective-permute-done.6.rest, ...), custom_call_target="tpu_custom_call" | custom-call | flops 8049999872 | bytes 21000000 | tf_op jit(solution)/shard_map/pallas_call | solution.py:384
  144.1 7.0 %shard_map.188 = (bf16[2,2,1024,512]{3,2,1,0:T(8,128)(2,1)}, bf16[2,1024,512]{2,1,0:T(8,128)(2,1)}, bf16[2,1024,512]{2,1,0:T(8,128)(2,1)}, f32[2,1024,128]{2,1,0:T(8,128)}) custom-call(s32[10]{0:T(128)} %stack.105.kind, bf16[2,272,512]{2,1,0:T(8,128)(2,1)} %collective-permute-done.7.own, bf16[2,3,272,512]{3,2,1,0:T(8,128)(2,1)} %collective-permute-done.8.rest, ...), custom_call_target="tpu_custom_call" | custom-call | flops 8049999872 | bytes 21000000 | tf_op jit(solution)/shard_map/pallas_call | solution.py:384
  157.3 1.6 collective-permute-start.9
  158.9 1.2 collective-permute-start.10
  160.4 5.3 %collective-permute-done.9.own0 = bf16[272,512]{1,0:T(8,128)(2,1)S(1)} collective-permute-done((bf16[272,512]{1,0:T(8,128)(2,1)S(1)}, bf16[272,512]{1,0:T(8,128)(2,1)S(1)}, u32[]{:S(2)}, u32[]{:S(2)}) %collective-permute-start.9) | collective-permute-done | bytes 278560 | tf_op jit(solution)/shard_map/ppermute | solution.py:800
  165.7 2.5 collective-permute-start.29
  168.1 13.7 %collective-permute-done.10.own1 = bf16[272,512]{1,0:T(8,128)(2,1)S(1)} collective-permute-done((bf16[272,512]{1,0:T(8,128)(2,1)S(1)}, bf16[272,512]{1,0:T(8,128)(2,1)S(1)}, u32[]{:S(2)}, u32[]{:S(2)}) %collective-permute-start.10) | collective-permute-done | bytes 278560 | tf_op jit(solution)/shard_map/ppermute | solution.py:796
  181.9 2.9 collective-permute-start.22
  186.6 13.8 %shard_map.189 = (f32[1024,256]{1,0:T(8,128)}, f32[1024,256]{1,0:T(8,128)}, f32[1024,256]{1,0:T(8,128)}, bf16[2,1024,512]{2,1,0:T(8,128)(2,1)}, bf16[2,1024,512]{2,1,0:T(8,128)(2,1)}) custom-call(s32[10]{0:T(128)} %stack.105.kind, bf16[2,2,1024,512]{3,2,1,0:T(8,128)(2,1)} %get-tuple-element.80.mix0, bf16[2,2,1024,512]{3,2,1,0:T(8,128)(2,1)} %get-tuple-element.81.mix1, ...), custom_call_target="tpu_custom_call" | custom-call | flops 13799999488 | bytes 36000000 | tf_op jit(solution)/shard_map/pallas_call | solution.py:466
  200.3 5.7 %shard_map.190 = (f32[16,4,64,64]{3,2,1,0:T(8,128)}, bf16[16,64,256]{2,1,0:T(8,128)(2,1)}) custom-call(s32[16]{0:T(128)} %select_n.408.lengths, f32[1]{0:T(128)} %bitcast.62.carry, f32[1024,256]{1,0:T(8,128)} %get-tuple-element.106.k_ref, f32[1024,256]{1,0:T(8,128)} %get-tuple-element.107.v_ref, f32[1024,256]{1,0:T(8,128)} %get-tuple-element.108.w_ref, ...), custom_call_target="tpu_custom_call" | custom-call | flops 8049999872 | bytes 21000000 | tf_op jit(solution)/shard_map/pallas_call | solution.py:635
  212.7 6.9 %shard_map.191.r_ref = f32[1024,256]{1,0:T(8,128)} custom-call(s32[10]{0:T(128)} %stack.105.kind, bf16[2,1024,512]{2,1,0:T(8,128)(2,1)} %get-tuple-element.115.mix0, bf16[2,1024,512]{2,1,0:T(8,128)(2,1)} %get-tuple-element.116.mix1, bf16[2,1024,512]{2,1,0:T(8,128)(2,1)} %get-tuple-element.117.mix2, bf16[2,1024,512]{2,1,0:T(8,128)(2,1)} %get-tuple-element.118.mix3, ...), custom_call_target="tpu_custom_call" | custom-call | flops 6899999744 | bytes 18000000 | tf_op jit(solution)/shard_map/pallas_call | solution.py:500
  219.6 11.9 %shard_map.192.normed = f32[1024,256]{1,0:T(8,128)} custom-call(s32[16]{0:T(128)} %select_n.408.lengths, f32[1024,256]{1,0:T(8,128)} %shard_map.191.r_ref, f32[1024,256]{1,0:T(8,128)} %get-tuple-element.106.k_ref, f32[1024,256]{1,0:T(8,128)} %get-tuple-element.107.v_ref, f32[1024,256]{1,0:T(8,128)} %get-tuple-element.108.w_ref, ...), custom_call_target="tpu_custom_call" | custom-call | flops 13799999488 | bytes 36000000 | tf_op jit(solution)/shard_map/pallas_call | solution.py:721
  233.6 7.1 %shard_map.193 = (bf16[2,4,32,256]{3,2,1,0:T(8,128)(2,1)}, bf16[2,4,32,256]{3,2,1,0:T(8,128)(2,1)}, bf16[2,4,32,256]{3,2,1,0:T(8,128)(2,1)}, bf16[2,4,32,256]{3,2,1,0:T(8,128)(2,1)}) custom-call(s32[10]{0:T(128)} %stack.105.kind, s32[16]{0:T(128)} %select_n.408.lengths, bf16[2,1024,512]{2,1,0:T(8,128)(2,1)} %get-tuple-element.77.mix0, ...), custom_call_target="tpu_custom_call" | custom-call | flops 8049999872 | bytes 21000000 | tf_op jit(solution)/shard_map/pallas_call | solution.py:564
  242.4 2.1 collective-permute-start.35
  244.6 2.7 collective-permute-start.59
  247.5 1.3 collective-permute-start.38
  248.8 4.6 %collective-permute-start.37 = (bf16[512,256]{1,0:T(8,128)(2,1)S(1)}, bf16[512,256]{1,0:T(8,128)(2,1)S(1)}, u32[]{:S(2)}, u32[]{:S(2)}) collective-permute-start(bf16[512,256]{1,0:T(8,128)(2,1)S(1)} %bitcast.200), channel_id=1, source_target_pairs={{0,8},{8,16},{16,24},{1,9},{9,17},{17,25},{2,10},{10,18},{18,26},{... | collective-permute-start | bytes 786440 | tf_op jit(solution)/shard_map/ppermute | solution.py:809
  253.4 13.1 %collective-permute-done.35.h2 = bf16[512,256]{1,0:T(8,128)(2,1)S(1)} collective-permute-done((bf16[512,256]{1,0:T(8,128)(2,1)S(1)}, bf16[512,256]{1,0:T(8,128)(2,1)S(1)}, u32[]{:S(2)}, u32[]{:S(2)}) %collective-permute-start.35) | collective-permute-done | bytes 262176 | tf_op jit(solution)/shard_map/ppermute | solution.py:788
  266.6 1.3 collective-permute-start.36
  267.9 8.5 %collective-permute-done.59 = bf16[3,4,64,64]{3,2,1,0:T(8,128)(2,1)S(1)} collective-permute-done((bf16[3,4,64,64]{3,2,1,0:T(8,128)(2,1)S(1)}, bf16[3,4,64,64]{3,2,1,0:T(8,128)(2,1)S(1)}, u32[]{:S(2)}, u32[]{:S(2)}) %collective-permute-start.59) | collective-permute-done | bytes 98336 | tf_op jit(solution)/shard_map/ppermute | solution.py:788
  276.4 1.3 collective-permute-start.60
  277.7 1.3 collective-permute-start.50
  279.0 7.6 %collective-permute-start.49 = (bf16[512,256]{1,0:T(8,128)(2,1)S(1)}, bf16[512,256]{1,0:T(8,128)(2,1)S(1)}, u32[]{:S(2)}, u32[]{:S(2)}) collective-permute-start(bf16[512,256]{1,0:T(8,128)(2,1)S(1)} %bitcast.196), channel_id=1, source_target_pairs={{0,8},{8,16},{16,24},{1,9},{9,17},{17,25},{2,10},{10,18},{18,26},{... | collective-permute-start | bytes 786440 | tf_op jit(solution)/shard_map/ppermute | solution.py:809
  287.7 1.5 collective-permute-start.48
  290.1 4.5 %shard_map.194 = (bf16[4,32,1024]{2,1,0:T(8,128)(2,1)}, bf16[4,32,1024]{2,1,0:T(8,128)(2,1)}, bf16[4,32,1024]{2,1,0:T(8,128)(2,1)}, bf16[4,32,1024]{2,1,0:T(8,128)(2,1)}) custom-call(s32[4]{0:T(128)} %pad_add_fusion.1.block_of, bf16[512,256]{1,0:T(8,128)(2,1)} %bitcast.201, bf16[512,256]{1,0:T(8,128)(2,1)} %get-tuple-element.185.h1, ...), custom_call_target="tpu_custom_call" | custom-call | flops 5175000064 | bytes 13500000 | tf_op jit(solution)/shard_map/pallas_call | solution.py:750
  294.6 1.9 collective-permute-start.42
  298.2 1.4 collective-permute-done.48
  300.4 4.5 %shard_map.195 = (bf16[4,32,1024]{2,1,0:T(8,128)(2,1)}, bf16[4,32,1024]{2,1,0:T(8,128)(2,1)}, bf16[4,32,1024]{2,1,0:T(8,128)(2,1)}, bf16[4,32,1024]{2,1,0:T(8,128)(2,1)}) custom-call(s32[4]{0:T(128)} %pad_add_fusion.1.block_of, bf16[512,256]{1,0:T(8,128)(2,1)} %bitcast.197, bf16[512,256]{1,0:T(8,128)(2,1)} %get-tuple-element.179.h1, ...), custom_call_target="tpu_custom_call" | custom-call | flops 5175000064 | bytes 13500000 | tf_op jit(solution)/shard_map/pallas_call | solution.py:750
  304.9 1.8 collective-permute-start.53
  307.3 2.3 collective-permute-done.41
  311.3 3.8 %collective-permute-start.43 = (bf16[32,1024]{1,0:T(8,128)(2,1)S(1)}, bf16[32,1024]{1,0:T(8,128)(2,1)S(1)}, u32[]{:S(2)}, u32[]{:S(2)}) collective-permute-start(bf16[32,1024]{1,0:T(8,128)(2,1)S(1)} %get-tuple-element.182), channel_id=1, source_target_pairs={{0,8},{8,16},{16,24},{24,0},{1,9},{9,17},{17,25},{25,1},{2,10},{10... | collective-permute-start | bytes 196616 | tf_op jit(solution)/shard_map/ppermute | solution.py:788
  315.3 7.2 %collective-permute-start.44 = (bf16[32,1024]{1,0:T(8,128)(2,1)S(1)}, bf16[32,1024]{1,0:T(8,128)(2,1)S(1)}, u32[]{:S(2)}, u32[]{:S(2)}) collective-permute-start(bf16[32,1024]{1,0:T(8,128)(2,1)S(1)} %get-tuple-element.181), channel_id=1, source_target_pairs={{0,16},{8,24},{16,0},{24,8},{1,17},{9,25},{17,1},{25,9},{2,18},{10... | collective-permute-start | bytes 196616 | tf_op jit(solution)/shard_map/ppermute | solution.py:788
  322.6 3.2 collective-permute-start.45
  327.6 2.9 collective-permute-start.55
  334.4 1.4 collective-permute-done.55.refs_6_
  336.5 1.9 shard_map.196
  (251 shorter events, 49.7 us)
Async XLA Ops:
  3.1 2.2 collective-permute-start
  9.1 29.4 %collective-permute-start.1 = (bf16[2,272,512]{2,1,0:T(8,128)(2,1)}, bf16[2,272,512]{2,1,0:T(8,128)(2,1)S(1)}, u32[]{:S(2)}, u32[]{:S(2)}) collective-permute-start(bf16[2,272,512]{2,1,0:T(8,128)(2,1)} %shard_map.185.own), channel_id=1, source_target_pairs={{0,16},{8,24},{16,0},{24,8},{1,17},{9,25},{17,1},{25,9},{2,18},{10... | collective-permute-start | bytes 1671176 | tf_op jit(solution)/shard_map/ppermute | solution.py:788
  12.7 34.3 %collective-permute-start.4 = (bf16[2,272,512]{2,1,0:T(8,128)(2,1)}, bf16[2,272,512]{2,1,0:T(8,128)(2,1)S(1)}, u32[]{:S(2)}, u32[]{:S(2)}) collective-permute-start(bf16[2,272,512]{2,1,0:T(8,128)(2,1)} %shard_map.185.own), channel_id=1, source_target_pairs={{8,0},{16,8},{24,16},{9,1},{17,9},{25,17},{10,2},{18,10},{26,18},{... | collective-permute-start | bytes 1671176 | tf_op jit(solution)/shard_map/ppermute | solution.py:810
  14.0 26.9 %collective-permute-start.5 = (bf16[2,272,512]{2,1,0:T(8,128)(2,1)}, bf16[2,272,512]{2,1,0:T(8,128)(2,1)}, u32[]{:S(2)}, u32[]{:S(2)}) collective-permute-start(bf16[2,272,512]{2,1,0:T(8,128)(2,1)} %shard_map.185.own), channel_id=1, source_target_pairs={{0,1},{1,0},{2,3},{3,2},{4,5},{5,4},{6,7},{7,6},{8,9},{9,8},{10,11... | collective-permute-start | bytes 1671176 | tf_op jit(solution)/shard_map/ppermute | solution.py:796
  15.6 28.4 %collective-permute-start.7 = (bf16[2,272,512]{2,1,0:T(8,128)(2,1)}, bf16[2,272,512]{2,1,0:T(8,128)(2,1)}, u32[]{:S(2)}, u32[]{:S(2)}) collective-permute-start(bf16[2,272,512]{2,1,0:T(8,128)(2,1)} %shard_map.185.own), channel_id=1, source_target_pairs={{0,2},{2,0},{1,3},{3,1},{4,6},{6,4},{5,7},{7,5},{8,10},{10,8},{9,1... | collective-permute-start | bytes 1671176 | tf_op jit(solution)/shard_map/ppermute | solution.py:800
  30.3 15.4 %collective-permute-start.39 = (bf16[1024,512]{1,0:T(8,128)(2,1)S(1)}, bf16[1024,512]{1,0:T(8,128)(2,1)}, u32[]{:S(2)}, u32[]{:S(2)}) collective-permute-start(bf16[1024,512]{1,0:T(8,128)(2,1)S(1)} %copy-done.5), channel_id=1, source_target_pairs={{0,4},{4,0},{1,5},{5,1},{2,6},{6,2},{3,7},{7,3},{8,12},{12,8},{9,1... | collective-permute-start | bytes 3145736 | tf_op jit(solution)/shard_map/ppermute | solution.py:792
  38.4 14.9 %collective-permute-start.3 = (bf16[2,272,512]{2,1,0:T(8,128)(2,1)}, bf16[2,272,512]{2,1,0:T(8,128)(2,1)S(1)}, u32[]{:S(2)}, u32[]{:S(2)}) collective-permute-start(bf16[2,272,512]{2,1,0:T(8,128)(2,1)} %shard_map.185.own), channel_id=1, source_target_pairs={{0,8},{8,16},{16,24},{1,9},{9,17},{17,25},{2,10},{10,18},{18,26},{... | collective-permute-start | bytes 1671176 | tf_op jit(solution)/shard_map/ppermute | solution.py:809
  41.0 16.2 %collective-permute-start.2 = (bf16[2,272,512]{2,1,0:T(8,128)(2,1)S(1)}, bf16[2,272,512]{2,1,0:T(8,128)(2,1)S(1)}, u32[]{:S(2)}, u32[]{:S(2)}) collective-permute-start(bf16[2,272,512]{2,1,0:T(8,128)(2,1)S(1)} %collective-permute-done.1), channel_id=1, source_target_pairs={{8,0},{16,24},{9,1},{17,25},{10,2},{18,26},{11,3},{19,27},{12,4},{... | collective-permute-start | bytes 1671176 | tf_op jit(solution)/shard_map/ppermute | solution.py:812
  57.5 74.4 %collective-permute-start.6 = (bf16[2,3,272,512]{3,2,1,0:T(8,128)(2,1)S(1)}, bf16[2,3,272,512]{3,2,1,0:T(8,128)(2,1)}, u32[]{:S(2)}, u32[]{:S(2)}) collective-permute-start(bf16[2,3,272,512]{3,2,1,0:T(8,128)(2,1)S(1)} %pad_maximum_fusion.2.rest), channel_id=1, source_target_pairs={{0,1},{1,0},{2,3},{3,2},{4,5},{5,4},{6,7},{7,6},{8,9},{9,8},{10,11... | collective-permute-start | bytes 5013512 | tf_op jit(solution)/shard_map/ppermute | solution.py:796
  59.5 75.0 %collective-permute-start.8 = (bf16[2,3,272,512]{3,2,1,0:T(8,128)(2,1)S(1)}, bf16[2,3,272,512]{3,2,1,0:T(8,128)(2,1)}, u32[]{:S(2)}, u32[]{:S(2)}) collective-permute-start(bf16[2,3,272,512]{3,2,1,0:T(8,128)(2,1)S(1)} %pad_maximum_fusion.2.rest), channel_id=1, source_target_pairs={{0,2},{2,0},{1,3},{3,1},{4,6},{6,4},{5,7},{7,5},{8,10},{10,8},{9,1... | collective-permute-start | bytes 5013512 | tf_op jit(solution)/shard_map/ppermute | solution.py:800
  62.7 46.8 %copy-start.21 = (bf16[1,512,256]{2,1,0:T(8,128)(2,1)S(1)}, bf16[1,512,256]{2,1,0:T(8,128)(2,1)}, u32[]{:S(2)}) copy-start(bf16[1,512,256]{2,1,0:T(8,128)(2,1)} %get-tuple-element.101) | copy-start | bytes 786436
  62.7 71.8 %collective-permute-start.13 = (bf16[2,512,256]{2,1,0:T(8,128)(2,1)}, bf16[2,512,256]{2,1,0:T(8,128)(2,1)}, u32[]{:S(2)}, u32[]{:S(2)}) collective-permute-start(bf16[2,512,256]{2,1,0:T(8,128)(2,1)} %get-tuple-element.89), channel_id=1, source_target_pairs={{0,8},{8,16},{16,24},{24,0},{1,9},{9,17},{17,25},{25,1},{2,10},{10... | collective-permute-start | bytes 1572872 | tf_op jit(solution)/shard_map/ppermute | solution.py:788
  62.7 46.8 %collective-permute-start.14 = (bf16[2,512,256]{2,1,0:T(8,128)(2,1)S(1)}, bf16[2,512,256]{2,1,0:T(8,128)(2,1)}, u32[]{:S(2)}, u32[]{:S(2)}) collective-permute-start(bf16[2,512,256]{2,1,0:T(8,128)(2,1)S(1)} %copy-done.16), channel_id=1, source_target_pairs={{0,16},{8,24},{16,0},{24,8},{1,17},{9,25},{17,1},{25,9},{2,18},{10... | collective-permute-start | bytes 1572872 | tf_op jit(solution)/shard_map/ppermute | solution.py:788
  76.4 58.1 %collective-permute-start.15 = (bf16[2,512,256]{2,1,0:T(8,128)(2,1)}, bf16[2,512,256]{2,1,0:T(8,128)(2,1)}, u32[]{:S(2)}, u32[]{:S(2)}) collective-permute-start(bf16[2,512,256]{2,1,0:T(8,128)(2,1)} %get-tuple-element.91), channel_id=1, source_target_pairs={{0,24},{8,0},{16,8},{24,16},{1,25},{9,1},{17,9},{25,17},{2,26},{10... | collective-permute-start | bytes 1572872 | tf_op jit(solution)/shard_map/ppermute | solution.py:788
  109.5 22.4 %collective-permute-start.20 = (bf16[1,512,256]{2,1,0:T(8,128)(2,1)S(1)}, bf16[1,512,256]{2,1,0:T(8,128)(2,1)}, u32[]{:S(2)}, u32[]{:S(2)}) collective-permute-start(bf16[1,512,256]{2,1,0:T(8,128)(2,1)S(1)} %copy-done.21), channel_id=1, source_target_pairs={{0,16},{8,24},{16,0},{24,8},{1,17},{9,25},{17,1},{25,9},{2,18},{10... | collective-permute-start | bytes 786440 | tf_op jit(solution)/shard_map/ppermute | solution.py:788
  134.0 47.9 %collective-permute-start.11 = (bf16[3,272,512]{2,1,0:T(8,128)(2,1)}, bf16[3,272,512]{2,1,0:T(8,128)(2,1)}, u32[]{:S(2)}, u32[]{:S(2)}) collective-permute-start(bf16[3,272,512]{2,1,0:T(8,128)(2,1)} %slice_bitcast_fusion.1), channel_id=1, source_target_pairs={{0,2},{2,0},{1,3},{3,1},{4,6},{6,4},{5,7},{7,5},{8,10},{10,8},{9,1... | collective-permute-start | bytes 2506760 | tf_op jit(solution)/shard_map/ppermute | solution.py:800
  134.5 19.9 %collective-permute-start.16 = (bf16[2,512,256]{2,1,0:T(8,128)(2,1)S(1)}, bf16[2,512,256]{2,1,0:T(8,128)(2,1)S(1)}, u32[]{:S(2)}, u32[]{:S(2)}) collective-permute-start(bf16[2,512,256]{2,1,0:T(8,128)(2,1)S(1)} %get-tuple-element.92), channel_id=1, source_target_pairs={{0,4},{4,0},{1,5},{5,1},{2,6},{6,2},{3,7},{7,3},{8,12},{12,8},{9,1... | collective-permute-start | bytes 1572872 | tf_op jit(solution)/shard_map/ppermute | solution.py:792
  134.8 22.4 %collective-permute-start.17 = (bf16[2,512,256]{2,1,0:T(8,128)(2,1)}, bf16[2,512,256]{2,1,0:T(8,128)(2,1)S(1)}, u32[]{:S(2)}, u32[]{:S(2)}) collective-permute-start(bf16[2,512,256]{2,1,0:T(8,128)(2,1)} %collective-permute-done.13), channel_id=1, source_target_pairs={{0,4},{4,0},{1,5},{5,1},{2,6},{6,2},{3,7},{7,3},{8,12},{12,8},{9,1... | collective-permute-start | bytes 1572872 | tf_op jit(solution)/shard_map/ppermute | solution.py:792
  135.4 23.5 %collective-permute-start.18 = (bf16[2,512,256]{2,1,0:T(8,128)(2,1)}, bf16[2,512,256]{2,1,0:T(8,128)(2,1)S(1)}, u32[]{:S(2)}, u32[]{:S(2)}) collective-permute-start(bf16[2,512,256]{2,1,0:T(8,128)(2,1)} %collective-permute-done.14), channel_id=1, source_target_pairs={{0,4},{4,0},{1,5},{5,1},{2,6},{6,2},{3,7},{7,3},{8,12},{12,8},{9,1... | collective-permute-start | bytes 1572872 | tf_op jit(solution)/shard_map/ppermute | solution.py:792
  135.5 24.7 %collective-permute-start.19 = (bf16[2,512,256]{2,1,0:T(8,128)(2,1)}, bf16[2,512,256]{2,1,0:T(8,128)(2,1)S(1)}, u32[]{:S(2)}, u32[]{:S(2)}) collective-permute-start(bf16[2,512,256]{2,1,0:T(8,128)(2,1)} %collective-permute-done.15), channel_id=1, source_target_pairs={{0,4},{4,0},{1,5},{5,1},{2,6},{6,2},{3,7},{7,3},{8,12},{12,8},{9,1... | collective-permute-start | bytes 1572872 | tf_op jit(solution)/shard_map/ppermute | solution.py:792
  155.3 29.6 %collective-permute-start.12 = (bf16[3,272,512]{2,1,0:T(8,128)(2,1)S(1)}, bf16[3,272,512]{2,1,0:T(8,128)(2,1)S(1)}, u32[]{:S(2)}, u32[]{:S(2)}) collective-permute-start(bf16[3,272,512]{2,1,0:T(8,128)(2,1)S(1)} %slice_bitcast_fusion), channel_id=1, source_target_pairs={{0,1},{1,0},{2,3},{3,2},{4,5},{5,4},{6,7},{7,6},{8,9},{9,8},{10,11... | collective-permute-start | bytes 2506760 | tf_op jit(solution)/shard_map/ppermute | solution.py:796
  157.3 8.4 %collective-permute-start.9 = (bf16[272,512]{1,0:T(8,128)(2,1)S(1)}, bf16[272,512]{1,0:T(8,128)(2,1)S(1)}, u32[]{:S(2)}, u32[]{:S(2)}) collective-permute-start(bf16[272,512]{1,0:T(8,128)(2,1)S(1)} %copy-done.18), channel_id=1, source_target_pairs={{0,2},{2,0},{1,3},{3,1},{4,6},{6,4},{5,7},{7,5},{8,10},{10,8},{9,1... | collective-permute-start | bytes 835592 | tf_op jit(solution)/shard_map/ppermute | solution.py:800
  158.9 22.9 %collective-permute-start.10 = (bf16[272,512]{1,0:T(8,128)(2,1)S(1)}, bf16[272,512]{1,0:T(8,128)(2,1)S(1)}, u32[]{:S(2)}, u32[]{:S(2)}) collective-permute-start(bf16[272,512]{1,0:T(8,128)(2,1)S(1)} %copy-done.17), channel_id=1, source_target_pairs={{0,1},{1,0},{2,3},{3,2},{4,5},{5,4},{6,7},{7,6},{8,9},{9,8},{10,11... | collective-permute-start | bytes 835592 | tf_op jit(solution)/shard_map/ppermute | solution.py:796
  160.2 46.8 %collective-permute-start.28 = (bf16[1,512,256]{2,1,0:T(8,128)(2,1)S(1)}, bf16[1,512,256]{2,1,0:T(8,128)(2,1)S(1)}, u32[]{:S(2)}, u32[]{:S(2)}) collective-permute-start(bf16[1,512,256]{2,1,0:T(8,128)(2,1)S(1)} %copy-done.20), channel_id=1, source_target_pairs={{0,8},{8,16},{16,24},{24,0},{1,9},{9,17},{17,25},{25,1},{2,10},{10... | collective-permute-start | bytes 786440 | tf_op jit(solution)/shard_map/ppermute | solution.py:788
  165.7 41.3 %collective-permute-start.29 = (bf16[1,512,256]{2,1,0:T(8,128)(2,1)S(1)}, bf16[1,512,256]{2,1,0:T(8,128)(2,1)S(1)}, u32[]{:S(2)}, u32[]{:S(2)}) collective-permute-start(bf16[1,512,256]{2,1,0:T(8,128)(2,1)S(1)} %copy-done.19), channel_id=1, source_target_pairs={{0,24},{8,0},{16,8},{24,16},{1,25},{9,1},{17,9},{25,17},{2,26},{10... | collective-permute-start | bytes 786440 | tf_op jit(solution)/shard_map/ppermute | solution.py:788
  181.8 24.3 %collective-permute-start.21 = (bf16[1,512,256]{2,1,0:T(8,128)(2,1)}, bf16[1,512,256]{2,1,0:T(8,128)(2,1)S(1)}, u32[]{:S(2)}, u32[]{:S(2)}) collective-permute-start(bf16[1,512,256]{2,1,0:T(8,128)(2,1)} %get-tuple-element.103), channel_id=1, source_target_pairs={{0,8},{8,16},{16,24},{24,0},{1,9},{9,17},{17,25},{25,1},{2,10},{10... | collective-permute-start | bytes 786440 | tf_op jit(solution)/shard_map/ppermute | solution.py:788
  181.9 24.2 %collective-permute-start.22 = (bf16[1,512,256]{2,1,0:T(8,128)(2,1)}, bf16[1,512,256]{2,1,0:T(8,128)(2,1)S(1)}, u32[]{:S(2)}, u32[]{:S(2)}) collective-permute-start(bf16[1,512,256]{2,1,0:T(8,128)(2,1)} %get-tuple-element.104), channel_id=1, source_target_pairs={{0,16},{8,24},{16,0},{24,8},{1,17},{9,25},{17,1},{25,9},{2,18},{10... | collective-permute-start | bytes 786440 | tf_op jit(solution)/shard_map/ppermute | solution.py:788
  185.7 20.4 %collective-permute-start.23 = (bf16[1,512,256]{2,1,0:T(8,128)(2,1)}, bf16[1,512,256]{2,1,0:T(8,128)(2,1)S(1)}, u32[]{:S(2)}, u32[]{:S(2)}) collective-permute-start(bf16[1,512,256]{2,1,0:T(8,128)(2,1)} %get-tuple-element.105), channel_id=1, source_target_pairs={{0,24},{8,0},{16,8},{24,16},{1,25},{9,1},{17,9},{25,17},{2,26},{10... | collective-permute-start | bytes 786440 | tf_op jit(solution)/shard_map/ppermute | solution.py:788
  206.1 25.3 %collective-permute-start.24 = (bf16[1,512,256]{2,1,0:T(8,128)(2,1)S(1)}, bf16[1,512,256]{2,1,0:T(8,128)(2,1)S(1)}, u32[]{:S(2)}, u32[]{:S(2)}) collective-permute-start(bf16[1,512,256]{2,1,0:T(8,128)(2,1)S(1)} %get-tuple-element.111), channel_id=1, source_target_pairs={{0,4},{4,0},{1,5},{5,1},{2,6},{6,2},{3,7},{7,3},{8,12},{12,8},{9,1... | collective-permute-start | bytes 786440 | tf_op jit(solution)/shard_map/ppermute | solution.py:792
  206.3 25.3 %collective-permute-start.25 = (bf16[1,512,256]{2,1,0:T(8,128)(2,1)S(1)}, bf16[1,512,256]{2,1,0:T(8,128)(2,1)}, u32[]{:S(2)}, u32[]{:S(2)}) collective-permute-start(bf16[1,512,256]{2,1,0:T(8,128)(2,1)S(1)} %collective-permute-done.21), channel_id=1, source_target_pairs={{0,4},{4,0},{1,5},{5,1},{2,6},{6,2},{3,7},{7,3},{8,12},{12,8},{9,1... | collective-permute-start | bytes 786440 | tf_op jit(solution)/shard_map/ppermute | solution.py:792
  206.9 25.6 %collective-permute-start.26 = (bf16[1,512,256]{2,1,0:T(8,128)(2,1)S(1)}, bf16[1,512,256]{2,1,0:T(8,128)(2,1)S(1)}, u32[]{:S(2)}, u32[]{:S(2)}) collective-permute-start(bf16[1,512,256]{2,1,0:T(8,128)(2,1)S(1)} %collective-permute-done.22), channel_id=1, source_target_pairs={{0,4},{4,0},{1,5},{5,1},{2,6},{6,2},{3,7},{7,3},{8,12},{12,8},{9,1... | collective-permute-start | bytes 786440 | tf_op jit(solution)/shard_map/ppermute | solution.py:792
  207.0 2.1 collective-permute-start.30
  207.7 2.1 collective-permute-start.31
  209.2 1.9 collective-permute-start.32
  209.8 1.7 collective-permute-start.33
  211.1 21.5 %collective-permute-start.27 = (bf16[1,512,256]{2,1,0:T(8,128)(2,1)S(1)}, bf16[1,512,256]{2,1,0:T(8,128)(2,1)S(1)}, u32[]{:S(2)}, u32[]{:S(2)}) collective-permute-start(bf16[1,512,256]{2,1,0:T(8,128)(2,1)S(1)} %collective-permute-done.23), channel_id=1, source_target_pairs={{0,4},{4,0},{1,5},{5,1},{2,6},{6,2},{3,7},{7,3},{8,12},{12,8},{9,1... | collective-permute-start | bytes 786440 | tf_op jit(solution)/shard_map/ppermute | solution.py:792
  211.5 29.8 %collective-permute-start.57 = (bf16[4,2,4,64,64]{4,3,2,1,0:T(8,128)(2,1)S(1)}, bf16[4,2,4,64,64]{4,3,2,1,0:T(8,128)(2,1)S(1)}, u32[]{:S(2)}, u32[]{:S(2)}) collective-permute-start(bf16[4,2,4,64,64]{4,3,2,1,0:T(8,128)(2,1)S(1)} %dynamic-slice_bitcast_fusion), channel_id=1, source_target_pairs={{0,4},{4,0},{1,5},{5,1},{2,6},{6,2},{3,7},{7,3},{8,12},{12,8},{9,1... | collective-permute-start | bytes 786440 | tf_op jit(solution)/shard_map/ppermute | solution.py:792
  240.7 1.6 collective-permute-start.34
  241.1 7.7 %collective-permute-start.46 = (bf16[2,4,32,256]{3,2,1,0:T(8,128)(2,1)}, bf16[2,4,32,256]{3,2,1,0:T(8,128)(2,1)S(1)}, u32[]{:S(2)}, u32[]{:S(2)}) collective-permute-start(bf16[2,4,32,256]{3,2,1,0:T(8,128)(2,1)} %get-tuple-element.138), channel_id=1, source_target_pairs={{0,4},{4,0},{1,5},{5,1},{2,6},{6,2},{3,7},{7,3},{8,12},{12,8},{9,1... | collective-permute-start | bytes 393224 | tf_op jit(solution)/shard_map/ppermute | solution.py:792
  242.4 47.7 %copy-start.24 = (bf16[4,4,32,256]{3,2,1,0:T(8,128)(2,1)}, bf16[4,4,32,256]{3,2,1,0:T(8,128)(2,1)S(1)}, u32[]{:S(2)}) copy-start(bf16[4,4,32,256]{3,2,1,0:T(8,128)(2,1)S(1)} %pad_maximum_fusion.4) | copy-start | bytes 786436
  242.4 24.2 %collective-permute-start.35 = (bf16[512,256]{1,0:T(8,128)(2,1)S(1)}, bf16[512,256]{1,0:T(8,128)(2,1)S(1)}, u32[]{:S(2)}, u32[]{:S(2)}) collective-permute-start(bf16[512,256]{1,0:T(8,128)(2,1)S(1)} %bitcast.198), channel_id=1, source_target_pairs={{0,16},{8,24},{16,0},{24,8},{1,17},{9,25},{17,1},{25,9},{2,18},{10... | collective-permute-start | bytes 786440 | tf_op jit(solution)/shard_map/ppermute | solution.py:788
  244.5 22.0 %collective-permute-start.58 = (bf16[3,4,64,64]{3,2,1,0:T(8,128)(2,1)S(1)}, bf16[3,4,64,64]{3,2,1,0:T(8,128)(2,1)S(1)}, u32[]{:S(2)}, u32[]{:S(2)}) collective-permute-start(bf16[3,4,64,64]{3,2,1,0:T(8,128)(2,1)S(1)} %get-tuple-element.171), channel_id=1, source_target_pairs={{0,8},{8,16},{16,24},{24,0},{1,9},{9,17},{17,25},{25,1},{2,10},{10... | collective-permute-start | bytes 294920 | tf_op jit(solution)/shard_map/ppermute | solution.py:788
  244.6 31.8 %collective-permute-start.59 = (bf16[3,4,64,64]{3,2,1,0:T(8,128)(2,1)S(1)}, bf16[3,4,64,64]{3,2,1,0:T(8,128)(2,1)S(1)}, u32[]{:S(2)}, u32[]{:S(2)}) collective-permute-start(bf16[3,4,64,64]{3,2,1,0:T(8,128)(2,1)S(1)} %get-tuple-element.170), channel_id=1, source_target_pairs={{0,16},{8,24},{16,0},{24,8},{1,17},{9,25},{17,1},{25,9},{2,18},{10... | collective-permute-start | bytes 294920 | tf_op jit(solution)/shard_map/ppermute | solution.py:788
  247.5 30.2 %collective-permute-start.38 = (bf16[512,256]{1,0:T(8,128)(2,1)S(1)}, bf16[512,256]{1,0:T(8,128)(2,1)S(1)}, u32[]{:S(2)}, u32[]{:S(2)}) collective-permute-start(bf16[512,256]{1,0:T(8,128)(2,1)S(1)} %bitcast.199), channel_id=1, source_target_pairs={{8,0},{16,8},{24,16},{9,1},{17,9},{25,17},{10,2},{18,10},{26,18},{... | collective-permute-start | bytes 786440 | tf_op jit(solution)/shard_map/ppermute | solution.py:810
  248.8 30.2 %collective-permute-start.37 = (bf16[512,256]{1,0:T(8,128)(2,1)S(1)}, bf16[512,256]{1,0:T(8,128)(2,1)S(1)}, u32[]{:S(2)}, u32[]{:S(2)}) collective-permute-start(bf16[512,256]{1,0:T(8,128)(2,1)S(1)} %bitcast.200), channel_id=1, source_target_pairs={{0,8},{8,16},{16,24},{1,9},{9,17},{17,25},{2,10},{10,18},{18,26},{... | collective-permute-start | bytes 786440 | tf_op jit(solution)/shard_map/ppermute | solution.py:809
  253.4 41.2 %copy-start.23 = (bf16[4,4,32,256]{3,2,1,0:T(8,128)(2,1)}, bf16[4,4,32,256]{3,2,1,0:T(8,128)(2,1)S(1)}, u32[]{:S(2)}) copy-start(bf16[4,4,32,256]{3,2,1,0:T(8,128)(2,1)S(1)} %pad_maximum_fusion.5) | copy-start | bytes 786436
  266.6 21.2 %collective-permute-start.47 = (bf16[512,256]{1,0:T(8,128)(2,1)S(1)}, bf16[512,256]{1,0:T(8,128)(2,1)S(1)}, u32[]{:S(2)}, u32[]{:S(2)}) collective-permute-start(bf16[512,256]{1,0:T(8,128)(2,1)S(1)} %bitcast.194), channel_id=1, source_target_pairs={{0,16},{8,24},{16,0},{24,8},{1,17},{9,25},{17,1},{25,9},{2,18},{10... | collective-permute-start | bytes 786440 | tf_op jit(solution)/shard_map/ppermute | solution.py:788
  266.6 22.7 %collective-permute-start.36 = (bf16[512,256]{1,0:T(8,128)(2,1)S(1)}, bf16[512,256]{1,0:T(8,128)(2,1)S(1)}, u32[]{:S(2)}, u32[]{:S(2)}) collective-permute-start(bf16[512,256]{1,0:T(8,128)(2,1)S(1)} %collective-permute-done.35.h2), channel_id=1, source_target_pairs={{8,0},{16,24},{9,1},{17,25},{10,2},{18,26},{11,3},{19,27},{12,4},{... | collective-permute-start | bytes 786440 | tf_op jit(solution)/shard_map/ppermute | solution.py:812
  276.4 51.1 %collective-permute-start.60 = (bf16[3,4,64,64]{3,2,1,0:T(8,128)(2,1)S(1)}, bf16[3,4,64,64]{3,2,1,0:T(8,128)(2,1)S(1)}, u32[]{:S(2)}, u32[]{:S(2)}) collective-permute-start(bf16[3,4,64,64]{3,2,1,0:T(8,128)(2,1)S(1)} %get-tuple-element.169), channel_id=1, source_target_pairs={{0,24},{8,0},{16,8},{24,16},{1,25},{9,1},{17,9},{25,17},{2,26},{10... | collective-permute-start | bytes 294920 | tf_op jit(solution)/shard_map/ppermute | solution.py:788
  277.7 18.8 %collective-permute-start.50 = (bf16[512,256]{1,0:T(8,128)(2,1)S(1)}, bf16[512,256]{1,0:T(8,128)(2,1)S(1)}, u32[]{:S(2)}, u32[]{:S(2)}) collective-permute-start(bf16[512,256]{1,0:T(8,128)(2,1)S(1)} %bitcast.195), channel_id=1, source_target_pairs={{8,0},{16,8},{24,16},{9,1},{17,9},{25,17},{10,2},{18,10},{26,18},{... | collective-permute-start | bytes 786440 | tf_op jit(solution)/shard_map/ppermute | solution.py:810
  279.0 18.0 %collective-permute-start.49 = (bf16[512,256]{1,0:T(8,128)(2,1)S(1)}, bf16[512,256]{1,0:T(8,128)(2,1)S(1)}, u32[]{:S(2)}, u32[]{:S(2)}) collective-permute-start(bf16[512,256]{1,0:T(8,128)(2,1)S(1)} %bitcast.196), channel_id=1, source_target_pairs={{0,8},{8,16},{16,24},{1,9},{9,17},{17,25},{2,10},{10,18},{18,26},{... | collective-permute-start | bytes 786440 | tf_op jit(solution)/shard_map/ppermute | solution.py:809
  287.7 11.9 %collective-permute-start.48 = (bf16[512,256]{1,0:T(8,128)(2,1)S(1)}, bf16[512,256]{1,0:T(8,128)(2,1)S(1)}, u32[]{:S(2)}, u32[]{:S(2)}) collective-permute-start(bf16[512,256]{1,0:T(8,128)(2,1)S(1)} %collective-permute-done.47.h2), channel_id=1, source_target_pairs={{8,0},{16,24},{9,1},{17,25},{10,2},{18,26},{11,3},{19,27},{12,4},{... | collective-permute-start | bytes 786440 | tf_op jit(solution)/shard_map/ppermute | solution.py:812
  294.6 12.2 %collective-permute-start.42 = (bf16[4,32,1024]{2,1,0:T(8,128)(2,1)}, bf16[4,32,1024]{2,1,0:T(8,128)(2,1)S(1)}, u32[]{:S(2)}, u32[]{:S(2)}) collective-permute-start(bf16[4,32,1024]{2,1,0:T(8,128)(2,1)} %get-tuple-element.136), channel_id=1, source_target_pairs={{0,3},{1,2},{2,1},{3,0},{4,7},{5,6},{6,5},{7,4},{8,11},{9,10},{10,... | collective-permute-start | bytes 786440 | tf_op jit(solution)/shard_map/ppermute | solution.py:1054
  296.5 13.1 %collective-permute-start.41 = (bf16[4,32,1024]{2,1,0:T(8,128)(2,1)}, bf16[4,32,1024]{2,1,0:T(8,128)(2,1)S(1)}, u32[]{:S(2)}, u32[]{:S(2)}) collective-permute-start(bf16[4,32,1024]{2,1,0:T(8,128)(2,1)} %get-tuple-element.135), channel_id=1, source_target_pairs={{0,2},{2,0},{1,3},{3,1},{4,6},{6,4},{5,7},{7,5},{8,10},{10,8},{9,1... | collective-permute-start | bytes 786440 | tf_op jit(solution)/shard_map/ppermute | solution.py:800
  297.0 13.5 %collective-permute-start.40 = (bf16[4,32,1024]{2,1,0:T(8,128)(2,1)}, bf16[4,32,1024]{2,1,0:T(8,128)(2,1)S(1)}, u32[]{:S(2)}, u32[]{:S(2)}) collective-permute-start(bf16[4,32,1024]{2,1,0:T(8,128)(2,1)} %get-tuple-element.134), channel_id=1, source_target_pairs={{0,1},{1,0},{2,3},{3,2},{4,5},{5,4},{6,7},{7,6},{8,9},{9,8},{10,11... | collective-permute-start | bytes 786440 | tf_op jit(solution)/shard_map/ppermute | solution.py:796
  304.9 10.4 %collective-permute-start.53 = (bf16[4,32,1024]{2,1,0:T(8,128)(2,1)}, bf16[4,32,1024]{2,1,0:T(8,128)(2,1)S(1)}, u32[]{:S(2)}, u32[]{:S(2)}) collective-permute-start(bf16[4,32,1024]{2,1,0:T(8,128)(2,1)} %get-tuple-element.143), channel_id=1, source_target_pairs={{0,3},{1,2},{2,1},{3,0},{4,7},{5,6},{6,5},{7,4},{8,11},{9,10},{10,... | collective-permute-start | bytes 786440 | tf_op jit(solution)/shard_map/ppermute | solution.py:1054
  306.8 15.8 %collective-permute-start.52 = (bf16[4,32,1024]{2,1,0:T(8,128)(2,1)}, bf16[4,32,1024]{2,1,0:T(8,128)(2,1)S(1)}, u32[]{:S(2)}, u32[]{:S(2)}) collective-permute-start(bf16[4,32,1024]{2,1,0:T(8,128)(2,1)} %get-tuple-element.142), channel_id=1, source_target_pairs={{0,2},{2,0},{1,3},{3,1},{4,6},{6,4},{5,7},{7,5},{8,10},{10,8},{9,1... | collective-permute-start | bytes 786440 | tf_op jit(solution)/shard_map/ppermute | solution.py:800
  309.6 16.2 %collective-permute-start.51 = (bf16[4,32,1024]{2,1,0:T(8,128)(2,1)}, bf16[4,32,1024]{2,1,0:T(8,128)(2,1)S(1)}, u32[]{:S(2)}, u32[]{:S(2)}) collective-permute-start(bf16[4,32,1024]{2,1,0:T(8,128)(2,1)} %get-tuple-element.141), channel_id=1, source_target_pairs={{0,1},{1,0},{2,3},{3,2},{4,5},{5,4},{6,7},{7,6},{8,9},{9,8},{10,11... | collective-permute-start | bytes 786440 | tf_op jit(solution)/shard_map/ppermute | solution.py:796
  311.3 19.2 %collective-permute-start.43 = (bf16[32,1024]{1,0:T(8,128)(2,1)S(1)}, bf16[32,1024]{1,0:T(8,128)(2,1)S(1)}, u32[]{:S(2)}, u32[]{:S(2)}) collective-permute-start(bf16[32,1024]{1,0:T(8,128)(2,1)S(1)} %get-tuple-element.182), channel_id=1, source_target_pairs={{0,8},{8,16},{16,24},{24,0},{1,9},{9,17},{17,25},{25,1},{2,10},{10... | collective-permute-start | bytes 196616 | tf_op jit(solution)/shard_map/ppermute | solution.py:788
  315.3 18.2 %collective-permute-start.44 = (bf16[32,1024]{1,0:T(8,128)(2,1)S(1)}, bf16[32,1024]{1,0:T(8,128)(2,1)S(1)}, u32[]{:S(2)}, u32[]{:S(2)}) collective-permute-start(bf16[32,1024]{1,0:T(8,128)(2,1)S(1)} %get-tuple-element.181), channel_id=1, source_target_pairs={{0,16},{8,24},{16,0},{24,8},{1,17},{9,25},{17,1},{25,9},{2,18},{10... | collective-permute-start | bytes 196616 | tf_op jit(solution)/shard_map/ppermute | solution.py:788
  322.6 11.0 %collective-permute-start.45 = (bf16[32,1024]{1,0:T(8,128)(2,1)S(1)}, bf16[32,1024]{1,0:T(8,128)(2,1)S(1)}, u32[]{:S(2)}, u32[]{:S(2)}) collective-permute-start(bf16[32,1024]{1,0:T(8,128)(2,1)S(1)} %get-tuple-element.180), channel_id=1, source_target_pairs={{0,24},{8,0},{16,8},{24,16},{1,25},{9,1},{17,9},{25,17},{2,26},{10... | collective-permute-start | bytes 196616 | tf_op jit(solution)/shard_map/ppermute | solution.py:788
  327.6 6.8 %collective-permute-start.54 = (bf16[32,1024]{1,0:T(8,128)(2,1)S(1)}, bf16[32,1024]{1,0:T(8,128)(2,1)S(1)}, u32[]{:S(2)}, u32[]{:S(2)}) collective-permute-start(bf16[32,1024]{1,0:T(8,128)(2,1)S(1)} %get-tuple-element.176), channel_id=1, source_target_pairs={{0,8},{8,16},{16,24},{24,0},{1,9},{9,17},{17,25},{25,1},{2,10},{10... | collective-permute-start | bytes 196616 | tf_op jit(solution)/shard_map/ppermute | solution.py:788
  327.6 8.2 %collective-permute-start.55 = (bf16[32,1024]{1,0:T(8,128)(2,1)S(1)}, bf16[32,1024]{1,0:T(8,128)(2,1)S(1)}, u32[]{:S(2)}, u32[]{:S(2)}) collective-permute-start(bf16[32,1024]{1,0:T(8,128)(2,1)S(1)} %get-tuple-element.175), channel_id=1, source_target_pairs={{0,16},{8,24},{16,0},{24,8},{1,17},{9,25},{17,1},{25,9},{2,18},{10... | collective-permute-start | bytes 196616 | tf_op jit(solution)/shard_map/ppermute | solution.py:788
  330.5 5.3 %collective-permute-start.56 = (bf16[32,1024]{1,0:T(8,128)(2,1)S(1)}, bf16[32,1024]{1,0:T(8,128)(2,1)S(1)}, u32[]{:S(2)}, u32[]{:S(2)}) collective-permute-start(bf16[32,1024]{1,0:T(8,128)(2,1)S(1)} %get-tuple-element.174), channel_id=1, source_target_pairs={{0,24},{8,0},{16,8},{24,16},{1,25},{9,1},{17,9},{25,17},{2,26},{10... | collective-permute-start | bytes 196616 | tf_op jit(solution)/shard_map/ppermute | solution.py:788
  (38 other events, 237.7 us)

commit v5 on v4

--- a/solution.py
+++ b/solution.py
@@ -428,7 +428,7 @@
     totals = [None] * 2
 
     def add(which, rel, half, mixed):
-        weight = (own_weight, sibling_weight)[half][kind[2 + rel], which]
+        weight = (own_weight, sibling_weight)[half][kind[10 + rel], which]
         part = jnp.dot(mixed, weight, preferred_element_type=f32)
         totals[which] = part if totals[which] is None else totals[which] + part
 
@@ -482,7 +482,7 @@
     half = pl.program_id(0)
     part = None
     for rel, mixes in enumerate((mix0, mix1, mix2, mix3)):
-        weight = jnp.where(half == 0, own[kind[2 + rel], 0], sibling[kind[2 + rel], 0])
+        weight = jnp.where(half == 0, own[kind[10 + rel], 0], sibling[kind[10 + rel], 0])
         new = jnp.dot(mixes[0], weight, preferred_element_type=f32)
         part = new if part is None else part + new
 
@@ -527,7 +527,7 @@
     half = pl.program_id(0)
     part = None
     for rel, mixes in enumerate((mix0, mix1, mix2, mix3)):
-        weight = jnp.where(half == 0, own[kind[2 + rel], 0], sibling[kind[2 + rel], 0])
+        weight = jnp.where(half == 0, own[kind[10 + rel], 0], sibling[kind[10 + rel], 0])
         new = jnp.dot(mixes[0], weight, preferred_element_type=f32)
         part = new if part is None else part + new
 
@@ -805,12 +805,20 @@
     return [blocks(z)] + [turned(blocks((z + k) % length), "z", k) for k in range(1, length)]
 
 
-def spread_along(piece, z):
+def near_along(piece):
+    two = turned(piece, "z", 2)
     one = lax.ppermute(piece, "z", [(0, 1), (1, 2), (2, 3)])
     three = lax.ppermute(piece, "z", [(1, 0), (2, 1), (3, 2)])
-    two = turned(piece, "z", 2)
-    far = lax.ppermute(two, "z", [(1, 0), (2, 3)])
-    return piece, one, two, three, far
+    return one, two, three
+
+
+def far_along(two):
+    return lax.ppermute(two, "z", [(1, 0), (2, 3)])
+
+
+def spread_along(piece, z):
+    one, two, three = near_along(piece)
+    return piece, one, two, three, far_along(two)
 
 
 def in_place(spread, z, at=0):
@@ -868,6 +876,7 @@
         [is_long.astype(jnp.int32), jnp.where(is_long, rows, slot_rows).astype(jnp.int32)]
         + [(mp ^ rel).astype(jnp.int32) for rel in range(4)]
         + [((z - k) % lines).astype(jnp.int32) for k in range(4)]
+        + [((z - (mp ^ rel)) % lines).astype(jnp.int32) for rel in range(4)]
     )
     given = given_to_other_core(
         kind, prompt_live_extents, continued_prompt_entries, padded_prompt_entries
@@ -914,13 +923,14 @@
             carried_memory,
         )
     )
-    spread = spread_along(block, z)
-    _, one, two, three, far = spread
+    one, two, three = near_along(block)
     own_x, own_y = over_x(block), over_y(block)
+    one, two, three, own_x, own_y = lax.optimization_barrier((one, two, three, own_x, own_y))
+    far = far_along(two)
     own_xy = (over_y(own_x[0]), over_x(own_y[1]))
+    far, own_xy = lax.optimization_barrier((far, own_xy))
     rest = jnp.stack([jnp.where(z == 0, far, one), two, jnp.where(z == 3, far, three)], axis=1)
     rest_x, rest_y = over_x(rest), over_y(rest)
-    rest_xy = (over_y(rest_x[0]), over_x(rest_y[1]))
     extents = in_order(
         [part[2 * group_rows + 1, : 2 * requests] for part in (block[0],) + tuple(rest[0])], z
     ).reshape(2 * lines * requests)
@@ -939,22 +949,25 @@
 
     def columns_of(weights, *ready):
         stacked = jnp.stack(weights)
-
-        def block(j):
-            return lax.dynamic_slice_in_dim(stacked, j * width, width, 2)
-
-        blocks = [block((z + k) % lines) for k in range(lines)]
+        blocks = [
+            lax.dynamic_slice_in_dim(stacked, (z + k) % lines * width, width, 2)
+            for k in range(lines)
+        ]
         blocks = lax.optimization_barrier((tuple(blocks),) + ready)[0]
-        pieces = [blocks[0]] + [turned(blocks[k], "z", k) for k in range(1, lines)]
-        return pieces
+        return (blocks[0],) + tuple(turned(blocks[k], "z", k) for k in range(1, lines))
 
     def both_cores(pieces):
-        return in_order(pieces, z), in_order([flipped_core(piece) for piece in pieces], z)
-
-    kv_pieces = columns_of([lookup_transform, payload_transform], rest)
-    r_pieces = columns_of([acceptance_transform], kv_pieces[2])
-    gate_pieces = columns_of([gating_transform], r_pieces[2])
-    own_kv, sibling_kv = both_cores(after(tuple(kv_pieces), rest_x, rest_y))
+        own = jnp.stack(pieces)
+        return own, flipped_core(own)
+
+    kv_pieces = columns_of([lookup_transform, payload_transform], rest, own_xy)
+    kv_pieces, rest_x, rest_y = lax.optimization_barrier((kv_pieces, rest_x, rest_y))
+    rest_xy = (over_y(rest_x[0]), over_x(rest_y[1]))
+    r_pieces = columns_of([acceptance_transform], rest_x, rest_y, kv_pieces)
+    own_kv, sibling_kv = both_cores(kv_pieces)
+    rest_xy, r_pieces = lax.optimization_barrier((rest_xy, r_pieces))
+    gate_pieces = columns_of([gating_transform], r_pieces, rest_xy)
+    own_r, sibling_r = both_cores(r_pieces)
 
     def mine_of(vector):
         return lax.dynamic_slice_in_dim(vector, z * width, width, 0)[None]
@@ -975,7 +988,6 @@
         lax.dynamic_slice_in_dim(fading_right_factor, z * width, width, 1),
         mine_of(fading_baseline),
     )
-    own_r, sibling_r = both_cores(after(tuple(r_pieces), decay))
     recept = plain_product(kind, (r0, r1, r2, r3), own_r, sibling_r)
     entered = lax.dynamic_slice_in_dim(carried_memory, z * heads, heads, 0)
     bonus = lax.dynamic_slice_in_dim(present_reward, z * heads, heads, 0).reshape(1, width)
@@ -998,7 +1010,7 @@
         mine_of(group_layer_scaling),
         mine_of(group_layer_shift_term),
     )
-    own_gate, sibling_gate = both_cores(after(tuple(gate_pieces), states))
+    own_gate, sibling_gate = both_cores(after(gate_pieces, states))
     kept0, sent0, kept1, sent1 = gated(
         kind, extents, (gate0, gate1, gate2, gate3), own_gate, sibling_gate, normed
     )
@@ -1009,7 +1021,7 @@
     bundle = jnp.concatenate(
         [jnp.where(is_long, held, passed)[:, -1:], jnp.where(is_long, passed, held)], axis=1
     ).astype(bf16)
-    bundle = after(bundle, gate_pieces[2])
+    bundle = after(bundle, gate_pieces)
     arrived = in_order(
         dealt(lambda j: lax.dynamic_index_in_dim(bundle, j, 0, keepdims=False), z), z
     ).astype(f32)

time: 340 us -> 307 us (0.903)
  waiting for transfers between devices: 111 us -> 86.8 us
  local copies, waits for them, and re-layouts: 34 us -> 24 us
    ppermute x21, waiting for transfers between devices: 76 us -> 59.8 us  [turned(): lax.ppermute(x, axis, [(i, (i + by) % length) for i in range(length)])]
    ppermute x6, waiting for transfers between devices: 13.7 us -> 2.29 us  [over_x(): return lax.ppermute(x, 'x', [(0, 1), (1, 0)])]
    dynamic_update_slice x32 -> x8, local copies, waits for them, and re-layouts: 6.21 us -> 0.28 us  [in_order(): whole = lax.dynamic_update_index_in_dim(whole, piece, (z - k) % length, 0)]
    ppermute x9, waiting for transfers between devices: 11.6 us -> 16.8 us  [the longest x3 14.1 us: far_along(): return lax.ppermute(two, 'z', [(1, 0), (2, 3)])]
    ppermute x9, starting transfers between devices: 22.6 us -> 26.6 us  [the longest x3 18.7 us: near_along(): one = lax.ppermute(piece, 'z', [(0, 1), (1, 2), (2, 3)])]
  transfers between devices with their start and end apart: 61 -> 52, of which waited for: 17 -> 17; matrix products, arithmetic and copies ran while one was open for 13% -> 11% of each run, Pallas kernels for 22% -> 22%
where the time goes in v5:
time: 307 us; the launch traced here: 306 us
  starting transfers between devices  94.9 us (31%)
  waiting for transfers between devices  86.8 us (28%)
  Pallas kernels  81.1 us (26%)
  local copies, waits for them, and re-layouts  24 us (8%)
  other arithmetic  17.7 us (6%)
    ppermute x21, waiting for transfers between devices, turned(): lax.ppermute(x, axis, [(i, (i + by) % length) for i in range(length)])  59.8 us
    ppermute x21, starting transfers between devices, turned(): lax.ppermute(x, axis, [(i, (i + by) % length) for i in range(length)])  47.2 us
    pallas_call x3, Pallas kernels, mixes_of(): pl.pallas_call(mix_kernel, grid=(2,), out_shape=outs, in_specs=[in_smem()...  20.8 us
    ppermute x3, starting transfers between devices, near_along(): one = lax.ppermute(piece, 'z', [(0, 1), (1, 2), (2, 3)])  18.7 us
    ppermute x3, waiting for transfers between devices, far_along(): return lax.ppermute(two, 'z', [(1, 0), (2, 3)])  14.1 us
    pallas_call x1, Pallas kernels, projected(): pl.pallas_call(project_kernel, grid=(rows // TILE,), out_shape=[flat] * 3...  14 us
    pallas_call x1, Pallas kernels, sweep(): pl.pallas_call(sweep_kernel, out_shape=jax.ShapeDtypeStruct(r.shape, f32)...  11.9 us
    pallas_call x2, Pallas kernels, final_product(): pl.pallas_call(final_kernel, out_shape=[out] * 4, in_specs=[in_smem()] +...  9.03 us
  transfers between devices with their start and end apart: 52, of which 17 were waited for; matrix products, arithmetic and copies ran while one was open for 11% of the time, Pallas kernels for 22%

profile of v5, /device:TPU:0, one launch (start us, length us, event | category | flops | bytes accessed | tf_op | source)
XLA Modules:
  0.0 306.0 jit_solution(9823914173277360797)
XLA Ops:
  1.5 1.8 shard_map.184
  6.2 2.0 shard_map.185.own
  8.2 5.4 %collective-permute-start.1 = (bf16[2,272,512]{2,1,0:T(8,128)(2,1)}, bf16[2,272,512]{2,1,0:T(8,128)(2,1)}, u32[]{:S(2)}, u32[]{:S(2)}) collective-permute-start(bf16[2,272,512]{2,1,0:T(8,128)(2,1)} %shard_map.185.own), channel_id=1, source_target_pairs={{0,8},{8,16},{16,24},{1,9},{9,17},{17,25},{2,10},{10,18},{18,26},{... | collective-permute-start | bytes 1671176 | tf_op jit(solution)/shard_map/ppermute | solution.py:810
  13.7 1.8 collective-permute-start.2
  15.5 1.3 collective-permute-start.3
  16.8 1.6 collective-permute-start.4
  18.4 1.5 collective-permute-start.5
  25.3 1.6 dynamic-slice_select_fusion.s_ref
  28.2 1.4 dynamic_slice.153
  29.6 1.3 dynamic_slice.160
  30.9 1.4 dynamic_slice.161
  32.3 2.5 fusion
  36.4 5.4 %collective-permute-done.2 = bf16[2,272,512]{2,1,0:T(8,128)(2,1)S(1)} collective-permute-done((bf16[2,272,512]{2,1,0:T(8,128)(2,1)}, bf16[2,272,512]{2,1,0:T(8,128)(2,1)S(1)}, u32[]{:S(2)}, u32[]{:S(2)}) %collective-permute-start.2) | collective-permute-done | bytes 557088 | tf_op jit(solution)/shard_map/ppermute | solution.py:788
  41.8 1.9 collective-permute-done.3
  43.8 1.3 collective-permute-start.6
  46.0 1.6 collective-permute-start.7
  48.6 1.6 collective-permute-start.8
  50.3 3.4 %collective-permute-done.7.own0 = bf16[272,512]{1,0:T(8,128)(2,1)S(1)} collective-permute-done((bf16[272,512]{1,0:T(8,128)(2,1)S(1)}, bf16[272,512]{1,0:T(8,128)(2,1)S(1)}, u32[]{:S(2)}, u32[]{:S(2)}) %collective-permute-start.7) | collective-permute-done | bytes 278560 | tf_op jit(solution)/shard_map/ppermute | solution.py:800
  53.7 2.3 collective-permute-done.8.own1
  56.0 11.9 %collective-permute-done.6 = bf16[2,272,512]{2,1,0:T(8,128)(2,1)S(1)} collective-permute-done((bf16[2,272,512]{2,1,0:T(8,128)(2,1)S(1)}, bf16[2,272,512]{2,1,0:T(8,128)(2,1)S(1)}, u32[]{:S(2)}, u32[]{:S(2)}) %collective-permute-start.6) | collective-permute-done | bytes 557088 | tf_op jit(solution)/shard_map/ppermute | solution.py:816
  69.4 1.6 collective-permute-start.12
  70.9 1.5 collective-permute-start.13
  73.0 1.6 pad_maximum_fusion.2.weight
  75.3 2.6 collective-permute-start.10
  79.2 6.8 %shard_map.186 = (bf16[2,2,1024,512]{3,2,1,0:T(8,128)(2,1)}, bf16[2,1024,512]{2,1,0:T(8,128)(2,1)}, bf16[2,1024,512]{2,1,0:T(8,128)(2,1)}, f32[2,1024,128]{2,1,0:T(8,128)}) custom-call(s32[14]{0:T(128)} %stack.166.kind, bf16[2,272,512]{2,1,0:T(8,128)(2,1)} %shard_map.185.own, bf16[2,3,272,512]{3,2,1,0:T(8,128)(2,1)} %copy-done.3, ...), custom_call_target="tpu_custom_call" | custom-call | flops 8049999872 | bytes 21000000 | tf_op jit(solution)/shard_map/pallas_call | solution.py:384
  85.9 6.4 %collective-permute-done.9 = bf16[2,512,256]{2,1,0:T(8,128)(2,1)S(1)} collective-permute-done((bf16[2,512,256]{2,1,0:T(8,128)(2,1)}, bf16[2,512,256]{2,1,0:T(8,128)(2,1)S(1)}, u32[]{:S(2)}, u32[]{:S(2)}) %collective-permute-start.9) | collective-permute-done | bytes 524320 | tf_op jit(solution)/shard_map/ppermute | solution.py:788
  92.3 20.2 %collective-permute-done.10 = bf16[2,512,256]{2,1,0:T(8,128)(2,1)S(1)} collective-permute-done((bf16[2,512,256]{2,1,0:T(8,128)(2,1)}, bf16[2,512,256]{2,1,0:T(8,128)(2,1)S(1)}, u32[]{:S(2)}, u32[]{:S(2)}) %collective-permute-start.10) | collective-permute-done | bytes 524320 | tf_op jit(solution)/shard_map/ppermute | solution.py:788
  112.9 2.0 slice_bitcast_fusion.1
  117.6 10.7 %collective-permute-start.16 = (bf16[1,512,256]{2,1,0:T(8,128)(2,1)S(1)}, bf16[1,512,256]{2,1,0:T(8,128)(2,1)S(1)}, u32[]{:S(2)}, u32[]{:S(2)}) collective-permute-start(bf16[1,512,256]{2,1,0:T(8,128)(2,1)S(1)} %copy-done.17), channel_id=1, source_target_pairs={{0,8},{8,16},{16,24},{24,0},{1,9},{9,17},{17,25},{25,1},{2,10},{10... | collective-permute-start | bytes 786440 | tf_op jit(solution)/shard_map/ppermute | solution.py:788
  128.4 7.1 %shard_map.187 = (bf16[2,2,1024,512]{3,2,1,0:T(8,128)(2,1)}, bf16[2,1024,512]{2,1,0:T(8,128)(2,1)}, bf16[2,1024,512]{2,1,0:T(8,128)(2,1)}, f32[2,1024,128]{2,1,0:T(8,128)}) custom-call(s32[14]{0:T(128)} %stack.166.kind, bf16[2,272,512]{2,1,0:T(8,128)(2,1)} %collective-permute-done.4.own, bf16[2,3,272,512]{3,2,1,0:T(8,128)(2,1)} %collective-permute-done.12.rest, ...), custom_call_target="tpu_custom_call" | custom-call | flops 8049999872 | bytes 21000000 | tf_op jit(solution)/shard_map/pallas_call | solution.py:384
  135.5 2.5 collective-permute-start.18
  137.9 7.0 %shard_map.188 = (bf16[2,2,1024,512]{3,2,1,0:T(8,128)(2,1)}, bf16[2,1024,512]{2,1,0:T(8,128)(2,1)}, bf16[2,1024,512]{2,1,0:T(8,128)(2,1)}, f32[2,1024,128]{2,1,0:T(8,128)}) custom-call(s32[14]{0:T(128)} %stack.166.kind, bf16[2,272,512]{2,1,0:T(8,128)(2,1)} %collective-permute-done.5.own, bf16[2,3,272,512]{3,2,1,0:T(8,128)(2,1)} %collective-permute-done.13.rest, ...), custom_call_target="tpu_custom_call" | custom-call | flops 8049999872 | bytes 21000000 | tf_op jit(solution)/shard_map/pallas_call | solution.py:384
  144.9 3.2 %collective-permute-done.18 = bf16[1,512,256]{2,1,0:T(8,128)(2,1)S(1)} collective-permute-done((bf16[1,512,256]{2,1,0:T(8,128)(2,1)S(1)}, bf16[1,512,256]{2,1,0:T(8,128)(2,1)S(1)}, u32[]{:S(2)}, u32[]{:S(2)}) %collective-permute-start.18) | collective-permute-done | bytes 262176 | tf_op jit(solution)/shard_map/ppermute | solution.py:788
  148.1 5.2 %collective-permute-start.20 = (bf16[1,512,256]{2,1,0:T(8,128)(2,1)S(1)}, bf16[1,512,256]{2,1,0:T(8,128)(2,1)S(1)}, u32[]{:S(2)}, u32[]{:S(2)}) collective-permute-start(bf16[1,512,256]{2,1,0:T(8,128)(2,1)S(1)} %copy-done.14), channel_id=1, source_target_pairs={{0,8},{8,16},{16,24},{24,0},{1,9},{9,17},{17,25},{25,1},{2,10},{10... | collective-permute-start | bytes 786440 | tf_op jit(solution)/shard_map/ppermute | solution.py:788
  153.3 4.1 %collective-permute-start.21 = (bf16[1,512,256]{2,1,0:T(8,128)(2,1)S(1)}, bf16[1,512,256]{2,1,0:T(8,128)(2,1)S(1)}, u32[]{:S(2)}, u32[]{:S(2)}) collective-permute-start(bf16[1,512,256]{2,1,0:T(8,128)(2,1)S(1)} %copy-done.13), channel_id=1, source_target_pairs={{0,16},{8,24},{16,0},{24,8},{1,17},{9,25},{17,1},{25,9},{2,18},{10... | collective-permute-start | bytes 786440 | tf_op jit(solution)/shard_map/ppermute | solution.py:788
  157.4 1.7 collective-permute-start.22
  159.4 14.0 %shard_map.189 = (f32[1024,256]{1,0:T(8,128)}, f32[1024,256]{1,0:T(8,128)}, f32[1024,256]{1,0:T(8,128)}, bf16[2,1024,512]{2,1,0:T(8,128)(2,1)}, bf16[2,1024,512]{2,1,0:T(8,128)(2,1)}) custom-call(s32[14]{0:T(128)} %stack.166.kind, bf16[2,2,1024,512]{3,2,1,0:T(8,128)(2,1)} %get-tuple-element.108.mix0, bf16[2,2,1024,512]{3,2,1,0:T(8,128)(2,1)} %get-tuple-element.109.mix1, ...), custom_call_target="tpu_custom_call" | custom-call | flops 13799999488 | bytes 36000000 | tf_op jit(solution)/shard_map/pallas_call | solution.py:466
  173.3 5.8 %shard_map.190 = (f32[16,4,64,64]{3,2,1,0:T(8,128)}, bf16[16,64,256]{2,1,0:T(8,128)(2,1)}) custom-call(s32[16]{0:T(128)} %select_n.354.lengths, f32[1]{0:T(128)} %bitcast.62.carry, f32[1024,256]{1,0:T(8,128)} %get-tuple-element.137.k_ref, f32[1024,256]{1,0:T(8,128)} %get-tuple-element.138.v_ref, f32[1024,256]{1,0:T(8,128)} %get-tuple-element.139.w_ref, ...), custom_call_target="tpu_custom_call" | custom-call | flops 8049999872 | bytes 21000000 | tf_op jit(solution)/shard_map/pallas_call | solution.py:635
  179.6 1.4 copy-done.11
  182.5 6.8 %shard_map.191.r_ref = f32[1024,256]{1,0:T(8,128)} custom-call(s32[14]{0:T(128)} %stack.166.kind, bf16[2,1024,512]{2,1,0:T(8,128)(2,1)} %get-tuple-element.146.mix0, bf16[2,1024,512]{2,1,0:T(8,128)(2,1)} %get-tuple-element.147.mix1, bf16[2,1024,512]{2,1,0:T(8,128)(2,1)} %get-tuple-element.148.mix2, bf16[2,1024,512]{2,1,0:T(8,128)(2,1)} %get-tuple-element.149.mix3, ...), custom_call_target="tpu_custom_call" | custom-call | flops 6899999744 | bytes 18000000 | tf_op jit(solution)/shard_map/pallas_call | solution.py:500
  189.3 11.9 %shard_map.192.normed = f32[1024,256]{1,0:T(8,128)} custom-call(s32[16]{0:T(128)} %select_n.354.lengths, f32[1024,256]{1,0:T(8,128)} %shard_map.191.r_ref, f32[1024,256]{1,0:T(8,128)} %get-tuple-element.137.k_ref, f32[1024,256]{1,0:T(8,128)} %get-tuple-element.138.v_ref, f32[1024,256]{1,0:T(8,128)} %get-tuple-element.139.w_ref, ...), custom_call_target="tpu_custom_call" | custom-call | flops 13799999488 | bytes 36000000 | tf_op jit(solution)/shard_map/pallas_call | solution.py:721
  202.3 7.1 %shard_map.193 = (bf16[2,4,32,256]{3,2,1,0:T(8,128)(2,1)}, bf16[2,4,32,256]{3,2,1,0:T(8,128)(2,1)}, bf16[2,4,32,256]{3,2,1,0:T(8,128)(2,1)}, bf16[2,4,32,256]{3,2,1,0:T(8,128)(2,1)}) custom-call(s32[14]{0:T(128)} %stack.166.kind, s32[16]{0:T(128)} %select_n.354.lengths, bf16[2,1024,512]{2,1,0:T(8,128)(2,1)} %get-tuple-element.95.mix0, ...), custom_call_target="tpu_custom_call" | custom-call | flops 8049999872 | bytes 21000000 | tf_op jit(solution)/shard_map/pallas_call | solution.py:564
  212.7 2.7 collective-permute-start.50
  215.6 1.3 collective-permute-start.29
  216.9 4.6 %collective-permute-start.28 = (bf16[512,256]{1,0:T(8,128)(2,1)S(1)}, bf16[512,256]{1,0:T(8,128)(2,1)S(1)}, u32[]{:S(2)}, u32[]{:S(2)}) collective-permute-start(bf16[512,256]{1,0:T(8,128)(2,1)S(1)} %bitcast.174), channel_id=1, source_target_pairs={{0,8},{8,16},{16,24},{1,9},{9,17},{17,25},{2,10},{10,18},{18,26},{... | collective-permute-start | bytes 786440 | tf_op jit(solution)/shard_map/ppermute | solution.py:810
  221.5 14.4 %collective-permute-done.26.h2 = bf16[512,256]{1,0:T(8,128)(2,1)S(1)} collective-permute-done((bf16[512,256]{1,0:T(8,128)(2,1)S(1)}, bf16[512,256]{1,0:T(8,128)(2,1)S(1)}, u32[]{:S(2)}, u32[]{:S(2)}) %collective-permute-start.26) | collective-permute-done | bytes 262176 | tf_op jit(solution)/shard_map/ppermute | solution.py:788
  236.0 1.3 collective-permute-start.27
  237.3 7.8 %collective-permute-done.50 = bf16[3,4,64,64]{3,2,1,0:T(8,128)(2,1)S(1)} collective-permute-done((bf16[3,4,64,64]{3,2,1,0:T(8,128)(2,1)S(1)}, bf16[3,4,64,64]{3,2,1,0:T(8,128)(2,1)S(1)}, u32[]{:S(2)}, u32[]{:S(2)}) %collective-permute-start.50) | collective-permute-done | bytes 98336 | tf_op jit(solution)/shard_map/ppermute | solution.py:788
  245.2 1.3 collective-permute-start.41
  246.5 8.7 %collective-permute-start.40 = (bf16[512,256]{1,0:T(8,128)(2,1)S(1)}, bf16[512,256]{1,0:T(8,128)(2,1)S(1)}, u32[]{:S(2)}, u32[]{:S(2)}) collective-permute-start(bf16[512,256]{1,0:T(8,128)(2,1)S(1)} %bitcast.170), channel_id=1, source_target_pairs={{0,8},{8,16},{16,24},{1,9},{9,17},{17,25},{2,10},{10,18},{18,26},{... | collective-permute-start | bytes 786440 | tf_op jit(solution)/shard_map/ppermute | solution.py:810
  256.4 1.5 collective-permute-start.39
  258.8 4.5 %shard_map.194 = (bf16[4,32,1024]{2,1,0:T(8,128)(2,1)}, bf16[4,32,1024]{2,1,0:T(8,128)(2,1)}, bf16[4,32,1024]{2,1,0:T(8,128)(2,1)}, bf16[4,32,1024]{2,1,0:T(8,128)(2,1)}) custom-call(s32[4]{0:T(128)} %pad_add_fusion.1.block_of, bf16[512,256]{1,0:T(8,128)(2,1)} %bitcast.175, bf16[512,256]{1,0:T(8,128)(2,1)} %get-tuple-element.209.h1, ...), custom_call_target="tpu_custom_call" | custom-call | flops 5175000064 | bytes 13500000 | tf_op jit(solution)/shard_map/pallas_call | solution.py:750
  263.3 2.2 collective-permute-start.33
  267.4 1.5 collective-permute-start.31
  268.9 2.2 collective-permute-done.39
  271.9 4.5 %shard_map.195 = (bf16[4,32,1024]{2,1,0:T(8,128)(2,1)}, bf16[4,32,1024]{2,1,0:T(8,128)(2,1)}, bf16[4,32,1024]{2,1,0:T(8,128)(2,1)}, bf16[4,32,1024]{2,1,0:T(8,128)(2,1)}) custom-call(s32[4]{0:T(128)} %pad_add_fusion.1.block_of, bf16[512,256]{1,0:T(8,128)(2,1)} %bitcast.171, bf16[512,256]{1,0:T(8,128)(2,1)} %get-tuple-element.203.h1, ...), custom_call_target="tpu_custom_call" | custom-call | flops 5175000064 | bytes 13500000 | tf_op jit(solution)/shard_map/pallas_call | solution.py:750
  276.4 2.1 collective-permute-start.44
  280.8 3.3 %collective-permute-start.34 = (bf16[32,1024]{1,0:T(8,128)(2,1)S(1)}, bf16[32,1024]{1,0:T(8,128)(2,1)S(1)}, u32[]{:S(2)}, u32[]{:S(2)}) collective-permute-start(bf16[32,1024]{1,0:T(8,128)(2,1)S(1)} %get-tuple-element.206), channel_id=1, source_target_pairs={{0,8},{8,16},{16,24},{24,0},{1,9},{9,17},{17,25},{25,1},{2,10},{10... | collective-permute-start | bytes 196616 | tf_op jit(solution)/shard_map/ppermute | solution.py:788
  284.1 2.8 collective-permute-done.44
  286.9 3.0 collective-permute-start.35
  290.8 2.6 collective-permute-start.36
  295.1 2.9 collective-permute-start.46
  298.1 2.2 collective-permute-start.47
  304.0 1.9 shard_map.196
  (200 shorter events, 41.4 us)
Async XLA Ops:
  0.6 34.3 %copy-start = (bf16[128,1024]{1,0:T(8,128)(2,1)S(1)}, bf16[128,1024]{1,0:T(8,128)(2,1)}, u32[]{:S(2)}) copy-start(bf16[128,1024]{1,0:T(8,128)(2,1)} %param.29) | copy-start | bytes 786436
  3.3 2.2 collective-permute-start
  5.5 14.4 %copy-start.22 = (f32[5,4096]{1,0:T(8,128)S(1)}, f32[5,4096]{1,0:T(8,128)}, u32[]{:S(2)}) copy-start(f32[5,4096]{1,0:T(8,128)} %param.22) | copy-start | bytes 245764
  5.5 14.4 %copy-start.5 = (bf16[4096,128]{1,0:T(8,128)(2,1)S(1)}, bf16[4096,128]{1,0:T(8,128)(2,1)}, u32[]{:S(2)}) copy-start(bf16[4096,128]{1,0:T(8,128)(2,1)} %param.28) | copy-start | bytes 3145732
  8.2 14.5 %copy-start.6 = (bf16[512,1024]{1,0:T(8,128)(2,1)S(1)}, bf16[512,1024]{1,0:T(8,128)(2,1)}, u32[]{:S(2)}) copy-start(bf16[512,1024]{1,0:T(8,128)(2,1)} %param.23) | copy-start | bytes 3145732
  8.2 26.6 %collective-permute-start.1 = (bf16[2,272,512]{2,1,0:T(8,128)(2,1)}, bf16[2,272,512]{2,1,0:T(8,128)(2,1)}, u32[]{:S(2)}, u32[]{:S(2)}) collective-permute-start(bf16[2,272,512]{2,1,0:T(8,128)(2,1)} %shard_map.185.own), channel_id=1, source_target_pairs={{0,8},{8,16},{16,24},{1,9},{9,17},{17,25},{2,10},{10,18},{18,26},{... | collective-permute-start | bytes 1671176 | tf_op jit(solution)/shard_map/ppermute | solution.py:810
  13.7 28.2 %collective-permute-start.2 = (bf16[2,272,512]{2,1,0:T(8,128)(2,1)}, bf16[2,272,512]{2,1,0:T(8,128)(2,1)S(1)}, u32[]{:S(2)}, u32[]{:S(2)}) collective-permute-start(bf16[2,272,512]{2,1,0:T(8,128)(2,1)} %shard_map.185.own), channel_id=1, source_target_pairs={{0,16},{8,24},{16,0},{24,8},{1,17},{9,25},{17,1},{25,9},{2,18},{10... | collective-permute-start | bytes 1671176 | tf_op jit(solution)/shard_map/ppermute | solution.py:788
  15.5 28.2 %collective-permute-start.3 = (bf16[2,272,512]{2,1,0:T(8,128)(2,1)}, bf16[2,272,512]{2,1,0:T(8,128)(2,1)}, u32[]{:S(2)}, u32[]{:S(2)}) collective-permute-start(bf16[2,272,512]{2,1,0:T(8,128)(2,1)} %shard_map.185.own), channel_id=1, source_target_pairs={{8,0},{16,8},{24,16},{9,1},{17,9},{25,17},{10,2},{18,10},{26,18},{... | collective-permute-start | bytes 1671176 | tf_op jit(solution)/shard_map/ppermute | solution.py:811
  16.8 27.0 %collective-permute-start.4 = (bf16[2,272,512]{2,1,0:T(8,128)(2,1)}, bf16[2,272,512]{2,1,0:T(8,128)(2,1)}, u32[]{:S(2)}, u32[]{:S(2)}) collective-permute-start(bf16[2,272,512]{2,1,0:T(8,128)(2,1)} %shard_map.185.own), channel_id=1, source_target_pairs={{0,1},{1,0},{2,3},{3,2},{4,5},{5,4},{6,7},{7,6},{8,9},{9,8},{10,11... | collective-permute-start | bytes 1671176 | tf_op jit(solution)/shard_map/ppermute | solution.py:796
  18.4 25.4 %collective-permute-start.5 = (bf16[2,272,512]{2,1,0:T(8,128)(2,1)}, bf16[2,272,512]{2,1,0:T(8,128)(2,1)}, u32[]{:S(2)}, u32[]{:S(2)}) collective-permute-start(bf16[2,272,512]{2,1,0:T(8,128)(2,1)} %shard_map.185.own), channel_id=1, source_target_pairs={{0,2},{2,0},{1,3},{3,1},{4,6},{6,4},{5,7},{7,5},{8,10},{10,8},{9,1... | collective-permute-start | bytes 1671176 | tf_op jit(solution)/shard_map/ppermute | solution.py:800
  34.8 15.4 %collective-permute-start.30 = (bf16[1024,512]{1,0:T(8,128)(2,1)S(1)}, bf16[1024,512]{1,0:T(8,128)(2,1)S(1)}, u32[]{:S(2)}, u32[]{:S(2)}) collective-permute-start(bf16[1024,512]{1,0:T(8,128)(2,1)S(1)} %copy-done.4), channel_id=1, source_target_pairs={{0,4},{4,0},{1,5},{5,1},{2,6},{6,2},{3,7},{7,3},{8,12},{12,8},{9,1... | collective-permute-start | bytes 3145736 | tf_op jit(solution)/shard_map/ppermute | solution.py:792
  43.8 24.2 %collective-permute-start.6 = (bf16[2,272,512]{2,1,0:T(8,128)(2,1)S(1)}, bf16[2,272,512]{2,1,0:T(8,128)(2,1)S(1)}, u32[]{:S(2)}, u32[]{:S(2)}) collective-permute-start(bf16[2,272,512]{2,1,0:T(8,128)(2,1)S(1)} %collective-permute-done.2), channel_id=1, source_target_pairs={{8,0},{16,24},{9,1},{17,25},{10,2},{18,26},{11,3},{19,27},{12,4},{... | collective-permute-start | bytes 1671176 | tf_op jit(solution)/shard_map/ppermute | solution.py:816
  46.0 7.7 %collective-permute-start.7 = (bf16[272,512]{1,0:T(8,128)(2,1)S(1)}, bf16[272,512]{1,0:T(8,128)(2,1)S(1)}, u32[]{:S(2)}, u32[]{:S(2)}) collective-permute-start(bf16[272,512]{1,0:T(8,128)(2,1)S(1)} %slice_bitcast_fusion.6), channel_id=1, source_target_pairs={{0,2},{2,0},{1,3},{3,1},{4,6},{6,4},{5,7},{7,5},{8,10},{10,8},{9,1... | collective-permute-start | bytes 835592 | tf_op jit(solution)/shard_map/ppermute | solution.py:800
  48.6 7.4 %collective-permute-start.8 = (bf16[272,512]{1,0:T(8,128)(2,1)S(1)}, bf16[272,512]{1,0:T(8,128)(2,1)S(1)}, u32[]{:S(2)}, u32[]{:S(2)}) collective-permute-start(bf16[272,512]{1,0:T(8,128)(2,1)S(1)} %slice_bitcast_fusion.5), channel_id=1, source_target_pairs={{0,1},{1,0},{2,3},{3,2},{4,5},{5,4},{6,7},{7,6},{8,9},{9,8},{10,11... | collective-permute-start | bytes 835592 | tf_op jit(solution)/shard_map/ppermute | solution.py:796
  53.7 15.4 %copy-start.29 = (bf16[272,512]{1,0:T(8,128)(2,1)}, bf16[272,512]{1,0:T(8,128)(2,1)S(1)}, u32[]{:S(2)}) copy-start(bf16[272,512]{1,0:T(8,128)(2,1)S(1)} %collective-permute-done.7.own0) | copy-start | bytes 835588
  69.4 43.2 %collective-permute-start.12 = (bf16[2,3,272,512]{3,2,1,0:T(8,128)(2,1)S(1)}, bf16[2,3,272,512]{3,2,1,0:T(8,128)(2,1)}, u32[]{:S(2)}, u32[]{:S(2)}) collective-permute-start(bf16[2,3,272,512]{3,2,1,0:T(8,128)(2,1)S(1)} %pad_maximum_fusion.3.rest), channel_id=1, source_target_pairs={{0,1},{1,0},{2,3},{3,2},{4,5},{5,4},{6,7},{7,6},{8,9},{9,8},{10,11... | collective-permute-start | bytes 5013512 | tf_op jit(solution)/shard_map/ppermute | solution.py:796
  70.9 41.6 %collective-permute-start.13 = (bf16[2,3,272,512]{3,2,1,0:T(8,128)(2,1)S(1)}, bf16[2,3,272,512]{3,2,1,0:T(8,128)(2,1)}, u32[]{:S(2)}, u32[]{:S(2)}) collective-permute-start(bf16[2,3,272,512]{3,2,1,0:T(8,128)(2,1)S(1)} %pad_maximum_fusion.3.rest), channel_id=1, source_target_pairs={{0,2},{2,0},{1,3},{3,1},{4,6},{6,4},{5,7},{7,5},{8,10},{10,8},{9,1... | collective-permute-start | bytes 5013512 | tf_op jit(solution)/shard_map/ppermute | solution.py:800
  75.3 17.0 %collective-permute-start.9 = (bf16[2,512,256]{2,1,0:T(8,128)(2,1)}, bf16[2,512,256]{2,1,0:T(8,128)(2,1)S(1)}, u32[]{:S(2)}, u32[]{:S(2)}) collective-permute-start(bf16[2,512,256]{2,1,0:T(8,128)(2,1)} %get-tuple-element.101), channel_id=1, source_target_pairs={{0,8},{8,16},{16,24},{24,0},{1,9},{9,17},{17,25},{25,1},{2,10},{10... | collective-permute-start | bytes 1572872 | tf_op jit(solution)/shard_map/ppermute | solution.py:788
  75.3 37.2 %collective-permute-start.10 = (bf16[2,512,256]{2,1,0:T(8,128)(2,1)}, bf16[2,512,256]{2,1,0:T(8,128)(2,1)S(1)}, u32[]{:S(2)}, u32[]{:S(2)}) collective-permute-start(bf16[2,512,256]{2,1,0:T(8,128)(2,1)} %get-tuple-element.102), channel_id=1, source_target_pairs={{0,16},{8,24},{16,0},{24,8},{1,17},{9,25},{17,1},{25,9},{2,18},{10... | collective-permute-start | bytes 1572872 | tf_op jit(solution)/shard_map/ppermute | solution.py:788
  78.0 34.5 %collective-permute-start.11 = (bf16[2,512,256]{2,1,0:T(8,128)(2,1)}, bf16[2,512,256]{2,1,0:T(8,128)(2,1)S(1)}, u32[]{:S(2)}, u32[]{:S(2)}) collective-permute-start(bf16[2,512,256]{2,1,0:T(8,128)(2,1)} %get-tuple-element.103), channel_id=1, source_target_pairs={{0,24},{8,0},{16,8},{24,16},{1,25},{9,1},{17,9},{25,17},{2,26},{10... | collective-permute-start | bytes 1572872 | tf_op jit(solution)/shard_map/ppermute | solution.py:788
  112.8 22.6 %copy-start.2 = (bf16[4,2,512,256]{3,2,1,0:T(8,128)(2,1)}, bf16[4,2,512,256]{3,2,1,0:T(8,128)(2,1)S(1)}, u32[]{:S(2)}) copy-start(bf16[4,2,512,256]{3,2,1,0:T(8,128)(2,1)S(1)} %pad_maximum_fusion.own_weight) | copy-start | bytes 6291460
  112.8 15.6 %copy-start.16 = (bf16[1,512,256]{2,1,0:T(8,128)(2,1)S(1)}, bf16[1,512,256]{2,1,0:T(8,128)(2,1)}, u32[]{:S(2)}) copy-start(bf16[1,512,256]{2,1,0:T(8,128)(2,1)} %get-tuple-element.121) | copy-start | bytes 786436
  112.8 46.5 %collective-permute-start.19 = (bf16[4,2,512,256]{3,2,1,0:T(8,128)(2,1)S(1)}, bf16[4,2,512,256]{3,2,1,0:T(8,128)(2,1)}, u32[]{:S(2)}, u32[]{:S(2)}) collective-permute-start(bf16[4,2,512,256]{3,2,1,0:T(8,128)(2,1)S(1)} %pad_maximum_fusion.own_weight), channel_id=1, source_target_pairs={{0,4},{4,0},{1,5},{5,1},{2,6},{6,2},{3,7},{7,3},{8,12},{12,8},{9,1... | collective-permute-start | bytes 6291464 | tf_op jit(solution)/shard_map/ppermute | solution.py:792
  114.9 33.2 %collective-permute-start.14 = (bf16[3,272,512]{2,1,0:T(8,128)(2,1)S(1)}, bf16[3,272,512]{2,1,0:T(8,128)(2,1)S(1)}, u32[]{:S(2)}, u32[]{:S(2)}) collective-permute-start(bf16[3,272,512]{2,1,0:T(8,128)(2,1)S(1)} %slice_bitcast_fusion.1), channel_id=1, source_target_pairs={{0,2},{2,0},{1,3},{3,1},{4,6},{6,4},{5,7},{7,5},{8,10},{10,8},{9,1... | collective-permute-start | bytes 2506760 | tf_op jit(solution)/shard_map/ppermute | solution.py:800
  116.7 31.4 %collective-permute-start.15 = (bf16[3,272,512]{2,1,0:T(8,128)(2,1)S(1)}, bf16[3,272,512]{2,1,0:T(8,128)(2,1)}, u32[]{:S(2)}, u32[]{:S(2)}) collective-permute-start(bf16[3,272,512]{2,1,0:T(8,128)(2,1)S(1)} %slice_bitcast_fusion), channel_id=1, source_target_pairs={{0,1},{1,0},{2,3},{3,2},{4,5},{5,4},{6,7},{7,6},{8,9},{9,8},{10,11... | collective-permute-start | bytes 2506760 | tf_op jit(solution)/shard_map/ppermute | solution.py:796
  117.6 17.8 %collective-permute-start.16 = (bf16[1,512,256]{2,1,0:T(8,128)(2,1)S(1)}, bf16[1,512,256]{2,1,0:T(8,128)(2,1)S(1)}, u32[]{:S(2)}, u32[]{:S(2)}) collective-permute-start(bf16[1,512,256]{2,1,0:T(8,128)(2,1)S(1)} %copy-done.17), channel_id=1, source_target_pairs={{0,8},{8,16},{16,24},{24,0},{1,9},{9,17},{17,25},{25,1},{2,10},{10... | collective-permute-start | bytes 786440 | tf_op jit(solution)/shard_map/ppermute | solution.py:788
  128.4 16.6 %collective-permute-start.17 = (bf16[1,512,256]{2,1,0:T(8,128)(2,1)S(1)}, bf16[1,512,256]{2,1,0:T(8,128)(2,1)S(1)}, u32[]{:S(2)}, u32[]{:S(2)}) collective-permute-start(bf16[1,512,256]{2,1,0:T(8,128)(2,1)S(1)} %copy-done.16), channel_id=1, source_target_pairs={{0,16},{8,24},{16,0},{24,8},{1,17},{9,25},{17,1},{25,9},{2,18},{10... | collective-permute-start | bytes 786440 | tf_op jit(solution)/shard_map/ppermute | solution.py:788
  135.5 12.6 %collective-permute-start.18 = (bf16[1,512,256]{2,1,0:T(8,128)(2,1)S(1)}, bf16[1,512,256]{2,1,0:T(8,128)(2,1)S(1)}, u32[]{:S(2)}, u32[]{:S(2)}) collective-permute-start(bf16[1,512,256]{2,1,0:T(8,128)(2,1)S(1)} %copy-done.15), channel_id=1, source_target_pairs={{0,24},{8,0},{16,8},{24,16},{1,25},{9,1},{17,9},{25,17},{2,26},{10... | collective-permute-start | bytes 786440 | tf_op jit(solution)/shard_map/ppermute | solution.py:788
  137.9 15.3 %copy-start.13 = (bf16[1,512,256]{2,1,0:T(8,128)(2,1)S(1)}, bf16[1,512,256]{2,1,0:T(8,128)(2,1)}, u32[]{:S(2)}) copy-start(bf16[1,512,256]{2,1,0:T(8,128)(2,1)} %get-tuple-element.135) | copy-start | bytes 786436
  137.9 19.5 %copy-start.12 = (bf16[1,512,256]{2,1,0:T(8,128)(2,1)S(1)}, bf16[1,512,256]{2,1,0:T(8,128)(2,1)}, u32[]{:S(2)}) copy-start(bf16[1,512,256]{2,1,0:T(8,128)(2,1)} %get-tuple-element.136) | copy-start | bytes 786436
  148.1 31.0 %collective-permute-start.20 = (bf16[1,512,256]{2,1,0:T(8,128)(2,1)S(1)}, bf16[1,512,256]{2,1,0:T(8,128)(2,1)S(1)}, u32[]{:S(2)}, u32[]{:S(2)}) collective-permute-start(bf16[1,512,256]{2,1,0:T(8,128)(2,1)S(1)} %copy-done.14), channel_id=1, source_target_pairs={{0,8},{8,16},{16,24},{24,0},{1,9},{9,17},{17,25},{25,1},{2,10},{10... | collective-permute-start | bytes 786440 | tf_op jit(solution)/shard_map/ppermute | solution.py:788
  153.3 25.8 %collective-permute-start.21 = (bf16[1,512,256]{2,1,0:T(8,128)(2,1)S(1)}, bf16[1,512,256]{2,1,0:T(8,128)(2,1)S(1)}, u32[]{:S(2)}, u32[]{:S(2)}) collective-permute-start(bf16[1,512,256]{2,1,0:T(8,128)(2,1)S(1)} %copy-done.13), channel_id=1, source_target_pairs={{0,16},{8,24},{16,0},{24,8},{1,17},{9,25},{17,1},{25,9},{2,18},{10... | collective-permute-start | bytes 786440 | tf_op jit(solution)/shard_map/ppermute | solution.py:788
  157.4 21.7 %collective-permute-start.22 = (bf16[1,512,256]{2,1,0:T(8,128)(2,1)S(1)}, bf16[1,512,256]{2,1,0:T(8,128)(2,1)S(1)}, u32[]{:S(2)}, u32[]{:S(2)}) collective-permute-start(bf16[1,512,256]{2,1,0:T(8,128)(2,1)S(1)} %copy-done.12), channel_id=1, source_target_pairs={{0,24},{8,0},{16,8},{24,16},{1,25},{9,1},{17,9},{25,17},{2,26},{10... | collective-permute-start | bytes 786440 | tf_op jit(solution)/shard_map/ppermute | solution.py:788
  159.3 22.2 %collective-permute-start.24 = (bf16[4,1,512,256]{3,2,1,0:T(8,128)(2,1)S(1)}, bf16[4,1,512,256]{3,2,1,0:T(8,128)(2,1)S(1)}, u32[]{:S(2)}, u32[]{:S(2)}) collective-permute-start(bf16[4,1,512,256]{3,2,1,0:T(8,128)(2,1)S(1)} %pad_maximum_fusion.5.own), channel_id=1, source_target_pairs={{0,4},{4,0},{1,5},{5,1},{2,6},{6,2},{3,7},{7,3},{8,12},{12,8},{9,1... | collective-permute-start | bytes 3145736 | tf_op jit(solution)/shard_map/ppermute | solution.py:792
  179.3 22.0 %collective-permute-start.23 = (bf16[4,1,512,256]{3,2,1,0:T(8,128)(2,1)S(1)}, bf16[4,1,512,256]{3,2,1,0:T(8,128)(2,1)S(1)}, u32[]{:S(2)}, u32[]{:S(2)}) collective-permute-start(bf16[4,1,512,256]{3,2,1,0:T(8,128)(2,1)S(1)} %pad_maximum_fusion.4.own), channel_id=1, source_target_pairs={{0,4},{4,0},{1,5},{5,1},{2,6},{6,2},{3,7},{7,3},{8,12},{12,8},{9,1... | collective-permute-start | bytes 3145736 | tf_op jit(solution)/shard_map/ppermute | solution.py:792
  181.1 20.0 %collective-permute-start.48 = (bf16[4,2,4,64,64]{4,3,2,1,0:T(8,128)(2,1)S(1)}, bf16[4,2,4,64,64]{4,3,2,1,0:T(8,128)(2,1)S(1)}, u32[]{:S(2)}, u32[]{:S(2)}) collective-permute-start(bf16[4,2,4,64,64]{4,3,2,1,0:T(8,128)(2,1)S(1)} %dynamic-slice_bitcast_fusion), channel_id=1, source_target_pairs={{0,4},{4,0},{1,5},{5,1},{2,6},{6,2},{3,7},{7,3},{8,12},{12,8},{9,1... | collective-permute-start | bytes 786440 | tf_op jit(solution)/shard_map/ppermute | solution.py:792
  209.4 1.6 collective-permute-start.25
  209.8 7.1 %collective-permute-start.37 = (bf16[2,4,32,256]{3,2,1,0:T(8,128)(2,1)}, bf16[2,4,32,256]{3,2,1,0:T(8,128)(2,1)S(1)}, u32[]{:S(2)}, u32[]{:S(2)}) collective-permute-start(bf16[2,4,32,256]{3,2,1,0:T(8,128)(2,1)} %get-tuple-element.162), channel_id=1, source_target_pairs={{0,4},{4,0},{1,5},{5,1},{2,6},{6,2},{3,7},{7,3},{8,12},{12,8},{9,1... | collective-permute-start | bytes 393224 | tf_op jit(solution)/shard_map/ppermute | solution.py:792
  211.9 46.9 %copy-start.20 = (bf16[4,4,32,256]{3,2,1,0:T(8,128)(2,1)}, bf16[4,4,32,256]{3,2,1,0:T(8,128)(2,1)S(1)}, u32[]{:S(2)}) copy-start(bf16[4,4,32,256]{3,2,1,0:T(8,128)(2,1)S(1)} %pad_maximum_fusion.7) | copy-start | bytes 786436
  211.9 24.0 %collective-permute-start.26 = (bf16[512,256]{1,0:T(8,128)(2,1)S(1)}, bf16[512,256]{1,0:T(8,128)(2,1)S(1)}, u32[]{:S(2)}, u32[]{:S(2)}) collective-permute-start(bf16[512,256]{1,0:T(8,128)(2,1)S(1)} %bitcast.172), channel_id=1, source_target_pairs={{0,16},{8,24},{16,0},{24,8},{1,17},{9,25},{17,1},{25,9},{2,18},{10... | collective-permute-start | bytes 786440 | tf_op jit(solution)/shard_map/ppermute | solution.py:788
  212.1 23.9 %collective-permute-start.49 = (bf16[3,4,64,64]{3,2,1,0:T(8,128)(2,1)S(1)}, bf16[3,4,64,64]{3,2,1,0:T(8,128)(2,1)S(1)}, u32[]{:S(2)}, u32[]{:S(2)}) collective-permute-start(bf16[3,4,64,64]{3,2,1,0:T(8,128)(2,1)S(1)} %get-tuple-element.195), channel_id=1, source_target_pairs={{0,8},{8,16},{16,24},{24,0},{1,9},{9,17},{17,25},{25,1},{2,10},{10... | collective-permute-start | bytes 294920 | tf_op jit(solution)/shard_map/ppermute | solution.py:788
  212.7 32.4 %collective-permute-start.50 = (bf16[3,4,64,64]{3,2,1,0:T(8,128)(2,1)S(1)}, bf16[3,4,64,64]{3,2,1,0:T(8,128)(2,1)S(1)}, u32[]{:S(2)}, u32[]{:S(2)}) collective-permute-start(bf16[3,4,64,64]{3,2,1,0:T(8,128)(2,1)S(1)} %get-tuple-element.194), channel_id=1, source_target_pairs={{0,16},{8,24},{16,0},{24,8},{1,17},{9,25},{17,1},{25,9},{2,18},{10... | collective-permute-start | bytes 294920 | tf_op jit(solution)/shard_map/ppermute | solution.py:788
  215.6 29.6 %collective-permute-start.29 = (bf16[512,256]{1,0:T(8,128)(2,1)S(1)}, bf16[512,256]{1,0:T(8,128)(2,1)S(1)}, u32[]{:S(2)}, u32[]{:S(2)}) collective-permute-start(bf16[512,256]{1,0:T(8,128)(2,1)S(1)} %bitcast.173), channel_id=1, source_target_pairs={{8,0},{16,8},{24,16},{9,1},{17,9},{25,17},{10,2},{18,10},{26,18},{... | collective-permute-start | bytes 786440 | tf_op jit(solution)/shard_map/ppermute | solution.py:811
  216.9 29.6 %collective-permute-start.28 = (bf16[512,256]{1,0:T(8,128)(2,1)S(1)}, bf16[512,256]{1,0:T(8,128)(2,1)S(1)}, u32[]{:S(2)}, u32[]{:S(2)}) collective-permute-start(bf16[512,256]{1,0:T(8,128)(2,1)S(1)} %bitcast.174), channel_id=1, source_target_pairs={{0,8},{8,16},{16,24},{1,9},{9,17},{17,25},{2,10},{10,18},{18,26},{... | collective-permute-start | bytes 786440 | tf_op jit(solution)/shard_map/ppermute | solution.py:810
  221.5 41.8 %copy-start.19 = (bf16[4,4,32,256]{3,2,1,0:T(8,128)(2,1)}, bf16[4,4,32,256]{3,2,1,0:T(8,128)(2,1)S(1)}, u32[]{:S(2)}) copy-start(bf16[4,4,32,256]{3,2,1,0:T(8,128)(2,1)S(1)} %pad_maximum_fusion.8) | copy-start | bytes 786436
  236.0 22.8 %copy-start.31 = (bf16[512,256]{1,0:T(8,128)(2,1)}, bf16[512,256]{1,0:T(8,128)(2,1)S(1)}, u32[]{:S(2)}) copy-start(bf16[512,256]{1,0:T(8,128)(2,1)S(1)} %collective-permute-done.26.h2) | copy-start | bytes 786436
  236.0 20.4 %collective-permute-start.38 = (bf16[512,256]{1,0:T(8,128)(2,1)S(1)}, bf16[512,256]{1,0:T(8,128)(2,1)S(1)}, u32[]{:S(2)}, u32[]{:S(2)}) collective-permute-start(bf16[512,256]{1,0:T(8,128)(2,1)S(1)} %bitcast.168), channel_id=1, source_target_pairs={{0,16},{8,24},{16,0},{24,8},{1,17},{9,25},{17,1},{25,9},{2,18},{10... | collective-permute-start | bytes 786440 | tf_op jit(solution)/shard_map/ppermute | solution.py:788
  236.0 21.9 %collective-permute-start.27 = (bf16[512,256]{1,0:T(8,128)(2,1)S(1)}, bf16[512,256]{1,0:T(8,128)(2,1)S(1)}, u32[]{:S(2)}, u32[]{:S(2)}) collective-permute-start(bf16[512,256]{1,0:T(8,128)(2,1)S(1)} %collective-permute-done.26.h2), channel_id=1, source_target_pairs={{8,0},{16,24},{9,1},{17,25},{10,2},{18,26},{11,3},{19,27},{12,4},{... | collective-permute-start | bytes 786440 | tf_op jit(solution)/shard_map/ppermute | solution.py:816
  245.1 50.0 %collective-permute-start.51 = (bf16[3,4,64,64]{3,2,1,0:T(8,128)(2,1)S(1)}, bf16[3,4,64,64]{3,2,1,0:T(8,128)(2,1)S(1)}, u32[]{:S(2)}, u32[]{:S(2)}) collective-permute-start(bf16[3,4,64,64]{3,2,1,0:T(8,128)(2,1)S(1)} %get-tuple-element.193), channel_id=1, source_target_pairs={{0,24},{8,0},{16,8},{24,16},{1,25},{9,1},{17,9},{25,17},{2,26},{10... | collective-permute-start | bytes 294920 | tf_op jit(solution)/shard_map/ppermute | solution.py:788
  245.2 21.0 %collective-permute-start.41 = (bf16[512,256]{1,0:T(8,128)(2,1)S(1)}, bf16[512,256]{1,0:T(8,128)(2,1)S(1)}, u32[]{:S(2)}, u32[]{:S(2)}) collective-permute-start(bf16[512,256]{1,0:T(8,128)(2,1)S(1)} %bitcast.169), channel_id=1, source_target_pairs={{8,0},{16,8},{24,16},{9,1},{17,9},{25,17},{10,2},{18,10},{26,18},{... | collective-permute-start | bytes 786440 | tf_op jit(solution)/shard_map/ppermute | solution.py:811
  246.5 20.9 %collective-permute-start.40 = (bf16[512,256]{1,0:T(8,128)(2,1)S(1)}, bf16[512,256]{1,0:T(8,128)(2,1)S(1)}, u32[]{:S(2)}, u32[]{:S(2)}) collective-permute-start(bf16[512,256]{1,0:T(8,128)(2,1)S(1)} %bitcast.170), channel_id=1, source_target_pairs={{0,8},{8,16},{16,24},{1,9},{9,17},{17,25},{2,10},{10,18},{18,26},{... | collective-permute-start | bytes 786440 | tf_op jit(solution)/shard_map/ppermute | solution.py:810
  256.4 14.7 %collective-permute-start.39 = (bf16[512,256]{1,0:T(8,128)(2,1)S(1)}, bf16[512,256]{1,0:T(8,128)(2,1)S(1)}, u32[]{:S(2)}, u32[]{:S(2)}) collective-permute-start(bf16[512,256]{1,0:T(8,128)(2,1)S(1)} %collective-permute-done.38.h2), channel_id=1, source_target_pairs={{8,0},{16,24},{9,1},{17,25},{10,2},{18,26},{11,3},{19,27},{12,4},{... | collective-permute-start | bytes 786440 | tf_op jit(solution)/shard_map/ppermute | solution.py:816
  263.3 15.2 %collective-permute-start.33 = (bf16[4,32,1024]{2,1,0:T(8,128)(2,1)}, bf16[4,32,1024]{2,1,0:T(8,128)(2,1)S(1)}, u32[]{:S(2)}, u32[]{:S(2)}) collective-permute-start(bf16[4,32,1024]{2,1,0:T(8,128)(2,1)} %get-tuple-element.160), channel_id=1, source_target_pairs={{0,3},{1,2},{2,1},{3,0},{4,7},{5,6},{6,5},{7,4},{8,11},{9,10},{10,... | collective-permute-start | bytes 786440 | tf_op jit(solution)/shard_map/ppermute | solution.py:1066
  266.2 12.9 %collective-permute-start.32 = (bf16[4,32,1024]{2,1,0:T(8,128)(2,1)}, bf16[4,32,1024]{2,1,0:T(8,128)(2,1)S(1)}, u32[]{:S(2)}, u32[]{:S(2)}) collective-permute-start(bf16[4,32,1024]{2,1,0:T(8,128)(2,1)} %get-tuple-element.159), channel_id=1, source_target_pairs={{0,2},{2,0},{1,3},{3,1},{4,6},{6,4},{5,7},{7,5},{8,10},{10,8},{9,1... | collective-permute-start | bytes 786440 | tf_op jit(solution)/shard_map/ppermute | solution.py:800
  267.4 12.5 %collective-permute-start.31 = (bf16[4,32,1024]{2,1,0:T(8,128)(2,1)}, bf16[4,32,1024]{2,1,0:T(8,128)(2,1)S(1)}, u32[]{:S(2)}, u32[]{:S(2)}) collective-permute-start(bf16[4,32,1024]{2,1,0:T(8,128)(2,1)} %get-tuple-element.158), channel_id=1, source_target_pairs={{0,1},{1,0},{2,3},{3,2},{4,5},{5,4},{6,7},{7,6},{8,9},{9,8},{10,11... | collective-permute-start | bytes 786440 | tf_op jit(solution)/shard_map/ppermute | solution.py:796
  276.4 10.4 %collective-permute-start.44 = (bf16[4,32,1024]{2,1,0:T(8,128)(2,1)}, bf16[4,32,1024]{2,1,0:T(8,128)(2,1)S(1)}, u32[]{:S(2)}, u32[]{:S(2)}) collective-permute-start(bf16[4,32,1024]{2,1,0:T(8,128)(2,1)} %get-tuple-element.167), channel_id=1, source_target_pairs={{0,3},{1,2},{2,1},{3,0},{4,7},{5,6},{6,5},{7,4},{8,11},{9,10},{10,... | collective-permute-start | bytes 786440 | tf_op jit(solution)/shard_map/ppermute | solution.py:1066
  278.6 12.2 %collective-permute-start.43 = (bf16[4,32,1024]{2,1,0:T(8,128)(2,1)}, bf16[4,32,1024]{2,1,0:T(8,128)(2,1)S(1)}, u32[]{:S(2)}, u32[]{:S(2)}) collective-permute-start(bf16[4,32,1024]{2,1,0:T(8,128)(2,1)} %get-tuple-element.166), channel_id=1, source_target_pairs={{0,2},{2,0},{1,3},{3,1},{4,6},{6,4},{5,7},{7,5},{8,10},{10,8},{9,1... | collective-permute-start | bytes 786440 | tf_op jit(solution)/shard_map/ppermute | solution.py:800
  279.1 14.3 %collective-permute-start.42 = (bf16[4,32,1024]{2,1,0:T(8,128)(2,1)}, bf16[4,32,1024]{2,1,0:T(8,128)(2,1)S(1)}, u32[]{:S(2)}, u32[]{:S(2)}) collective-permute-start(bf16[4,32,1024]{2,1,0:T(8,128)(2,1)} %get-tuple-element.165), channel_id=1, source_target_pairs={{0,1},{1,0},{2,3},{3,2},{4,5},{5,4},{6,7},{7,6},{8,9},{9,8},{10,11... | collective-permute-start | bytes 786440 | tf_op jit(solution)/shard_map/ppermute | solution.py:796
  280.8 17.3 %collective-permute-start.34 = (bf16[32,1024]{1,0:T(8,128)(2,1)S(1)}, bf16[32,1024]{1,0:T(8,128)(2,1)S(1)}, u32[]{:S(2)}, u32[]{:S(2)}) collective-permute-start(bf16[32,1024]{1,0:T(8,128)(2,1)S(1)} %get-tuple-element.206), channel_id=1, source_target_pairs={{0,8},{8,16},{16,24},{24,0},{1,9},{9,17},{17,25},{25,1},{2,10},{10... | collective-permute-start | bytes 196616 | tf_op jit(solution)/shard_map/ppermute | solution.py:788
  286.9 15.4 %collective-permute-start.35 = (bf16[32,1024]{1,0:T(8,128)(2,1)S(1)}, bf16[32,1024]{1,0:T(8,128)(2,1)S(1)}, u32[]{:S(2)}, u32[]{:S(2)}) collective-permute-start(bf16[32,1024]{1,0:T(8,128)(2,1)S(1)} %get-tuple-element.205), channel_id=1, source_target_pairs={{0,16},{8,24},{16,0},{24,8},{1,17},{9,25},{17,1},{25,9},{2,18},{10... | collective-permute-start | bytes 196616 | tf_op jit(solution)/shard_map/ppermute | solution.py:788
  290.8 11.5 %collective-permute-start.36 = (bf16[32,1024]{1,0:T(8,128)(2,1)S(1)}, bf16[32,1024]{1,0:T(8,128)(2,1)S(1)}, u32[]{:S(2)}, u32[]{:S(2)}) collective-permute-start(bf16[32,1024]{1,0:T(8,128)(2,1)S(1)} %get-tuple-element.204), channel_id=1, source_target_pairs={{0,24},{8,0},{16,8},{24,16},{1,25},{9,1},{17,9},{25,17},{2,26},{10... | collective-permute-start | bytes 196616 | tf_op jit(solution)/shard_map/ppermute | solution.py:788
  295.1 7.1 %collective-permute-start.45 = (bf16[32,1024]{1,0:T(8,128)(2,1)S(1)}, bf16[32,1024]{1,0:T(8,128)(2,1)S(1)}, u32[]{:S(2)}, u32[]{:S(2)}) collective-permute-start(bf16[32,1024]{1,0:T(8,128)(2,1)S(1)} %get-tuple-element.200), channel_id=1, source_target_pairs={{0,8},{8,16},{16,24},{24,0},{1,9},{9,17},{17,25},{25,1},{2,10},{10... | collective-permute-start | bytes 196616 | tf_op jit(solution)/shard_map/ppermute | solution.py:788
  295.1 8.2 %collective-permute-start.46 = (bf16[32,1024]{1,0:T(8,128)(2,1)S(1)}, bf16[32,1024]{1,0:T(8,128)(2,1)S(1)}, u32[]{:S(2)}, u32[]{:S(2)}) collective-permute-start(bf16[32,1024]{1,0:T(8,128)(2,1)S(1)} %get-tuple-element.199), channel_id=1, source_target_pairs={{0,16},{8,24},{16,0},{24,8},{1,17},{9,25},{17,1},{25,9},{2,18},{10... | collective-permute-start | bytes 196616 | tf_op jit(solution)/shard_map/ppermute | solution.py:788
  298.1 5.3 %collective-permute-start.47 = (bf16[32,1024]{1,0:T(8,128)(2,1)S(1)}, bf16[32,1024]{1,0:T(8,128)(2,1)S(1)}, u32[]{:S(2)}, u32[]{:S(2)}) collective-permute-start(bf16[32,1024]{1,0:T(8,128)(2,1)S(1)} %get-tuple-element.198), channel_id=1, source_target_pairs={{0,24},{8,0},{16,8},{24,16},{1,25},{9,1},{17,9},{25,17},{2,26},{10... | collective-permute-start | bytes 196616 | tf_op jit(solution)/shard_map/ppermute | solution.py:788
  (27 other events, 139.3 us)

commit v6 on v5

--- a/solution.py
+++ b/solution.py
@@ -271,6 +271,7 @@
     return pltpu.CompilerParams(vmem_limit_bytes=VMEM_LIMIT)
 
 
+FIRST_PART = 48
 EXTRA = 16
 
 
@@ -393,6 +394,38 @@
     )(kind, own, rest, ratios, left)
 
 
+def pair_kernel(kind, mix0, mix1, mix2, own, sibling, keys_ref, values_ref):
+    half = pl.program_id(0)
+    for which, out in enumerate((keys_ref, values_ref)):
+        part = None
+        for rel, mixes in enumerate((mix0, mix1, mix2)):
+            at = kind[10 + rel]
+            weight = jnp.where(half == 0, own[at, which], sibling[at, which])
+            new = jnp.dot(mixes[0, which], weight, preferred_element_type=f32)
+            part = new if part is None else part + new
+
+        @pl.when(half == 0)
+        def _():
+            out[...] = part
+
+        @pl.when(half == 1)
+        def _():
+            out[...] += part
+
+
+def pair_product(kind, mixes, own, sibling):
+    rows, width = mixes[0].shape[2], own.shape[3]
+    return pl.pallas_call(
+        pair_kernel,
+        grid=(2,),
+        out_shape=[jax.ShapeDtypeStruct((rows, width), f32)] * 2,
+        in_specs=[in_smem()] + [half_block(mix.shape) for mix in mixes] + [in_vmem()] * 2,
+        out_specs=[pl.BlockSpec((rows, width), lambda i: (0, 0))] * 2,
+        compiler_params=kernel_params(),
+        cost_estimate=takes(8),
+    )(kind, *mixes, own, sibling)
+
+
 def project_kernel(
     kind,
     mix0,
@@ -401,20 +434,24 @@
     low0,
     low1,
     low2,
+    keys_part,
+    values_part,
     own0,
     own1,
     rest0,
     rest1,
     ratios,
     left,
-    own_weight,
-    sibling_weight,
+    own_kv,
+    sibling_kv,
+    own_r,
+    sibling_r,
     right,
     base,
+    recept_ref,
     keys_ref,
     values_ref,
     decay_ref,
-    r_mix,
     gate_mix,
     held,
 ):
@@ -425,87 +462,52 @@
         for half, (own, rest) in enumerate(((own0, rest0), (own1, rest1))):
             gather_blocks(kind, own, rest, held.at[half])
 
-    totals = [None] * 2
-
-    def add(which, rel, half, mixed):
-        weight = (own_weight, sibling_weight)[half][kind[10 + rel], which]
-        part = jnp.dot(mixed, weight, preferred_element_type=f32)
-        totals[which] = part if totals[which] is None else totals[which] + part
-
+    last = kind[13]
+    totals = [jnp.zeros(recept_ref.shape, f32), keys_part[...], values_part[...]]
     squeezed = low0[0] + low0[1] + low1[0] + low1[1] + low2[0] + low2[1]
     for half in range(2):
         here, step = here_and_step(held.at[half], kind[0], kind[1], tile)
+        kv, r = ((own_kv, own_r), (sibling_kv, sibling_r))[half]
 
         def mix(which):
             return (here + ratios[half, which : which + 1, :] * step).astype(bf16)
 
-        r_mix[half] = mix(0)
-        add(0, 3, half, mix(1))
-        add(1, 3, half, mix(2))
+        for which, weight in enumerate((r[last, 0], kv[last, 0], kv[last, 1])):
+            totals[which] += jnp.dot(mix(which), weight, preferred_element_type=f32)
         gate_mix[half] = mix(3)
         squeezed = squeezed + jnp.dot(mix(4), left[half], preferred_element_type=f32)
     for rel, mixes in enumerate((mix0, mix1, mix2)):
         for half in range(2):
-            for which in range(2):
-                add(which, rel, half, mixes[half, which])
-    keys_ref[...] = totals[0]
-    values_ref[...] = totals[1]
+            weight = (own_r, sibling_r)[half][kind[10 + rel], 0]
+            totals[0] += jnp.dot(mixes[half], weight, preferred_element_type=f32)
+    recept_ref[...] = totals[0]
+    keys_ref[...] = totals[1]
+    values_ref[...] = totals[2]
     squeezed = jnp.tanh(squeezed).astype(bf16)
     grown = jnp.dot(squeezed, right[...], preferred_element_type=f32)
     decay_ref[...] = -jnp.exp(base[...] + grown)
 
 
-def projected(kind, mixes, lows, owns, rests, *rest):
-    rows, depth = mixes[0].shape[2:]
-    own_weight = rest[2]
-    width, rank = own_weight.shape[3], lows[0].shape[2]
+def projected(kind, mixes, lows, parts, owns, rests, *rest):
+    rows, depth = mixes[0].shape[1:]
+    width, rank = parts[0].shape[1], lows[0].shape[2]
     flat = jax.ShapeDtypeStruct((rows, width), f32)
-    wide = jax.ShapeDtypeStruct((2, rows, depth), bf16)
     tile_of = pl.BlockSpec((TILE, width), lambda i: (i, 0))
     wide_of = pl.BlockSpec((2, TILE, depth), lambda i: (0, i, 0))
     return pl.pallas_call(
         project_kernel,
         grid=(rows // TILE,),
-        out_shape=[flat] * 3 + [wide] * 2,
+        out_shape=[flat] * 4 + [jax.ShapeDtypeStruct((2, rows, depth), bf16)],
         in_specs=[in_smem()]
-        + [pl.BlockSpec((2, 2, TILE, depth), lambda i: (0, 0, i, 0))] * 3
+        + [wide_of] * 3
         + [pl.BlockSpec((2, TILE, rank), lambda i: (0, i, 0))] * 3
+        + [tile_of] * 2
         + [in_vmem()] * (4 + len(rest)),
-        out_specs=[tile_of] * 3 + [wide_of] * 2,
+        out_specs=[tile_of] * 4 + [wide_of],
         scratch_shapes=[pltpu.VMEM((2, rests[0].shape[0] + 1) + owns[0].shape, bf16)],
         compiler_params=kernel_params(),
-        cost_estimate=takes(12),
-    )(kind, *mixes, *lows, *owns, *rests, *rest)
-
-
-def plain_kernel(kind, mix0, mix1, mix2, mix3, own, sibling, out_ref):
-    half = pl.program_id(0)
-    part = None
-    for rel, mixes in enumerate((mix0, mix1, mix2, mix3)):
-        weight = jnp.where(half == 0, own[kind[10 + rel], 0], sibling[kind[10 + rel], 0])
-        new = jnp.dot(mixes[0], weight, preferred_element_type=f32)
-        part = new if part is None else part + new
-
-    @pl.when(half == 0)
-    def _():
-        out_ref[...] = part
-
-    @pl.when(half == 1)
-    def _():
-        out_ref[...] += part
-
-
-def plain_product(kind, mixes, own, sibling):
-    rows, width = mixes[0].shape[1], own.shape[3]
-    return pl.pallas_call(
-        plain_kernel,
-        grid=(2,),
-        out_shape=jax.ShapeDtypeStruct((rows, width), f32),
-        in_specs=[in_smem()] + [half_block(mix.shape) for mix in mixes] + [in_vmem()] * 2,
-        out_specs=pl.BlockSpec((rows, width), lambda i: (0, 0)),
-        compiler_params=kernel_params(),
-        cost_estimate=takes(6),
-    )(kind, *mixes, own, sibling)
+        cost_estimate=takes(11),
+    )(kind, *mixes, *lows, *parts, *owns, *rests, *rest)
 
 
 def gate_kernel(
@@ -541,7 +543,7 @@
         value = normed[...] * (gate * jax.nn.sigmoid(gate))
         row = lax.broadcasted_iota(jnp.int32, (BLK, value.shape[1]), 0)
         is_long = kind[0] == 1
-        half_rows = BLK // 2
+        cut = kept0.shape[2]
 
         def lived(n):
             block = value[n * BLK : (n + 1) * BLK]
@@ -552,21 +554,24 @@
                 even, odd = lived(4 * line + block), lived(4 * line + 2 + block)
                 kept = jnp.where(is_long, even, odd)
                 sent = jnp.where(is_long, odd, even)
-                kept0[block, line] = kept[:half_rows]
-                kept1[block, line] = kept[half_rows:]
-                sent0[block, line] = sent[:half_rows]
-                sent1[block, line] = sent[half_rows:]
+                kept0[block, line] = kept[:cut]
+                kept1[block, line] = kept[cut:]
+                sent0[block, line] = sent[:cut]
+                sent1[block, line] = sent[cut:]
 
 
 def gated(kind, lengths, mixes, own, sibling, normed):
     rows, width = normed.shape
-    quarter = jax.ShapeDtypeStruct((2, rows // TILE, BLK // 2, width), bf16)
+    outs = [
+        jax.ShapeDtypeStruct((2, rows // TILE, part, width), bf16)
+        for part in (FIRST_PART, FIRST_PART, BLK - FIRST_PART, BLK - FIRST_PART)
+    ]
     return pl.pallas_call(
         gate_kernel,
         grid=(2,),
-        out_shape=[quarter] * 4,
+        out_shape=outs,
         in_specs=[in_smem()] * 2 + [half_block(mix.shape) for mix in mixes] + [in_vmem()] * 3,
-        out_specs=[pl.BlockSpec(quarter.shape, lambda i: (0, 0, 0, 0))] * 4,
+        out_specs=[pl.BlockSpec(out.shape, lambda i: (0, 0, 0, 0)) for out in outs],
         scratch_shapes=[pltpu.VMEM((rows, width), f32)],
         compiler_params=kernel_params(),
         cost_estimate=takes(7),
@@ -760,18 +765,21 @@
 
 def lay_kernel(at, *refs):
     pieces, out_ref = refs[:-1], refs[-1]
-    rows, width = pieces[0].shape
+    width = pieces[0].shape[1]
     lines = out_ref.shape[1] // width
+    row = 0
     for n, piece in enumerate(pieces):
         column = pl.multiple_of(at[n % lines] * width, width)
-        out_ref[n // lines * rows : (n // lines + 1) * rows, pl.ds(column, width)] = piece[...]
+        out_ref[row : row + piece.shape[0], pl.ds(column, width)] = piece[...]
+        if n % lines == lines - 1:
+            row += piece.shape[0]
 
 
 def laid(at, pieces, lines):
-    rows, width = pieces[0].shape
+    rows, width = sum(piece.shape[0] for piece in pieces) // lines, pieces[0].shape[1]
     return pl.pallas_call(
         lay_kernel,
-        out_shape=jax.ShapeDtypeStruct((len(pieces) // lines * rows, lines * width), bf16),
+        out_shape=jax.ShapeDtypeStruct((rows, lines * width), bf16),
         in_specs=[in_smem()] + [in_vmem()] * len(pieces),
         out_specs=in_vmem(),
         compiler_params=kernel_params(),
@@ -926,9 +934,25 @@
     one, two, three = near_along(block)
     own_x, own_y = over_x(block), over_y(block)
     one, two, three, own_x, own_y = lax.optimization_barrier((one, two, three, own_x, own_y))
+    def blocks_of(*weights):
+        stacked = jnp.stack(weights)
+        return tuple(
+            lax.dynamic_slice_in_dim(stacked, (z + k) % lines * width, width, 2)
+            for k in range(lines)
+        )
+
+    def both_cores(*pieces):
+        own = jnp.stack(pieces)
+        return own, flipped_core(own)
+
+    kv = blocks_of(lookup_transform, payload_transform)
+    r = blocks_of(acceptance_transform)
+    gate = blocks_of(gating_transform)
+    kv = after(kv, two)
     far = far_along(two)
     own_xy = (over_y(own_x[0]), over_x(own_y[1]))
-    far, own_xy = lax.optimization_barrier((far, own_xy))
+    kv_two = turned(kv[2], "z", 2)
+    far, own_xy, kv_two, kv, r = lax.optimization_barrier((far, own_xy, kv_two, kv, r))
     rest = jnp.stack([jnp.where(z == 0, far, one), two, jnp.where(z == 3, far, three)], axis=1)
     rest_x, rest_y = over_x(rest), over_y(rest)
     extents = in_order(
@@ -947,27 +971,17 @@
     ratios = [part.transpose(0, 2, 1) for part in chunk_order(token_mixing_ratios.T)]
     left = chunk_order(fading_left_factor)
 
-    def columns_of(weights, *ready):
-        stacked = jnp.stack(weights)
-        blocks = [
-            lax.dynamic_slice_in_dim(stacked, (z + k) % lines * width, width, 2)
-            for k in range(lines)
-        ]
-        blocks = lax.optimization_barrier((tuple(blocks),) + ready)[0]
-        return (blocks[0],) + tuple(turned(blocks[k], "z", k) for k in range(1, lines))
-
-    def both_cores(pieces):
-        own = jnp.stack(pieces)
-        return own, flipped_core(own)
-
-    kv_pieces = columns_of([lookup_transform, payload_transform], rest, own_xy)
-    kv_pieces, rest_x, rest_y = lax.optimization_barrier((kv_pieces, rest_x, rest_y))
+    kv_one, kv_three = turned(kv[1], "z", 1), turned(kv[3], "z", 3)
+    r_two = turned(r[2], "z", 2)
+    rest_x, rest_y, kv_one, kv_three, r_two, r = lax.optimization_barrier(
+        (rest_x, rest_y, kv_one, kv_three, r_two, r)
+    )
     rest_xy = (over_y(rest_x[0]), over_x(rest_y[1]))
-    r_pieces = columns_of([acceptance_transform], rest_x, rest_y, kv_pieces)
-    own_kv, sibling_kv = both_cores(kv_pieces)
-    rest_xy, r_pieces = lax.optimization_barrier((rest_xy, r_pieces))
-    gate_pieces = columns_of([gating_transform], r_pieces, rest_xy)
-    own_r, sibling_r = both_cores(r_pieces)
+    own_kv, sibling_kv = both_cores(kv[0], kv_one, kv_two, kv_three)
+    r_one, r_three = turned(r[1], "z", 1), turned(r[3], "z", 3)
+    rest_xy, r_one, r_three, gate = lax.optimization_barrier((rest_xy, r_one, r_three, gate))
+    own_r, sibling_r = both_cores(r[0], r_one, r_two, r_three)
+    gate_pieces = (gate[0],) + tuple(turned(gate[k], "z", k) for k in range(1, lines))
 
     def mine_of(vector):
         return lax.dynamic_slice_in_dim(vector, z * width, width, 0)[None]
@@ -975,20 +989,23 @@
     kv0, r0, gate0, low0 = mixes_of(kind, block, rest, ratios[0], left[0])
     kv1, r1, gate1, low1 = mixes_of(kind, own_x, rest_x, ratios[1], left[1])
     kv2, r2, gate2, low2 = mixes_of(kind, own_y, rest_y, ratios[2], left[2])
-    keys, values, decay, r3, gate3 = projected(
+    parts = pair_product(kind, (kv0, kv1, kv2), own_kv, sibling_kv)
+    recept, keys, values, decay, gate3 = projected(
         kind,
-        (kv0, kv1, kv2),
+        (r0, r1, r2),
         (low0, low1, low2),
+        parts,
         own_xy,
         rest_xy,
         ratios[3],
         left[3],
         own_kv,
         sibling_kv,
+        own_r,
+        sibling_r,
         lax.dynamic_slice_in_dim(fading_right_factor, z * width, width, 1),
         mine_of(fading_baseline),
     )
-    recept = plain_product(kind, (r0, r1, r2, r3), own_r, sibling_r)
     entered = lax.dynamic_slice_in_dim(carried_memory, z * heads, heads, 0)
     bonus = lax.dynamic_slice_in_dim(present_reward, z * heads, heads, 0).reshape(1, width)
     states, states_in = states_of(
@@ -999,6 +1016,15 @@
         decay,
         jnp.where(is_long, entered, 0.0),
     )
+    states = states.reshape(lines, 2, requests, heads, span, span)
+    passed = flipped_core(lax.dynamic_index_in_dim(states, 1 - core, 1, keepdims=False))
+    held = lax.dynamic_index_in_dim(states, core, 1, keepdims=False)
+    bundle = jnp.concatenate(
+        [jnp.where(is_long, held, passed)[:, -1:], jnp.where(is_long, passed, held)], axis=1
+    ).astype(bf16)
+    bundle = after(bundle, gate_pieces)
+    states_in = after(states_in, bundle)
+    arrived = dealt(lambda j: lax.dynamic_index_in_dim(bundle, j, 0, keepdims=False), z)
     normed = sweep(
         extents,
         recept,
@@ -1010,21 +1036,13 @@
         mine_of(group_layer_scaling),
         mine_of(group_layer_shift_term),
     )
-    own_gate, sibling_gate = both_cores(after(gate_pieces, states))
+    own_gate, sibling_gate = both_cores(*after(gate_pieces, states))
+    normed, arrived = lax.optimization_barrier((normed, arrived))
     kept0, sent0, kept1, sent1 = gated(
         kind, extents, (gate0, gate1, gate2, gate3), own_gate, sibling_gate, normed
     )
 
-    states = states.reshape(lines, 2, requests, heads, span, span)
-    passed = flipped_core(lax.dynamic_index_in_dim(states, 1 - core, 1, keepdims=False))
-    held = lax.dynamic_index_in_dim(states, core, 1, keepdims=False)
-    bundle = jnp.concatenate(
-        [jnp.where(is_long, held, passed)[:, -1:], jnp.where(is_long, passed, held)], axis=1
-    ).astype(bf16)
-    bundle = after(bundle, gate_pieces)
-    arrived = in_order(
-        dealt(lambda j: lax.dynamic_index_in_dim(bundle, j, 0, keepdims=False), z), z
-    ).astype(f32)
+    arrived = in_order(arrived, z).astype(f32)
     span_states = arrived[:, 0].reshape(1, lines * heads, span, span)
     request_states = jnp.swapaxes(arrived[:, 1:], 0, 1).reshape(
         requests, lines * heads, span, span
@@ -1052,7 +1070,7 @@
     spreads = []
     for kept, sent in ((kept0, sent0), (kept1, sent1)):
         part = jnp.concatenate([kept, flipped_core(sent)], axis=0)
-        part = part.reshape(2 * rows // 4, width)
+        part = part.reshape(-1, width)
         if spreads:
             part = after(part, spreads[0][2])
         spreads.append(spread_along(part, z))

time: 307 us -> 329 us (1.072)
  waiting for transfers between devices: 86.8 us -> 103 us
  starting transfers between devices: 94.9 us -> 88 us
  Pallas kernels: 81.1 us -> 86.6 us
  other arithmetic: 17.7 us -> 21.7 us
    ppermute x21, waiting for transfers between devices: 59.8 us -> 77.9 us  [turned(): lax.ppermute(x, axis, [(i, (i + by) % length) for i in range(length)])]
    ppermute x3, waiting for transfers between devices: 14.1 us -> 5.85 us  [far_along(): return lax.ppermute(two, 'z', [(1, 0), (2, 3)])]
    pallas_call x4, Pallas kernels: 29.8 us -> 35 us  [the longest x1 13.5 us: pair_product(): pl.pallas_call(pair_kernel, grid=(2,), out_shape=[jax.ShapeDtypeStruct((r...]
    ppermute x6, waiting for transfers between devices: 2.29 us -> 7.28 us  [over_x(): return lax.ppermute(x, 'x', [(0, 1), (1, 0)])]
    ppermute x2, starting transfers between devices: 4.29 us -> 0.94 us  [on_core(): across = lax.ppermute(to_xy, ('y', 'x'), [(i, 3 - i) for i in range(4)])]
  transfers between devices with their start and end apart: 52 -> 52, of which waited for: 17 -> 20; matrix products, arithmetic and copies ran while one was open for 11% -> 12% of each run, Pallas kernels for 22% -> 25%
where the time goes in v6:
time: 329 us; the launch traced here: 328 us
  waiting for transfers between devices  103 us (31%)
  starting transfers between devices  88 us (27%)
  Pallas kernels  86.6 us (26%)
  local copies, waits for them, and re-layouts  26.9 us (8%)
  other arithmetic  21.7 us (7%)
    ppermute x21, waiting for transfers between devices, turned(): lax.ppermute(x, axis, [(i, (i + by) % length) for i in range(length)])  77.9 us
    ppermute x21, starting transfers between devices, turned(): lax.ppermute(x, axis, [(i, (i + by) % length) for i in range(length)])  45.4 us
    pallas_call x3, Pallas kernels, mixes_of(): pl.pallas_call(mix_kernel, grid=(2,), out_shape=outs, in_specs=[in_smem()...  20.9 us
    ppermute x3, starting transfers between devices, near_along(): one = lax.ppermute(piece, 'z', [(0, 1), (1, 2), (2, 3)])  16.8 us
    pallas_call x1, Pallas kernels, pair_product(): pl.pallas_call(pair_kernel, grid=(2,), out_shape=[jax.ShapeDtypeStruct((r...  13.5 us
    pallas_call x1, Pallas kernels, projected(): pl.pallas_call(project_kernel, grid=(rows // TILE,), out_shape=[flat] * 4...  12.4 us
    pallas_call x1, Pallas kernels, sweep(): pl.pallas_call(sweep_kernel, out_shape=jax.ShapeDtypeStruct(r.shape, f32)...  11.9 us
    pallas_call x2, Pallas kernels, final_product(): pl.pallas_call(final_kernel, out_shape=[out] * 4, in_specs=[in_smem()] +...  9.15 us
  transfers between devices with their start and end apart: 52, of which 20 were waited for; matrix products, arithmetic and copies ran while one was open for 12% of the time, Pallas kernels for 25%

profile of v6, /device:TPU:0, one launch (start us, length us, event | category | flops | bytes accessed | tf_op | source)
XLA Modules:
  0.0 328.0 jit_solution(11627142654043974487)
XLA Ops:
  1.5 1.8 shard_map.184
  5.9 2.0 shard_map.185.own
  7.9 5.0 %collective-permute-start.1 = (bf16[2,272,512]{2,1,0:T(8,128)(2,1)}, bf16[2,272,512]{2,1,0:T(8,128)(2,1)S(1)}, u32[]{:S(2)}, u32[]{:S(2)}) collective-permute-start(bf16[2,272,512]{2,1,0:T(8,128)(2,1)} %shard_map.185.own), channel_id=1, source_target_pairs={{0,8},{8,16},{16,24},{1,9},{9,17},{17,25},{2,10},{10,18},{18,26},{... | collective-permute-start | bytes 1671176 | tf_op jit(solution)/shard_map/ppermute | solution.py:818
  12.9 2.6 collective-permute-start.2
  16.8 1.6 collective-permute-start.4
  18.4 1.5 collective-permute-start.5
  26.5 15.1 %collective-permute-done.2 = bf16[2,272,512]{2,1,0:T(8,128)(2,1)S(1)} collective-permute-done((bf16[2,272,512]{2,1,0:T(8,128)(2,1)}, bf16[2,272,512]{2,1,0:T(8,128)(2,1)S(1)}, u32[]{:S(2)}, u32[]{:S(2)}) %collective-permute-start.2) | collective-permute-done | bytes 557088 | tf_op jit(solution)/shard_map/ppermute | solution.py:796
  42.6 1.3 collective-permute-start.6
  43.9 1.6 collective-permute-start.7
  45.5 12.2 %collective-permute-start.9 = (bf16[2,512,256]{2,1,0:T(8,128)(2,1)S(1)}, bf16[2,512,256]{2,1,0:T(8,128)(2,1)S(1)}, u32[]{:S(2)}, u32[]{:S(2)}) collective-permute-start(bf16[2,512,256]{2,1,0:T(8,128)(2,1)S(1)} %get-tuple-element.104), channel_id=1, source_target_pairs={{0,16},{8,24},{16,0},{24,8},{1,17},{9,25},{17,1},{25,9},{2,18},{10... | collective-permute-start | bytes 1572872 | tf_op jit(solution)/shard_map/ppermute | solution.py:796
  57.7 1.6 collective-permute-start.8
  59.2 1.6 dynamic-slice_select_fusion.s_ref
  60.8 3.9 %collective-permute-done.8.own1 = bf16[272,512]{1,0:T(8,128)(2,1)S(1)} collective-permute-done((bf16[272,512]{1,0:T(8,128)(2,1)S(1)}, bf16[272,512]{1,0:T(8,128)(2,1)S(1)}, u32[]{:S(2)}, u32[]{:S(2)}) %collective-permute-start.8) | collective-permute-done | bytes 278560 | tf_op jit(solution)/shard_map/ppermute | solution.py:804
  64.8 14.9 %collective-permute-done.9 = bf16[2,512,256]{2,1,0:T(8,128)(2,1)S(1)} collective-permute-done((bf16[2,512,256]{2,1,0:T(8,128)(2,1)S(1)}, bf16[2,512,256]{2,1,0:T(8,128)(2,1)S(1)}, u32[]{:S(2)}, u32[]{:S(2)}) %collective-permute-start.9) | collective-permute-done | bytes 524320 | tf_op jit(solution)/shard_map/ppermute | solution.py:796
  80.7 1.4 pad_maximum_fusion.3.rest
  82.0 1.5 collective-permute-start.10
  84.7 1.3 dynamic_slice.158
  87.0 2.2 reverse_select_fusion.1
  89.3 3.8 %collective-permute-start.13 = (bf16[2,512,256]{2,1,0:T(8,128)(2,1)}, bf16[2,512,256]{2,1,0:T(8,128)(2,1)}, u32[]{:S(2)}, u32[]{:S(2)}) collective-permute-start(bf16[2,512,256]{2,1,0:T(8,128)(2,1)} %get-tuple-element.116), channel_id=1, source_target_pairs={{0,24},{8,0},{16,8},{24,16},{1,25},{9,1},{17,9},{25,17},{2,26},{10... | collective-permute-start | bytes 1572872 | tf_op jit(solution)/shard_map/ppermute | solution.py:796
  93.1 6.8 %shard_map.186 = (bf16[2,2,1024,512]{3,2,1,0:T(8,128)(2,1)}, bf16[2,1024,512]{2,1,0:T(8,128)(2,1)}, bf16[2,1024,512]{2,1,0:T(8,128)(2,1)}, f32[2,1024,128]{2,1,0:T(8,128)}) custom-call(s32[14]{0:T(128)} %stack.166.kind, bf16[2,272,512]{2,1,0:T(8,128)(2,1)} %shard_map.185.own, bf16[2,3,272,512]{3,2,1,0:T(8,128)(2,1)} %pad_maximum_fusion.3.rest, ...), custom_call_target="tpu_custom_call" | custom-call | flops 8049999872 | bytes 21000000 | tf_op jit(solution)/shard_map/pallas_call | solution.py:385
  100.1 24.1 %collective-permute-done.14 = bf16[1,512,256]{2,1,0:T(8,128)(2,1)} collective-permute-done((bf16[1,512,256]{2,1,0:T(8,128)(2,1)}, bf16[1,512,256]{2,1,0:T(8,128)(2,1)}, u32[]{:S(2)}, u32[]{:S(2)}) %collective-permute-start.14) | collective-permute-done | bytes 262176 | tf_op jit(solution)/shard_map/ppermute | solution.py:796
  125.0 1.5 pad_maximum_fusion.own.own_kv
  126.6 2.9 slice_bitcast_fusion.1
  129.5 1.5 collective-permute-start.16
  131.0 2.1 slice_bitcast_fusion
  134.3 3.8 %collective-permute-start.19 = (bf16[1,512,256]{2,1,0:T(8,128)(2,1)S(1)}, bf16[1,512,256]{2,1,0:T(8,128)(2,1)S(1)}, u32[]{:S(2)}, u32[]{:S(2)}) collective-permute-start(bf16[1,512,256]{2,1,0:T(8,128)(2,1)S(1)} %copy-done.18), channel_id=1, source_target_pairs={{0,24},{8,0},{16,8},{24,16},{1,25},{9,1},{17,9},{25,17},{2,26},{10... | collective-permute-start | bytes 786440 | tf_op jit(solution)/shard_map/ppermute | solution.py:796
  138.2 6.9 %shard_map.187 = (bf16[2,2,1024,512]{3,2,1,0:T(8,128)(2,1)}, bf16[2,1024,512]{2,1,0:T(8,128)(2,1)}, bf16[2,1024,512]{2,1,0:T(8,128)(2,1)}, f32[2,1024,128]{2,1,0:T(8,128)}) custom-call(s32[14]{0:T(128)} %stack.166.kind, bf16[2,272,512]{2,1,0:T(8,128)(2,1)} %copy-done.22, bf16[2,3,272,512]{3,2,1,0:T(8,128)(2,1)} %collective-permute-done.10.rest, ...), custom_call_target="tpu_custom_call" | custom-call | flops 8049999872 | bytes 21000000 | tf_op jit(solution)/shard_map/pallas_call | solution.py:385
  145.4 2.0 collective-permute-done.19
  147.3 2.7 collective-permute-done.16.rest0
  150.0 3.3 %collective-permute-done.17.rest1 = bf16[3,272,512]{2,1,0:T(8,128)(2,1)} collective-permute-done((bf16[3,272,512]{2,1,0:T(8,128)(2,1)}, bf16[3,272,512]{2,1,0:T(8,128)(2,1)}, u32[]{:S(2)}, u32[]{:S(2)}) %collective-permute-start.17) | collective-permute-done | bytes 835616 | tf_op jit(solution)/shard_map/ppermute | solution.py:804
  154.6 7.2 %shard_map.188 = (bf16[2,2,1024,512]{3,2,1,0:T(8,128)(2,1)}, bf16[2,1024,512]{2,1,0:T(8,128)(2,1)}, bf16[2,1024,512]{2,1,0:T(8,128)(2,1)}, f32[2,1024,128]{2,1,0:T(8,128)}) custom-call(s32[14]{0:T(128)} %stack.166.kind, bf16[2,272,512]{2,1,0:T(8,128)(2,1)} %copy-done.21, bf16[2,3,272,512]{3,2,1,0:T(8,128)(2,1)} %collective-permute-done.11.rest, ...), custom_call_target="tpu_custom_call" | custom-call | flops 8049999872 | bytes 21000000 | tf_op jit(solution)/shard_map/pallas_call | solution.py:385
  161.8 1.7 collective-permute-start.22
  163.5 2.3 collective-permute-start.23
  165.9 13.5 %shard_map.189 = (f32[1024,256]{1,0:T(8,128)}, f32[1024,256]{1,0:T(8,128)}) custom-call(s32[14]{0:T(128)} %stack.166.kind, bf16[2,2,1024,512]{3,2,1,0:T(8,128)(2,1)} %get-tuple-element.131.mix0, bf16[2,2,1024,512]{3,2,1,0:T(8,128)(2,1)} %get-tuple-element.132.mix1, bf16[2,2,1024,512]{3,2,1,0:T(8,128)(2,1)} %get-tuple-element.133.mix2, ...), custom_call_target="tpu_custom_call" | custom-call | flops 9200000000 | bytes 24000000 | tf_op jit(solution)/shard_map/pallas_call | solution.py:418
  180.3 12.4 %shard_map.190 = (f32[1024,256]{1,0:T(8,128)}, f32[1024,256]{1,0:T(8,128)}, f32[1024,256]{1,0:T(8,128)}, f32[1024,256]{1,0:T(8,128)}, bf16[2,1024,512]{2,1,0:T(8,128)(2,1)}) custom-call(s32[14]{0:T(128)} %stack.166.kind, bf16[2,1024,512]{2,1,0:T(8,128)(2,1)} %get-tuple-element.125.mix0, bf16[2,1024,512]{2,1,0:T(8,128)(2,1)} %get-tuple-element.126.mix1, ...), custom_call_target="tpu_custom_call" | custom-call | flops 12650000384 | bytes 33000000 | tf_op jit(solution)/shard_map/pallas_call | solution.py:497
  192.8 5.9 %shard_map.191 = (f32[16,4,64,64]{3,2,1,0:T(8,128)}, bf16[16,64,256]{2,1,0:T(8,128)(2,1)}) custom-call(s32[16]{0:T(128)} %select_n.368.lengths, f32[1]{0:T(128)} %bitcast.66.carry, f32[1024,256]{1,0:T(8,128)} %get-tuple-element.158.k_ref, f32[1024,256]{1,0:T(8,128)} %get-tuple-element.159.v_ref, f32[1024,256]{1,0:T(8,128)} %get-tuple-element.160.w_ref, ...), custom_call_target="tpu_custom_call" | custom-call | flops 8049999872 | bytes 21000000 | tf_op jit(solution)/shard_map/pallas_call | solution.py:640
  198.7 1.3 dynamic-slice_bitcast_fusion
  202.0 1.3 dynamic_slice.163
  203.3 1.3 dynamic_slice.164
  206.5 1.6 select_convert_fusion
  208.8 1.5 collective-permute-start.27
  210.3 2.8 collective-permute-start.28
  213.2 11.9 %shard_map.192.normed = f32[1024,256]{1,0:T(8,128)} custom-call(s32[16]{0:T(128)} %select_n.368.lengths, f32[1024,256]{1,0:T(8,128)} %get-tuple-element.167.r_ref, f32[1024,256]{1,0:T(8,128)} %get-tuple-element.158.k_ref, f32[1024,256]{1,0:T(8,128)} %get-tuple-element.159.v_ref, f32[1024,256]{1,0:T(8,128)} %get-tuple-element.160.w_ref, ...), custom_call_target="tpu_custom_call" | custom-call | flops 13799999488 | bytes 36000000 | tf_op jit(solution)/shard_map/pallas_call | solution.py:726
  226.8 7.1 %shard_map.193 = (bf16[2,4,48,256]{3,2,1,0:T(8,128)(2,1)}, bf16[2,4,48,256]{3,2,1,0:T(8,128)(2,1)}, bf16[2,4,16,256]{3,2,1,0:T(8,128)(2,1)}, bf16[2,4,16,256]{3,2,1,0:T(8,128)(2,1)}) custom-call(s32[14]{0:T(128)} %stack.166.kind, s32[16]{0:T(128)} %select_n.368.lengths, bf16[2,1024,512]{2,1,0:T(8,128)(2,1)} %get-tuple-element.114.mix0, ...), custom_call_target="tpu_custom_call" | custom-call | flops 8049999872 | bytes 21000000 | tf_op jit(solution)/shard_map/pallas_call | solution.py:569
  235.7 2.9 collective-permute-start.30
  239.4 1.6 pad_maximum_fusion.2.weight
  241.0 15.4 %collective-permute-done.30.h2 = bf16[768,256]{1,0:T(8,128)(2,1)S(1)} collective-permute-done((bf16[768,256]{1,0:T(8,128)(2,1)S(1)}, bf16[768,256]{1,0:T(8,128)(2,1)S(1)}, u32[]{:S(2)}, u32[]{:S(2)}) %collective-permute-start.30) | collective-permute-done | bytes 393248 | tf_op jit(solution)/shard_map/ppermute | solution.py:796
  258.0 6.6 %collective-permute-start.44 = (bf16[256,256]{1,0:T(8,128)(2,1)S(1)}, bf16[256,256]{1,0:T(8,128)(2,1)S(1)}, u32[]{:S(2)}, u32[]{:S(2)}) collective-permute-start(bf16[256,256]{1,0:T(8,128)(2,1)S(1)} %bitcast.174), channel_id=1, source_target_pairs={{0,8},{8,16},{16,24},{1,9},{9,17},{17,25},{2,10},{10,18},{18,26},{... | collective-permute-start | bytes 393224 | tf_op jit(solution)/shard_map/ppermute | solution.py:818
  268.3 5.2 %collective-permute-start.32 = (bf16[768,256]{1,0:T(8,128)(2,1)S(1)}, bf16[768,256]{1,0:T(8,128)(2,1)S(1)}, u32[]{:S(2)}, u32[]{:S(2)}) collective-permute-start(bf16[768,256]{1,0:T(8,128)(2,1)S(1)} %bitcast.167), channel_id=1, source_target_pairs={{0,8},{8,16},{16,24},{1,9},{9,17},{17,25},{2,10},{10,18},{18,26},{... | collective-permute-start | bytes 1179656 | tf_op jit(solution)/shard_map/ppermute | solution.py:818
  273.5 1.5 collective-permute-start.31
  275.8 3.7 %shard_map.195 = (bf16[4,16,1024]{2,1,0:T(8,128)(2,1)}, bf16[4,16,1024]{2,1,0:T(8,128)(2,1)}, bf16[4,16,1024]{2,1,0:T(8,128)(2,1)}, bf16[4,16,1024]{2,1,0:T(8,128)(2,1)}) custom-call(s32[4]{0:T(128)} %pad_add_fusion.1.block_of, bf16[256,256]{1,0:T(8,128)(2,1)} %bitcast.175, bf16[256,256]{1,0:T(8,128)(2,1)} %get-tuple-element.234.h1, ...), custom_call_target="tpu_custom_call" | custom-call | flops 5175000064 | bytes 13500000 | tf_op jit(solution)/shard_map/pallas_call | solution.py:755
  279.9 1.5 collective-permute-start.47
  283.0 5.8 %collective-permute-done.31 = bf16[768,256]{1,0:T(8,128)(2,1)S(1)} collective-permute-done((bf16[768,256]{1,0:T(8,128)(2,1)S(1)}, bf16[768,256]{1,0:T(8,128)(2,1)S(1)}, u32[]{:S(2)}, u32[]{:S(2)}) %collective-permute-start.31) | collective-permute-done | bytes 393248 | tf_op jit(solution)/shard_map/ppermute | solution.py:824
  289.8 5.5 %shard_map.194 = (bf16[4,48,1024]{2,1,0:T(8,128)(2,1)}, bf16[4,48,1024]{2,1,0:T(8,128)(2,1)}, bf16[4,48,1024]{2,1,0:T(8,128)(2,1)}, bf16[4,48,1024]{2,1,0:T(8,128)(2,1)}) custom-call(s32[4]{0:T(128)} %pad_add_fusion.1.block_of, bf16[768,256]{1,0:T(8,128)(2,1)} %bitcast.168, bf16[768,256]{1,0:T(8,128)(2,1)} %get-tuple-element.228.h1, ...), custom_call_target="tpu_custom_call" | custom-call | flops 5175000064 | bytes 13500000 | tf_op jit(solution)/shard_map/pallas_call | solution.py:755
  295.7 1.5 collective-permute-start.36
  297.2 1.5 collective-permute-start.35
  299.5 3.9 %collective-permute-start.50 = (bf16[16,1024]{1,0:T(8,128)(2,1)S(1)}, bf16[16,1024]{1,0:T(8,128)(2,1)S(1)}, u32[]{:S(2)}, u32[]{:S(2)}) collective-permute-start(bf16[16,1024]{1,0:T(8,128)(2,1)S(1)} %get-tuple-element.230), channel_id=1, source_target_pairs={{0,16},{8,24},{16,0},{24,8},{1,17},{9,25},{17,1},{25,9},{2,18},{10... | collective-permute-start | bytes 98312 | tf_op jit(solution)/shard_map/ppermute | solution.py:796
  303.4 5.0 %collective-permute-done.37 = bf16[4,48,1024]{2,1,0:T(8,128)(2,1)S(1)} collective-permute-done((bf16[4,48,1024]{2,1,0:T(8,128)(2,1)}, bf16[4,48,1024]{2,1,0:T(8,128)(2,1)S(1)}, u32[]{:S(2)}, u32[]{:S(2)}) %collective-permute-start.37) | collective-permute-done | bytes 393248 | tf_op jit(solution)/shard_map/ppermute | solution.py:1084
  308.4 3.4 %collective-permute-start.51 = (bf16[16,1024]{1,0:T(8,128)(2,1)S(1)}, bf16[16,1024]{1,0:T(8,128)(2,1)S(1)}, u32[]{:S(2)}, u32[]{:S(2)}) collective-permute-start(bf16[16,1024]{1,0:T(8,128)(2,1)S(1)} %get-tuple-element.229), channel_id=1, source_target_pairs={{0,24},{8,0},{16,8},{24,16},{1,25},{9,1},{17,9},{25,17},{2,26},{10... | collective-permute-start | bytes 98312 | tf_op jit(solution)/shard_map/ppermute | solution.py:796
  311.8 1.5 collective-permute-done.36
  315.3 3.2 collective-permute-start.39
  321.1 1.7 collective-permute-done.38.refs_1_
  322.9 2.5 collective-permute-done.39.refs_2_
  326.1 1.9 shard_map.196
  (208 shorter events, 44.3 us)
Async XLA Ops:
  0.6 83.4 %copy-start = (bf16[128,1024]{1,0:T(8,128)(2,1)S(1)}, bf16[128,1024]{1,0:T(8,128)(2,1)}, u32[]{:S(2)}) copy-start(bf16[128,1024]{1,0:T(8,128)(2,1)} %param.29) | copy-start | bytes 786436
  3.3 1.9 collective-permute-start
  5.0 16.1 %copy-start.4 = (bf16[512,1024]{1,0:T(8,128)(2,1)S(1)}, bf16[512,1024]{1,0:T(8,128)(2,1)}, u32[]{:S(2)}) copy-start(bf16[512,1024]{1,0:T(8,128)(2,1)} %param.23) | copy-start | bytes 3145732
  7.9 18.6 %collective-permute-start.1 = (bf16[2,272,512]{2,1,0:T(8,128)(2,1)}, bf16[2,272,512]{2,1,0:T(8,128)(2,1)S(1)}, u32[]{:S(2)}, u32[]{:S(2)}) collective-permute-start(bf16[2,272,512]{2,1,0:T(8,128)(2,1)} %shard_map.185.own), channel_id=1, source_target_pairs={{0,8},{8,16},{16,24},{1,9},{9,17},{17,25},{2,10},{10,18},{18,26},{... | collective-permute-start | bytes 1671176 | tf_op jit(solution)/shard_map/ppermute | solution.py:818
  12.9 28.6 %collective-permute-start.2 = (bf16[2,272,512]{2,1,0:T(8,128)(2,1)}, bf16[2,272,512]{2,1,0:T(8,128)(2,1)S(1)}, u32[]{:S(2)}, u32[]{:S(2)}) collective-permute-start(bf16[2,272,512]{2,1,0:T(8,128)(2,1)} %shard_map.185.own), channel_id=1, source_target_pairs={{0,16},{8,24},{16,0},{24,8},{1,17},{9,25},{17,1},{25,9},{2,18},{10... | collective-permute-start | bytes 1671176 | tf_op jit(solution)/shard_map/ppermute | solution.py:796
  15.5 27.1 %collective-permute-start.3 = (bf16[2,272,512]{2,1,0:T(8,128)(2,1)}, bf16[2,272,512]{2,1,0:T(8,128)(2,1)S(1)}, u32[]{:S(2)}, u32[]{:S(2)}) collective-permute-start(bf16[2,272,512]{2,1,0:T(8,128)(2,1)} %shard_map.185.own), channel_id=1, source_target_pairs={{8,0},{16,8},{24,16},{9,1},{17,9},{25,17},{10,2},{18,10},{26,18},{... | collective-permute-start | bytes 1671176 | tf_op jit(solution)/shard_map/ppermute | solution.py:819
  16.8 25.8 %collective-permute-start.4 = (bf16[2,272,512]{2,1,0:T(8,128)(2,1)}, bf16[2,272,512]{2,1,0:T(8,128)(2,1)S(1)}, u32[]{:S(2)}, u32[]{:S(2)}) collective-permute-start(bf16[2,272,512]{2,1,0:T(8,128)(2,1)} %shard_map.185.own), channel_id=1, source_target_pairs={{0,1},{1,0},{2,3},{3,2},{4,5},{5,4},{6,7},{7,6},{8,9},{9,8},{10,11... | collective-permute-start | bytes 1671176 | tf_op jit(solution)/shard_map/ppermute | solution.py:804
  18.4 24.2 %collective-permute-start.5 = (bf16[2,272,512]{2,1,0:T(8,128)(2,1)}, bf16[2,272,512]{2,1,0:T(8,128)(2,1)S(1)}, u32[]{:S(2)}, u32[]{:S(2)}) collective-permute-start(bf16[2,272,512]{2,1,0:T(8,128)(2,1)} %shard_map.185.own), channel_id=1, source_target_pairs={{0,2},{2,0},{1,3},{3,1},{4,6},{6,4},{5,7},{7,5},{8,10},{10,8},{9,1... | collective-permute-start | bytes 1671176 | tf_op jit(solution)/shard_map/ppermute | solution.py:808
  24.1 36.7 %copy-start.23 = (bf16[2,272,512]{2,1,0:T(8,128)(2,1)S(1)}, bf16[2,272,512]{2,1,0:T(8,128)(2,1)}, u32[]{:S(2)}) copy-start(bf16[2,272,512]{2,1,0:T(8,128)(2,1)} %shard_map.185.own) | copy-start | bytes 1671172
  42.6 38.1 %copy-start.22 = (bf16[2,272,512]{2,1,0:T(8,128)(2,1)}, bf16[2,272,512]{2,1,0:T(8,128)(2,1)S(1)}, u32[]{:S(2)}) copy-start(bf16[2,272,512]{2,1,0:T(8,128)(2,1)S(1)} %collective-permute-done.4.own) | copy-start | bytes 1671172
  42.6 38.1 %copy-start.21 = (bf16[2,272,512]{2,1,0:T(8,128)(2,1)}, bf16[2,272,512]{2,1,0:T(8,128)(2,1)S(1)}, u32[]{:S(2)}) copy-start(bf16[2,272,512]{2,1,0:T(8,128)(2,1)S(1)} %collective-permute-done.5.own) | copy-start | bytes 1671172
  42.6 37.1 %collective-permute-start.6 = (bf16[2,272,512]{2,1,0:T(8,128)(2,1)S(1)}, bf16[2,272,512]{2,1,0:T(8,128)(2,1)S(1)}, u32[]{:S(2)}, u32[]{:S(2)}) collective-permute-start(bf16[2,272,512]{2,1,0:T(8,128)(2,1)S(1)} %collective-permute-done.2), channel_id=1, source_target_pairs={{8,0},{16,24},{9,1},{17,25},{10,2},{18,26},{11,3},{19,27},{12,4},{... | collective-permute-start | bytes 1671176 | tf_op jit(solution)/shard_map/ppermute | solution.py:824
  43.9 16.9 %collective-permute-start.7 = (bf16[272,512]{1,0:T(8,128)(2,1)S(1)}, bf16[272,512]{1,0:T(8,128)(2,1)S(1)}, u32[]{:S(2)}, u32[]{:S(2)}) collective-permute-start(bf16[272,512]{1,0:T(8,128)(2,1)S(1)} %slice_bitcast_fusion.6), channel_id=1, source_target_pairs={{0,2},{2,0},{1,3},{3,1},{4,6},{6,4},{5,7},{7,5},{8,10},{10,8},{9,1... | collective-permute-start | bytes 835592 | tf_op jit(solution)/shard_map/ppermute | solution.py:808
  45.5 34.2 %collective-permute-start.9 = (bf16[2,512,256]{2,1,0:T(8,128)(2,1)S(1)}, bf16[2,512,256]{2,1,0:T(8,128)(2,1)S(1)}, u32[]{:S(2)}, u32[]{:S(2)}) collective-permute-start(bf16[2,512,256]{2,1,0:T(8,128)(2,1)S(1)} %get-tuple-element.104), channel_id=1, source_target_pairs={{0,16},{8,24},{16,0},{24,8},{1,17},{9,25},{17,1},{25,9},{2,18},{10... | collective-permute-start | bytes 1572872 | tf_op jit(solution)/shard_map/ppermute | solution.py:796
  57.7 7.1 %collective-permute-start.8 = (bf16[272,512]{1,0:T(8,128)(2,1)S(1)}, bf16[272,512]{1,0:T(8,128)(2,1)S(1)}, u32[]{:S(2)}, u32[]{:S(2)}) collective-permute-start(bf16[272,512]{1,0:T(8,128)(2,1)S(1)} %slice_bitcast_fusion.5), channel_id=1, source_target_pairs={{0,1},{1,0},{2,3},{3,2},{4,5},{5,4},{6,7},{7,6},{8,9},{9,8},{10,11... | collective-permute-start | bytes 835592 | tf_op jit(solution)/shard_map/ppermute | solution.py:804
  60.8 25.2 %copy-start.33 = (bf16[272,512]{1,0:T(8,128)(2,1)}, bf16[272,512]{1,0:T(8,128)(2,1)S(1)}, u32[]{:S(2)}) copy-start(bf16[272,512]{1,0:T(8,128)(2,1)S(1)} %collective-permute-done.7.own0) | copy-start | bytes 835588
  64.8 21.2 %copy-start.34 = (bf16[272,512]{1,0:T(8,128)(2,1)}, bf16[272,512]{1,0:T(8,128)(2,1)S(1)}, u32[]{:S(2)}) copy-start(bf16[272,512]{1,0:T(8,128)(2,1)S(1)} %collective-permute-done.8.own1) | copy-start | bytes 835588
  82.0 42.2 %collective-permute-start.10 = (bf16[2,3,272,512]{3,2,1,0:T(8,128)(2,1)}, bf16[2,3,272,512]{3,2,1,0:T(8,128)(2,1)}, u32[]{:S(2)}, u32[]{:S(2)}) collective-permute-start(bf16[2,3,272,512]{3,2,1,0:T(8,128)(2,1)} %pad_maximum_fusion.3.rest), channel_id=1, source_target_pairs={{0,1},{1,0},{2,3},{3,2},{4,5},{5,4},{6,7},{7,6},{8,9},{9,8},{10,11... | collective-permute-start | bytes 5013512 | tf_op jit(solution)/shard_map/ppermute | solution.py:804
  83.5 40.7 %collective-permute-start.11 = (bf16[2,3,272,512]{3,2,1,0:T(8,128)(2,1)}, bf16[2,3,272,512]{3,2,1,0:T(8,128)(2,1)}, u32[]{:S(2)}, u32[]{:S(2)}) collective-permute-start(bf16[2,3,272,512]{3,2,1,0:T(8,128)(2,1)} %pad_maximum_fusion.3.rest), channel_id=1, source_target_pairs={{0,2},{2,0},{1,3},{3,1},{4,6},{6,4},{5,7},{7,5},{8,10},{10,8},{9,1... | collective-permute-start | bytes 5013512 | tf_op jit(solution)/shard_map/ppermute | solution.py:808
  89.2 35.0 %collective-permute-start.12 = (bf16[2,512,256]{2,1,0:T(8,128)(2,1)}, bf16[2,512,256]{2,1,0:T(8,128)(2,1)S(1)}, u32[]{:S(2)}, u32[]{:S(2)}) collective-permute-start(bf16[2,512,256]{2,1,0:T(8,128)(2,1)} %get-tuple-element.115), channel_id=1, source_target_pairs={{0,8},{8,16},{16,24},{24,0},{1,9},{9,17},{17,25},{25,1},{2,10},{10... | collective-permute-start | bytes 1572872 | tf_op jit(solution)/shard_map/ppermute | solution.py:796
  89.3 34.9 %collective-permute-start.13 = (bf16[2,512,256]{2,1,0:T(8,128)(2,1)}, bf16[2,512,256]{2,1,0:T(8,128)(2,1)}, u32[]{:S(2)}, u32[]{:S(2)}) collective-permute-start(bf16[2,512,256]{2,1,0:T(8,128)(2,1)} %get-tuple-element.116), channel_id=1, source_target_pairs={{0,24},{8,0},{16,8},{24,16},{1,25},{9,1},{17,9},{25,17},{2,26},{10... | collective-permute-start | bytes 1572872 | tf_op jit(solution)/shard_map/ppermute | solution.py:796
  93.1 31.1 %collective-permute-start.14 = (bf16[1,512,256]{2,1,0:T(8,128)(2,1)}, bf16[1,512,256]{2,1,0:T(8,128)(2,1)}, u32[]{:S(2)}, u32[]{:S(2)}) collective-permute-start(bf16[1,512,256]{2,1,0:T(8,128)(2,1)} %get-tuple-element.117), channel_id=1, source_target_pairs={{0,16},{8,24},{16,0},{24,8},{1,17},{9,25},{17,1},{25,9},{2,18},{10... | collective-permute-start | bytes 786440 | tf_op jit(solution)/shard_map/ppermute | solution.py:796
  93.1 31.9 %copy-start.13 = (bf16[2,512,256]{2,1,0:T(8,128)(2,1)S(1)}, bf16[2,512,256]{2,1,0:T(8,128)(2,1)}, u32[]{:S(2)}) copy-start(bf16[2,512,256]{2,1,0:T(8,128)(2,1)} %copy-done.12) | copy-start | bytes 1572868
  126.5 18.6 %copy-start.2 = (bf16[4,2,512,256]{3,2,1,0:T(8,128)(2,1)}, bf16[4,2,512,256]{3,2,1,0:T(8,128)(2,1)S(1)}, u32[]{:S(2)}) copy-start(bf16[4,2,512,256]{3,2,1,0:T(8,128)(2,1)S(1)} %pad_maximum_fusion.own.own_kv) | copy-start | bytes 6291460
  126.5 39.4 %collective-permute-start.15 = (bf16[4,2,512,256]{3,2,1,0:T(8,128)(2,1)S(1)}, bf16[4,2,512,256]{3,2,1,0:T(8,128)(2,1)}, u32[]{:S(2)}, u32[]{:S(2)}) collective-permute-start(bf16[4,2,512,256]{3,2,1,0:T(8,128)(2,1)S(1)} %pad_maximum_fusion.own.own_kv), channel_id=1, source_target_pairs={{0,4},{4,0},{1,5},{5,1},{2,6},{6,2},{3,7},{7,3},{8,12},{12,8},{9,1... | collective-permute-start | bytes 6291464 | tf_op jit(solution)/shard_map/ppermute | solution.py:800
  129.5 20.5 %collective-permute-start.16 = (bf16[3,272,512]{2,1,0:T(8,128)(2,1)}, bf16[3,272,512]{2,1,0:T(8,128)(2,1)}, u32[]{:S(2)}, u32[]{:S(2)}) collective-permute-start(bf16[3,272,512]{2,1,0:T(8,128)(2,1)} %slice_bitcast_fusion.1), channel_id=1, source_target_pairs={{0,2},{2,0},{1,3},{3,1},{4,6},{6,4},{5,7},{7,5},{8,10},{10,8},{9,1... | collective-permute-start | bytes 2506760 | tf_op jit(solution)/shard_map/ppermute | solution.py:808
  133.2 20.2 %collective-permute-start.17 = (bf16[3,272,512]{2,1,0:T(8,128)(2,1)}, bf16[3,272,512]{2,1,0:T(8,128)(2,1)}, u32[]{:S(2)}, u32[]{:S(2)}) collective-permute-start(bf16[3,272,512]{2,1,0:T(8,128)(2,1)} %slice_bitcast_fusion), channel_id=1, source_target_pairs={{0,1},{1,0},{2,3},{3,2},{4,5},{5,4},{6,7},{7,6},{8,9},{9,8},{10,11... | collective-permute-start | bytes 2506760 | tf_op jit(solution)/shard_map/ppermute | solution.py:804
  134.3 11.0 %collective-permute-start.18 = (bf16[1,512,256]{2,1,0:T(8,128)(2,1)S(1)}, bf16[1,512,256]{2,1,0:T(8,128)(2,1)S(1)}, u32[]{:S(2)}, u32[]{:S(2)}) collective-permute-start(bf16[1,512,256]{2,1,0:T(8,128)(2,1)S(1)} %copy-done.19), channel_id=1, source_target_pairs={{0,8},{8,16},{16,24},{24,0},{1,9},{9,17},{17,25},{25,1},{2,10},{10... | collective-permute-start | bytes 786440 | tf_op jit(solution)/shard_map/ppermute | solution.py:796
  134.3 13.0 %collective-permute-start.19 = (bf16[1,512,256]{2,1,0:T(8,128)(2,1)S(1)}, bf16[1,512,256]{2,1,0:T(8,128)(2,1)S(1)}, u32[]{:S(2)}, u32[]{:S(2)}) collective-permute-start(bf16[1,512,256]{2,1,0:T(8,128)(2,1)S(1)} %copy-done.18), channel_id=1, source_target_pairs={{0,24},{8,0},{16,8},{24,16},{1,25},{9,1},{17,9},{25,17},{2,26},{10... | collective-permute-start | bytes 786440 | tf_op jit(solution)/shard_map/ppermute | solution.py:796
  154.5 24.9 %collective-permute-start.20 = (bf16[4,1,512,256]{3,2,1,0:T(8,128)(2,1)S(1)}, bf16[4,1,512,256]{3,2,1,0:T(8,128)(2,1)S(1)}, u32[]{:S(2)}, u32[]{:S(2)}) collective-permute-start(bf16[4,1,512,256]{3,2,1,0:T(8,128)(2,1)S(1)} %pad_maximum_fusion.4.own_r), channel_id=1, source_target_pairs={{0,4},{4,0},{1,5},{5,1},{2,6},{6,2},{3,7},{7,3},{8,12},{12,8},{9,1... | collective-permute-start | bytes 3145736 | tf_op jit(solution)/shard_map/ppermute | solution.py:800
  161.7 43.4 %collective-permute-start.21 = (bf16[1,512,256]{2,1,0:T(8,128)(2,1)}, bf16[1,512,256]{2,1,0:T(8,128)(2,1)}, u32[]{:S(2)}, u32[]{:S(2)}) collective-permute-start(bf16[1,512,256]{2,1,0:T(8,128)(2,1)} %get-tuple-element.155), channel_id=1, source_target_pairs={{0,8},{8,16},{16,24},{24,0},{1,9},{9,17},{17,25},{25,1},{2,10},{10... | collective-permute-start | bytes 786440 | tf_op jit(solution)/shard_map/ppermute | solution.py:796
  161.8 43.3 %collective-permute-start.22 = (bf16[1,512,256]{2,1,0:T(8,128)(2,1)S(1)}, bf16[1,512,256]{2,1,0:T(8,128)(2,1)}, u32[]{:S(2)}, u32[]{:S(2)}) collective-permute-start(bf16[1,512,256]{2,1,0:T(8,128)(2,1)S(1)} %copy-done.17), channel_id=1, source_target_pairs={{0,16},{8,24},{16,0},{24,8},{1,17},{9,25},{17,1},{25,9},{2,18},{10... | collective-permute-start | bytes 786440 | tf_op jit(solution)/shard_map/ppermute | solution.py:796
  163.5 41.6 %collective-permute-start.23 = (bf16[1,512,256]{2,1,0:T(8,128)(2,1)S(1)}, bf16[1,512,256]{2,1,0:T(8,128)(2,1)}, u32[]{:S(2)}, u32[]{:S(2)}) collective-permute-start(bf16[1,512,256]{2,1,0:T(8,128)(2,1)S(1)} %copy-done.16), channel_id=1, source_target_pairs={{0,24},{8,0},{16,8},{24,16},{1,25},{9,1},{17,9},{25,17},{2,26},{10... | collective-permute-start | bytes 786440 | tf_op jit(solution)/shard_map/ppermute | solution.py:796
  200.0 6.5 %collective-permute-start.25 = (bf16[4,2,4,64,64]{4,3,2,1,0:T(8,128)(2,1)S(1)}, bf16[4,2,4,64,64]{4,3,2,1,0:T(8,128)(2,1)S(1)}, u32[]{:S(2)}, u32[]{:S(2)}) collective-permute-start(bf16[4,2,4,64,64]{4,3,2,1,0:T(8,128)(2,1)S(1)} %dynamic-slice_bitcast_fusion), channel_id=1, source_target_pairs={{0,4},{4,0},{1,5},{5,1},{2,6},{6,2},{3,7},{7,3},{8,12},{12,8},{9,1... | collective-permute-start | bytes 786440 | tf_op jit(solution)/shard_map/ppermute | solution.py:800
  204.7 29.3 %collective-permute-start.34 = (bf16[1024,512]{1,0:T(8,128)(2,1)S(1)}, bf16[1024,512]{1,0:T(8,128)(2,1)S(1)}, u32[]{:S(2)}, u32[]{:S(2)}) collective-permute-start(bf16[1024,512]{1,0:T(8,128)(2,1)S(1)} %copy-done.3), channel_id=1, source_target_pairs={{0,4},{4,0},{1,5},{5,1},{2,6},{6,2},{3,7},{7,3},{8,12},{12,8},{9,1... | collective-permute-start | bytes 3145736 | tf_op jit(solution)/shard_map/ppermute | solution.py:800
  206.4 19.4 %collective-permute-start.24 = (bf16[4,1,512,256]{3,2,1,0:T(8,128)(2,1)S(1)}, bf16[4,1,512,256]{3,2,1,0:T(8,128)(2,1)S(1)}, u32[]{:S(2)}, u32[]{:S(2)}) collective-permute-start(bf16[4,1,512,256]{3,2,1,0:T(8,128)(2,1)S(1)} %pad_maximum_fusion.5.own), channel_id=1, source_target_pairs={{0,4},{4,0},{1,5},{5,1},{2,6},{6,2},{3,7},{7,3},{8,12},{12,8},{9,1... | collective-permute-start | bytes 3145736 | tf_op jit(solution)/shard_map/ppermute | solution.py:800
  208.4 16.6 %collective-permute-start.26 = (bf16[3,4,64,64]{3,2,1,0:T(8,128)(2,1)S(1)}, bf16[3,4,64,64]{3,2,1,0:T(8,128)(2,1)S(1)}, u32[]{:S(2)}, u32[]{:S(2)}) collective-permute-start(bf16[3,4,64,64]{3,2,1,0:T(8,128)(2,1)S(1)} %get-tuple-element.219), channel_id=1, source_target_pairs={{0,8},{8,16},{16,24},{24,0},{1,9},{9,17},{17,25},{25,1},{2,10},{10... | collective-permute-start | bytes 294920 | tf_op jit(solution)/shard_map/ppermute | solution.py:796
  208.8 17.0 %collective-permute-start.27 = (bf16[3,4,64,64]{3,2,1,0:T(8,128)(2,1)S(1)}, bf16[3,4,64,64]{3,2,1,0:T(8,128)(2,1)S(1)}, u32[]{:S(2)}, u32[]{:S(2)}) collective-permute-start(bf16[3,4,64,64]{3,2,1,0:T(8,128)(2,1)S(1)} %get-tuple-element.218), channel_id=1, source_target_pairs={{0,16},{8,24},{16,0},{24,8},{1,17},{9,25},{17,1},{25,9},{2,18},{10... | collective-permute-start | bytes 294920 | tf_op jit(solution)/shard_map/ppermute | solution.py:796
  210.3 15.5 %collective-permute-start.28 = (bf16[3,4,64,64]{3,2,1,0:T(8,128)(2,1)S(1)}, bf16[3,4,64,64]{3,2,1,0:T(8,128)(2,1)S(1)}, u32[]{:S(2)}, u32[]{:S(2)}) collective-permute-start(bf16[3,4,64,64]{3,2,1,0:T(8,128)(2,1)S(1)} %get-tuple-element.217), channel_id=1, source_target_pairs={{0,24},{8,0},{16,8},{24,16},{1,25},{9,1},{17,9},{25,17},{2,26},{10... | collective-permute-start | bytes 294920 | tf_op jit(solution)/shard_map/ppermute | solution.py:796
  233.9 1.7 collective-permute-start.29
  235.7 32.6 %copy-start.15 = (bf16[4,4,48,256]{3,2,1,0:T(8,128)(2,1)}, bf16[4,4,48,256]{3,2,1,0:T(8,128)(2,1)S(1)}, u32[]{:S(2)}) copy-start(bf16[4,4,48,256]{3,2,1,0:T(8,128)(2,1)S(1)} %pad_maximum_fusion.7) | copy-start | bytes 1179652
  235.7 20.7 %collective-permute-start.30 = (bf16[768,256]{1,0:T(8,128)(2,1)S(1)}, bf16[768,256]{1,0:T(8,128)(2,1)S(1)}, u32[]{:S(2)}, u32[]{:S(2)}) collective-permute-start(bf16[768,256]{1,0:T(8,128)(2,1)S(1)} %bitcast.165), channel_id=1, source_target_pairs={{0,16},{8,24},{16,0},{24,8},{1,17},{9,25},{17,1},{25,9},{2,18},{10... | collective-permute-start | bytes 1179656 | tf_op jit(solution)/shard_map/ppermute | solution.py:796
  239.4 1.6 collective-permute-start.41
  241.0 34.8 %copy-start.26 = (bf16[4,4,16,256]{3,2,1,0:T(8,128)(2,1)}, bf16[4,4,16,256]{3,2,1,0:T(8,128)(2,1)S(1)}, u32[]{:S(2)}) copy-start(bf16[4,4,16,256]{3,2,1,0:T(8,128)(2,1)S(1)} %pad_maximum_fusion.8) | copy-start | bytes 393220
  256.4 23.0 %copy-start.31 = (bf16[768,256]{1,0:T(8,128)(2,1)}, bf16[768,256]{1,0:T(8,128)(2,1)S(1)}, u32[]{:S(2)}) copy-start(bf16[768,256]{1,0:T(8,128)(2,1)S(1)} %collective-permute-done.30.h2) | copy-start | bytes 1179652
  256.4 9.2 %collective-permute-start.42 = (bf16[256,256]{1,0:T(8,128)(2,1)S(1)}, bf16[256,256]{1,0:T(8,128)(2,1)S(1)}, u32[]{:S(2)}, u32[]{:S(2)}) collective-permute-start(bf16[256,256]{1,0:T(8,128)(2,1)S(1)} %bitcast.172), channel_id=1, source_target_pairs={{0,16},{8,24},{16,0},{24,8},{1,17},{9,25},{17,1},{25,9},{2,18},{10... | collective-permute-start | bytes 393224 | tf_op jit(solution)/shard_map/ppermute | solution.py:796
  256.7 16.8 %collective-permute-start.45 = (bf16[256,256]{1,0:T(8,128)(2,1)S(1)}, bf16[256,256]{1,0:T(8,128)(2,1)S(1)}, u32[]{:S(2)}, u32[]{:S(2)}) collective-permute-start(bf16[256,256]{1,0:T(8,128)(2,1)S(1)} %bitcast.173), channel_id=1, source_target_pairs={{8,0},{16,8},{24,16},{9,1},{17,9},{25,17},{10,2},{18,10},{26,18},{... | collective-permute-start | bytes 393224 | tf_op jit(solution)/shard_map/ppermute | solution.py:819
  258.0 17.1 %collective-permute-start.44 = (bf16[256,256]{1,0:T(8,128)(2,1)S(1)}, bf16[256,256]{1,0:T(8,128)(2,1)S(1)}, u32[]{:S(2)}, u32[]{:S(2)}) collective-permute-start(bf16[256,256]{1,0:T(8,128)(2,1)S(1)} %bitcast.174), channel_id=1, source_target_pairs={{0,8},{8,16},{16,24},{1,9},{9,17},{17,25},{2,10},{10,18},{18,26},{... | collective-permute-start | bytes 393224 | tf_op jit(solution)/shard_map/ppermute | solution.py:818
  265.7 9.4 %collective-permute-start.43 = (bf16[256,256]{1,0:T(8,128)(2,1)S(1)}, bf16[256,256]{1,0:T(8,128)(2,1)S(1)}, u32[]{:S(2)}, u32[]{:S(2)}) collective-permute-start(bf16[256,256]{1,0:T(8,128)(2,1)S(1)} %collective-permute-done.42.h2), channel_id=1, source_target_pairs={{8,0},{16,24},{9,1},{17,25},{10,2},{18,26},{11,3},{19,27},{12,4},{... | collective-permute-start | bytes 393224 | tf_op jit(solution)/shard_map/ppermute | solution.py:824
  267.0 15.3 %collective-permute-start.33 = (bf16[768,256]{1,0:T(8,128)(2,1)S(1)}, bf16[768,256]{1,0:T(8,128)(2,1)S(1)}, u32[]{:S(2)}, u32[]{:S(2)}) collective-permute-start(bf16[768,256]{1,0:T(8,128)(2,1)S(1)} %bitcast.166), channel_id=1, source_target_pairs={{8,0},{16,8},{24,16},{9,1},{17,9},{25,17},{10,2},{18,10},{26,18},{... | collective-permute-start | bytes 1179656 | tf_op jit(solution)/shard_map/ppermute | solution.py:819
  268.3 14.7 %collective-permute-start.32 = (bf16[768,256]{1,0:T(8,128)(2,1)S(1)}, bf16[768,256]{1,0:T(8,128)(2,1)S(1)}, u32[]{:S(2)}, u32[]{:S(2)}) collective-permute-start(bf16[768,256]{1,0:T(8,128)(2,1)S(1)} %bitcast.167), channel_id=1, source_target_pairs={{0,8},{8,16},{16,24},{1,9},{9,17},{17,25},{2,10},{10,18},{18,26},{... | collective-permute-start | bytes 1179656 | tf_op jit(solution)/shard_map/ppermute | solution.py:818
  273.5 15.3 %collective-permute-start.31 = (bf16[768,256]{1,0:T(8,128)(2,1)S(1)}, bf16[768,256]{1,0:T(8,128)(2,1)S(1)}, u32[]{:S(2)}, u32[]{:S(2)}) collective-permute-start(bf16[768,256]{1,0:T(8,128)(2,1)S(1)} %collective-permute-done.30.h2), channel_id=1, source_target_pairs={{8,0},{16,24},{9,1},{17,25},{10,2},{18,26},{11,3},{19,27},{12,4},{... | collective-permute-start | bytes 1179656 | tf_op jit(solution)/shard_map/ppermute | solution.py:824
  279.5 17.7 %collective-permute-start.48 = (bf16[4,16,1024]{2,1,0:T(8,128)(2,1)}, bf16[4,16,1024]{2,1,0:T(8,128)(2,1)S(1)}, u32[]{:S(2)}, u32[]{:S(2)}) collective-permute-start(bf16[4,16,1024]{2,1,0:T(8,128)(2,1)} %get-tuple-element.188), channel_id=1, source_target_pairs={{0,3},{1,2},{2,1},{3,0},{4,7},{5,6},{6,5},{7,4},{8,11},{9,10},{10,... | collective-permute-start | bytes 393224 | tf_op jit(solution)/shard_map/ppermute | solution.py:1084
  279.9 18.8 %collective-permute-start.47 = (bf16[4,16,1024]{2,1,0:T(8,128)(2,1)}, bf16[4,16,1024]{2,1,0:T(8,128)(2,1)S(1)}, u32[]{:S(2)}, u32[]{:S(2)}) collective-permute-start(bf16[4,16,1024]{2,1,0:T(8,128)(2,1)} %get-tuple-element.187), channel_id=1, source_target_pairs={{0,2},{2,0},{1,3},{3,1},{4,6},{6,4},{5,7},{7,5},{8,10},{10,8},{9,1... | collective-permute-start | bytes 393224 | tf_op jit(solution)/shard_map/ppermute | solution.py:808
  282.3 16.5 %collective-permute-start.46 = (bf16[4,16,1024]{2,1,0:T(8,128)(2,1)}, bf16[4,16,1024]{2,1,0:T(8,128)(2,1)S(1)}, u32[]{:S(2)}, u32[]{:S(2)}) collective-permute-start(bf16[4,16,1024]{2,1,0:T(8,128)(2,1)} %get-tuple-element.186), channel_id=1, source_target_pairs={{0,1},{1,0},{2,3},{3,2},{4,5},{5,4},{6,7},{7,6},{8,9},{9,8},{10,11... | collective-permute-start | bytes 393224 | tf_op jit(solution)/shard_map/ppermute | solution.py:804
  295.2 13.2 %collective-permute-start.37 = (bf16[4,48,1024]{2,1,0:T(8,128)(2,1)}, bf16[4,48,1024]{2,1,0:T(8,128)(2,1)S(1)}, u32[]{:S(2)}, u32[]{:S(2)}) collective-permute-start(bf16[4,48,1024]{2,1,0:T(8,128)(2,1)} %get-tuple-element.181), channel_id=1, source_target_pairs={{0,3},{1,2},{2,1},{3,0},{4,7},{5,6},{6,5},{7,4},{8,11},{9,10},{10,... | collective-permute-start | bytes 1179656 | tf_op jit(solution)/shard_map/ppermute | solution.py:1084
  295.7 17.6 %collective-permute-start.36 = (bf16[4,48,1024]{2,1,0:T(8,128)(2,1)}, bf16[4,48,1024]{2,1,0:T(8,128)(2,1)S(1)}, u32[]{:S(2)}, u32[]{:S(2)}) collective-permute-start(bf16[4,48,1024]{2,1,0:T(8,128)(2,1)} %get-tuple-element.180), channel_id=1, source_target_pairs={{0,2},{2,0},{1,3},{3,1},{4,6},{6,4},{5,7},{7,5},{8,10},{10,8},{9,1... | collective-permute-start | bytes 1179656 | tf_op jit(solution)/shard_map/ppermute | solution.py:808
  297.2 16.1 %collective-permute-start.35 = (bf16[4,48,1024]{2,1,0:T(8,128)(2,1)}, bf16[4,48,1024]{2,1,0:T(8,128)(2,1)S(1)}, u32[]{:S(2)}, u32[]{:S(2)}) collective-permute-start(bf16[4,48,1024]{2,1,0:T(8,128)(2,1)} %get-tuple-element.179), channel_id=1, source_target_pairs={{0,1},{1,0},{2,3},{3,2},{4,5},{5,4},{6,7},{7,6},{8,9},{9,8},{10,11... | collective-permute-start | bytes 1179656 | tf_op jit(solution)/shard_map/ppermute | solution.py:804
  299.5 19.0 %collective-permute-start.49 = (bf16[16,1024]{1,0:T(8,128)(2,1)S(1)}, bf16[16,1024]{1,0:T(8,128)(2,1)S(1)}, u32[]{:S(2)}, u32[]{:S(2)}) collective-permute-start(bf16[16,1024]{1,0:T(8,128)(2,1)S(1)} %get-tuple-element.231), channel_id=1, source_target_pairs={{0,8},{8,16},{16,24},{24,0},{1,9},{9,17},{17,25},{25,1},{2,10},{10... | collective-permute-start | bytes 98312 | tf_op jit(solution)/shard_map/ppermute | solution.py:796
  299.5 21.6 %collective-permute-start.50 = (bf16[16,1024]{1,0:T(8,128)(2,1)S(1)}, bf16[16,1024]{1,0:T(8,128)(2,1)S(1)}, u32[]{:S(2)}, u32[]{:S(2)}) collective-permute-start(bf16[16,1024]{1,0:T(8,128)(2,1)S(1)} %get-tuple-element.230), channel_id=1, source_target_pairs={{0,16},{8,24},{16,0},{24,8},{1,17},{9,25},{17,1},{25,9},{2,18},{10... | collective-permute-start | bytes 98312 | tf_op jit(solution)/shard_map/ppermute | solution.py:796
  308.4 12.7 %collective-permute-start.51 = (bf16[16,1024]{1,0:T(8,128)(2,1)S(1)}, bf16[16,1024]{1,0:T(8,128)(2,1)S(1)}, u32[]{:S(2)}, u32[]{:S(2)}) collective-permute-start(bf16[16,1024]{1,0:T(8,128)(2,1)S(1)} %get-tuple-element.229), channel_id=1, source_target_pairs={{0,24},{8,0},{16,8},{24,16},{1,25},{9,1},{17,9},{25,17},{2,26},{10... | collective-permute-start | bytes 98312 | tf_op jit(solution)/shard_map/ppermute | solution.py:796
  315.3 7.6 %collective-permute-start.38 = (bf16[48,1024]{1,0:T(8,128)(2,1)S(1)}, bf16[48,1024]{1,0:T(8,128)(2,1)S(1)}, u32[]{:S(2)}, u32[]{:S(2)}) collective-permute-start(bf16[48,1024]{1,0:T(8,128)(2,1)S(1)} %get-tuple-element.225), channel_id=1, source_target_pairs={{0,8},{8,16},{16,24},{24,0},{1,9},{9,17},{17,25},{25,1},{2,10},{10... | collective-permute-start | bytes 294920 | tf_op jit(solution)/shard_map/ppermute | solution.py:796
  315.3 10.1 %collective-permute-start.39 = (bf16[48,1024]{1,0:T(8,128)(2,1)S(1)}, bf16[48,1024]{1,0:T(8,128)(2,1)S(1)}, u32[]{:S(2)}, u32[]{:S(2)}) collective-permute-start(bf16[48,1024]{1,0:T(8,128)(2,1)S(1)} %get-tuple-element.224), channel_id=1, source_target_pairs={{0,16},{8,24},{16,0},{24,8},{1,17},{9,25},{17,1},{25,9},{2,18},{10... | collective-permute-start | bytes 294920 | tf_op jit(solution)/shard_map/ppermute | solution.py:796
  318.5 6.9 %collective-permute-start.40 = (bf16[48,1024]{1,0:T(8,128)(2,1)S(1)}, bf16[48,1024]{1,0:T(8,128)(2,1)S(1)}, u32[]{:S(2)}, u32[]{:S(2)}) collective-permute-start(bf16[48,1024]{1,0:T(8,128)(2,1)S(1)} %get-tuple-element.223), channel_id=1, source_target_pairs={{0,24},{8,0},{16,8},{24,16},{1,25},{9,1},{17,9},{25,17},{2,26},{10... | collective-permute-start | bytes 294920 | tf_op jit(solution)/shard_map/ppermute | solution.py:796
  (31 other events, 169.9 us)

commit v7 on v5

--- a/solution.py
+++ b/solution.py
@@ -1,6 +1,5 @@
 import jax
 import jax.numpy as jnp
-import numpy as np
 from jax import lax
 from jax.experimental import pallas as pl
 from jax.experimental.pallas import tpu as pltpu
@@ -249,7 +248,7 @@
 
 f32 = jnp.float32
 bf16 = jnp.bfloat16
-VMEM_LIMIT = 56 * 1024 * 1024
+VMEM_LIMIT = 24 * 1024 * 1024
 TILE = 256
 
 
@@ -353,7 +352,19 @@
         held[kind[7 + k]] = rest[k]
 
 
-def mix_kernel(kind, own, rest, ratios, left, kv_mix, r_mix, gate_mix, squeezed, held):
+def keep_kv(half, which, at, value, kv_own, kv_sibling):
+    @pl.when(half == 0)
+    def _():
+        kv_own[which, at, :] = value
+
+    @pl.when(half == 1)
+    def _():
+        kv_sibling[which, at, :] = value
+
+
+def mix_kernel(
+    kind, own, rest, ratios, left, kv_own, kv_sibling, r_mix, gate_mix, squeezed, held
+):
     gather_blocks(kind, own.at[0], rest.at[0], held)
 
     @pl.loop(0, held.shape[0], unroll=2)
@@ -365,8 +376,8 @@
             return (here + ratios[0, which : which + 1, :] * step).astype(bf16)
 
         r_mix[0, at, :] = mix(0)
-        kv_mix[0, 0, at, :] = mix(1)
-        kv_mix[0, 1, at, :] = mix(2)
+        for which in range(2):
+            keep_kv(pl.program_id(0), which, at, mix(1 + which), kv_own, kv_sibling)
         gate_mix[0, at, :] = mix(3)
         squeezed[0, at, :] = jnp.dot(mix(4), left[0], preferred_element_type=f32)
 
@@ -376,7 +387,8 @@
     lines = rest.shape[1] + 1
     whole = lines * rows
     outs = [
-        jax.ShapeDtypeStruct((2, 2, whole, depth), bf16),
+        jax.ShapeDtypeStruct((2, whole, depth), bf16),
+        jax.ShapeDtypeStruct((2, whole, depth), bf16),
         jax.ShapeDtypeStruct((2, whole, depth), bf16),
         jax.ShapeDtypeStruct((2, whole, depth), bf16),
         jax.ShapeDtypeStruct((2, whole, left.shape[2]), f32),
@@ -386,11 +398,80 @@
         grid=(2,),
         out_shape=outs,
         in_specs=[in_smem()] + [half_block(a.shape) for a in (own, rest, ratios, left)],
-        out_specs=[half_block(out.shape) for out in outs],
+        out_specs=[pl.BlockSpec(outs[0].shape, lambda i: (0, 0, 0))] * 2
+        + [half_block(out.shape) for out in outs[2:]],
         scratch_shapes=[pltpu.VMEM((lines, rows + EXTRA, depth), bf16)],
         compiler_params=kernel_params(),
         cost_estimate=takes(7),
     )(kind, own, rest, ratios, left)
+
+
+def mix_project_kernel(rel, kind, own, rest, ratios, left, own_kv, *refs):
+    earlier = refs[:-7]
+    kv_sibling, r_mix, gate_mix, squeezed, keys_ref, values_ref, held = refs[-7:]
+    half = pl.program_id(0)
+    gather_blocks(kind, own.at[0], rest.at[0], held)
+
+    @pl.loop(0, held.shape[0], unroll=2)
+    def _(tile):
+        here, step = here_and_step(held, kind[0], kind[1], tile)
+        at = pl.ds(pl.multiple_of(tile * TILE, TILE), TILE)
+
+        def mix(which):
+            return (here + ratios[0, which : which + 1, :] * step).astype(bf16)
+
+        r_mix[0, at, :] = mix(0)
+        gate_mix[0, at, :] = mix(3)
+        squeezed[0, at, :] = jnp.dot(mix(4), left[0], preferred_element_type=f32)
+
+        @pl.when(half == 0)
+        def _():
+            for which, out in enumerate((keys_ref, values_ref)):
+                part = jnp.dot(
+                    mix(1 + which), own_kv[kind[10 + rel], which], preferred_element_type=f32
+                )
+                if len(earlier) == 1:
+                    part = part + jnp.dot(
+                        earlier[0][which, at, :],
+                        own_kv[kind[10], which],
+                        preferred_element_type=f32,
+                    )
+                else:
+                    part = part + earlier[which][at, :]
+                out[at, :] = part
+
+        @pl.when(half == 1)
+        def _():
+            for which in range(2):
+                kv_sibling[which, at, :] = mix(1 + which)
+
+
+def mix_and_project(rel, kind, own, rest, ratios, left, own_kv, *earlier):
+    rows, depth = own.shape[1] - EXTRA, own.shape[2]
+    lines = rest.shape[1] + 1
+    whole, width = lines * rows, own_kv.shape[3]
+    kept = jax.ShapeDtypeStruct((2, whole, depth), bf16)
+    outs = [
+        jax.ShapeDtypeStruct((2, whole, depth), bf16),
+        jax.ShapeDtypeStruct((2, whole, depth), bf16),
+        jax.ShapeDtypeStruct((2, whole, left.shape[2]), f32),
+    ]
+    flat = jax.ShapeDtypeStruct((whole, width), f32)
+    whole_of = pl.BlockSpec((whole, width), lambda i: (0, 0))
+    return pl.pallas_call(
+        lambda *refs: mix_project_kernel(rel, *refs),
+        grid=(2,),
+        out_shape=[kept] + outs + [flat] * 2,
+        in_specs=[in_smem()]
+        + [half_block(a.shape) for a in (own, rest, ratios, left)]
+        + [in_vmem()] * (1 + len(earlier)),
+        out_specs=[pl.BlockSpec(kept.shape, lambda i: (0, 0, 0))]
+        + [half_block(out.shape) for out in outs]
+        + [whole_of] * 2,
+        scratch_shapes=[pltpu.VMEM((lines, rows + EXTRA, depth), bf16)],
+        compiler_params=kernel_params(),
+        cost_estimate=takes(6),
+    )(kind, own, rest, ratios, left, own_kv, *earlier)
 
 
 def project_kernel(
@@ -401,14 +482,16 @@
     low0,
     low1,
     low2,
+    keys_part,
+    values_part,
     own0,
     own1,
     rest0,
     rest1,
     ratios,
     left,
-    own_weight,
-    sibling_weight,
+    own_kv,
+    sibling_kv,
     right,
     base,
     keys_ref,
@@ -425,29 +508,27 @@
         for half, (own, rest) in enumerate(((own0, rest0), (own1, rest1))):
             gather_blocks(kind, own, rest, held.at[half])
 
-    totals = [None] * 2
-
-    def add(which, rel, half, mixed):
-        weight = (own_weight, sibling_weight)[half][kind[10 + rel], which]
-        part = jnp.dot(mixed, weight, preferred_element_type=f32)
-        totals[which] = part if totals[which] is None else totals[which] + part
-
+    totals = [keys_part[...], values_part[...]]
     squeezed = low0[0] + low0[1] + low1[0] + low1[1] + low2[0] + low2[1]
     for half in range(2):
         here, step = here_and_step(held.at[half], kind[0], kind[1], tile)
+        weight = (own_kv, sibling_kv)[half]
 
         def mix(which):
             return (here + ratios[half, which : which + 1, :] * step).astype(bf16)
 
         r_mix[half] = mix(0)
-        add(0, 3, half, mix(1))
-        add(1, 3, half, mix(2))
         gate_mix[half] = mix(3)
+        for which in range(2):
+            totals[which] += jnp.dot(
+                mix(1 + which), weight[kind[13], which], preferred_element_type=f32
+            )
         squeezed = squeezed + jnp.dot(mix(4), left[half], preferred_element_type=f32)
     for rel, mixes in enumerate((mix0, mix1, mix2)):
-        for half in range(2):
-            for which in range(2):
-                add(which, rel, half, mixes[half, which])
+        for which in range(2):
+            totals[which] += jnp.dot(
+                mixes[which], sibling_kv[kind[10 + rel], which], preferred_element_type=f32
+            )
     keys_ref[...] = totals[0]
     values_ref[...] = totals[1]
     squeezed = jnp.tanh(squeezed).astype(bf16)
@@ -455,10 +536,9 @@
     decay_ref[...] = -jnp.exp(base[...] + grown)
 
 
-def projected(kind, mixes, lows, owns, rests, *rest):
-    rows, depth = mixes[0].shape[2:]
-    own_weight = rest[2]
-    width, rank = own_weight.shape[3], lows[0].shape[2]
+def projected(kind, mixes, lows, parts, owns, rests, *rest):
+    rows, width = parts[0].shape
+    rank, depth = lows[0].shape[2], owns[0].shape[1]
     flat = jax.ShapeDtypeStruct((rows, width), f32)
     wide = jax.ShapeDtypeStruct((2, rows, depth), bf16)
     tile_of = pl.BlockSpec((TILE, width), lambda i: (i, 0))
@@ -468,14 +548,15 @@
         grid=(rows // TILE,),
         out_shape=[flat] * 3 + [wide] * 2,
         in_specs=[in_smem()]
-        + [pl.BlockSpec((2, 2, TILE, depth), lambda i: (0, 0, i, 0))] * 3
+        + [wide_of] * 3
         + [pl.BlockSpec((2, TILE, rank), lambda i: (0, i, 0))] * 3
+        + [tile_of] * 2
         + [in_vmem()] * (4 + len(rest)),
         out_specs=[tile_of] * 3 + [wide_of] * 2,
         scratch_shapes=[pltpu.VMEM((2, rests[0].shape[0] + 1) + owns[0].shape, bf16)],
         compiler_params=kernel_params(),
-        cost_estimate=takes(12),
-    )(kind, *mixes, *lows, *owns, *rests, *rest)
+        cost_estimate=takes(8),
+    )(kind, *mixes, *lows, *parts, *owns, *rests, *rest)
 
 
 def plain_kernel(kind, mix0, mix1, mix2, mix3, own, sibling, out_ref):
@@ -972,13 +1053,18 @@
     def mine_of(vector):
         return lax.dynamic_slice_in_dim(vector, z * width, width, 0)[None]
 
-    kv0, r0, gate0, low0 = mixes_of(kind, block, rest, ratios[0], left[0])
-    kv1, r1, gate1, low1 = mixes_of(kind, own_x, rest_x, ratios[1], left[1])
-    kv2, r2, gate2, low2 = mixes_of(kind, own_y, rest_y, ratios[2], left[2])
+    kv_own, kv0, r0, gate0, low0 = mixes_of(kind, block, rest, ratios[0], left[0])
+    kv1, r1, gate1, low1, *parts = mix_and_project(
+        1, kind, own_x, rest_x, ratios[1], left[1], own_kv, kv_own
+    )
+    kv2, r2, gate2, low2, *parts = mix_and_project(
+        2, kind, own_y, rest_y, ratios[2], left[2], own_kv, *parts
+    )
     keys, values, decay, r3, gate3 = projected(
         kind,
         (kv0, kv1, kv2),
         (low0, low1, low2),
+        parts,
         own_xy,
         rest_xy,
         ratios[3],
@@ -988,7 +1074,6 @@
         lax.dynamic_slice_in_dim(fading_right_factor, z * width, width, 1),
         mine_of(fading_baseline),
     )
-    recept = plain_product(kind, (r0, r1, r2, r3), own_r, sibling_r)
     entered = lax.dynamic_slice_in_dim(carried_memory, z * heads, heads, 0)
     bonus = lax.dynamic_slice_in_dim(present_reward, z * heads, heads, 0).reshape(1, width)
     states, states_in = states_of(
@@ -999,6 +1084,16 @@
         decay,
         jnp.where(is_long, entered, 0.0),
     )
+    states = states.reshape(lines, 2, requests, heads, span, span)
+    passed = flipped_core(lax.dynamic_index_in_dim(states, 1 - core, 1, keepdims=False))
+    held = lax.dynamic_index_in_dim(states, core, 1, keepdims=False)
+    bundle = jnp.concatenate(
+        [jnp.where(is_long, held, passed)[:, -1:], jnp.where(is_long, passed, held)], axis=1
+    ).astype(bf16)
+    bundle = after(bundle, gate_pieces)
+    r3 = after(r3, bundle)
+    arrived = dealt(lambda j: lax.dynamic_index_in_dim(bundle, j, 0, keepdims=False), z)
+    recept = plain_product(kind, (r0, r1, r2, r3), own_r, sibling_r)
     normed = sweep(
         extents,
         recept,
@@ -1011,20 +1106,12 @@
         mine_of(group_layer_shift_term),
     )
     own_gate, sibling_gate = both_cores(after(gate_pieces, states))
+    normed, arrived = lax.optimization_barrier((normed, arrived))
     kept0, sent0, kept1, sent1 = gated(
         kind, extents, (gate0, gate1, gate2, gate3), own_gate, sibling_gate, normed
     )
 
-    states = states.reshape(lines, 2, requests, heads, span, span)
-    passed = flipped_core(lax.dynamic_index_in_dim(states, 1 - core, 1, keepdims=False))
-    held = lax.dynamic_index_in_dim(states, core, 1, keepdims=False)
-    bundle = jnp.concatenate(
-        [jnp.where(is_long, held, passed)[:, -1:], jnp.where(is_long, passed, held)], axis=1
-    ).astype(bf16)
-    bundle = after(bundle, gate_pieces)
-    arrived = in_order(
-        dealt(lambda j: lax.dynamic_index_in_dim(bundle, j, 0, keepdims=False), z), z
-    ).astype(f32)
+    arrived = in_order(arrived, z).astype(f32)
     span_states = arrived[:, 0].reshape(1, lines * heads, span, span)
     request_states = jnp.swapaxes(arrived[:, 1:], 0, 1).reshape(
         requests, lines * heads, span, span

time: 307 us -> 273 us (0.89)
  Pallas kernels: 81.1 us -> 52 us
  waiting for transfers between devices: 86.8 us -> 63.2 us
  local copies, waits for them, and re-layouts: 24 us -> 37.3 us
  starting transfers between devices: 94.9 us -> 103 us
    ppermute x21, waiting for transfers between devices: 59.8 us -> 40.5 us  [turned(): lax.ppermute(x, axis, [(i, (i + by) % length) for i in range(length)])]
    unnamed x78 -> x134, local copies, waits for them, and re-layouts: 4.89 us -> 20.5 us
    pallas_call x3 -> x1, Pallas kernels: 20.8 us -> 5.96 us  [mixes_of(): pl.pallas_call(mix_kernel, grid=(2,), out_shape=outs, in_specs=[in_smem()...]
    pallas_call x0 -> x2, Pallas kernels: none -> 12 us  [mix_and_project(): pl.pallas_call(lambda *refs: mix_project_kernel(rel, *refs), grid=(2,), o...]
    ppermute x21, starting transfers between devices: 47.2 us -> 53.3 us  [turned(): lax.ppermute(x, axis, [(i, (i + by) % length) for i in range(length)])]
    pallas_call x1, Pallas kernels: 14 us -> 8.16 us  [projected(): pl.pallas_call(project_kernel, grid=(rows // TILE,), out_shape=[flat] * 3...]
    pallas_call x2, Pallas kernels: 9.03 us -> 4.26 us  [final_product(): pl.pallas_call(final_kernel, out_shape=[out] * 4, in_specs=[in_smem()] +...]
    dynamic_update_slice x8, local copies, waits for them, and re-layouts: 0.28 us -> 4.02 us  [in_order(): whole = lax.dynamic_update_index_in_dim(whole, piece, (z - k) % length, 0)]
  transfers between devices with their start and end apart: 52 -> 52, of which waited for: 17 -> 15; matrix products, arithmetic and copies ran while one was open for 11% -> 11% of each run, Pallas kernels for 22% -> 17%
where the time goes in v7:
time: 273 us; the launch traced here: 272 us
  starting transfers between devices  103 us (38%)
  waiting for transfers between devices  63.2 us (23%)
  Pallas kernels  52 us (19%)
  local copies, waits for them, and re-layouts  37.3 us (14%)
  other arithmetic  15.5 us (6%)
    ppermute x21, starting transfers between devices, turned(): lax.ppermute(x, axis, [(i, (i + by) % length) for i in range(length)])  53.3 us
    ppermute x21, waiting for transfers between devices, turned(): lax.ppermute(x, axis, [(i, (i + by) % length) for i in range(length)])  40.5 us
    ppermute x3, starting transfers between devices, near_along(): one = lax.ppermute(piece, 'z', [(0, 1), (1, 2), (2, 3)])  21.3 us
    unnamed x134, local copies, waits for them, and re-layouts  20.5 us
    ppermute x3, waiting for transfers between devices, far_along(): return lax.ppermute(two, 'z', [(1, 0), (2, 3)])  15.5 us
    pallas_call x2, Pallas kernels, mix_and_project(): pl.pallas_call(lambda *refs: mix_project_kernel(rel, *refs), grid=(2,), o...  12 us
    pallas_call x1, Pallas kernels, sweep(): pl.pallas_call(sweep_kernel, out_shape=jax.ShapeDtypeStruct(r.shape, f32)...  9.17 us
    pallas_call x1, Pallas kernels, projected(): pl.pallas_call(project_kernel, grid=(rows // TILE,), out_shape=[flat] * 3...  8.16 us
  transfers between devices with their start and end apart: 52, of which 15 were waited for; matrix products, arithmetic and copies ran while one was open for 11% of the time, Pallas kernels for 17%

profile of v7, /device:TPU:0, one launch (start us, length us, event | category | flops | bytes accessed | tf_op | source)
XLA Modules:
  0.0 272.3 jit_solution(10855769279320025838)
XLA Ops:
  6.5 5.0 %collective-permute-start.1 = (bf16[2,272,512]{2,1,0:T(8,128)(2,1)S(1)}, bf16[2,272,512]{2,1,0:T(8,128)(2,1)S(1)}, u32[]{:S(2)}, u32[]{:S(2)}) collective-permute-start(bf16[2,272,512]{2,1,0:T(8,128)(2,1)S(1)} %shard_map.185.own), channel_id=1, source_target_pairs={{0,8},{8,16},{16,24},{1,9},{9,17},{17,25},{2,10},{10,18},{18,26},{... | collective-permute-start | bytes 1671176 | tf_op jit(solution)/shard_map/ppermute | solution.py:891
  11.5 2.6 collective-permute-start.2
  15.4 1.6 collective-permute-start.4
  17.0 1.5 collective-permute-start.5
  23.3 1.4 fusion
  26.5 13.5 %collective-permute-done.2 = bf16[2,272,512]{2,1,0:T(8,128)(2,1)} collective-permute-done((bf16[2,272,512]{2,1,0:T(8,128)(2,1)S(1)}, bf16[2,272,512]{2,1,0:T(8,128)(2,1)}, u32[]{:S(2)}, u32[]{:S(2)}) %collective-permute-start.2) | collective-permute-done | bytes 557088 | tf_op jit(solution)/shard_map/ppermute | solution.py:869
  41.0 1.3 collective-permute-start.6
  43.1 1.5 collective-permute-start.7
  45.4 1.5 collective-permute-start.8
  50.9 1.4 collective-permute-done.8.own1
  52.4 12.3 %collective-permute-done.6 = bf16[2,272,512]{2,1,0:T(8,128)(2,1)S(1)} collective-permute-done((bf16[2,272,512]{2,1,0:T(8,128)(2,1)}, bf16[2,272,512]{2,1,0:T(8,128)(2,1)S(1)}, u32[]{:S(2)}, u32[]{:S(2)}) %collective-permute-start.6) | collective-permute-done | bytes 557088 | tf_op jit(solution)/shard_map/ppermute | solution.py:897
  66.1 1.6 collective-permute-start.12
  67.6 1.5 collective-permute-start.13
  70.7 1.7 broadcast_select_fusion.1
  72.4 1.6 pad_maximum_fusion.1
  75.1 3.9 %collective-permute-start.10 = (bf16[2,512,256]{2,1,0:T(8,128)(2,1)}, bf16[2,512,256]{2,1,0:T(8,128)(2,1)}, u32[]{:S(2)}, u32[]{:S(2)}) collective-permute-start(bf16[2,512,256]{2,1,0:T(8,128)(2,1)} %get-tuple-element.113), channel_id=1, source_target_pairs={{0,16},{8,24},{16,0},{24,8},{1,17},{9,25},{17,1},{25,9},{2,18},{10... | collective-permute-start | bytes 1572872 | tf_op jit(solution)/shard_map/ppermute | solution.py:869
  79.6 1.3 dynamic_update_slice.27
  80.9 1.3 dynamic_update_slice.28
  82.1 1.3 dynamic_update_slice.29
  86.9 6.0 %shard_map.186 = (bf16[2,1024,512]{2,1,0:T(8,128)(2,1)S(1)}, bf16[2,1024,512]{2,1,0:T(8,128)(2,1)S(1)}, bf16[2,1024,512]{2,1,0:T(8,128)(2,1)S(1)}, bf16[2,1024,512]{2,1,0:T(8,128)(2,1)S(1)}, f32[2,1024,128]{2,1,0:T(8,128)S(1)}) custom-call(s32[14]{0:T(128)S(1)} %copy-done.21, bf16[2,272,512]{2,1,0:T(8,128)(2,1)S(1)} %copy-done.13, ...), custom_call_target="tpu_custom_call" | custom-call | flops 8049999872 | bytes 21000000 | tf_op jit(solution)/shard_map/pallas_call | solution.py:396
  92.8 1.3 copy-done.33
  94.2 1.4 copy-done.35
  95.6 1.3 copy-done.37
  96.9 1.3 copy-done.41
  99.2 12.3 %collective-permute-done.10 = bf16[2,512,256]{2,1,0:T(8,128)(2,1)} collective-permute-done((bf16[2,512,256]{2,1,0:T(8,128)(2,1)}, bf16[2,512,256]{2,1,0:T(8,128)(2,1)}, u32[]{:S(2)}, u32[]{:S(2)}) %collective-permute-start.10) | collective-permute-done | bytes 524320 | tf_op jit(solution)/shard_map/ppermute | solution.py:869
  112.8 1.7 pad_maximum_fusion.refs_5_.own_kv
  114.7 1.3 slice_bitcast_fusion.1
  117.3 11.7 %collective-permute-start.16 = (bf16[1,512,256]{2,1,0:T(8,128)(2,1)S(1)}, bf16[1,512,256]{2,1,0:T(8,128)(2,1)S(1)}, u32[]{:S(2)}, u32[]{:S(2)}) collective-permute-start(bf16[1,512,256]{2,1,0:T(8,128)(2,1)S(1)} %copy-done.62), channel_id=1, source_target_pairs={{0,8},{8,16},{16,24},{24,0},{1,9},{9,17},{17,25},{25,1},{2,10},{10... | collective-permute-start | bytes 786440 | tf_op jit(solution)/shard_map/ppermute | solution.py:869
  129.6 1.6 copy-done.42
  131.2 6.6 %shard_map.187 = (bf16[2,1024,512]{2,1,0:T(8,128)(2,1)S(1)}, bf16[2,1024,512]{2,1,0:T(8,128)(2,1)S(1)}, bf16[2,1024,512]{2,1,0:T(8,128)(2,1)S(1)}, f32[2,1024,12...) custom-call(s32[14]{0:T(128)S(1)} %copy-done.22, bf16[2,272,512]{2,1,0:T(8,128)(2,1)S(1)} %copy-done.11, ...), custom_call_target="tpu_custom_call" | custom-call | flops 6899999744 | bytes 18000000 | tf_op jit(solution)/shard_map/pallas_call | solution.py:461
  137.9 1.8 collective-permute-start.18
  139.7 5.4 %shard_map.188 = (bf16[2,1024,512]{2,1,0:T(8,128)(2,1)S(1)}, bf16[2,1024,512]{2,1,0:T(8,128)(2,1)S(1)}, bf16[2,1024,512]{2,1,0:T(8,128)(2,1)S(1)}, f32[2,1024,12...) custom-call(s32[14]{0:T(128)S(1)} %copy-done.22, bf16[2,272,512]{2,1,0:T(8,128)(2,1)S(1)} %copy-done.9, ...), custom_call_target="tpu_custom_call" | custom-call | flops 6899999744 | bytes 18000000 | tf_op jit(solution)/shard_map/pallas_call | solution.py:461
  147.1 3.9 %collective-permute-done.18 = bf16[1,512,256]{2,1,0:T(8,128)(2,1)S(1)} collective-permute-done((bf16[1,512,256]{2,1,0:T(8,128)(2,1)S(1)}, bf16[1,512,256]{2,1,0:T(8,128)(2,1)S(1)}, u32[]{:S(2)}, u32[]{:S(2)}) %collective-permute-start.18) | collective-permute-done | bytes 262176 | tf_op jit(solution)/shard_map/ppermute | solution.py:869
  151.1 1.9 collective-permute-start.20
  153.0 2.3 collective-permute-start.21
  158.2 8.2 %shard_map.189 = (f32[1024,256]{1,0:T(8,128)S(1)}, f32[1024,256]{1,0:T(8,128)S(1)}, f32[1024,256]{1,0:T(8,128)S(1)}, bf16[2,1024,512]{2,1,0:T(8,128)(2,1)S(1)}, bf16[2,1024,512]{2,1,0:T(8,128)(2,1)S(1)}) custom-call(s32[14]{0:T(128)S(1)} %copy-done.22, bf16[2,1024,512]{2,1,0:T(8,128)(2,1)S(1)} %copy-done.36, ...), custom_call_target="tpu_custom_call" | custom-call | flops 9200000000 | bytes 24000000 | tf_op jit(solution)/shard_map/pallas_call | solution.py:546
  166.4 3.1 %shard_map.190 = (f32[16,4,64,64]{3,2,1,0:T(8,128)S(1)}, bf16[16,64,256]{2,1,0:T(8,128)(2,1)S(1)}) custom-call(s32[16]{0:T(128)S(1)} %select_n.354.lengths, f32[1]{0:T(128)} %bitcast.62.carry, f32[1024,256]{1,0:T(8,128)S(1)} %get-tuple-element.153.k_ref, f32[1024,256]{1,0:T(8,128)S(1)} %get-tuple-element.154.v_ref, ...), custom_call_target="tpu_custom_call" | custom-call | flops 8049999872 | bytes 21000000 | tf_op jit(solution)/shard_map/pallas_call | solution.py:716
  170.3 1.7 collective-permute-done.21
  172.7 6.1 %collective-permute-start.26 = (bf16[3,4,64,64]{3,2,1,0:T(8,128)(2,1)S(1)}, bf16[3,4,64,64]{3,2,1,0:T(8,128)(2,1)S(1)}, u32[]{:S(2)}, u32[]{:S(2)}) collective-permute-start(bf16[3,4,64,64]{3,2,1,0:T(8,128)(2,1)S(1)} %get-tuple-element.217), channel_id=1, source_target_pairs={{0,8},{8,16},{16,24},{24,0},{1,9},{9,17},{17,25},{25,1},{2,10},{10... | collective-permute-start | bytes 294920 | tf_op jit(solution)/shard_map/ppermute | solution.py:869
  181.2 3.2 %shard_map.191.r_ref = f32[1024,256]{1,0:T(8,128)S(1)} custom-call(s32[14]{0:T(128)S(1)} %copy-done.22, bf16[2,1024,512]{2,1,0:T(8,128)(2,1)S(1)} %copy-done.34, bf16[2,1024,512]{2,1,0:T(8,128)(2,1)S(1)} %get-tuple-element.163.mix1, bf16[2,1024,512]{2,1,0:T(8,128)(2,1)S(1)} %get-tuple-element.164.mix2, bf16[2,1024,512]{2,1,0:T(8,128)(2,1)S(1)} %get-tuple-element.167.mix3, ...), custom_call_target="tpu_custom_call" | custom-call | flops 6899999744 | bytes 18000000 | tf_op jit(solution)/shard_map/pallas_call | solution.py:581
  184.5 9.2 %shard_map.192.normed = f32[1024,256]{1,0:T(8,128)S(1)} custom-call(s32[16]{0:T(128)S(1)} %select_n.354.lengths, f32[1024,256]{1,0:T(8,128)S(1)} %shard_map.191.r_ref, f32[1024,256]{1,0:T(8,128)S(1)} %get-tuple-element.153.k_ref, f32[1024,256]{1,0:T(8,128)S(1)} %get-tuple-element.154.v_ref, f32[1024,256]{1,0:T(8,128)S(1)} %get-tuple-element.155.w_ref, ...), custom_call_target="tpu_custom_call" | custom-call | flops 13799999488 | bytes 36000000 | tf_op jit(solution)/shard_map/pallas_call | solution.py:802
  193.8 3.5 %shard_map.193 = (bf16[2,4,32,256]{3,2,1,0:T(8,128)(2,1)S(1)}, bf16[2,4,32,256]{3,2,1,0:T(8,128)(2,1)S(1)}, bf16[2,4,32,256]{3,2,1,0:T(8,128)(2,1)S(1)}, bf16[2,4,32,256]{3,2,1,0:T(8,128)(2,1)S(1)}) custom-call(s32[14]{0:T(128)S(1)} %copy-done.22, s32[16]{0:T(128)S(1)} %select_n.354.lengths, bf16[2,1024,512]{2,1,0:T(8,128)(2,1)S(1)} %copy-done.38, ...), custom_call_target="tpu_custom_call" | custom-call | flops 8049999872 | bytes 21000000 | tf_op jit(solution)/shard_map/pallas_call | solution.py:645
  198.7 3.5 %collective-permute-start.30 = (bf16[512,256]{1,0:T(8,128)(2,1)S(1)}, bf16[512,256]{1,0:T(8,128)(2,1)S(1)}, u32[]{:S(2)}, u32[]{:S(2)}) collective-permute-start(bf16[512,256]{1,0:T(8,128)(2,1)S(1)} %bitcast.155), channel_id=1, source_target_pairs={{0,16},{8,24},{16,0},{24,8},{1,17},{9,25},{17,1},{25,9},{2,18},{10... | collective-permute-start | bytes 786440 | tf_op jit(solution)/shard_map/ppermute | solution.py:869
  202.4 1.3 collective-permute-start.33
  203.7 5.3 %collective-permute-start.32 = (bf16[512,256]{1,0:T(8,128)(2,1)S(1)}, bf16[512,256]{1,0:T(8,128)(2,1)S(1)}, u32[]{:S(2)}, u32[]{:S(2)}) collective-permute-start(bf16[512,256]{1,0:T(8,128)(2,1)S(1)} %bitcast.157), channel_id=1, source_target_pairs={{0,8},{8,16},{16,24},{1,9},{9,17},{17,25},{2,10},{10,18},{18,26},{... | collective-permute-start | bytes 786440 | tf_op jit(solution)/shard_map/ppermute | solution.py:891
  209.0 5.9 %collective-permute-done.30.h2 = bf16[512,256]{1,0:T(8,128)(2,1)S(1)} collective-permute-done((bf16[512,256]{1,0:T(8,128)(2,1)S(1)}, bf16[512,256]{1,0:T(8,128)(2,1)S(1)}, u32[]{:S(2)}, u32[]{:S(2)}) %collective-permute-start.30) | collective-permute-done | bytes 262176 | tf_op jit(solution)/shard_map/ppermute | solution.py:869
  214.9 1.3 collective-permute-start.31
  216.3 1.3 collective-permute-start.45
  217.6 11.0 %collective-permute-start.44 = (bf16[512,256]{1,0:T(8,128)(2,1)S(1)}, bf16[512,256]{1,0:T(8,128)(2,1)S(1)}, u32[]{:S(2)}, u32[]{:S(2)}) collective-permute-start(bf16[512,256]{1,0:T(8,128)(2,1)S(1)} %bitcast.153), channel_id=1, source_target_pairs={{0,8},{8,16},{16,24},{1,9},{9,17},{17,25},{2,10},{10,18},{18,26},{... | collective-permute-start | bytes 786440 | tf_op jit(solution)/shard_map/ppermute | solution.py:891
  228.7 3.2 %collective-permute-done.42.h2 = bf16[512,256]{1,0:T(8,128)(2,1)S(1)} collective-permute-done((bf16[512,256]{1,0:T(8,128)(2,1)S(1)}, bf16[512,256]{1,0:T(8,128)(2,1)S(1)}, u32[]{:S(2)}, u32[]{:S(2)}) %collective-permute-start.42) | collective-permute-done | bytes 262176 | tf_op jit(solution)/shard_map/ppermute | solution.py:869
  231.8 1.5 collective-permute-start.43
  233.4 2.1 shard_map.194
  235.6 2.4 collective-permute-start.37
  239.8 3.1 %collective-permute-done.43 = bf16[512,256]{1,0:T(8,128)(2,1)S(1)} collective-permute-done((bf16[512,256]{1,0:T(8,128)(2,1)S(1)}, bf16[512,256]{1,0:T(8,128)(2,1)S(1)}, u32[]{:S(2)}, u32[]{:S(2)}) %collective-permute-start.43) | collective-permute-done | bytes 262176 | tf_op jit(solution)/shard_map/ppermute | solution.py:897
  243.0 2.1 shard_map.195
  245.1 2.4 collective-permute-start.48
  248.7 2.7 collective-permute-done.36
  251.6 2.8 %collective-permute-start.38 = (bf16[32,1024]{1,0:T(8,128)(2,1)S(1)}, bf16[32,1024]{1,0:T(8,128)(2,1)S(1)}, u32[]{:S(2)}, u32[]{:S(2)}) collective-permute-start(bf16[32,1024]{1,0:T(8,128)(2,1)S(1)} %get-tuple-element.229), channel_id=1, source_target_pairs={{0,8},{8,16},{16,24},{24,0},{1,9},{9,17},{17,25},{25,1},{2,10},{10... | collective-permute-start | bytes 196616 | tf_op jit(solution)/shard_map/ppermute | solution.py:869
  254.4 1.7 collective-permute-start.39
  257.0 3.2 %collective-permute-start.40 = (bf16[32,1024]{1,0:T(8,128)(2,1)S(1)}, bf16[32,1024]{1,0:T(8,128)(2,1)S(1)}, u32[]{:S(2)}, u32[]{:S(2)}) collective-permute-start(bf16[32,1024]{1,0:T(8,128)(2,1)S(1)} %get-tuple-element.227), channel_id=1, source_target_pairs={{0,24},{8,0},{16,8},{24,16},{1,25},{9,1},{17,9},{25,17},{2,26},{10... | collective-permute-start | bytes 196616 | tf_op jit(solution)/shard_map/ppermute | solution.py:869
  261.1 2.4 collective-permute-start.49
  263.5 2.5 collective-permute-start.50
  266.0 2.8 %collective-permute-start.51 = (bf16[32,1024]{1,0:T(8,128)(2,1)S(1)}, bf16[32,1024]{1,0:T(8,128)(2,1)S(1)}, u32[]{:S(2)}, u32[]{:S(2)}) collective-permute-start(bf16[32,1024]{1,0:T(8,128)(2,1)S(1)} %get-tuple-element.221), channel_id=1, source_target_pairs={{0,24},{8,0},{16,8},{24,16},{1,25},{9,1},{17,9},{25,17},{2,26},{10... | collective-permute-start | bytes 196616 | tf_op jit(solution)/shard_map/ppermute | solution.py:869
  270.9 1.4 shard_map.196
  (256 shorter events, 49.7 us)
Async XLA Ops:
  0.6 25.0 %copy-start = (bf16[128,1024]{1,0:T(8,128)(2,1)S(1)}, bf16[128,1024]{1,0:T(8,128)(2,1)}, u32[]{:S(2)}) copy-start(bf16[128,1024]{1,0:T(8,128)(2,1)} %param.29) | copy-start | bytes 786436
  4.1 1.8 collective-permute-start
  6.5 19.9 %copy-start.12 = (bf16[2,272,512]{2,1,0:T(8,128)(2,1)}, bf16[2,272,512]{2,1,0:T(8,128)(2,1)S(1)}, u32[]{:S(2)}) copy-start(bf16[2,272,512]{2,1,0:T(8,128)(2,1)S(1)} %shard_map.185.own) | copy-start | bytes 1671172
  6.5 19.9 %collective-permute-start.1 = (bf16[2,272,512]{2,1,0:T(8,128)(2,1)S(1)}, bf16[2,272,512]{2,1,0:T(8,128)(2,1)S(1)}, u32[]{:S(2)}, u32[]{:S(2)}) collective-permute-start(bf16[2,272,512]{2,1,0:T(8,128)(2,1)S(1)} %shard_map.185.own), channel_id=1, source_target_pairs={{0,8},{8,16},{16,24},{1,9},{9,17},{17,25},{2,10},{10,18},{18,26},{... | collective-permute-start | bytes 1671176 | tf_op jit(solution)/shard_map/ppermute | solution.py:891
  11.5 28.5 %collective-permute-start.2 = (bf16[2,272,512]{2,1,0:T(8,128)(2,1)S(1)}, bf16[2,272,512]{2,1,0:T(8,128)(2,1)}, u32[]{:S(2)}, u32[]{:S(2)}) collective-permute-start(bf16[2,272,512]{2,1,0:T(8,128)(2,1)S(1)} %shard_map.185.own), channel_id=1, source_target_pairs={{0,16},{8,24},{16,0},{24,8},{1,17},{9,25},{17,1},{25,9},{2,18},{10... | collective-permute-start | bytes 1671176 | tf_op jit(solution)/shard_map/ppermute | solution.py:869
  14.1 26.9 %collective-permute-start.3 = (bf16[2,272,512]{2,1,0:T(8,128)(2,1)S(1)}, bf16[2,272,512]{2,1,0:T(8,128)(2,1)S(1)}, u32[]{:S(2)}, u32[]{:S(2)}) collective-permute-start(bf16[2,272,512]{2,1,0:T(8,128)(2,1)S(1)} %shard_map.185.own), channel_id=1, source_target_pairs={{8,0},{16,8},{24,16},{9,1},{17,9},{25,17},{10,2},{18,10},{26,18},{... | collective-permute-start | bytes 1671176 | tf_op jit(solution)/shard_map/ppermute | solution.py:892
  15.4 25.6 %collective-permute-start.4 = (bf16[2,272,512]{2,1,0:T(8,128)(2,1)S(1)}, bf16[2,272,512]{2,1,0:T(8,128)(2,1)S(1)}, u32[]{:S(2)}, u32[]{:S(2)}) collective-permute-start(bf16[2,272,512]{2,1,0:T(8,128)(2,1)S(1)} %shard_map.185.own), channel_id=1, source_target_pairs={{0,1},{1,0},{2,3},{3,2},{4,5},{5,4},{6,7},{7,6},{8,9},{9,8},{10,11... | collective-permute-start | bytes 1671176 | tf_op jit(solution)/shard_map/ppermute | solution.py:877
  17.0 24.0 %collective-permute-start.5 = (bf16[2,272,512]{2,1,0:T(8,128)(2,1)S(1)}, bf16[2,272,512]{2,1,0:T(8,128)(2,1)S(1)}, u32[]{:S(2)}, u32[]{:S(2)}) collective-permute-start(bf16[2,272,512]{2,1,0:T(8,128)(2,1)S(1)} %shard_map.185.own), channel_id=1, source_target_pairs={{0,2},{2,0},{1,3},{3,1},{4,6},{6,4},{5,7},{7,5},{8,10},{10,8},{9,1... | collective-permute-start | bytes 1671176 | tf_op jit(solution)/shard_map/ppermute | solution.py:881
  26.4 44.2 %collective-permute-start.34 = (bf16[1024,512]{1,0:T(8,128)(2,1)}, bf16[1024,512]{1,0:T(8,128)(2,1)}, u32[]{:S(2)}, u32[]{:S(2)}) collective-permute-start(bf16[1024,512]{1,0:T(8,128)(2,1)} %param.33), channel_id=1, source_target_pairs={{0,4},{4,0},{1,5},{5,1},{2,6},{6,2},{3,7},{7,3},{8,12},{12,8},{9,1... | collective-permute-start | bytes 3145736 | tf_op jit(solution)/shard_map/ppermute | solution.py:873
  41.0 23.7 %collective-permute-start.6 = (bf16[2,272,512]{2,1,0:T(8,128)(2,1)}, bf16[2,272,512]{2,1,0:T(8,128)(2,1)S(1)}, u32[]{:S(2)}, u32[]{:S(2)}) collective-permute-start(bf16[2,272,512]{2,1,0:T(8,128)(2,1)} %collective-permute-done.2), channel_id=1, source_target_pairs={{8,0},{16,24},{9,1},{17,25},{10,2},{18,26},{11,3},{19,27},{12,4},{... | collective-permute-start | bytes 1671176 | tf_op jit(solution)/shard_map/ppermute | solution.py:897
  43.1 7.8 %collective-permute-start.7 = (bf16[272,512]{1,0:T(8,128)(2,1)S(1)}, bf16[272,512]{1,0:T(8,128)(2,1)S(1)}, u32[]{:S(2)}, u32[]{:S(2)}) collective-permute-start(bf16[272,512]{1,0:T(8,128)(2,1)S(1)} %slice_bitcast_fusion.6), channel_id=1, source_target_pairs={{0,2},{2,0},{1,3},{3,1},{4,6},{6,4},{5,7},{7,5},{8,10},{10,8},{9,1... | collective-permute-start | bytes 835592 | tf_op jit(solution)/shard_map/ppermute | solution.py:881
  45.4 7.0 %collective-permute-start.8 = (bf16[272,512]{1,0:T(8,128)(2,1)}, bf16[272,512]{1,0:T(8,128)(2,1)S(1)}, u32[]{:S(2)}, u32[]{:S(2)}) collective-permute-start(bf16[272,512]{1,0:T(8,128)(2,1)} %slice_bitcast_fusion.5), channel_id=1, source_target_pairs={{0,1},{1,0},{2,3},{3,2},{4,5},{5,4},{6,7},{7,6},{8,9},{9,8},{10,11... | collective-permute-start | bytes 835592 | tf_op jit(solution)/shard_map/ppermute | solution.py:877
  50.0 16.1 %copy-start.65 = (bf16[4,4]{1,0:T(4,128)(2,1)}, bf16[4,4]{1,0:T(4,128)(2,1)S(1)}, u32[]{:S(2)}) copy-start(bf16[4,4]{1,0:T(4,128)(2,1)S(1)} %dynamic_update_slice.26) | copy-start | bytes 100
  66.1 45.5 %collective-permute-start.12 = (bf16[2,3,272,512]{3,2,1,0:T(8,128)(2,1)S(1)}, bf16[2,3,272,512]{3,2,1,0:T(8,128)(2,1)}, u32[]{:S(2)}, u32[]{:S(2)}) collective-permute-start(bf16[2,3,272,512]{3,2,1,0:T(8,128)(2,1)S(1)} %pad_maximum_fusion.3.rest), channel_id=1, source_target_pairs={{0,1},{1,0},{2,3},{3,2},{4,5},{5,4},{6,7},{7,6},{8,9},{9,8},{10,11... | collective-permute-start | bytes 5013512 | tf_op jit(solution)/shard_map/ppermute | solution.py:877
  67.6 43.9 %collective-permute-start.13 = (bf16[2,3,272,512]{3,2,1,0:T(8,128)(2,1)S(1)}, bf16[2,3,272,512]{3,2,1,0:T(8,128)(2,1)S(1)}, u32[]{:S(2)}, u32[]{:S(2)}) collective-permute-start(bf16[2,3,272,512]{3,2,1,0:T(8,128)(2,1)S(1)} %pad_maximum_fusion.3.rest), channel_id=1, source_target_pairs={{0,2},{2,0},{1,3},{3,1},{4,6},{6,4},{5,7},{7,5},{8,10},{10,8},{9,1... | collective-permute-start | bytes 5013512 | tf_op jit(solution)/shard_map/ppermute | solution.py:881
  75.1 24.1 %collective-permute-start.9 = (bf16[2,512,256]{2,1,0:T(8,128)(2,1)}, bf16[2,512,256]{2,1,0:T(8,128)(2,1)}, u32[]{:S(2)}, u32[]{:S(2)}) collective-permute-start(bf16[2,512,256]{2,1,0:T(8,128)(2,1)} %get-tuple-element.112), channel_id=1, source_target_pairs={{0,8},{8,16},{16,24},{24,0},{1,9},{9,17},{17,25},{25,1},{2,10},{10... | collective-permute-start | bytes 1572872 | tf_op jit(solution)/shard_map/ppermute | solution.py:869
  75.1 36.4 %collective-permute-start.10 = (bf16[2,512,256]{2,1,0:T(8,128)(2,1)}, bf16[2,512,256]{2,1,0:T(8,128)(2,1)}, u32[]{:S(2)}, u32[]{:S(2)}) collective-permute-start(bf16[2,512,256]{2,1,0:T(8,128)(2,1)} %get-tuple-element.113), channel_id=1, source_target_pairs={{0,16},{8,24},{16,0},{24,8},{1,17},{9,25},{17,1},{25,9},{2,18},{10... | collective-permute-start | bytes 1572872 | tf_op jit(solution)/shard_map/ppermute | solution.py:869
  79.0 32.5 %collective-permute-start.11 = (bf16[2,512,256]{2,1,0:T(8,128)(2,1)}, bf16[2,512,256]{2,1,0:T(8,128)(2,1)}, u32[]{:S(2)}, u32[]{:S(2)}) collective-permute-start(bf16[2,512,256]{2,1,0:T(8,128)(2,1)} %get-tuple-element.114), channel_id=1, source_target_pairs={{0,24},{8,0},{16,8},{24,16},{1,25},{9,1},{17,9},{25,17},{2,26},{10... | collective-permute-start | bytes 1572872 | tf_op jit(solution)/shard_map/ppermute | solution.py:869
  86.9 25.9 %copy-start.50 = (bf16[2,512,256]{2,1,0:T(8,128)(2,1)S(1)}, bf16[2,512,256]{2,1,0:T(8,128)(2,1)}, u32[]{:S(2)}) copy-start(bf16[2,512,256]{2,1,0:T(8,128)(2,1)} %get-tuple-element.116) | copy-start | bytes 1572868
  112.7 16.8 %copy-start.7 = (bf16[2,512,128]{2,1,0:T(8,128)(2,1)S(1)}, bf16[2,512,128]{2,1,0:T(8,128)(2,1)}, u32[]{:S(2)}) copy-start(bf16[2,512,128]{2,1,0:T(8,128)(2,1)} %get-tuple-element.238.refs_4_) | copy-start | bytes 786436
  112.8 16.8 %copy-start.11 = (bf16[2,272,512]{2,1,0:T(8,128)(2,1)S(1)}, bf16[2,272,512]{2,1,0:T(8,128)(2,1)}, u32[]{:S(2)}) copy-start(bf16[2,272,512]{2,1,0:T(8,128)(2,1)} %copy-done.10) | copy-start | bytes 1671172
  112.8 16.8 %copy-start.16 = (f32[2,5,512]{2,1,0:T(8,128)S(1)}, f32[2,5,512]{2,1,0:T(8,128)}, u32[]{:S(2)}) copy-start(f32[2,5,512]{2,1,0:T(8,128)} %get-tuple-element.240.refs_3_) | copy-start | bytes 61444
  114.5 15.1 %copy-start.22 = (s32[14]{0:T(128)S(1)}, s32[14]{0:T(128)}, u32[]{:S(2)}) copy-start(s32[14]{0:T(128)} %copy-done.20) | copy-start | bytes 172
  114.5 41.2 %collective-permute-start.19 = (bf16[4,2,512,256]{3,2,1,0:T(8,128)(2,1)S(1)}, bf16[4,2,512,256]{3,2,1,0:T(8,128)(2,1)}, u32[]{:S(2)}, u32[]{:S(2)}) collective-permute-start(bf16[4,2,512,256]{3,2,1,0:T(8,128)(2,1)S(1)} %pad_maximum_fusion.refs_5_.own_kv), channel_id=1, source_target_pairs={{0,4},{4,0},{1,5},{5,1},{2,6},{6,2},{3,7},{7,3},{8,12},{12,8},{9,1... | collective-permute-start | bytes 6291464 | tf_op jit(solution)/shard_map/ppermute | solution.py:873
  116.0 35.0 %collective-permute-start.14 = (bf16[3,272,512]{2,1,0:T(8,128)(2,1)S(1)}, bf16[3,272,512]{2,1,0:T(8,128)(2,1)S(1)}, u32[]{:S(2)}, u32[]{:S(2)}) collective-permute-start(bf16[3,272,512]{2,1,0:T(8,128)(2,1)S(1)} %slice_bitcast_fusion.1), channel_id=1, source_target_pairs={{0,2},{2,0},{1,3},{3,1},{4,6},{6,4},{5,7},{7,5},{8,10},{10,8},{9,1... | collective-permute-start | bytes 2506760 | tf_op jit(solution)/shard_map/ppermute | solution.py:881
  116.6 34.4 %collective-permute-start.15 = (bf16[3,272,512]{2,1,0:T(8,128)(2,1)S(1)}, bf16[3,272,512]{2,1,0:T(8,128)(2,1)S(1)}, u32[]{:S(2)}, u32[]{:S(2)}) collective-permute-start(bf16[3,272,512]{2,1,0:T(8,128)(2,1)S(1)} %slice_bitcast_fusion), channel_id=1, source_target_pairs={{0,1},{1,0},{2,3},{3,2},{4,5},{5,4},{6,7},{7,6},{8,9},{9,8},{10,11... | collective-permute-start | bytes 2506760 | tf_op jit(solution)/shard_map/ppermute | solution.py:877
  117.3 20.6 %collective-permute-start.16 = (bf16[1,512,256]{2,1,0:T(8,128)(2,1)S(1)}, bf16[1,512,256]{2,1,0:T(8,128)(2,1)S(1)}, u32[]{:S(2)}, u32[]{:S(2)}) collective-permute-start(bf16[1,512,256]{2,1,0:T(8,128)(2,1)S(1)} %copy-done.62), channel_id=1, source_target_pairs={{0,8},{8,16},{16,24},{24,0},{1,9},{9,17},{17,25},{25,1},{2,10},{10... | collective-permute-start | bytes 786440 | tf_op jit(solution)/shard_map/ppermute | solution.py:869
  129.0 18.2 %collective-permute-start.17 = (bf16[1,512,256]{2,1,0:T(8,128)(2,1)}, bf16[1,512,256]{2,1,0:T(8,128)(2,1)S(1)}, u32[]{:S(2)}, u32[]{:S(2)}) collective-permute-start(bf16[1,512,256]{2,1,0:T(8,128)(2,1)} %get-tuple-element.137), channel_id=1, source_target_pairs={{0,16},{8,24},{16,0},{24,8},{1,17},{9,25},{17,1},{25,9},{2,18},{10... | collective-permute-start | bytes 786440 | tf_op jit(solution)/shard_map/ppermute | solution.py:869
  137.9 13.2 %collective-permute-start.18 = (bf16[1,512,256]{2,1,0:T(8,128)(2,1)S(1)}, bf16[1,512,256]{2,1,0:T(8,128)(2,1)S(1)}, u32[]{:S(2)}, u32[]{:S(2)}) collective-permute-start(bf16[1,512,256]{2,1,0:T(8,128)(2,1)S(1)} %copy-done.61), channel_id=1, source_target_pairs={{0,24},{8,0},{16,8},{24,16},{1,25},{9,1},{17,9},{25,17},{2,26},{10... | collective-permute-start | bytes 786440 | tf_op jit(solution)/shard_map/ppermute | solution.py:869
  139.7 15.6 %copy-start.58 = (bf16[1,512,256]{2,1,0:T(8,128)(2,1)S(1)}, bf16[1,512,256]{2,1,0:T(8,128)(2,1)}, u32[]{:S(2)}) copy-start(bf16[1,512,256]{2,1,0:T(8,128)(2,1)} %get-tuple-element.152) | copy-start | bytes 786436
  139.7 15.8 %copy-start.57 = (bf16[1,512,256]{2,1,0:T(8,128)(2,1)S(1)}, bf16[1,512,256]{2,1,0:T(8,128)(2,1)}, u32[]{:S(2)}) copy-start(bf16[1,512,256]{2,1,0:T(8,128)(2,1)} %get-tuple-element.145) | copy-start | bytes 786436
  139.7 16.0 %copy-start.36 = (bf16[2,1024,512]{2,1,0:T(8,128)(2,1)S(1)}, bf16[2,1024,512]{2,1,0:T(8,128)(2,1)}, u32[]{:S(2)}) copy-start(bf16[2,1024,512]{2,1,0:T(8,128)(2,1)} %copy-done.35) | copy-start | bytes 6291460
  151.1 19.3 %collective-permute-start.20 = (bf16[1,512,256]{2,1,0:T(8,128)(2,1)S(1)}, bf16[1,512,256]{2,1,0:T(8,128)(2,1)S(1)}, u32[]{:S(2)}, u32[]{:S(2)}) collective-permute-start(bf16[1,512,256]{2,1,0:T(8,128)(2,1)S(1)} %copy-done.60), channel_id=1, source_target_pairs={{0,8},{8,16},{16,24},{24,0},{1,9},{9,17},{17,25},{25,1},{2,10},{10... | collective-permute-start | bytes 786440 | tf_op jit(solution)/shard_map/ppermute | solution.py:869
  153.0 19.0 %collective-permute-start.21 = (bf16[1,512,256]{2,1,0:T(8,128)(2,1)S(1)}, bf16[1,512,256]{2,1,0:T(8,128)(2,1)S(1)}, u32[]{:S(2)}, u32[]{:S(2)}) collective-permute-start(bf16[1,512,256]{2,1,0:T(8,128)(2,1)S(1)} %copy-done.59), channel_id=1, source_target_pairs={{0,16},{8,24},{16,0},{24,8},{1,17},{9,25},{17,1},{25,9},{2,18},{10... | collective-permute-start | bytes 786440 | tf_op jit(solution)/shard_map/ppermute | solution.py:869
  155.3 16.7 %collective-permute-start.22 = (bf16[1,512,256]{2,1,0:T(8,128)(2,1)S(1)}, bf16[1,512,256]{2,1,0:T(8,128)(2,1)S(1)}, u32[]{:S(2)}, u32[]{:S(2)}) collective-permute-start(bf16[1,512,256]{2,1,0:T(8,128)(2,1)S(1)} %copy-done.58), channel_id=1, source_target_pairs={{0,24},{8,0},{16,8},{24,16},{1,25},{9,1},{17,9},{25,17},{2,26},{10... | collective-permute-start | bytes 786440 | tf_op jit(solution)/shard_map/ppermute | solution.py:869
  155.6 25.6 %collective-permute-start.25 = (bf16[4,1,512,256]{3,2,1,0:T(8,128)(2,1)S(1)}, bf16[4,1,512,256]{3,2,1,0:T(8,128)(2,1)S(1)}, u32[]{:S(2)}, u32[]{:S(2)}) collective-permute-start(bf16[4,1,512,256]{3,2,1,0:T(8,128)(2,1)S(1)} %pad_maximum_fusion.5.own), channel_id=1, source_target_pairs={{0,4},{4,0},{1,5},{5,1},{2,6},{6,2},{3,7},{7,3},{8,12},{12,8},{9,1... | collective-permute-start | bytes 3145736 | tf_op jit(solution)/shard_map/ppermute | solution.py:873
  169.6 2.6 collective-permute-start.24
  172.1 21.6 %collective-permute-start.23 = (bf16[4,1,512,256]{3,2,1,0:T(8,128)(2,1)S(1)}, bf16[4,1,512,256]{3,2,1,0:T(8,128)(2,1)S(1)}, u32[]{:S(2)}, u32[]{:S(2)}) collective-permute-start(bf16[4,1,512,256]{3,2,1,0:T(8,128)(2,1)S(1)} %pad_maximum_fusion.4.own), channel_id=1, source_target_pairs={{0,4},{4,0},{1,5},{5,1},{2,6},{6,2},{3,7},{7,3},{8,12},{12,8},{9,1... | collective-permute-start | bytes 3145736 | tf_op jit(solution)/shard_map/ppermute | solution.py:873
  172.7 21.0 %collective-permute-start.26 = (bf16[3,4,64,64]{3,2,1,0:T(8,128)(2,1)S(1)}, bf16[3,4,64,64]{3,2,1,0:T(8,128)(2,1)S(1)}, u32[]{:S(2)}, u32[]{:S(2)}) collective-permute-start(bf16[3,4,64,64]{3,2,1,0:T(8,128)(2,1)S(1)} %get-tuple-element.217), channel_id=1, source_target_pairs={{0,8},{8,16},{16,24},{24,0},{1,9},{9,17},{17,25},{25,1},{2,10},{10... | collective-permute-start | bytes 294920 | tf_op jit(solution)/shard_map/ppermute | solution.py:869
  178.8 14.9 %collective-permute-start.27 = (bf16[3,4,64,64]{3,2,1,0:T(8,128)(2,1)S(1)}, bf16[3,4,64,64]{3,2,1,0:T(8,128)(2,1)S(1)}, u32[]{:S(2)}, u32[]{:S(2)}) collective-permute-start(bf16[3,4,64,64]{3,2,1,0:T(8,128)(2,1)S(1)} %get-tuple-element.216), channel_id=1, source_target_pairs={{0,16},{8,24},{16,0},{24,8},{1,17},{9,25},{17,1},{25,9},{2,18},{10... | collective-permute-start | bytes 294920 | tf_op jit(solution)/shard_map/ppermute | solution.py:869
  180.0 13.7 %collective-permute-start.28 = (bf16[3,4,64,64]{3,2,1,0:T(8,128)(2,1)S(1)}, bf16[3,4,64,64]{3,2,1,0:T(8,128)(2,1)S(1)}, u32[]{:S(2)}, u32[]{:S(2)}) collective-permute-start(bf16[3,4,64,64]{3,2,1,0:T(8,128)(2,1)S(1)} %get-tuple-element.215), channel_id=1, source_target_pairs={{0,24},{8,0},{16,8},{24,16},{1,25},{9,1},{17,9},{25,17},{2,26},{10... | collective-permute-start | bytes 294920 | tf_op jit(solution)/shard_map/ppermute | solution.py:869
  197.2 1.4 collective-permute-start.29
  197.6 11.4 %collective-permute-start.41 = (bf16[2,4,32,256]{3,2,1,0:T(8,128)(2,1)S(1)}, bf16[2,4,32,256]{3,2,1,0:T(8,128)(2,1)S(1)}, u32[]{:S(2)}, u32[]{:S(2)}) collective-permute-start(bf16[2,4,32,256]{3,2,1,0:T(8,128)(2,1)S(1)} %get-tuple-element.181), channel_id=1, source_target_pairs={{0,4},{4,0},{1,5},{5,1},{2,6},{6,2},{3,7},{7,3},{8,12},{12,8},{9,1... | collective-permute-start | bytes 393224 | tf_op jit(solution)/shard_map/ppermute | solution.py:873
  198.6 34.8 %copy-start.19 = (s32[4]{0:T(128)S(1)}, s32[4]{0:T(128)}, u32[]{:S(2)}) copy-start(s32[4]{0:T(128)} %pad_add_fusion.1.block_of) | copy-start | bytes 52
  198.7 16.3 %collective-permute-start.30 = (bf16[512,256]{1,0:T(8,128)(2,1)S(1)}, bf16[512,256]{1,0:T(8,128)(2,1)S(1)}, u32[]{:S(2)}, u32[]{:S(2)}) collective-permute-start(bf16[512,256]{1,0:T(8,128)(2,1)S(1)} %bitcast.155), channel_id=1, source_target_pairs={{0,16},{8,24},{16,0},{24,8},{1,17},{9,25},{17,1},{25,9},{2,18},{10... | collective-permute-start | bytes 786440 | tf_op jit(solution)/shard_map/ppermute | solution.py:869
  202.4 15.2 %collective-permute-start.33 = (bf16[512,256]{1,0:T(8,128)(2,1)S(1)}, bf16[512,256]{1,0:T(8,128)(2,1)S(1)}, u32[]{:S(2)}, u32[]{:S(2)}) collective-permute-start(bf16[512,256]{1,0:T(8,128)(2,1)S(1)} %bitcast.156), channel_id=1, source_target_pairs={{8,0},{16,8},{24,16},{9,1},{17,9},{25,17},{10,2},{18,10},{26,18},{... | collective-permute-start | bytes 786440 | tf_op jit(solution)/shard_map/ppermute | solution.py:892
  203.7 29.6 %collective-permute-start.32 = (bf16[512,256]{1,0:T(8,128)(2,1)S(1)}, bf16[512,256]{1,0:T(8,128)(2,1)S(1)}, u32[]{:S(2)}, u32[]{:S(2)}) collective-permute-start(bf16[512,256]{1,0:T(8,128)(2,1)S(1)} %bitcast.157), channel_id=1, source_target_pairs={{0,8},{8,16},{16,24},{1,9},{9,17},{17,25},{2,10},{10,18},{18,26},{... | collective-permute-start | bytes 786440 | tf_op jit(solution)/shard_map/ppermute | solution.py:891
  214.9 16.9 %collective-permute-start.42 = (bf16[512,256]{1,0:T(8,128)(2,1)S(1)}, bf16[512,256]{1,0:T(8,128)(2,1)S(1)}, u32[]{:S(2)}, u32[]{:S(2)}) collective-permute-start(bf16[512,256]{1,0:T(8,128)(2,1)S(1)} %bitcast.151), channel_id=1, source_target_pairs={{0,16},{8,24},{16,0},{24,8},{1,17},{9,25},{17,1},{25,9},{2,18},{10... | collective-permute-start | bytes 786440 | tf_op jit(solution)/shard_map/ppermute | solution.py:869
  214.9 18.4 %collective-permute-start.31 = (bf16[512,256]{1,0:T(8,128)(2,1)S(1)}, bf16[512,256]{1,0:T(8,128)(2,1)S(1)}, u32[]{:S(2)}, u32[]{:S(2)}) collective-permute-start(bf16[512,256]{1,0:T(8,128)(2,1)S(1)} %collective-permute-done.30.h2), channel_id=1, source_target_pairs={{8,0},{16,24},{9,1},{17,25},{10,2},{18,26},{11,3},{19,27},{12,4},{... | collective-permute-start | bytes 786440 | tf_op jit(solution)/shard_map/ppermute | solution.py:897
  216.3 22.3 %collective-permute-start.45 = (bf16[512,256]{1,0:T(8,128)(2,1)S(1)}, bf16[512,256]{1,0:T(8,128)(2,1)S(1)}, u32[]{:S(2)}, u32[]{:S(2)}) collective-permute-start(bf16[512,256]{1,0:T(8,128)(2,1)S(1)} %bitcast.152), channel_id=1, source_target_pairs={{8,0},{16,8},{24,16},{9,1},{17,9},{25,17},{10,2},{18,10},{26,18},{... | collective-permute-start | bytes 786440 | tf_op jit(solution)/shard_map/ppermute | solution.py:892
  217.6 22.2 %collective-permute-start.44 = (bf16[512,256]{1,0:T(8,128)(2,1)S(1)}, bf16[512,256]{1,0:T(8,128)(2,1)S(1)}, u32[]{:S(2)}, u32[]{:S(2)}) collective-permute-start(bf16[512,256]{1,0:T(8,128)(2,1)S(1)} %bitcast.153), channel_id=1, source_target_pairs={{0,8},{8,16},{16,24},{1,9},{9,17},{17,25},{2,10},{10,18},{18,26},{... | collective-permute-start | bytes 786440 | tf_op jit(solution)/shard_map/ppermute | solution.py:891
  231.8 11.1 %collective-permute-start.43 = (bf16[512,256]{1,0:T(8,128)(2,1)S(1)}, bf16[512,256]{1,0:T(8,128)(2,1)S(1)}, u32[]{:S(2)}, u32[]{:S(2)}) collective-permute-start(bf16[512,256]{1,0:T(8,128)(2,1)S(1)} %collective-permute-done.42.h2), channel_id=1, source_target_pairs={{8,0},{16,24},{9,1},{17,25},{10,2},{18,26},{11,3},{19,27},{12,4},{... | collective-permute-start | bytes 786440 | tf_op jit(solution)/shard_map/ppermute | solution.py:897
  235.6 12.5 %collective-permute-start.37 = (bf16[4,32,1024]{2,1,0:T(8,128)(2,1)S(1)}, bf16[4,32,1024]{2,1,0:T(8,128)(2,1)S(1)}, u32[]{:S(2)}, u32[]{:S(2)}) collective-permute-start(bf16[4,32,1024]{2,1,0:T(8,128)(2,1)S(1)} %get-tuple-element.179), channel_id=1, source_target_pairs={{0,3},{1,2},{2,1},{3,0},{4,7},{5,6},{6,5},{7,4},{8,11},{9,10},{10,... | collective-permute-start | bytes 786440 | tf_op jit(solution)/shard_map/ppermute | solution.py:1153
  238.0 13.4 %collective-permute-start.36 = (bf16[4,32,1024]{2,1,0:T(8,128)(2,1)S(1)}, bf16[4,32,1024]{2,1,0:T(8,128)(2,1)S(1)}, u32[]{:S(2)}, u32[]{:S(2)}) collective-permute-start(bf16[4,32,1024]{2,1,0:T(8,128)(2,1)S(1)} %get-tuple-element.178), channel_id=1, source_target_pairs={{0,2},{2,0},{1,3},{3,1},{4,6},{6,4},{5,7},{7,5},{8,10},{10,8},{9,1... | collective-permute-start | bytes 786440 | tf_op jit(solution)/shard_map/ppermute | solution.py:881
  238.6 12.8 %collective-permute-start.35 = (bf16[4,32,1024]{2,1,0:T(8,128)(2,1)S(1)}, bf16[4,32,1024]{2,1,0:T(8,128)(2,1)S(1)}, u32[]{:S(2)}, u32[]{:S(2)}) collective-permute-start(bf16[4,32,1024]{2,1,0:T(8,128)(2,1)S(1)} %get-tuple-element.177), channel_id=1, source_target_pairs={{0,1},{1,0},{2,3},{3,2},{4,5},{5,4},{6,7},{7,6},{8,9},{9,8},{10,11... | collective-permute-start | bytes 786440 | tf_op jit(solution)/shard_map/ppermute | solution.py:877
  245.1 11.9 %collective-permute-start.48 = (bf16[4,32,1024]{2,1,0:T(8,128)(2,1)S(1)}, bf16[4,32,1024]{2,1,0:T(8,128)(2,1)S(1)}, u32[]{:S(2)}, u32[]{:S(2)}) collective-permute-start(bf16[4,32,1024]{2,1,0:T(8,128)(2,1)S(1)} %get-tuple-element.186), channel_id=1, source_target_pairs={{0,3},{1,2},{2,1},{3,0},{4,7},{5,6},{6,5},{7,4},{8,11},{9,10},{10,... | collective-permute-start | bytes 786440 | tf_op jit(solution)/shard_map/ppermute | solution.py:1153
  247.5 13.2 %collective-permute-start.47 = (bf16[4,32,1024]{2,1,0:T(8,128)(2,1)S(1)}, bf16[4,32,1024]{2,1,0:T(8,128)(2,1)S(1)}, u32[]{:S(2)}, u32[]{:S(2)}) collective-permute-start(bf16[4,32,1024]{2,1,0:T(8,128)(2,1)S(1)} %get-tuple-element.185), channel_id=1, source_target_pairs={{0,2},{2,0},{1,3},{3,1},{4,6},{6,4},{5,7},{7,5},{8,10},{10,8},{9,1... | collective-permute-start | bytes 786440 | tf_op jit(solution)/shard_map/ppermute | solution.py:881
  248.1 12.7 %collective-permute-start.46 = (bf16[4,32,1024]{2,1,0:T(8,128)(2,1)S(1)}, bf16[4,32,1024]{2,1,0:T(8,128)(2,1)S(1)}, u32[]{:S(2)}, u32[]{:S(2)}) collective-permute-start(bf16[4,32,1024]{2,1,0:T(8,128)(2,1)S(1)} %get-tuple-element.184), channel_id=1, source_target_pairs={{0,1},{1,0},{2,3},{3,2},{4,5},{5,4},{6,7},{7,6},{8,9},{9,8},{10,11... | collective-permute-start | bytes 786440 | tf_op jit(solution)/shard_map/ppermute | solution.py:877
  251.6 14.5 %collective-permute-start.38 = (bf16[32,1024]{1,0:T(8,128)(2,1)S(1)}, bf16[32,1024]{1,0:T(8,128)(2,1)S(1)}, u32[]{:S(2)}, u32[]{:S(2)}) collective-permute-start(bf16[32,1024]{1,0:T(8,128)(2,1)S(1)} %get-tuple-element.229), channel_id=1, source_target_pairs={{0,8},{8,16},{16,24},{24,0},{1,9},{9,17},{17,25},{25,1},{2,10},{10... | collective-permute-start | bytes 196616 | tf_op jit(solution)/shard_map/ppermute | solution.py:869
  254.4 16.4 %collective-permute-start.39 = (bf16[32,1024]{1,0:T(8,128)(2,1)S(1)}, bf16[32,1024]{1,0:T(8,128)(2,1)S(1)}, u32[]{:S(2)}, u32[]{:S(2)}) collective-permute-start(bf16[32,1024]{1,0:T(8,128)(2,1)S(1)} %get-tuple-element.228), channel_id=1, source_target_pairs={{0,16},{8,24},{16,0},{24,8},{1,17},{9,25},{17,1},{25,9},{2,18},{10... | collective-permute-start | bytes 196616 | tf_op jit(solution)/shard_map/ppermute | solution.py:869
  257.0 13.9 %collective-permute-start.40 = (bf16[32,1024]{1,0:T(8,128)(2,1)S(1)}, bf16[32,1024]{1,0:T(8,128)(2,1)S(1)}, u32[]{:S(2)}, u32[]{:S(2)}) collective-permute-start(bf16[32,1024]{1,0:T(8,128)(2,1)S(1)} %get-tuple-element.227), channel_id=1, source_target_pairs={{0,24},{8,0},{16,8},{24,16},{1,25},{9,1},{17,9},{25,17},{2,26},{10... | collective-permute-start | bytes 196616 | tf_op jit(solution)/shard_map/ppermute | solution.py:869
  261.1 9.8 %collective-permute-start.49 = (bf16[32,1024]{1,0:T(8,128)(2,1)S(1)}, bf16[32,1024]{1,0:T(8,128)(2,1)S(1)}, u32[]{:S(2)}, u32[]{:S(2)}) collective-permute-start(bf16[32,1024]{1,0:T(8,128)(2,1)S(1)} %get-tuple-element.223), channel_id=1, source_target_pairs={{0,8},{8,16},{16,24},{24,0},{1,9},{9,17},{17,25},{25,1},{2,10},{10... | collective-permute-start | bytes 196616 | tf_op jit(solution)/shard_map/ppermute | solution.py:869
  263.5 7.4 %collective-permute-start.50 = (bf16[32,1024]{1,0:T(8,128)(2,1)S(1)}, bf16[32,1024]{1,0:T(8,128)(2,1)S(1)}, u32[]{:S(2)}, u32[]{:S(2)}) collective-permute-start(bf16[32,1024]{1,0:T(8,128)(2,1)S(1)} %get-tuple-element.222), channel_id=1, source_target_pairs={{0,16},{8,24},{16,0},{24,8},{1,17},{9,25},{17,1},{25,9},{2,18},{10... | collective-permute-start | bytes 196616 | tf_op jit(solution)/shard_map/ppermute | solution.py:869
  266.0 4.8 %collective-permute-start.51 = (bf16[32,1024]{1,0:T(8,128)(2,1)S(1)}, bf16[32,1024]{1,0:T(8,128)(2,1)S(1)}, u32[]{:S(2)}, u32[]{:S(2)}) collective-permute-start(bf16[32,1024]{1,0:T(8,128)(2,1)S(1)} %get-tuple-element.221), channel_id=1, source_target_pairs={{0,24},{8,0},{16,8},{24,16},{1,25},{9,1},{17,9},{25,17},{2,26},{10... | collective-permute-start | bytes 196616 | tf_op jit(solution)/shard_map/ppermute | solution.py:869
  (55 other events, 269.9 us)

commit v8 on v7

--- a/solution.py
+++ b/solution.py
@@ -742,7 +742,7 @@
     def against(a, b):
         return lax.dot_general(a, b, (((1,), (1,)), ((), ())), preferred_element_type=f32)
 
-    @pl.loop(0, r_ref.shape[0] // span, unroll=4)
+    @pl.loop(0, r_ref.shape[0] // span, unroll=8)
     def _(n):
         at = pl.ds(pl.multiple_of(n * span, span), span)
         live = row < lengths[n]
@@ -1004,12 +1004,29 @@
             carried_memory,
         )
     )
+    def blocks_of(*weights):
+        stacked = jnp.stack(weights)
+        return tuple(
+            lax.dynamic_slice_in_dim(stacked, (z + k) % lines * width, width, 2)
+            for k in range(lines)
+        )
+
+    def both_cores(pieces):
+        own = jnp.stack(pieces)
+        return own, flipped_core(own)
+
+    kv = blocks_of(lookup_transform, payload_transform)
+    r = blocks_of(acceptance_transform)
+    gate = blocks_of(gating_transform)
     one, two, three = near_along(block)
     own_x, own_y = over_x(block), over_y(block)
-    one, two, three, own_x, own_y = lax.optimization_barrier((one, two, three, own_x, own_y))
+    one, two, three, own_x, own_y, kv, r = lax.optimization_barrier(
+        (one, two, three, own_x, own_y, kv, r)
+    )
     far = far_along(two)
     own_xy = (over_y(own_x[0]), over_x(own_y[1]))
-    far, own_xy = lax.optimization_barrier((far, own_xy))
+    kv_two = turned(kv[2], "z", 2)
+    far, own_xy, kv, r = lax.optimization_barrier((far, own_xy, kv, r))
     rest = jnp.stack([jnp.where(z == 0, far, one), two, jnp.where(z == 3, far, three)], axis=1)
     rest_x, rest_y = over_x(rest), over_y(rest)
     extents = in_order(
@@ -1028,27 +1045,19 @@
     ratios = [part.transpose(0, 2, 1) for part in chunk_order(token_mixing_ratios.T)]
     left = chunk_order(fading_left_factor)
 
-    def columns_of(weights, *ready):
-        stacked = jnp.stack(weights)
-        blocks = [
-            lax.dynamic_slice_in_dim(stacked, (z + k) % lines * width, width, 2)
-            for k in range(lines)
-        ]
-        blocks = lax.optimization_barrier((tuple(blocks),) + ready)[0]
-        return (blocks[0],) + tuple(turned(blocks[k], "z", k) for k in range(1, lines))
-
-    def both_cores(pieces):
-        own = jnp.stack(pieces)
-        return own, flipped_core(own)
-
-    kv_pieces = columns_of([lookup_transform, payload_transform], rest, own_xy)
-    kv_pieces, rest_x, rest_y = lax.optimization_barrier((kv_pieces, rest_x, rest_y))
+    kv_one, kv_three = turned(kv[1], "z", 1), turned(kv[3], "z", 3)
+    rest_x, rest_y, kv_one, kv_two, kv_three, r, gate = lax.optimization_barrier(
+        (rest_x, rest_y, kv_one, kv_two, kv_three, r, gate)
+    )
     rest_xy = (over_y(rest_x[0]), over_x(rest_y[1]))
-    r_pieces = columns_of([acceptance_transform], rest_x, rest_y, kv_pieces)
-    own_kv, sibling_kv = both_cores(kv_pieces)
-    rest_xy, r_pieces = lax.optimization_barrier((rest_xy, r_pieces))
-    gate_pieces = columns_of([gating_transform], r_pieces, rest_xy)
-    own_r, sibling_r = both_cores(r_pieces)
+    own_kv, sibling_kv = both_cores((kv[0], kv_one, kv_two, kv_three))
+    r_one, r_two, r_three = (turned(r[k], "z", k) for k in range(1, lines))
+    rest_xy, r_one, r_two, r_three, gate = lax.optimization_barrier(
+        (rest_xy, r_one, r_two, r_three, gate)
+    )
+    gate_two = turned(gate[2], "z", 2)
+    gate_pieces = (gate[0], turned(gate[1], "z", 1), gate_two, turned(gate[3], "z", 3))
+    own_r, sibling_r = both_cores((r[0], r_one, r_two, r_three))
 
     def mine_of(vector):
         return lax.dynamic_slice_in_dim(vector, z * width, width, 0)[None]
@@ -1106,11 +1115,13 @@
         mine_of(group_layer_shift_term),
     )
     own_gate, sibling_gate = both_cores(after(gate_pieces, states))
-    normed, arrived = lax.optimization_barrier((normed, arrived))
     kept0, sent0, kept1, sent1 = gated(
         kind, extents, (gate0, gate1, gate2, gate3), own_gate, sibling_gate, normed
     )
 
+    kept0, sent0, kept1, sent1, arrived = lax.optimization_barrier(
+        (kept0, sent0, kept1, sent1, arrived)
+    )
     arrived = in_order(arrived, z).astype(f32)
     span_states = arrived[:, 0].reshape(1, lines * heads, span, span)
     request_states = jnp.swapaxes(arrived[:, 1:], 0, 1).reshape(

time: 273 us -> 257 us (0.941)
  waiting for transfers between devices: 63.2 us -> 52.5 us
  starting transfers between devices: 103 us -> 96.5 us
    ppermute x3, waiting for transfers between devices: 15.5 us -> 3.52 us  [far_along(): return lax.ppermute(two, 'z', [(1, 0), (2, 3)])]
    ppermute x21, starting transfers between devices: 53.3 us -> 47.7 us  [turned(): lax.ppermute(x, axis, [(i, (i + by) % length) for i in range(length)])]
    ppermute x6, waiting for transfers between devices: 3.32 us -> 7.55 us  [over_y(): return lax.ppermute(x, 'y', [(0, 1), (1, 0)])]
  transfers between devices with their start and end apart: 52 -> 52, of which waited for: 15 -> 15; matrix products, arithmetic and copies ran while one was open for 11% -> 12% of each run, Pallas kernels for 17% -> 19%
where the time goes in v8:
time: 257 us; the launch traced here: 256 us
  starting transfers between devices  96.5 us (38%)
  waiting for transfers between devices  52.5 us (20%)
  Pallas kernels  51.5 us (20%)
  local copies, waits for them, and re-layouts  38 us (15%)
  other arithmetic  15.4 us (6%)
    ppermute x21, starting transfers between devices, turned(): lax.ppermute(x, axis, [(i, (i + by) % length) for i in range(length)])  47.7 us
    ppermute x21, waiting for transfers between devices, turned(): lax.ppermute(x, axis, [(i, (i + by) % length) for i in range(length)])  38.3 us
    unnamed x134, local copies, waits for them, and re-layouts  21.3 us
    ppermute x3, starting transfers between devices, near_along(): one = lax.ppermute(piece, 'z', [(0, 1), (1, 2), (2, 3)])  20.8 us
    pallas_call x2, Pallas kernels, mix_and_project(): pl.pallas_call(lambda *refs: mix_project_kernel(rel, *refs), grid=(2,), o...  12 us
    pallas_call x1, Pallas kernels, sweep(): pl.pallas_call(sweep_kernel, out_shape=jax.ShapeDtypeStruct(r.shape, f32)...  8.66 us
    pallas_call x1, Pallas kernels, projected(): pl.pallas_call(project_kernel, grid=(rows // TILE,), out_shape=[flat] * 3...  8.16 us
    ppermute x6, waiting for transfers between devices, over_y(): return lax.ppermute(x, 'y', [(0, 1), (1, 0)])  7.55 us
  transfers between devices with their start and end apart: 52, of which 15 were waited for; matrix products, arithmetic and copies ran while one was open for 12% of the time, Pallas kernels for 19%

profile of v8, /device:TPU:0, one launch (start us, length us, event | category | flops | bytes accessed | tf_op | source)
XLA Modules:
  0.0 255.8 jit_solution(4290961522063142379)
XLA Ops:
  6.5 5.0 %collective-permute-start.1 = (bf16[2,272,512]{2,1,0:T(8,128)(2,1)S(1)}, bf16[2,272,512]{2,1,0:T(8,128)(2,1)S(1)}, u32[]{:S(2)}, u32[]{:S(2)}) collective-permute-start(bf16[2,272,512]{2,1,0:T(8,128)(2,1)S(1)} %shard_map.185.own), channel_id=1, source_target_pairs={{0,8},{8,16},{16,24},{1,9},{9,17},{17,25},{2,10},{10,18},{18,26},{... | collective-permute-start | bytes 1671176 | tf_op jit(solution)/shard_map/ppermute | solution.py:891
  11.5 2.6 %collective-permute-start.2 = (bf16[2,272,512]{2,1,0:T(8,128)(2,1)S(1)}, bf16[2,272,512]{2,1,0:T(8,128)(2,1)}, u32[]{:S(2)}, u32[]{:S(2)}) collective-permute-start(bf16[2,272,512]{2,1,0:T(8,128)(2,1)S(1)} %shard_map.185.own), channel_id=1, source_target_pairs={{0,16},{8,24},{16,0},{24,8},{1,17},{9,25},{17,1},{25,9},{2,18},{10... | collective-permute-start | bytes 1671176 | tf_op jit(solution)/shard_map/ppermute | solution.py:869
  14.1 1.3 collective-permute-start.3
  15.4 1.6 collective-permute-start.4
  17.0 1.5 collective-permute-start.5
  22.7 1.4 fusion
  26.5 13.5 %collective-permute-done.2 = bf16[2,272,512]{2,1,0:T(8,128)(2,1)} collective-permute-done((bf16[2,272,512]{2,1,0:T(8,128)(2,1)S(1)}, bf16[2,272,512]{2,1,0:T(8,128)(2,1)}, u32[]{:S(2)}, u32[]{:S(2)}) %collective-permute-start.2) | collective-permute-done | bytes 557088 | tf_op jit(solution)/shard_map/ppermute | solution.py:869
  41.0 1.3 collective-permute-start.6
  43.1 1.5 collective-permute-start.7
  45.4 1.5 collective-permute-start.8
  50.9 12.3 %collective-permute-start.12 = (bf16[2,512,256]{2,1,0:T(8,128)(2,1)}, bf16[2,512,256]{2,1,0:T(8,128)(2,1)}, u32[]{:S(2)}, u32[]{:S(2)}) collective-permute-start(bf16[2,512,256]{2,1,0:T(8,128)(2,1)} %get-tuple-element.122), channel_id=1, source_target_pairs={{0,16},{8,24},{16,0},{24,8},{1,17},{9,25},{17,1},{25,9},{2,18},{10... | collective-permute-start | bytes 1572872 | tf_op jit(solution)/shard_map/ppermute | solution.py:869
  63.2 1.8 collective-permute-done.6
  66.4 1.6 collective-permute-start.9
  67.9 1.5 collective-permute-start.10
  71.0 1.7 broadcast_select_fusion.1
  72.7 1.6 pad_maximum_fusion.1
  75.4 4.9 %collective-permute-start.13 = (bf16[2,512,256]{2,1,0:T(8,128)(2,1)}, bf16[2,512,256]{2,1,0:T(8,128)(2,1)}, u32[]{:S(2)}, u32[]{:S(2)}) collective-permute-start(bf16[2,512,256]{2,1,0:T(8,128)(2,1)} %get-tuple-element.135), channel_id=1, source_target_pairs={{0,24},{8,0},{16,8},{24,16},{1,25},{9,1},{17,9},{25,17},{2,26},{10... | collective-permute-start | bytes 1572872 | tf_op jit(solution)/shard_map/ppermute | solution.py:869
  80.4 1.3 dynamic_update_slice.27
  81.6 1.3 dynamic_update_slice.28
  82.9 1.3 dynamic_update_slice.29
  87.6 6.0 %shard_map.186 = (bf16[2,1024,512]{2,1,0:T(8,128)(2,1)S(1)}, bf16[2,1024,512]{2,1,0:T(8,128)(2,1)S(1)}, bf16[2,1024,512]{2,1,0:T(8,128)(2,1)S(1)}, bf16[2,1024,512]{2,1,0:T(8,128)(2,1)S(1)}, f32[2,1024,128]{2,1,0:T(8,128)S(1)}) custom-call(s32[14]{0:T(128)S(1)} %copy-done.21, bf16[2,272,512]{2,1,0:T(8,128)(2,1)S(1)} %copy-done.13, ...), custom_call_target="tpu_custom_call" | custom-call | flops 8049999872 | bytes 21000000 | tf_op jit(solution)/shard_map/pallas_call | solution.py:396
  93.6 1.3 copy-done.33
  95.0 1.4 copy-done.35
  96.3 1.3 copy-done.37
  97.7 1.3 copy-done.41
  100.0 7.8 %collective-permute-done.13 = bf16[2,512,256]{2,1,0:T(8,128)(2,1)} collective-permute-done((bf16[2,512,256]{2,1,0:T(8,128)(2,1)}, bf16[2,512,256]{2,1,0:T(8,128)(2,1)}, u32[]{:S(2)}, u32[]{:S(2)}) %collective-permute-start.13) | collective-permute-done | bytes 524320 | tf_op jit(solution)/shard_map/ppermute | solution.py:869
  109.0 1.7 pad_maximum_fusion.refs_5_.own_kv
  111.0 1.3 slice_bitcast_fusion.1
  114.1 2.6 %collective-permute-start.17 = (bf16[1,512,256]{2,1,0:T(8,128)(2,1)}, bf16[1,512,256]{2,1,0:T(8,128)(2,1)S(1)}, u32[]{:S(2)}, u32[]{:S(2)}) collective-permute-start(bf16[1,512,256]{2,1,0:T(8,128)(2,1)} %get-tuple-element.163), channel_id=1, source_target_pairs={{0,16},{8,24},{16,0},{24,8},{1,17},{9,25},{17,1},{25,9},{2,18},{10... | collective-permute-start | bytes 786440 | tf_op jit(solution)/shard_map/ppermute | solution.py:869
  116.7 1.6 copy-done.42
  118.3 6.6 %shard_map.187 = (bf16[2,1024,512]{2,1,0:T(8,128)(2,1)S(1)}, bf16[2,1024,512]{2,1,0:T(8,128)(2,1)S(1)}, bf16[2,1024,512]{2,1,0:T(8,128)(2,1)S(1)}, f32[2,1024,12...) custom-call(s32[14]{0:T(128)S(1)} %copy-done.22, bf16[2,272,512]{2,1,0:T(8,128)(2,1)S(1)} %copy-done.11, ...), custom_call_target="tpu_custom_call" | custom-call | flops 6899999744 | bytes 18000000 | tf_op jit(solution)/shard_map/pallas_call | solution.py:461
  125.7 5.4 %shard_map.188 = (bf16[2,1024,512]{2,1,0:T(8,128)(2,1)S(1)}, bf16[2,1024,512]{2,1,0:T(8,128)(2,1)S(1)}, bf16[2,1024,512]{2,1,0:T(8,128)(2,1)S(1)}, f32[2,1024,12...) custom-call(s32[14]{0:T(128)S(1)} %copy-done.22, bf16[2,272,512]{2,1,0:T(8,128)(2,1)S(1)} %copy-done.9, ...), custom_call_target="tpu_custom_call" | custom-call | flops 6899999744 | bytes 18000000 | tf_op jit(solution)/shard_map/pallas_call | solution.py:461
  133.2 1.8 collective-permute-done.17
  134.9 2.8 %collective-permute-done.18 = bf16[1,512,256]{2,1,0:T(8,128)(2,1)S(1)} collective-permute-done((bf16[1,512,256]{2,1,0:T(8,128)(2,1)S(1)}, bf16[1,512,256]{2,1,0:T(8,128)(2,1)S(1)}, u32[]{:S(2)}, u32[]{:S(2)}) %collective-permute-start.18) | collective-permute-done | bytes 262176 | tf_op jit(solution)/shard_map/ppermute | solution.py:869
  137.8 2.9 %collective-permute-start.20 = (bf16[1,512,256]{2,1,0:T(8,128)(2,1)S(1)}, bf16[1,512,256]{2,1,0:T(8,128)(2,1)S(1)}, u32[]{:S(2)}, u32[]{:S(2)}) collective-permute-start(bf16[1,512,256]{2,1,0:T(8,128)(2,1)S(1)} %copy-done.60), channel_id=1, source_target_pairs={{0,8},{8,16},{16,24},{24,0},{1,9},{9,17},{17,25},{25,1},{2,10},{10... | collective-permute-start | bytes 786440 | tf_op jit(solution)/shard_map/ppermute | solution.py:869
  140.7 3.8 %collective-permute-start.21 = (bf16[1,512,256]{2,1,0:T(8,128)(2,1)S(1)}, bf16[1,512,256]{2,1,0:T(8,128)(2,1)S(1)}, u32[]{:S(2)}, u32[]{:S(2)}) collective-permute-start(bf16[1,512,256]{2,1,0:T(8,128)(2,1)S(1)} %copy-done.59), channel_id=1, source_target_pairs={{0,16},{8,24},{16,0},{24,8},{1,17},{9,25},{17,1},{25,9},{2,18},{10... | collective-permute-start | bytes 786440 | tf_op jit(solution)/shard_map/ppermute | solution.py:869
  148.1 8.2 %shard_map.189 = (f32[1024,256]{1,0:T(8,128)S(1)}, f32[1024,256]{1,0:T(8,128)S(1)}, f32[1024,256]{1,0:T(8,128)S(1)}, bf16[2,1024,512]{2,1,0:T(8,128)(2,1)S(1)}, bf16[2,1024,512]{2,1,0:T(8,128)(2,1)S(1)}) custom-call(s32[14]{0:T(128)S(1)} %copy-done.22, bf16[2,1024,512]{2,1,0:T(8,128)(2,1)S(1)} %copy-done.36, ...), custom_call_target="tpu_custom_call" | custom-call | flops 9200000000 | bytes 24000000 | tf_op jit(solution)/shard_map/pallas_call | solution.py:546
  156.3 3.1 %shard_map.190 = (f32[16,4,64,64]{3,2,1,0:T(8,128)S(1)}, bf16[16,64,256]{2,1,0:T(8,128)(2,1)S(1)}) custom-call(s32[16]{0:T(128)S(1)} %select_n.361.lengths, f32[1]{0:T(128)} %bitcast.62.carry, f32[1024,256]{1,0:T(8,128)S(1)} %get-tuple-element.178.k_ref, f32[1024,256]{1,0:T(8,128)S(1)} %get-tuple-element.179.v_ref, ...), custom_call_target="tpu_custom_call" | custom-call | flops 8049999872 | bytes 21000000 | tf_op jit(solution)/shard_map/pallas_call | solution.py:716
  162.0 2.6 %collective-permute-start.26 = (bf16[3,4,64,64]{3,2,1,0:T(8,128)(2,1)S(1)}, bf16[3,4,64,64]{3,2,1,0:T(8,128)(2,1)S(1)}, u32[]{:S(2)}, u32[]{:S(2)}) collective-permute-start(bf16[3,4,64,64]{3,2,1,0:T(8,128)(2,1)S(1)} %get-tuple-element.249), channel_id=1, source_target_pairs={{0,8},{8,16},{16,24},{24,0},{1,9},{9,17},{17,25},{25,1},{2,10},{10... | collective-permute-start | bytes 294920 | tf_op jit(solution)/shard_map/ppermute | solution.py:869
  165.8 1.2 collective-permute-start.28
  167.0 3.2 %shard_map.191.r_ref = f32[1024,256]{1,0:T(8,128)S(1)} custom-call(s32[14]{0:T(128)S(1)} %copy-done.22, bf16[2,1024,512]{2,1,0:T(8,128)(2,1)S(1)} %copy-done.34, bf16[2,1024,512]{2,1,0:T(8,128)(2,1)S(1)} %get-tuple-element.188.mix1, bf16[2,1024,512]{2,1,0:T(8,128)(2,1)S(1)} %get-tuple-element.189.mix2, bf16[2,1024,512]{2,1,0:T(8,128)(2,1)S(1)} %get-tuple-element.192.mix3, ...), custom_call_target="tpu_custom_call" | custom-call | flops 6899999744 | bytes 18000000 | tf_op jit(solution)/shard_map/pallas_call | solution.py:581
  170.3 8.7 %shard_map.192.normed = f32[1024,256]{1,0:T(8,128)S(1)} custom-call(s32[16]{0:T(128)S(1)} %select_n.361.lengths, f32[1024,256]{1,0:T(8,128)S(1)} %shard_map.191.r_ref, f32[1024,256]{1,0:T(8,128)S(1)} %get-tuple-element.178.k_ref, f32[1024,256]{1,0:T(8,128)S(1)} %get-tuple-element.179.v_ref, f32[1024,256]{1,0:T(8,128)S(1)} %get-tuple-element.180.w_ref, ...), custom_call_target="tpu_custom_call" | custom-call | flops 13799999488 | bytes 36000000 | tf_op jit(solution)/shard_map/pallas_call | solution.py:802
  179.0 3.5 %shard_map.193 = (bf16[2,4,32,256]{3,2,1,0:T(8,128)(2,1)S(1)}, bf16[2,4,32,256]{3,2,1,0:T(8,128)(2,1)S(1)}, bf16[2,4,32,256]{3,2,1,0:T(8,128)(2,1)S(1)}, bf16[2,4,32,256]{3,2,1,0:T(8,128)(2,1)S(1)}) custom-call(s32[14]{0:T(128)S(1)} %copy-done.22, s32[16]{0:T(128)S(1)} %select_n.361.lengths, bf16[2,1024,512]{2,1,0:T(8,128)(2,1)S(1)} %copy-done.38, ...), custom_call_target="tpu_custom_call" | custom-call | flops 8049999872 | bytes 21000000 | tf_op jit(solution)/shard_map/pallas_call | solution.py:645
  185.1 1.3 collective-permute-start.33
  186.4 4.8 %collective-permute-start.32 = (bf16[512,256]{1,0:T(8,128)(2,1)S(1)}, bf16[512,256]{1,0:T(8,128)(2,1)S(1)}, u32[]{:S(2)}, u32[]{:S(2)}) collective-permute-start(bf16[512,256]{1,0:T(8,128)(2,1)S(1)} %bitcast.157), channel_id=1, source_target_pairs={{0,8},{8,16},{16,24},{1,9},{9,17},{17,25},{2,10},{10,18},{18,26},{... | collective-permute-start | bytes 786440 | tf_op jit(solution)/shard_map/ppermute | solution.py:891
  191.3 8.5 %collective-permute-done.30.h2 = bf16[512,256]{1,0:T(8,128)(2,1)S(1)} collective-permute-done((bf16[512,256]{1,0:T(8,128)(2,1)S(1)}, bf16[512,256]{1,0:T(8,128)(2,1)S(1)}, u32[]{:S(2)}, u32[]{:S(2)}) %collective-permute-start.30) | collective-permute-done | bytes 262176 | tf_op jit(solution)/shard_map/ppermute | solution.py:869
  199.7 1.3 collective-permute-start.31
  201.1 1.3 collective-permute-start.45
  202.4 11.0 %collective-permute-start.44 = (bf16[512,256]{1,0:T(8,128)(2,1)S(1)}, bf16[512,256]{1,0:T(8,128)(2,1)S(1)}, u32[]{:S(2)}, u32[]{:S(2)}) collective-permute-start(bf16[512,256]{1,0:T(8,128)(2,1)S(1)} %bitcast.153), channel_id=1, source_target_pairs={{0,8},{8,16},{16,24},{1,9},{9,17},{17,25},{2,10},{10,18},{18,26},{... | collective-permute-start | bytes 786440 | tf_op jit(solution)/shard_map/ppermute | solution.py:891
  213.4 3.2 %collective-permute-done.42.h2 = bf16[512,256]{1,0:T(8,128)(2,1)S(1)} collective-permute-done((bf16[512,256]{1,0:T(8,128)(2,1)S(1)}, bf16[512,256]{1,0:T(8,128)(2,1)S(1)}, u32[]{:S(2)}, u32[]{:S(2)}) %collective-permute-start.42) | collective-permute-done | bytes 262176 | tf_op jit(solution)/shard_map/ppermute | solution.py:869
  216.6 1.5 collective-permute-start.43
  218.2 2.1 shard_map.194
  220.3 2.4 collective-permute-start.37
  223.9 1.7 collective-permute-done.43
  225.7 2.1 shard_map.195
  227.8 2.5 collective-permute-start.48
  232.0 5.6 %collective-permute-done.36 = bf16[4,32,1024]{2,1,0:T(8,128)(2,1)S(1)} collective-permute-done((bf16[4,32,1024]{2,1,0:T(8,128)(2,1)S(1)}, bf16[4,32,1024]{2,1,0:T(8,128)(2,1)S(1)}, u32[]{:S(2)}, u32[]{:S(2)}) %collective-permute-start.36) | collective-permute-done | bytes 262176 | tf_op jit(solution)/shard_map/ppermute | solution.py:881
  237.9 2.7 %collective-permute-start.38 = (bf16[32,1024]{1,0:T(8,128)(2,1)S(1)}, bf16[32,1024]{1,0:T(8,128)(2,1)S(1)}, u32[]{:S(2)}, u32[]{:S(2)}) collective-permute-start(bf16[32,1024]{1,0:T(8,128)(2,1)S(1)} %get-tuple-element.261), channel_id=1, source_target_pairs={{0,8},{8,16},{16,24},{24,0},{1,9},{9,17},{17,25},{25,1},{2,10},{10... | collective-permute-start | bytes 196616 | tf_op jit(solution)/shard_map/ppermute | solution.py:869
  240.6 1.3 collective-permute-done.48
  243.0 1.9 collective-permute-done.47
  245.1 2.4 collective-permute-start.49
  247.6 1.3 collective-permute-start.50
  248.8 2.8 %collective-permute-start.51 = (bf16[32,1024]{1,0:T(8,128)(2,1)S(1)}, bf16[32,1024]{1,0:T(8,128)(2,1)S(1)}, u32[]{:S(2)}, u32[]{:S(2)}) collective-permute-start(bf16[32,1024]{1,0:T(8,128)(2,1)S(1)} %get-tuple-element.253), channel_id=1, source_target_pairs={{0,24},{8,0},{16,8},{24,16},{1,25},{9,1},{17,9},{25,17},{2,26},{10... | collective-permute-start | bytes 196616 | tf_op jit(solution)/shard_map/ppermute | solution.py:869
  254.4 1.4 shard_map.196
  (256 shorter events, 50.4 us)
Async XLA Ops:
  0.6 25.0 %copy-start = (bf16[128,1024]{1,0:T(8,128)(2,1)S(1)}, bf16[128,1024]{1,0:T(8,128)(2,1)}, u32[]{:S(2)}) copy-start(bf16[128,1024]{1,0:T(8,128)(2,1)} %param.29) | copy-start | bytes 786436
  4.1 1.8 collective-permute-start
  5.8 12.7 %copy-start.63 = (f32[5,4096]{1,0:T(8,128)S(1)}, f32[5,4096]{1,0:T(8,128)}, u32[]{:S(2)}) copy-start(f32[5,4096]{1,0:T(8,128)} %param.22) | copy-start | bytes 245764
  5.8 12.7 %copy-start.51 = (bf16[4096,128]{1,0:T(8,128)(2,1)S(1)}, bf16[4096,128]{1,0:T(8,128)(2,1)}, u32[]{:S(2)}) copy-start(bf16[4096,128]{1,0:T(8,128)(2,1)} %param.28) | copy-start | bytes 3145732
  6.5 19.9 %copy-start.12 = (bf16[2,272,512]{2,1,0:T(8,128)(2,1)}, bf16[2,272,512]{2,1,0:T(8,128)(2,1)S(1)}, u32[]{:S(2)}) copy-start(bf16[2,272,512]{2,1,0:T(8,128)(2,1)S(1)} %shard_map.185.own) | copy-start | bytes 1671172
  6.5 12.9 %copy-start.52 = (bf16[512,1024]{1,0:T(8,128)(2,1)S(1)}, bf16[512,1024]{1,0:T(8,128)(2,1)}, u32[]{:S(2)}) copy-start(bf16[512,1024]{1,0:T(8,128)(2,1)} %param.23) | copy-start | bytes 3145732
  6.5 19.9 %collective-permute-start.1 = (bf16[2,272,512]{2,1,0:T(8,128)(2,1)S(1)}, bf16[2,272,512]{2,1,0:T(8,128)(2,1)S(1)}, u32[]{:S(2)}, u32[]{:S(2)}) collective-permute-start(bf16[2,272,512]{2,1,0:T(8,128)(2,1)S(1)} %shard_map.185.own), channel_id=1, source_target_pairs={{0,8},{8,16},{16,24},{1,9},{9,17},{17,25},{2,10},{10,18},{18,26},{... | collective-permute-start | bytes 1671176 | tf_op jit(solution)/shard_map/ppermute | solution.py:891
  11.5 28.5 %collective-permute-start.2 = (bf16[2,272,512]{2,1,0:T(8,128)(2,1)S(1)}, bf16[2,272,512]{2,1,0:T(8,128)(2,1)}, u32[]{:S(2)}, u32[]{:S(2)}) collective-permute-start(bf16[2,272,512]{2,1,0:T(8,128)(2,1)S(1)} %shard_map.185.own), channel_id=1, source_target_pairs={{0,16},{8,24},{16,0},{24,8},{1,17},{9,25},{17,1},{25,9},{2,18},{10... | collective-permute-start | bytes 1671176 | tf_op jit(solution)/shard_map/ppermute | solution.py:869
  14.1 26.9 %collective-permute-start.3 = (bf16[2,272,512]{2,1,0:T(8,128)(2,1)S(1)}, bf16[2,272,512]{2,1,0:T(8,128)(2,1)S(1)}, u32[]{:S(2)}, u32[]{:S(2)}) collective-permute-start(bf16[2,272,512]{2,1,0:T(8,128)(2,1)S(1)} %shard_map.185.own), channel_id=1, source_target_pairs={{8,0},{16,8},{24,16},{9,1},{17,9},{25,17},{10,2},{18,10},{26,18},{... | collective-permute-start | bytes 1671176 | tf_op jit(solution)/shard_map/ppermute | solution.py:892
  15.4 25.6 %collective-permute-start.4 = (bf16[2,272,512]{2,1,0:T(8,128)(2,1)S(1)}, bf16[2,272,512]{2,1,0:T(8,128)(2,1)S(1)}, u32[]{:S(2)}, u32[]{:S(2)}) collective-permute-start(bf16[2,272,512]{2,1,0:T(8,128)(2,1)S(1)} %shard_map.185.own), channel_id=1, source_target_pairs={{0,1},{1,0},{2,3},{3,2},{4,5},{5,4},{6,7},{7,6},{8,9},{9,8},{10,11... | collective-permute-start | bytes 1671176 | tf_op jit(solution)/shard_map/ppermute | solution.py:877
  17.0 24.0 %collective-permute-start.5 = (bf16[2,272,512]{2,1,0:T(8,128)(2,1)S(1)}, bf16[2,272,512]{2,1,0:T(8,128)(2,1)S(1)}, u32[]{:S(2)}, u32[]{:S(2)}) collective-permute-start(bf16[2,272,512]{2,1,0:T(8,128)(2,1)S(1)} %shard_map.185.own), channel_id=1, source_target_pairs={{0,2},{2,0},{1,3},{3,1},{4,6},{6,4},{5,7},{7,5},{8,10},{10,8},{9,1... | collective-permute-start | bytes 1671176 | tf_op jit(solution)/shard_map/ppermute | solution.py:881
  26.4 44.5 %collective-permute-start.34 = (bf16[1024,512]{1,0:T(8,128)(2,1)}, bf16[1024,512]{1,0:T(8,128)(2,1)}, u32[]{:S(2)}, u32[]{:S(2)}) collective-permute-start(bf16[1024,512]{1,0:T(8,128)(2,1)} %param.33), channel_id=1, source_target_pairs={{0,4},{4,0},{1,5},{5,1},{2,6},{6,2},{3,7},{7,3},{8,12},{12,8},{9,1... | collective-permute-start | bytes 3145736 | tf_op jit(solution)/shard_map/ppermute | solution.py:873
  41.0 24.0 %collective-permute-start.6 = (bf16[2,272,512]{2,1,0:T(8,128)(2,1)}, bf16[2,272,512]{2,1,0:T(8,128)(2,1)S(1)}, u32[]{:S(2)}, u32[]{:S(2)}) collective-permute-start(bf16[2,272,512]{2,1,0:T(8,128)(2,1)} %collective-permute-done.2), channel_id=1, source_target_pairs={{8,0},{16,24},{9,1},{17,25},{10,2},{18,26},{11,3},{19,27},{12,4},{... | collective-permute-start | bytes 1671176 | tf_op jit(solution)/shard_map/ppermute | solution.py:897
  43.1 20.0 %collective-permute-start.7 = (bf16[272,512]{1,0:T(8,128)(2,1)S(1)}, bf16[272,512]{1,0:T(8,128)(2,1)S(1)}, u32[]{:S(2)}, u32[]{:S(2)}) collective-permute-start(bf16[272,512]{1,0:T(8,128)(2,1)S(1)} %slice_bitcast_fusion.6), channel_id=1, source_target_pairs={{0,2},{2,0},{1,3},{3,1},{4,6},{6,4},{5,7},{7,5},{8,10},{10,8},{9,1... | collective-permute-start | bytes 835592 | tf_op jit(solution)/shard_map/ppermute | solution.py:881
  45.4 17.8 %collective-permute-start.8 = (bf16[272,512]{1,0:T(8,128)(2,1)}, bf16[272,512]{1,0:T(8,128)(2,1)S(1)}, u32[]{:S(2)}, u32[]{:S(2)}) collective-permute-start(bf16[272,512]{1,0:T(8,128)(2,1)} %slice_bitcast_fusion.5), channel_id=1, source_target_pairs={{0,1},{1,0},{2,3},{3,2},{4,5},{5,4},{6,7},{7,6},{8,9},{9,8},{10,11... | collective-permute-start | bytes 835592 | tf_op jit(solution)/shard_map/ppermute | solution.py:877
  50.0 16.4 %copy-start.65 = (bf16[4,4]{1,0:T(4,128)(2,1)}, bf16[4,4]{1,0:T(4,128)(2,1)S(1)}, u32[]{:S(2)}) copy-start(bf16[4,4]{1,0:T(4,128)(2,1)S(1)} %dynamic_update_slice.26) | copy-start | bytes 100
  50.9 49.1 %collective-permute-start.12 = (bf16[2,512,256]{2,1,0:T(8,128)(2,1)}, bf16[2,512,256]{2,1,0:T(8,128)(2,1)}, u32[]{:S(2)}, u32[]{:S(2)}) collective-permute-start(bf16[2,512,256]{2,1,0:T(8,128)(2,1)} %get-tuple-element.122), channel_id=1, source_target_pairs={{0,16},{8,24},{16,0},{24,8},{1,17},{9,25},{17,1},{25,9},{2,18},{10... | collective-permute-start | bytes 1572872 | tf_op jit(solution)/shard_map/ppermute | solution.py:869
  66.4 41.4 %collective-permute-start.9 = (bf16[2,3,272,512]{3,2,1,0:T(8,128)(2,1)S(1)}, bf16[2,3,272,512]{3,2,1,0:T(8,128)(2,1)}, u32[]{:S(2)}, u32[]{:S(2)}) collective-permute-start(bf16[2,3,272,512]{3,2,1,0:T(8,128)(2,1)S(1)} %pad_maximum_fusion.3.rest), channel_id=1, source_target_pairs={{0,1},{1,0},{2,3},{3,2},{4,5},{5,4},{6,7},{7,6},{8,9},{9,8},{10,11... | collective-permute-start | bytes 5013512 | tf_op jit(solution)/shard_map/ppermute | solution.py:877
  67.9 39.9 %collective-permute-start.10 = (bf16[2,3,272,512]{3,2,1,0:T(8,128)(2,1)S(1)}, bf16[2,3,272,512]{3,2,1,0:T(8,128)(2,1)S(1)}, u32[]{:S(2)}, u32[]{:S(2)}) collective-permute-start(bf16[2,3,272,512]{3,2,1,0:T(8,128)(2,1)S(1)} %pad_maximum_fusion.3.rest), channel_id=1, source_target_pairs={{0,2},{2,0},{1,3},{3,1},{4,6},{6,4},{5,7},{7,5},{8,10},{10,8},{9,1... | collective-permute-start | bytes 5013512 | tf_op jit(solution)/shard_map/ppermute | solution.py:881
  75.4 24.6 %collective-permute-start.11 = (bf16[2,512,256]{2,1,0:T(8,128)(2,1)}, bf16[2,512,256]{2,1,0:T(8,128)(2,1)}, u32[]{:S(2)}, u32[]{:S(2)}) collective-permute-start(bf16[2,512,256]{2,1,0:T(8,128)(2,1)} %get-tuple-element.134), channel_id=1, source_target_pairs={{0,8},{8,16},{16,24},{24,0},{1,9},{9,17},{17,25},{25,1},{2,10},{10... | collective-permute-start | bytes 1572872 | tf_op jit(solution)/shard_map/ppermute | solution.py:869
  75.4 32.4 %collective-permute-start.13 = (bf16[2,512,256]{2,1,0:T(8,128)(2,1)}, bf16[2,512,256]{2,1,0:T(8,128)(2,1)}, u32[]{:S(2)}, u32[]{:S(2)}) collective-permute-start(bf16[2,512,256]{2,1,0:T(8,128)(2,1)} %get-tuple-element.135), channel_id=1, source_target_pairs={{0,24},{8,0},{16,8},{24,16},{1,25},{9,1},{17,9},{25,17},{2,26},{10... | collective-permute-start | bytes 1572872 | tf_op jit(solution)/shard_map/ppermute | solution.py:869
  87.6 21.4 %copy-start.50 = (bf16[2,512,256]{2,1,0:T(8,128)(2,1)S(1)}, bf16[2,512,256]{2,1,0:T(8,128)(2,1)}, u32[]{:S(2)}) copy-start(bf16[2,512,256]{2,1,0:T(8,128)(2,1)} %get-tuple-element.142) | copy-start | bytes 1572868
  110.8 34.8 %collective-permute-start.19 = (bf16[4,2,512,256]{3,2,1,0:T(8,128)(2,1)S(1)}, bf16[4,2,512,256]{3,2,1,0:T(8,128)(2,1)}, u32[]{:S(2)}, u32[]{:S(2)}) collective-permute-start(bf16[4,2,512,256]{3,2,1,0:T(8,128)(2,1)S(1)} %pad_maximum_fusion.refs_5_.own_kv), channel_id=1, source_target_pairs={{0,4},{4,0},{1,5},{5,1},{2,6},{6,2},{3,7},{7,3},{8,12},{12,8},{9,1... | collective-permute-start | bytes 6291464 | tf_op jit(solution)/shard_map/ppermute | solution.py:873
  112.3 25.5 %collective-permute-start.14 = (bf16[3,272,512]{2,1,0:T(8,128)(2,1)S(1)}, bf16[3,272,512]{2,1,0:T(8,128)(2,1)S(1)}, u32[]{:S(2)}, u32[]{:S(2)}) collective-permute-start(bf16[3,272,512]{2,1,0:T(8,128)(2,1)S(1)} %slice_bitcast_fusion.1), channel_id=1, source_target_pairs={{0,2},{2,0},{1,3},{3,1},{4,6},{6,4},{5,7},{7,5},{8,10},{10,8},{9,1... | collective-permute-start | bytes 2506760 | tf_op jit(solution)/shard_map/ppermute | solution.py:881
  112.9 24.9 %collective-permute-start.15 = (bf16[3,272,512]{2,1,0:T(8,128)(2,1)S(1)}, bf16[3,272,512]{2,1,0:T(8,128)(2,1)S(1)}, u32[]{:S(2)}, u32[]{:S(2)}) collective-permute-start(bf16[3,272,512]{2,1,0:T(8,128)(2,1)S(1)} %slice_bitcast_fusion), channel_id=1, source_target_pairs={{0,1},{1,0},{2,3},{3,2},{4,5},{5,4},{6,7},{7,6},{8,9},{9,8},{10,11... | collective-permute-start | bytes 2506760 | tf_op jit(solution)/shard_map/ppermute | solution.py:877
  113.5 11.4 %collective-permute-start.16 = (bf16[1,512,256]{2,1,0:T(8,128)(2,1)S(1)}, bf16[1,512,256]{2,1,0:T(8,128)(2,1)S(1)}, u32[]{:S(2)}, u32[]{:S(2)}) collective-permute-start(bf16[1,512,256]{2,1,0:T(8,128)(2,1)S(1)} %copy-done.62), channel_id=1, source_target_pairs={{0,8},{8,16},{16,24},{24,0},{1,9},{9,17},{17,25},{25,1},{2,10},{10... | collective-permute-start | bytes 786440 | tf_op jit(solution)/shard_map/ppermute | solution.py:869
  114.1 20.8 %collective-permute-start.17 = (bf16[1,512,256]{2,1,0:T(8,128)(2,1)}, bf16[1,512,256]{2,1,0:T(8,128)(2,1)S(1)}, u32[]{:S(2)}, u32[]{:S(2)}) collective-permute-start(bf16[1,512,256]{2,1,0:T(8,128)(2,1)} %get-tuple-element.163), channel_id=1, source_target_pairs={{0,16},{8,24},{16,0},{24,8},{1,17},{9,25},{17,1},{25,9},{2,18},{10... | collective-permute-start | bytes 786440 | tf_op jit(solution)/shard_map/ppermute | solution.py:869
  125.0 12.8 %collective-permute-start.18 = (bf16[1,512,256]{2,1,0:T(8,128)(2,1)S(1)}, bf16[1,512,256]{2,1,0:T(8,128)(2,1)S(1)}, u32[]{:S(2)}, u32[]{:S(2)}) collective-permute-start(bf16[1,512,256]{2,1,0:T(8,128)(2,1)S(1)} %copy-done.61), channel_id=1, source_target_pairs={{0,24},{8,0},{16,8},{24,16},{1,25},{9,1},{17,9},{25,17},{2,26},{10... | collective-permute-start | bytes 786440 | tf_op jit(solution)/shard_map/ppermute | solution.py:869
  125.7 15.0 %copy-start.59 = (bf16[1,512,256]{2,1,0:T(8,128)(2,1)S(1)}, bf16[1,512,256]{2,1,0:T(8,128)(2,1)}, u32[]{:S(2)}) copy-start(bf16[1,512,256]{2,1,0:T(8,128)(2,1)} %get-tuple-element.176) | copy-start | bytes 786436
  125.7 18.7 %copy-start.58 = (bf16[1,512,256]{2,1,0:T(8,128)(2,1)S(1)}, bf16[1,512,256]{2,1,0:T(8,128)(2,1)}, u32[]{:S(2)}) copy-start(bf16[1,512,256]{2,1,0:T(8,128)(2,1)} %get-tuple-element.177) | copy-start | bytes 786436
  125.7 19.7 %copy-start.57 = (bf16[1,512,256]{2,1,0:T(8,128)(2,1)S(1)}, bf16[1,512,256]{2,1,0:T(8,128)(2,1)}, u32[]{:S(2)}) copy-start(bf16[1,512,256]{2,1,0:T(8,128)(2,1)} %get-tuple-element.193) | copy-start | bytes 786436
  125.7 19.9 %copy-start.36 = (bf16[2,1024,512]{2,1,0:T(8,128)(2,1)S(1)}, bf16[2,1024,512]{2,1,0:T(8,128)(2,1)}, u32[]{:S(2)}) copy-start(bf16[2,1024,512]{2,1,0:T(8,128)(2,1)} %copy-done.35) | copy-start | bytes 6291460
  137.8 22.5 %collective-permute-start.20 = (bf16[1,512,256]{2,1,0:T(8,128)(2,1)S(1)}, bf16[1,512,256]{2,1,0:T(8,128)(2,1)S(1)}, u32[]{:S(2)}, u32[]{:S(2)}) collective-permute-start(bf16[1,512,256]{2,1,0:T(8,128)(2,1)S(1)} %copy-done.60), channel_id=1, source_target_pairs={{0,8},{8,16},{16,24},{24,0},{1,9},{9,17},{17,25},{25,1},{2,10},{10... | collective-permute-start | bytes 786440 | tf_op jit(solution)/shard_map/ppermute | solution.py:869
  140.7 19.6 %collective-permute-start.21 = (bf16[1,512,256]{2,1,0:T(8,128)(2,1)S(1)}, bf16[1,512,256]{2,1,0:T(8,128)(2,1)S(1)}, u32[]{:S(2)}, u32[]{:S(2)}) collective-permute-start(bf16[1,512,256]{2,1,0:T(8,128)(2,1)S(1)} %copy-done.59), channel_id=1, source_target_pairs={{0,16},{8,24},{16,0},{24,8},{1,17},{9,25},{17,1},{25,9},{2,18},{10... | collective-permute-start | bytes 786440 | tf_op jit(solution)/shard_map/ppermute | solution.py:869
  144.5 15.8 %collective-permute-start.22 = (bf16[1,512,256]{2,1,0:T(8,128)(2,1)S(1)}, bf16[1,512,256]{2,1,0:T(8,128)(2,1)S(1)}, u32[]{:S(2)}, u32[]{:S(2)}) collective-permute-start(bf16[1,512,256]{2,1,0:T(8,128)(2,1)S(1)} %copy-done.58), channel_id=1, source_target_pairs={{0,24},{8,0},{16,8},{24,16},{1,25},{9,1},{17,9},{25,17},{2,26},{10... | collective-permute-start | bytes 786440 | tf_op jit(solution)/shard_map/ppermute | solution.py:869
  145.5 21.5 %collective-permute-start.25 = (bf16[4,1,512,256]{3,2,1,0:T(8,128)(2,1)S(1)}, bf16[4,1,512,256]{3,2,1,0:T(8,128)(2,1)S(1)}, u32[]{:S(2)}, u32[]{:S(2)}) collective-permute-start(bf16[4,1,512,256]{3,2,1,0:T(8,128)(2,1)S(1)} %pad_maximum_fusion.5.own), channel_id=1, source_target_pairs={{0,4},{4,0},{1,5},{5,1},{2,6},{6,2},{3,7},{7,3},{8,12},{12,8},{9,1... | collective-permute-start | bytes 3145736 | tf_op jit(solution)/shard_map/ppermute | solution.py:873
  159.5 2.1 collective-permute-start.24
  161.2 17.8 %collective-permute-start.23 = (bf16[4,1,512,256]{3,2,1,0:T(8,128)(2,1)S(1)}, bf16[4,1,512,256]{3,2,1,0:T(8,128)(2,1)S(1)}, u32[]{:S(2)}, u32[]{:S(2)}) collective-permute-start(bf16[4,1,512,256]{3,2,1,0:T(8,128)(2,1)S(1)} %pad_maximum_fusion.4.own), channel_id=1, source_target_pairs={{0,4},{4,0},{1,5},{5,1},{2,6},{6,2},{3,7},{7,3},{8,12},{12,8},{9,1... | collective-permute-start | bytes 3145736 | tf_op jit(solution)/shard_map/ppermute | solution.py:873
  162.0 20.5 %collective-permute-start.26 = (bf16[3,4,64,64]{3,2,1,0:T(8,128)(2,1)S(1)}, bf16[3,4,64,64]{3,2,1,0:T(8,128)(2,1)S(1)}, u32[]{:S(2)}, u32[]{:S(2)}) collective-permute-start(bf16[3,4,64,64]{3,2,1,0:T(8,128)(2,1)S(1)} %get-tuple-element.249), channel_id=1, source_target_pairs={{0,8},{8,16},{16,24},{24,0},{1,9},{9,17},{17,25},{25,1},{2,10},{10... | collective-permute-start | bytes 294920 | tf_op jit(solution)/shard_map/ppermute | solution.py:869
  164.6 17.9 %collective-permute-start.27 = (bf16[3,4,64,64]{3,2,1,0:T(8,128)(2,1)S(1)}, bf16[3,4,64,64]{3,2,1,0:T(8,128)(2,1)S(1)}, u32[]{:S(2)}, u32[]{:S(2)}) collective-permute-start(bf16[3,4,64,64]{3,2,1,0:T(8,128)(2,1)S(1)} %get-tuple-element.248), channel_id=1, source_target_pairs={{0,16},{8,24},{16,0},{24,8},{1,17},{9,25},{17,1},{25,9},{2,18},{10... | collective-permute-start | bytes 294920 | tf_op jit(solution)/shard_map/ppermute | solution.py:869
  165.8 16.7 %collective-permute-start.28 = (bf16[3,4,64,64]{3,2,1,0:T(8,128)(2,1)S(1)}, bf16[3,4,64,64]{3,2,1,0:T(8,128)(2,1)S(1)}, u32[]{:S(2)}, u32[]{:S(2)}) collective-permute-start(bf16[3,4,64,64]{3,2,1,0:T(8,128)(2,1)S(1)} %get-tuple-element.247), channel_id=1, source_target_pairs={{0,24},{8,0},{16,8},{24,16},{1,25},{9,1},{17,9},{25,17},{2,26},{10... | collective-permute-start | bytes 294920 | tf_op jit(solution)/shard_map/ppermute | solution.py:869
  182.5 1.4 collective-permute-start.29
  182.9 35.4 %copy-start.19 = (s32[4]{0:T(128)S(1)}, s32[4]{0:T(128)}, u32[]{:S(2)}) copy-start(s32[4]{0:T(128)} %pad_add_fusion.1.block_of) | copy-start | bytes 52
  182.9 8.4 %collective-permute-start.41 = (bf16[2,4,32,256]{3,2,1,0:T(8,128)(2,1)S(1)}, bf16[2,4,32,256]{3,2,1,0:T(8,128)(2,1)S(1)}, u32[]{:S(2)}, u32[]{:S(2)}) collective-permute-start(bf16[2,4,32,256]{3,2,1,0:T(8,128)(2,1)S(1)} %get-tuple-element.213), channel_id=1, source_target_pairs={{0,4},{4,0},{1,5},{5,1},{2,6},{6,2},{3,7},{7,3},{8,12},{12,8},{9,1... | collective-permute-start | bytes 393224 | tf_op jit(solution)/shard_map/ppermute | solution.py:873
  183.9 15.8 %collective-permute-start.30 = (bf16[512,256]{1,0:T(8,128)(2,1)S(1)}, bf16[512,256]{1,0:T(8,128)(2,1)S(1)}, u32[]{:S(2)}, u32[]{:S(2)}) collective-permute-start(bf16[512,256]{1,0:T(8,128)(2,1)S(1)} %bitcast.155), channel_id=1, source_target_pairs={{0,16},{8,24},{16,0},{24,8},{1,17},{9,25},{17,1},{25,9},{2,18},{10... | collective-permute-start | bytes 786440 | tf_op jit(solution)/shard_map/ppermute | solution.py:869
  185.1 17.3 %collective-permute-start.33 = (bf16[512,256]{1,0:T(8,128)(2,1)S(1)}, bf16[512,256]{1,0:T(8,128)(2,1)S(1)}, u32[]{:S(2)}, u32[]{:S(2)}) collective-permute-start(bf16[512,256]{1,0:T(8,128)(2,1)S(1)} %bitcast.156), channel_id=1, source_target_pairs={{8,0},{16,8},{24,16},{9,1},{17,9},{25,17},{10,2},{18,10},{26,18},{... | collective-permute-start | bytes 786440 | tf_op jit(solution)/shard_map/ppermute | solution.py:892
  186.4 31.7 %collective-permute-start.32 = (bf16[512,256]{1,0:T(8,128)(2,1)S(1)}, bf16[512,256]{1,0:T(8,128)(2,1)S(1)}, u32[]{:S(2)}, u32[]{:S(2)}) collective-permute-start(bf16[512,256]{1,0:T(8,128)(2,1)S(1)} %bitcast.157), channel_id=1, source_target_pairs={{0,8},{8,16},{16,24},{1,9},{9,17},{17,25},{2,10},{10,18},{18,26},{... | collective-permute-start | bytes 786440 | tf_op jit(solution)/shard_map/ppermute | solution.py:891
  199.7 16.9 %collective-permute-start.42 = (bf16[512,256]{1,0:T(8,128)(2,1)S(1)}, bf16[512,256]{1,0:T(8,128)(2,1)S(1)}, u32[]{:S(2)}, u32[]{:S(2)}) collective-permute-start(bf16[512,256]{1,0:T(8,128)(2,1)S(1)} %bitcast.151), channel_id=1, source_target_pairs={{0,16},{8,24},{16,0},{24,8},{1,17},{9,25},{17,1},{25,9},{2,18},{10... | collective-permute-start | bytes 786440 | tf_op jit(solution)/shard_map/ppermute | solution.py:869
  199.7 18.4 %collective-permute-start.31 = (bf16[512,256]{1,0:T(8,128)(2,1)S(1)}, bf16[512,256]{1,0:T(8,128)(2,1)S(1)}, u32[]{:S(2)}, u32[]{:S(2)}) collective-permute-start(bf16[512,256]{1,0:T(8,128)(2,1)S(1)} %collective-permute-done.30.h2), channel_id=1, source_target_pairs={{8,0},{16,24},{9,1},{17,25},{10,2},{18,26},{11,3},{19,27},{12,4},{... | collective-permute-start | bytes 786440 | tf_op jit(solution)/shard_map/ppermute | solution.py:897
  201.1 22.2 %collective-permute-start.45 = (bf16[512,256]{1,0:T(8,128)(2,1)S(1)}, bf16[512,256]{1,0:T(8,128)(2,1)S(1)}, u32[]{:S(2)}, u32[]{:S(2)}) collective-permute-start(bf16[512,256]{1,0:T(8,128)(2,1)S(1)} %bitcast.152), channel_id=1, source_target_pairs={{8,0},{16,8},{24,16},{9,1},{17,9},{25,17},{10,2},{18,10},{26,18},{... | collective-permute-start | bytes 786440 | tf_op jit(solution)/shard_map/ppermute | solution.py:892
  202.4 21.5 %collective-permute-start.44 = (bf16[512,256]{1,0:T(8,128)(2,1)S(1)}, bf16[512,256]{1,0:T(8,128)(2,1)S(1)}, u32[]{:S(2)}, u32[]{:S(2)}) collective-permute-start(bf16[512,256]{1,0:T(8,128)(2,1)S(1)} %bitcast.153), channel_id=1, source_target_pairs={{0,8},{8,16},{16,24},{1,9},{9,17},{17,25},{2,10},{10,18},{18,26},{... | collective-permute-start | bytes 786440 | tf_op jit(solution)/shard_map/ppermute | solution.py:891
  216.6 9.0 %collective-permute-start.43 = (bf16[512,256]{1,0:T(8,128)(2,1)S(1)}, bf16[512,256]{1,0:T(8,128)(2,1)S(1)}, u32[]{:S(2)}, u32[]{:S(2)}) collective-permute-start(bf16[512,256]{1,0:T(8,128)(2,1)S(1)} %collective-permute-done.42.h2), channel_id=1, source_target_pairs={{8,0},{16,24},{9,1},{17,25},{10,2},{18,26},{11,3},{19,27},{12,4},{... | collective-permute-start | bytes 786440 | tf_op jit(solution)/shard_map/ppermute | solution.py:897
  220.3 10.5 %collective-permute-start.37 = (bf16[4,32,1024]{2,1,0:T(8,128)(2,1)S(1)}, bf16[4,32,1024]{2,1,0:T(8,128)(2,1)S(1)}, u32[]{:S(2)}, u32[]{:S(2)}) collective-permute-start(bf16[4,32,1024]{2,1,0:T(8,128)(2,1)S(1)} %get-tuple-element.211), channel_id=1, source_target_pairs={{0,3},{1,2},{2,1},{3,0},{4,7},{5,6},{6,5},{7,4},{8,11},{9,10},{10,... | collective-permute-start | bytes 786440 | tf_op jit(solution)/shard_map/ppermute | solution.py:1164
  222.7 14.9 %collective-permute-start.36 = (bf16[4,32,1024]{2,1,0:T(8,128)(2,1)S(1)}, bf16[4,32,1024]{2,1,0:T(8,128)(2,1)S(1)}, u32[]{:S(2)}, u32[]{:S(2)}) collective-permute-start(bf16[4,32,1024]{2,1,0:T(8,128)(2,1)S(1)} %get-tuple-element.210), channel_id=1, source_target_pairs={{0,2},{2,0},{1,3},{3,1},{4,6},{6,4},{5,7},{7,5},{8,10},{10,8},{9,1... | collective-permute-start | bytes 786440 | tf_op jit(solution)/shard_map/ppermute | solution.py:881
  223.3 14.3 %collective-permute-start.35 = (bf16[4,32,1024]{2,1,0:T(8,128)(2,1)S(1)}, bf16[4,32,1024]{2,1,0:T(8,128)(2,1)S(1)}, u32[]{:S(2)}, u32[]{:S(2)}) collective-permute-start(bf16[4,32,1024]{2,1,0:T(8,128)(2,1)S(1)} %get-tuple-element.209), channel_id=1, source_target_pairs={{0,1},{1,0},{2,3},{3,2},{4,5},{5,4},{6,7},{7,6},{8,9},{9,8},{10,11... | collective-permute-start | bytes 786440 | tf_op jit(solution)/shard_map/ppermute | solution.py:877
  227.8 14.0 %collective-permute-start.48 = (bf16[4,32,1024]{2,1,0:T(8,128)(2,1)S(1)}, bf16[4,32,1024]{2,1,0:T(8,128)(2,1)S(1)}, u32[]{:S(2)}, u32[]{:S(2)}) collective-permute-start(bf16[4,32,1024]{2,1,0:T(8,128)(2,1)S(1)} %get-tuple-element.218), channel_id=1, source_target_pairs={{0,3},{1,2},{2,1},{3,0},{4,7},{5,6},{6,5},{7,4},{8,11},{9,10},{10,... | collective-permute-start | bytes 786440 | tf_op jit(solution)/shard_map/ppermute | solution.py:1164
  230.3 14.6 %collective-permute-start.47 = (bf16[4,32,1024]{2,1,0:T(8,128)(2,1)S(1)}, bf16[4,32,1024]{2,1,0:T(8,128)(2,1)S(1)}, u32[]{:S(2)}, u32[]{:S(2)}) collective-permute-start(bf16[4,32,1024]{2,1,0:T(8,128)(2,1)S(1)} %get-tuple-element.217), channel_id=1, source_target_pairs={{0,2},{2,0},{1,3},{3,1},{4,6},{6,4},{5,7},{7,5},{8,10},{10,8},{9,1... | collective-permute-start | bytes 786440 | tf_op jit(solution)/shard_map/ppermute | solution.py:881
  230.8 14.1 %collective-permute-start.46 = (bf16[4,32,1024]{2,1,0:T(8,128)(2,1)S(1)}, bf16[4,32,1024]{2,1,0:T(8,128)(2,1)S(1)}, u32[]{:S(2)}, u32[]{:S(2)}) collective-permute-start(bf16[4,32,1024]{2,1,0:T(8,128)(2,1)S(1)} %get-tuple-element.216), channel_id=1, source_target_pairs={{0,1},{1,0},{2,3},{3,2},{4,5},{5,4},{6,7},{7,6},{8,9},{9,8},{10,11... | collective-permute-start | bytes 786440 | tf_op jit(solution)/shard_map/ppermute | solution.py:877
  237.9 11.0 %collective-permute-start.38 = (bf16[32,1024]{1,0:T(8,128)(2,1)S(1)}, bf16[32,1024]{1,0:T(8,128)(2,1)S(1)}, u32[]{:S(2)}, u32[]{:S(2)}) collective-permute-start(bf16[32,1024]{1,0:T(8,128)(2,1)S(1)} %get-tuple-element.261), channel_id=1, source_target_pairs={{0,8},{8,16},{16,24},{24,0},{1,9},{9,17},{17,25},{25,1},{2,10},{10... | collective-permute-start | bytes 196616 | tf_op jit(solution)/shard_map/ppermute | solution.py:869
  240.6 13.1 %collective-permute-start.39 = (bf16[32,1024]{1,0:T(8,128)(2,1)S(1)}, bf16[32,1024]{1,0:T(8,128)(2,1)S(1)}, u32[]{:S(2)}, u32[]{:S(2)}) collective-permute-start(bf16[32,1024]{1,0:T(8,128)(2,1)S(1)} %get-tuple-element.260), channel_id=1, source_target_pairs={{0,16},{8,24},{16,0},{24,8},{1,17},{9,25},{17,1},{25,9},{2,18},{10... | collective-permute-start | bytes 196616 | tf_op jit(solution)/shard_map/ppermute | solution.py:869
  241.8 11.8 %collective-permute-start.40 = (bf16[32,1024]{1,0:T(8,128)(2,1)S(1)}, bf16[32,1024]{1,0:T(8,128)(2,1)S(1)}, u32[]{:S(2)}, u32[]{:S(2)}) collective-permute-start(bf16[32,1024]{1,0:T(8,128)(2,1)S(1)} %get-tuple-element.259), channel_id=1, source_target_pairs={{0,24},{8,0},{16,8},{24,16},{1,25},{9,1},{17,9},{25,17},{2,26},{10... | collective-permute-start | bytes 196616 | tf_op jit(solution)/shard_map/ppermute | solution.py:869
  245.1 8.5 %collective-permute-start.49 = (bf16[32,1024]{1,0:T(8,128)(2,1)S(1)}, bf16[32,1024]{1,0:T(8,128)(2,1)S(1)}, u32[]{:S(2)}, u32[]{:S(2)}) collective-permute-start(bf16[32,1024]{1,0:T(8,128)(2,1)S(1)} %get-tuple-element.255), channel_id=1, source_target_pairs={{0,8},{8,16},{16,24},{24,0},{1,9},{9,17},{17,25},{25,1},{2,10},{10... | collective-permute-start | bytes 196616 | tf_op jit(solution)/shard_map/ppermute | solution.py:869
  247.6 6.8 %collective-permute-start.50 = (bf16[32,1024]{1,0:T(8,128)(2,1)S(1)}, bf16[32,1024]{1,0:T(8,128)(2,1)S(1)}, u32[]{:S(2)}, u32[]{:S(2)}) collective-permute-start(bf16[32,1024]{1,0:T(8,128)(2,1)S(1)} %get-tuple-element.254), channel_id=1, source_target_pairs={{0,16},{8,24},{16,0},{24,8},{1,17},{9,25},{17,1},{25,9},{2,18},{10... | collective-permute-start | bytes 196616 | tf_op jit(solution)/shard_map/ppermute | solution.py:869
  248.8 5.5 %collective-permute-start.51 = (bf16[32,1024]{1,0:T(8,128)(2,1)S(1)}, bf16[32,1024]{1,0:T(8,128)(2,1)S(1)}, u32[]{:S(2)}, u32[]{:S(2)}) collective-permute-start(bf16[32,1024]{1,0:T(8,128)(2,1)S(1)} %get-tuple-element.253), channel_id=1, source_target_pairs={{0,24},{8,0},{16,8},{24,16},{1,25},{9,1},{17,9},{25,17},{2,26},{10... | collective-permute-start | bytes 196616 | tf_op jit(solution)/shard_map/ppermute | solution.py:869
  (55 other events, 238.2 us)

commit v9 on v8

--- a/solution.py
+++ b/solution.py
@@ -262,7 +262,7 @@
 
 def takes(us):
     return pl.CostEstimate(
-        flops=int(us * 1.15e9), bytes_accessed=int(us * 3.0e6), transcendentals=0
+        flops=int(us * 2.3e9), bytes_accessed=int(us * 6.0e6), transcendentals=0
     )
 
 

time: 257 us -> 253 us (0.984)
  local copies, waits for them, and re-layouts: 38 us -> 31.2 us
  other arithmetic: 15.4 us -> 18 us
    unnamed x134 -> x130, local copies, waits for them, and re-layouts: 21.3 us -> 14 us
    ppermute x21, waiting for transfers between devices: 38.3 us -> 34 us  [turned(): lax.ppermute(x, axis, [(i, (i + by) % length) for i in range(length)])]
    ppermute x3, waiting for transfers between devices: 3.52 us -> 6.81 us  [far_along(): return lax.ppermute(two, 'z', [(1, 0), (2, 3)])]
    ppermute x6, starting transfers between devices: 6.23 us -> 9.26 us  [over_y(): return lax.ppermute(x, 'y', [(0, 1), (1, 0)])]
  transfers between devices with their start and end apart: 52 -> 52, of which waited for: 15 -> 16; matrix products, arithmetic and copies ran while one was open for 12% -> 13% of each run, Pallas kernels for 19% -> 19%
where the time goes in v9:
time: 253 us; the launch traced here: 252 us
  starting transfers between devices  96.7 us (38%)
  waiting for transfers between devices  53.4 us (21%)
  Pallas kernels  51 us (20%)
  local copies, waits for them, and re-layouts  31.2 us (12%)
  other arithmetic  18 us (7%)
    ppermute x21, starting transfers between devices, turned(): lax.ppermute(x, axis, [(i, (i + by) % length) for i in range(length)])  47.2 us
    ppermute x21, waiting for transfers between devices, turned(): lax.ppermute(x, axis, [(i, (i + by) % length) for i in range(length)])  34 us
    ppermute x3, starting transfers between devices, near_along(): one = lax.ppermute(piece, 'z', [(0, 1), (1, 2), (2, 3)])  21.1 us
    unnamed x130, local copies, waits for them, and re-layouts  14 us
    pallas_call x2, Pallas kernels, mix_and_project(): pl.pallas_call(lambda *refs: mix_project_kernel(rel, *refs), grid=(2,), o...  12.2 us
    ppermute x6, starting transfers between devices, over_y(): return lax.ppermute(x, 'y', [(0, 1), (1, 0)])  9.26 us
    pallas_call x1, Pallas kernels, sweep(): pl.pallas_call(sweep_kernel, out_shape=jax.ShapeDtypeStruct(r.shape, f32)...  8.66 us
    ppermute x6, waiting for transfers between devices, over_y(): return lax.ppermute(x, 'y', [(0, 1), (1, 0)])  7.82 us
  transfers between devices with their start and end apart: 52, of which 16 were waited for; matrix products, arithmetic and copies ran while one was open for 13% of the time, Pallas kernels for 19%

profile of v9, /device:TPU:0, one launch (start us, length us, event | category | flops | bytes accessed | tf_op | source)
XLA Modules:
  0.0 252.3 jit_solution(9178360160198724667)
XLA Ops:
  6.5 5.0 %collective-permute-start.1 = (bf16[2,272,512]{2,1,0:T(8,128)(2,1)S(1)}, bf16[2,272,512]{2,1,0:T(8,128)(2,1)S(1)}, u32[]{:S(2)}, u32[]{:S(2)}) collective-permute-start(bf16[2,272,512]{2,1,0:T(8,128)(2,1)S(1)} %shard_map.185.own), channel_id=1, source_target_pairs={{0,8},{8,16},{16,24},{1,9},{9,17},{17,25},{2,10},{10,18},{18,26},{... | collective-permute-start | bytes 1671176 | tf_op jit(solution)/shard_map/ppermute | solution.py:891
  11.5 2.6 %collective-permute-start.2 = (bf16[2,272,512]{2,1,0:T(8,128)(2,1)S(1)}, bf16[2,272,512]{2,1,0:T(8,128)(2,1)}, u32[]{:S(2)}, u32[]{:S(2)}) collective-permute-start(bf16[2,272,512]{2,1,0:T(8,128)(2,1)S(1)} %shard_map.185.own), channel_id=1, source_target_pairs={{0,16},{8,24},{16,0},{24,8},{1,17},{9,25},{17,1},{25,9},{2,18},{10... | collective-permute-start | bytes 1671176 | tf_op jit(solution)/shard_map/ppermute | solution.py:869
  15.4 1.6 collective-permute-start.4
  16.9 1.5 collective-permute-start.5
  28.2 3.0 %fusion = (bf16[2,512,256]{2,1,0:T(8,128)(2,1)}, bf16[2,512,256]{2,1,0:T(8,128)(2,1)}, bf16[2,512,256]{2,1,0:T(8,128)(2,1)}, bf16[2,512,256]{2,1,0:T(8,128)(2,1)}) fusion(s32[]{:T(128)S(6)} %select_n.353, bf16[1,512,1024]{2,1,0:T(8,128)(2,1)} %bitcast.168, bf16[1,512,1024]{2,1,0:T(8,128)(2,1)} %bitcast.169, s32[]{:T(128)S(6)} %select_n.347, ...), kind=kLoop, calls=%fused_computation.24 | loop fusion | flops 4194304 | bytes 4194320 | tf_op jit(solution)/shard_map/stack | solution.py:1008
  32.3 7.8 %collective-permute-done.2 = bf16[2,272,512]{2,1,0:T(8,128)(2,1)} collective-permute-done((bf16[2,272,512]{2,1,0:T(8,128)(2,1)S(1)}, bf16[2,272,512]{2,1,0:T(8,128)(2,1)}, u32[]{:S(2)}, u32[]{:S(2)}) %collective-permute-start.2) | collective-permute-done | bytes 557088 | tf_op jit(solution)/shard_map/ppermute | solution.py:869
  41.1 1.3 collective-permute-start.6
  42.4 1.6 collective-permute-start.7
  45.0 1.6 collective-permute-start.8
  47.2 12.2 %collective-permute-start.12 = (bf16[2,512,256]{2,1,0:T(8,128)(2,1)}, bf16[2,512,256]{2,1,0:T(8,128)(2,1)}, u32[]{:S(2)}, u32[]{:S(2)}) collective-permute-start(bf16[2,512,256]{2,1,0:T(8,128)(2,1)} %get-tuple-element.122), channel_id=1, source_target_pairs={{0,16},{8,24},{16,0},{24,8},{1,17},{9,25},{17,1},{25,9},{2,18},{10... | collective-permute-start | bytes 1572872 | tf_op jit(solution)/shard_map/ppermute | solution.py:869
  59.5 1.6 pad_maximum_fusion.1
  61.1 4.0 %collective-permute-done.6 = bf16[2,272,512]{2,1,0:T(8,128)(2,1)S(1)} collective-permute-done((bf16[2,272,512]{2,1,0:T(8,128)(2,1)}, bf16[2,272,512]{2,1,0:T(8,128)(2,1)S(1)}, u32[]{:S(2)}, u32[]{:S(2)}) %collective-permute-start.6) | collective-permute-done | bytes 557088 | tf_op jit(solution)/shard_map/ppermute | solution.py:897
  66.4 1.3 pad_maximum_fusion.3.rest
  67.7 1.6 collective-permute-start.9
  69.3 1.5 collective-permute-start.10
  70.8 3.8 %collective-permute-start.13 = (bf16[2,512,256]{2,1,0:T(8,128)(2,1)}, bf16[2,512,256]{2,1,0:T(8,128)(2,1)}, u32[]{:S(2)}, u32[]{:S(2)}) collective-permute-start(bf16[2,512,256]{2,1,0:T(8,128)(2,1)} %get-tuple-element.135), channel_id=1, source_target_pairs={{0,24},{8,0},{16,8},{24,16},{1,25},{9,1},{17,9},{25,17},{2,26},{10... | collective-permute-start | bytes 1572872 | tf_op jit(solution)/shard_map/ppermute | solution.py:869
  74.6 6.0 %shard_map.186 = (bf16[2,1024,512]{2,1,0:T(8,128)(2,1)S(1)}, bf16[2,1024,512]{2,1,0:T(8,128)(2,1)S(1)}, bf16[2,1024,512]{2,1,0:T(8,128)(2,1)S(1)}, bf16[2,1024,512]{2,1,0:T(8,128)(2,1)S(1)}, f32[2,1024,128]{2,1,0:T(8,128)S(1)}) custom-call(s32[14]{0:T(128)S(1)} %copy-done.20, bf16[2,272,512]{2,1,0:T(8,128)(2,1)S(1)} %copy-done.11, ...), custom_call_target="tpu_custom_call" | custom-call | flops 16099999744 | bytes 42000000 | tf_op jit(solution)/shard_map/pallas_call | solution.py:396
  80.6 1.3 copy-done.32
  81.9 1.3 copy-done.36
  83.2 1.4 copy-done.40
  84.6 1.4 copy-done.42
  93.2 1.3 select_n.361.lengths
  94.5 9.4 %collective-permute-done.13 = bf16[2,512,256]{2,1,0:T(8,128)(2,1)} collective-permute-done((bf16[2,512,256]{2,1,0:T(8,128)(2,1)}, bf16[2,512,256]{2,1,0:T(8,128)(2,1)}, u32[]{:S(2)}, u32[]{:S(2)}) %collective-permute-start.13) | collective-permute-done | bytes 524320 | tf_op jit(solution)/shard_map/ppermute | solution.py:869
  107.0 1.6 collective-permute-start.14
  109.2 4.2 %collective-permute-start.17 = (bf16[1,512,256]{2,1,0:T(8,128)(2,1)S(1)}, bf16[1,512,256]{2,1,0:T(8,128)(2,1)S(1)}, u32[]{:S(2)}, u32[]{:S(2)}) collective-permute-start(bf16[1,512,256]{2,1,0:T(8,128)(2,1)S(1)} %copy-done.60), channel_id=1, source_target_pairs={{0,16},{8,24},{16,0},{24,8},{1,17},{9,25},{17,1},{25,9},{2,18},{10... | collective-permute-start | bytes 786440 | tf_op jit(solution)/shard_map/ppermute | solution.py:869
  113.5 1.8 pad_maximum_fusion.refs_5_.own_kv
  115.8 6.7 %shard_map.187 = (bf16[2,1024,512]{2,1,0:T(8,128)(2,1)S(1)}, bf16[2,1024,512]{2,1,0:T(8,128)(2,1)S(1)}, bf16[2,1024,512]{2,1,0:T(8,128)(2,1)S(1)}, f32[2,1024,12...) custom-call(s32[14]{0:T(128)S(1)} %copy-done.21, bf16[2,272,512]{2,1,0:T(8,128)(2,1)S(1)} %copy-done.9, ...), custom_call_target="tpu_custom_call" | custom-call | flops 13799999488 | bytes 36000000 | tf_op jit(solution)/shard_map/pallas_call | solution.py:461
  123.8 1.6 collective-permute-start.18
  125.5 5.5 %shard_map.188 = (bf16[2,1024,512]{2,1,0:T(8,128)(2,1)S(1)}, bf16[2,1024,512]{2,1,0:T(8,128)(2,1)S(1)}, bf16[2,1024,512]{2,1,0:T(8,128)(2,1)S(1)}, f32[2,1024,12...) custom-call(s32[14]{0:T(128)S(1)} %copy-done.21, bf16[2,272,512]{2,1,0:T(8,128)(2,1)S(1)} %copy-done.7, ...), custom_call_target="tpu_custom_call" | custom-call | flops 13799999488 | bytes 36000000 | tf_op jit(solution)/shard_map/pallas_call | solution.py:461
  131.0 2.0 collective-permute-done.18
  133.6 2.5 collective-permute-start.21
  137.4 1.6 copy-done.39
  139.0 1.6 copy-done.43
  140.6 7.4 %shard_map.189 = (f32[1024,256]{1,0:T(8,128)S(1)}, f32[1024,256]{1,0:T(8,128)S(1)}, f32[1024,256]{1,0:T(8,128)S(1)}, bf16[2,1024,512]{2,1,0:T(8,128)(2,1)S(1)}, bf16[2,1024,512]{2,1,0:T(8,128)(2,1)S(1)}) custom-call(s32[14]{0:T(128)S(1)} %copy-done.21, bf16[2,1024,512]{2,1,0:T(8,128)(2,1)S(1)} %copy-done.43, bf16[2,1024,512]{2,1,0:T(8,128)(2,1)S(1)} %copy-done.39, ...), custom_call_target="tpu_custom_call" | custom-call | flops 18400000000 | bytes 48000000 | tf_op jit(solution)/shard_map/pallas_call | solution.py:546
  148.0 3.1 %shard_map.190 = (f32[16,4,64,64]{3,2,1,0:T(8,128)S(1)}, bf16[16,64,256]{2,1,0:T(8,128)(2,1)S(1)}) custom-call(s32[16]{0:T(128)S(1)} %copy-done.18, f32[1]{0:T(128)} %bitcast.62.carry, f32[1024,256]{1,0:T(8,128)S(1)} %get-tuple-element.178.k_ref, f32[1024,256]{1,0:T(8,128)S(1)} %get-tuple-element.179.v_ref, f32[1024,256]{1,0:T(8,128)S(1)} %get-tuple-element.180.w_ref, ...), custom_call_target="tpu_custom_call" | custom-call | flops 16099999744 | bytes 42000000 | tf_op jit(solution)/shard_map/pallas_call | solution.py:716
  152.0 2.5 collective-permute-done.21
  155.2 5.5 %collective-permute-start.26 = (bf16[3,4,64,64]{3,2,1,0:T(8,128)(2,1)S(1)}, bf16[3,4,64,64]{3,2,1,0:T(8,128)(2,1)S(1)}, u32[]{:S(2)}, u32[]{:S(2)}) collective-permute-start(bf16[3,4,64,64]{3,2,1,0:T(8,128)(2,1)S(1)} %get-tuple-element.249), channel_id=1, source_target_pairs={{0,8},{8,16},{16,24},{24,0},{1,9},{9,17},{17,25},{25,1},{2,10},{10... | collective-permute-start | bytes 294920 | tf_op jit(solution)/shard_map/ppermute | solution.py:869
  160.6 2.4 collective-permute-start.28
  163.1 3.3 %shard_map.191.r_ref = f32[1024,256]{1,0:T(8,128)S(1)} custom-call(s32[14]{0:T(128)S(1)} %copy-done.21, bf16[2,1024,512]{2,1,0:T(8,128)(2,1)S(1)} %copy-done.33, bf16[2,1024,512]{2,1,0:T(8,128)(2,1)S(1)} %get-tuple-element.188.mix1, bf16[2,1024,512]{2,1,0:T(8,128)(2,1)S(1)} %get-tuple-element.189.mix2, bf16[2,1024,512]{2,1,0:T(8,128)(2,1)S(1)} %get-tuple-element.192.mix3, ...), custom_call_target="tpu_custom_call" | custom-call | flops 13799999488 | bytes 36000000 | tf_op jit(solution)/shard_map/pallas_call | solution.py:581
  166.4 8.7 %shard_map.192.normed = f32[1024,256]{1,0:T(8,128)S(1)} custom-call(s32[16]{0:T(128)S(1)} %copy-done.18, f32[1024,256]{1,0:T(8,128)S(1)} %shard_map.191.r_ref, f32[1024,256]{1,0:T(8,128)S(1)} %get-tuple-element.178.k_ref, f32[1024,256]{1,0:T(8,128)S(1)} %get-tuple-element.179.v_ref, f32[1024,256]{1,0:T(8,128)S(1)} %get-tuple-element.180.w_ref, ...), custom_call_target="tpu_custom_call" | custom-call | flops 27599998976 | bytes 72000000 | tf_op jit(solution)/shard_map/pallas_call | solution.py:802
  175.1 3.5 %shard_map.193 = (bf16[2,4,32,256]{3,2,1,0:T(8,128)(2,1)S(1)}, bf16[2,4,32,256]{3,2,1,0:T(8,128)(2,1)S(1)}, bf16[2,4,32,256]{3,2,1,0:T(8,128)(2,1)S(1)}, bf16[2,4,32,256]{3,2,1,0:T(8,128)(2,1)S(1)}) custom-call(s32[14]{0:T(128)S(1)} %copy-done.21, s32[16]{0:T(128)S(1)} %copy-done.18, bf16[2,1024,512]{2,1,0:T(8,128)(2,1)S(1)} %copy-done.41, ...), custom_call_target="tpu_custom_call" | custom-call | flops 16099999744 | bytes 42000000 | tf_op jit(solution)/shard_map/pallas_call | solution.py:645
  180.9 1.3 collective-permute-start.33
  182.2 5.0 %collective-permute-start.32 = (bf16[512,256]{1,0:T(8,128)(2,1)S(1)}, bf16[512,256]{1,0:T(8,128)(2,1)S(1)}, u32[]{:S(2)}, u32[]{:S(2)}) collective-permute-start(bf16[512,256]{1,0:T(8,128)(2,1)S(1)} %bitcast.157), channel_id=1, source_target_pairs={{0,8},{8,16},{16,24},{1,9},{9,17},{17,25},{2,10},{10,18},{18,26},{... | collective-permute-start | bytes 786440 | tf_op jit(solution)/shard_map/ppermute | solution.py:891
  187.3 7.7 %collective-permute-done.30.h2 = bf16[512,256]{1,0:T(8,128)(2,1)S(1)} collective-permute-done((bf16[512,256]{1,0:T(8,128)(2,1)S(1)}, bf16[512,256]{1,0:T(8,128)(2,1)S(1)}, u32[]{:S(2)}, u32[]{:S(2)}) %collective-permute-start.30) | collective-permute-done | bytes 262176 | tf_op jit(solution)/shard_map/ppermute | solution.py:869
  196.4 1.3 collective-permute-start.45
  197.7 11.0 %collective-permute-start.44 = (bf16[512,256]{1,0:T(8,128)(2,1)S(1)}, bf16[512,256]{1,0:T(8,128)(2,1)S(1)}, u32[]{:S(2)}, u32[]{:S(2)}) collective-permute-start(bf16[512,256]{1,0:T(8,128)(2,1)S(1)} %bitcast.153), channel_id=1, source_target_pairs={{0,8},{8,16},{16,24},{1,9},{9,17},{17,25},{2,10},{10,18},{18,26},{... | collective-permute-start | bytes 786440 | tf_op jit(solution)/shard_map/ppermute | solution.py:891
  208.7 3.2 %collective-permute-done.42.h2 = bf16[512,256]{1,0:T(8,128)(2,1)S(1)} collective-permute-done((bf16[512,256]{1,0:T(8,128)(2,1)S(1)}, bf16[512,256]{1,0:T(8,128)(2,1)S(1)}, u32[]{:S(2)}, u32[]{:S(2)}) %collective-permute-start.42) | collective-permute-done | bytes 262176 | tf_op jit(solution)/shard_map/ppermute | solution.py:869
  211.9 1.5 collective-permute-start.43
  213.5 2.1 shard_map.194
  215.6 1.5 collective-permute-start.37
  217.1 1.5 collective-permute-start.36
  219.2 2.8 %collective-permute-done.43 = bf16[512,256]{1,0:T(8,128)(2,1)S(1)} collective-permute-done((bf16[512,256]{1,0:T(8,128)(2,1)S(1)}, bf16[512,256]{1,0:T(8,128)(2,1)S(1)}, u32[]{:S(2)}, u32[]{:S(2)}) %collective-permute-start.43) | collective-permute-done | bytes 262176 | tf_op jit(solution)/shard_map/ppermute | solution.py:897
  222.0 2.1 shard_map.195
  224.1 1.5 collective-permute-start.48
  225.6 1.5 collective-permute-start.47
  227.7 3.8 %collective-permute-done.36 = bf16[4,32,1024]{2,1,0:T(8,128)(2,1)S(1)} collective-permute-done((bf16[4,32,1024]{2,1,0:T(8,128)(2,1)S(1)}, bf16[4,32,1024]{2,1,0:T(8,128)(2,1)S(1)}, u32[]{:S(2)}, u32[]{:S(2)}) %collective-permute-start.36) | collective-permute-done | bytes 262176 | tf_op jit(solution)/shard_map/ppermute | solution.py:881
  231.7 2.7 %collective-permute-start.38 = (bf16[32,1024]{1,0:T(8,128)(2,1)S(1)}, bf16[32,1024]{1,0:T(8,128)(2,1)S(1)}, u32[]{:S(2)}, u32[]{:S(2)}) collective-permute-start(bf16[32,1024]{1,0:T(8,128)(2,1)S(1)} %get-tuple-element.261), channel_id=1, source_target_pairs={{0,8},{8,16},{16,24},{24,0},{1,9},{9,17},{17,25},{25,1},{2,10},{10... | collective-permute-start | bytes 196616 | tf_op jit(solution)/shard_map/ppermute | solution.py:869
  234.7 2.4 collective-permute-done.48
  237.1 1.6 collective-permute-start.40
  238.7 2.9 %collective-permute-done.47 = bf16[4,32,1024]{2,1,0:T(8,128)(2,1)S(1)} collective-permute-done((bf16[4,32,1024]{2,1,0:T(8,128)(2,1)S(1)}, bf16[4,32,1024]{2,1,0:T(8,128)(2,1)S(1)}, u32[]{:S(2)}, u32[]{:S(2)}) %collective-permute-start.47) | collective-permute-done | bytes 262176 | tf_op jit(solution)/shard_map/ppermute | solution.py:881
  241.8 2.4 collective-permute-start.49
  244.5 2.8 %collective-permute-start.51 = (bf16[32,1024]{1,0:T(8,128)(2,1)S(1)}, bf16[32,1024]{1,0:T(8,128)(2,1)S(1)}, u32[]{:S(2)}, u32[]{:S(2)}) collective-permute-start(bf16[32,1024]{1,0:T(8,128)(2,1)S(1)} %get-tuple-element.253), channel_id=1, source_target_pairs={{0,24},{8,0},{16,8},{24,16},{1,25},{9,1},{17,9},{25,17},{2,26},{10... | collective-permute-start | bytes 196616 | tf_op jit(solution)/shard_map/ppermute | solution.py:869
  249.3 1.5 collective-permute-done.50.refs_6_
  250.9 1.4 shard_map.196
  (252 shorter events, 45.3 us)
Async XLA Ops:
  0.6 30.7 %copy-start = (bf16[128,1024]{1,0:T(8,128)(2,1)S(1)}, bf16[128,1024]{1,0:T(8,128)(2,1)}, u32[]{:S(2)}) copy-start(bf16[128,1024]{1,0:T(8,128)(2,1)} %param.29) | copy-start | bytes 786436
  4.1 1.7 collective-permute-start
  5.8 12.7 %copy-start.62 = (f32[5,4096]{1,0:T(8,128)S(1)}, f32[5,4096]{1,0:T(8,128)}, u32[]{:S(2)}) copy-start(f32[5,4096]{1,0:T(8,128)} %param.22) | copy-start | bytes 245764
  5.8 12.7 %copy-start.49 = (bf16[4096,128]{1,0:T(8,128)(2,1)S(1)}, bf16[4096,128]{1,0:T(8,128)(2,1)}, u32[]{:S(2)}) copy-start(bf16[4096,128]{1,0:T(8,128)(2,1)} %param.28) | copy-start | bytes 3145732
  6.5 18.6 %copy-start.10 = (bf16[2,272,512]{2,1,0:T(8,128)(2,1)}, bf16[2,272,512]{2,1,0:T(8,128)(2,1)S(1)}, u32[]{:S(2)}) copy-start(bf16[2,272,512]{2,1,0:T(8,128)(2,1)S(1)} %shard_map.185.own) | copy-start | bytes 1671172
  6.5 12.9 %copy-start.50 = (bf16[512,1024]{1,0:T(8,128)(2,1)S(1)}, bf16[512,1024]{1,0:T(8,128)(2,1)}, u32[]{:S(2)}) copy-start(bf16[512,1024]{1,0:T(8,128)(2,1)} %param.23) | copy-start | bytes 3145732
  6.5 24.7 %collective-permute-start.1 = (bf16[2,272,512]{2,1,0:T(8,128)(2,1)S(1)}, bf16[2,272,512]{2,1,0:T(8,128)(2,1)S(1)}, u32[]{:S(2)}, u32[]{:S(2)}) collective-permute-start(bf16[2,272,512]{2,1,0:T(8,128)(2,1)S(1)} %shard_map.185.own), channel_id=1, source_target_pairs={{0,8},{8,16},{16,24},{1,9},{9,17},{17,25},{2,10},{10,18},{18,26},{... | collective-permute-start | bytes 1671176 | tf_op jit(solution)/shard_map/ppermute | solution.py:891
  11.5 28.5 %collective-permute-start.2 = (bf16[2,272,512]{2,1,0:T(8,128)(2,1)S(1)}, bf16[2,272,512]{2,1,0:T(8,128)(2,1)}, u32[]{:S(2)}, u32[]{:S(2)}) collective-permute-start(bf16[2,272,512]{2,1,0:T(8,128)(2,1)S(1)} %shard_map.185.own), channel_id=1, source_target_pairs={{0,16},{8,24},{16,0},{24,8},{1,17},{9,25},{17,1},{25,9},{2,18},{10... | collective-permute-start | bytes 1671176 | tf_op jit(solution)/shard_map/ppermute | solution.py:869
  14.1 27.0 %collective-permute-start.3 = (bf16[2,272,512]{2,1,0:T(8,128)(2,1)S(1)}, bf16[2,272,512]{2,1,0:T(8,128)(2,1)}, u32[]{:S(2)}, u32[]{:S(2)}) collective-permute-start(bf16[2,272,512]{2,1,0:T(8,128)(2,1)S(1)} %shard_map.185.own), channel_id=1, source_target_pairs={{8,0},{16,8},{24,16},{9,1},{17,9},{25,17},{10,2},{18,10},{26,18},{... | collective-permute-start | bytes 1671176 | tf_op jit(solution)/shard_map/ppermute | solution.py:892
  15.4 25.7 %collective-permute-start.4 = (bf16[2,272,512]{2,1,0:T(8,128)(2,1)S(1)}, bf16[2,272,512]{2,1,0:T(8,128)(2,1)S(1)}, u32[]{:S(2)}, u32[]{:S(2)}) collective-permute-start(bf16[2,272,512]{2,1,0:T(8,128)(2,1)S(1)} %shard_map.185.own), channel_id=1, source_target_pairs={{0,1},{1,0},{2,3},{3,2},{4,5},{5,4},{6,7},{7,6},{8,9},{9,8},{10,11... | collective-permute-start | bytes 1671176 | tf_op jit(solution)/shard_map/ppermute | solution.py:877
  16.9 24.1 %collective-permute-start.5 = (bf16[2,272,512]{2,1,0:T(8,128)(2,1)S(1)}, bf16[2,272,512]{2,1,0:T(8,128)(2,1)S(1)}, u32[]{:S(2)}, u32[]{:S(2)}) collective-permute-start(bf16[2,272,512]{2,1,0:T(8,128)(2,1)S(1)} %shard_map.185.own), channel_id=1, source_target_pairs={{0,2},{2,0},{1,3},{3,1},{4,6},{6,4},{5,7},{7,5},{8,10},{10,8},{9,1... | collective-permute-start | bytes 1671176 | tf_op jit(solution)/shard_map/ppermute | solution.py:881
  31.2 28.1 %copy-start.54 = (bf16[2,272,512]{2,1,0:T(8,128)(2,1)}, bf16[2,272,512]{2,1,0:T(8,128)(2,1)S(1)}, u32[]{:S(2)}) copy-start(bf16[2,272,512]{2,1,0:T(8,128)(2,1)S(1)} %collective-permute-done.1) | copy-start | bytes 1671172
  31.2 28.1 %collective-permute-start.34 = (bf16[1024,512]{1,0:T(8,128)(2,1)S(1)}, bf16[1024,512]{1,0:T(8,128)(2,1)S(1)}, u32[]{:S(2)}, u32[]{:S(2)}) collective-permute-start(bf16[1024,512]{1,0:T(8,128)(2,1)S(1)} %copy-done.48), channel_id=1, source_target_pairs={{0,4},{4,0},{1,5},{5,1},{2,6},{6,2},{3,7},{7,3},{8,12},{12,8},{9,1... | collective-permute-start | bytes 3145736 | tf_op jit(solution)/shard_map/ppermute | solution.py:873
  41.1 18.4 %copy-start.8 = (bf16[2,272,512]{2,1,0:T(8,128)(2,1)}, bf16[2,272,512]{2,1,0:T(8,128)(2,1)S(1)}, u32[]{:S(2)}) copy-start(bf16[2,272,512]{2,1,0:T(8,128)(2,1)S(1)} %collective-permute-done.4.refs_1_) | copy-start | bytes 1671172
  41.1 18.4 %copy-start.6 = (bf16[2,272,512]{2,1,0:T(8,128)(2,1)}, bf16[2,272,512]{2,1,0:T(8,128)(2,1)S(1)}, u32[]{:S(2)}) copy-start(bf16[2,272,512]{2,1,0:T(8,128)(2,1)S(1)} %collective-permute-done.5.refs_1_) | copy-start | bytes 1671172
  41.1 24.1 %collective-permute-start.6 = (bf16[2,272,512]{2,1,0:T(8,128)(2,1)}, bf16[2,272,512]{2,1,0:T(8,128)(2,1)S(1)}, u32[]{:S(2)}, u32[]{:S(2)}) collective-permute-start(bf16[2,272,512]{2,1,0:T(8,128)(2,1)} %collective-permute-done.2), channel_id=1, source_target_pairs={{8,0},{16,24},{9,1},{17,25},{10,2},{18,26},{11,3},{19,27},{12,4},{... | collective-permute-start | bytes 1671176 | tf_op jit(solution)/shard_map/ppermute | solution.py:897
  42.4 18.7 %collective-permute-start.7 = (bf16[272,512]{1,0:T(8,128)(2,1)S(1)}, bf16[272,512]{1,0:T(8,128)(2,1)S(1)}, u32[]{:S(2)}, u32[]{:S(2)}) collective-permute-start(bf16[272,512]{1,0:T(8,128)(2,1)S(1)} %slice_bitcast_fusion.6), channel_id=1, source_target_pairs={{0,2},{2,0},{1,3},{3,1},{4,6},{6,4},{5,7},{7,5},{8,10},{10,8},{9,1... | collective-permute-start | bytes 835592 | tf_op jit(solution)/shard_map/ppermute | solution.py:881
  45.0 16.1 %collective-permute-start.8 = (bf16[272,512]{1,0:T(8,128)(2,1)S(1)}, bf16[272,512]{1,0:T(8,128)(2,1)S(1)}, u32[]{:S(2)}, u32[]{:S(2)}) collective-permute-start(bf16[272,512]{1,0:T(8,128)(2,1)S(1)} %slice_bitcast_fusion.5), channel_id=1, source_target_pairs={{0,1},{1,0},{2,3},{3,2},{4,5},{5,4},{6,7},{7,6},{8,9},{9,8},{10,11... | collective-permute-start | bytes 835592 | tf_op jit(solution)/shard_map/ppermute | solution.py:877
  47.2 47.4 %collective-permute-start.12 = (bf16[2,512,256]{2,1,0:T(8,128)(2,1)}, bf16[2,512,256]{2,1,0:T(8,128)(2,1)}, u32[]{:S(2)}, u32[]{:S(2)}) collective-permute-start(bf16[2,512,256]{2,1,0:T(8,128)(2,1)} %get-tuple-element.122), channel_id=1, source_target_pairs={{0,16},{8,24},{16,0},{24,8},{1,17},{9,25},{17,1},{25,9},{2,18},{10... | collective-permute-start | bytes 1572872 | tf_op jit(solution)/shard_map/ppermute | solution.py:869
  67.7 37.0 %collective-permute-start.9 = (bf16[2,3,272,512]{3,2,1,0:T(8,128)(2,1)S(1)}, bf16[2,3,272,512]{3,2,1,0:T(8,128)(2,1)}, u32[]{:S(2)}, u32[]{:S(2)}) collective-permute-start(bf16[2,3,272,512]{3,2,1,0:T(8,128)(2,1)S(1)} %pad_maximum_fusion.3.rest), channel_id=1, source_target_pairs={{0,1},{1,0},{2,3},{3,2},{4,5},{5,4},{6,7},{7,6},{8,9},{9,8},{10,11... | collective-permute-start | bytes 5013512 | tf_op jit(solution)/shard_map/ppermute | solution.py:877
  69.3 36.5 %collective-permute-start.10 = (bf16[2,3,272,512]{3,2,1,0:T(8,128)(2,1)S(1)}, bf16[2,3,272,512]{3,2,1,0:T(8,128)(2,1)S(1)}, u32[]{:S(2)}, u32[]{:S(2)}) collective-permute-start(bf16[2,3,272,512]{3,2,1,0:T(8,128)(2,1)S(1)} %pad_maximum_fusion.3.rest), channel_id=1, source_target_pairs={{0,2},{2,0},{1,3},{3,1},{4,6},{6,4},{5,7},{7,5},{8,10},{10,8},{9,1... | collective-permute-start | bytes 5013512 | tf_op jit(solution)/shard_map/ppermute | solution.py:881
  70.8 23.7 %collective-permute-start.11 = (bf16[2,512,256]{2,1,0:T(8,128)(2,1)}, bf16[2,512,256]{2,1,0:T(8,128)(2,1)}, u32[]{:S(2)}, u32[]{:S(2)}) collective-permute-start(bf16[2,512,256]{2,1,0:T(8,128)(2,1)} %get-tuple-element.134), channel_id=1, source_target_pairs={{0,8},{8,16},{16,24},{24,0},{1,9},{9,17},{17,25},{25,1},{2,10},{10... | collective-permute-start | bytes 1572872 | tf_op jit(solution)/shard_map/ppermute | solution.py:869
  70.8 33.1 %collective-permute-start.13 = (bf16[2,512,256]{2,1,0:T(8,128)(2,1)}, bf16[2,512,256]{2,1,0:T(8,128)(2,1)}, u32[]{:S(2)}, u32[]{:S(2)}) collective-permute-start(bf16[2,512,256]{2,1,0:T(8,128)(2,1)} %get-tuple-element.135), channel_id=1, source_target_pairs={{0,24},{8,0},{16,8},{24,16},{1,25},{9,1},{17,9},{25,17},{2,26},{10... | collective-permute-start | bytes 1572872 | tf_op jit(solution)/shard_map/ppermute | solution.py:869
  94.5 14.7 %copy-start.61 = (bf16[1,512,256]{2,1,0:T(8,128)(2,1)S(1)}, bf16[1,512,256]{2,1,0:T(8,128)(2,1)}, u32[]{:S(2)}) copy-start(bf16[1,512,256]{2,1,0:T(8,128)(2,1)} %get-tuple-element.162) | copy-start | bytes 786436
  94.5 14.7 %copy-start.60 = (bf16[1,512,256]{2,1,0:T(8,128)(2,1)S(1)}, bf16[1,512,256]{2,1,0:T(8,128)(2,1)}, u32[]{:S(2)}) copy-start(bf16[1,512,256]{2,1,0:T(8,128)(2,1)} %get-tuple-element.163) | copy-start | bytes 786436
  94.5 19.0 %copy-start.47 = (bf16[2,512,256]{2,1,0:T(8,128)(2,1)S(1)}, bf16[2,512,256]{2,1,0:T(8,128)(2,1)}, u32[]{:S(2)}) copy-start(bf16[2,512,256]{2,1,0:T(8,128)(2,1)} %get-tuple-element.142) | copy-start | bytes 1572868
  107.0 26.0 %collective-permute-start.14 = (bf16[3,272,512]{2,1,0:T(8,128)(2,1)S(1)}, bf16[3,272,512]{2,1,0:T(8,128)(2,1)S(1)}, u32[]{:S(2)}, u32[]{:S(2)}) collective-permute-start(bf16[3,272,512]{2,1,0:T(8,128)(2,1)S(1)} %slice_bitcast_fusion.1), channel_id=1, source_target_pairs={{0,2},{2,0},{1,3},{3,1},{4,6},{6,4},{5,7},{7,5},{8,10},{10,8},{9,1... | collective-permute-start | bytes 2506760 | tf_op jit(solution)/shard_map/ppermute | solution.py:881
  108.6 24.4 %collective-permute-start.15 = (bf16[3,272,512]{2,1,0:T(8,128)(2,1)S(1)}, bf16[3,272,512]{2,1,0:T(8,128)(2,1)S(1)}, u32[]{:S(2)}, u32[]{:S(2)}) collective-permute-start(bf16[3,272,512]{2,1,0:T(8,128)(2,1)S(1)} %slice_bitcast_fusion), channel_id=1, source_target_pairs={{0,1},{1,0},{2,3},{3,2},{4,5},{5,4},{6,7},{7,6},{8,9},{9,8},{10,11... | collective-permute-start | bytes 2506760 | tf_op jit(solution)/shard_map/ppermute | solution.py:877
  109.2 14.6 %collective-permute-start.16 = (bf16[1,512,256]{2,1,0:T(8,128)(2,1)S(1)}, bf16[1,512,256]{2,1,0:T(8,128)(2,1)S(1)}, u32[]{:S(2)}, u32[]{:S(2)}) collective-permute-start(bf16[1,512,256]{2,1,0:T(8,128)(2,1)S(1)} %copy-done.61), channel_id=1, source_target_pairs={{0,8},{8,16},{16,24},{24,0},{1,9},{9,17},{17,25},{25,1},{2,10},{10... | collective-permute-start | bytes 786440 | tf_op jit(solution)/shard_map/ppermute | solution.py:869
  109.2 21.8 %collective-permute-start.17 = (bf16[1,512,256]{2,1,0:T(8,128)(2,1)S(1)}, bf16[1,512,256]{2,1,0:T(8,128)(2,1)S(1)}, u32[]{:S(2)}, u32[]{:S(2)}) collective-permute-start(bf16[1,512,256]{2,1,0:T(8,128)(2,1)S(1)} %copy-done.60), channel_id=1, source_target_pairs={{0,16},{8,24},{16,0},{24,8},{1,17},{9,25},{17,1},{25,9},{2,18},{10... | collective-permute-start | bytes 786440 | tf_op jit(solution)/shard_map/ppermute | solution.py:869
  115.3 22.1 %collective-permute-start.19 = (bf16[4,2,512,256]{3,2,1,0:T(8,128)(2,1)S(1)}, bf16[4,2,512,256]{3,2,1,0:T(8,128)(2,1)S(1)}, u32[]{:S(2)}, u32[]{:S(2)}) collective-permute-start(bf16[4,2,512,256]{3,2,1,0:T(8,128)(2,1)S(1)} %pad_maximum_fusion.refs_5_.own_kv), channel_id=1, source_target_pairs={{0,4},{4,0},{1,5},{5,1},{2,6},{6,2},{3,7},{7,3},{8,12},{12,8},{9,1... | collective-permute-start | bytes 6291464 | tf_op jit(solution)/shard_map/ppermute | solution.py:873
  123.8 9.2 %collective-permute-start.18 = (bf16[1,512,256]{2,1,0:T(8,128)(2,1)S(1)}, bf16[1,512,256]{2,1,0:T(8,128)(2,1)S(1)}, u32[]{:S(2)}, u32[]{:S(2)}) collective-permute-start(bf16[1,512,256]{2,1,0:T(8,128)(2,1)S(1)} %copy-done.59), channel_id=1, source_target_pairs={{0,24},{8,0},{16,8},{24,16},{1,25},{9,1},{17,9},{25,17},{2,26},{10... | collective-permute-start | bytes 786440 | tf_op jit(solution)/shard_map/ppermute | solution.py:869
  133.0 19.0 %collective-permute-start.20 = (bf16[1,512,256]{2,1,0:T(8,128)(2,1)S(1)}, bf16[1,512,256]{2,1,0:T(8,128)(2,1)S(1)}, u32[]{:S(2)}, u32[]{:S(2)}) collective-permute-start(bf16[1,512,256]{2,1,0:T(8,128)(2,1)S(1)} %copy-done.58), channel_id=1, source_target_pairs={{0,8},{8,16},{16,24},{24,0},{1,9},{9,17},{17,25},{25,1},{2,10},{10... | collective-permute-start | bytes 786440 | tf_op jit(solution)/shard_map/ppermute | solution.py:869
  133.6 20.9 %collective-permute-start.21 = (bf16[1,512,256]{2,1,0:T(8,128)(2,1)S(1)}, bf16[1,512,256]{2,1,0:T(8,128)(2,1)S(1)}, u32[]{:S(2)}, u32[]{:S(2)}) collective-permute-start(bf16[1,512,256]{2,1,0:T(8,128)(2,1)S(1)} %copy-done.57), channel_id=1, source_target_pairs={{0,16},{8,24},{16,0},{24,8},{1,17},{9,25},{17,1},{25,9},{2,18},{10... | collective-permute-start | bytes 786440 | tf_op jit(solution)/shard_map/ppermute | solution.py:869
  136.1 18.4 %collective-permute-start.22 = (bf16[1,512,256]{2,1,0:T(8,128)(2,1)S(1)}, bf16[1,512,256]{2,1,0:T(8,128)(2,1)S(1)}, u32[]{:S(2)}, u32[]{:S(2)}) collective-permute-start(bf16[1,512,256]{2,1,0:T(8,128)(2,1)S(1)} %copy-done.56), channel_id=1, source_target_pairs={{0,24},{8,0},{16,8},{24,16},{1,25},{9,1},{17,9},{25,17},{2,26},{10... | collective-permute-start | bytes 786440 | tf_op jit(solution)/shard_map/ppermute | solution.py:869
  137.3 25.8 %collective-permute-start.25 = (bf16[4,1,512,256]{3,2,1,0:T(8,128)(2,1)S(1)}, bf16[4,1,512,256]{3,2,1,0:T(8,128)(2,1)S(1)}, u32[]{:S(2)}, u32[]{:S(2)}) collective-permute-start(bf16[4,1,512,256]{3,2,1,0:T(8,128)(2,1)S(1)} %pad_maximum_fusion.5.own), channel_id=1, source_target_pairs={{0,4},{4,0},{1,5},{5,1},{2,6},{6,2},{3,7},{7,3},{8,12},{12,8},{9,1... | collective-permute-start | bytes 3145736 | tf_op jit(solution)/shard_map/ppermute | solution.py:873
  151.2 3.5 %collective-permute-start.24 = (bf16[4,2,4,64,64]{4,3,2,1,0:T(8,128)(2,1)S(1)}, bf16[4,2,4,64,64]{4,3,2,1,0:T(8,128)(2,1)S(1)}, u32[]{:S(2)}, u32[]{:S(2)}) collective-permute-start(bf16[4,2,4,64,64]{4,3,2,1,0:T(8,128)(2,1)S(1)} %dynamic-slice_bitcast_fusion), channel_id=1, source_target_pairs={{0,4},{4,0},{1,5},{5,1},{2,6},{6,2},{3,7},{7,3},{8,12},{12,8},{9,1... | collective-permute-start | bytes 786440 | tf_op jit(solution)/shard_map/ppermute | solution.py:873
  154.6 20.5 %collective-permute-start.23 = (bf16[4,1,512,256]{3,2,1,0:T(8,128)(2,1)S(1)}, bf16[4,1,512,256]{3,2,1,0:T(8,128)(2,1)S(1)}, u32[]{:S(2)}, u32[]{:S(2)}) collective-permute-start(bf16[4,1,512,256]{3,2,1,0:T(8,128)(2,1)S(1)} %pad_maximum_fusion.4.own), channel_id=1, source_target_pairs={{0,4},{4,0},{1,5},{5,1},{2,6},{6,2},{3,7},{7,3},{8,12},{12,8},{9,1... | collective-permute-start | bytes 3145736 | tf_op jit(solution)/shard_map/ppermute | solution.py:873
  155.2 23.5 %collective-permute-start.26 = (bf16[3,4,64,64]{3,2,1,0:T(8,128)(2,1)S(1)}, bf16[3,4,64,64]{3,2,1,0:T(8,128)(2,1)S(1)}, u32[]{:S(2)}, u32[]{:S(2)}) collective-permute-start(bf16[3,4,64,64]{3,2,1,0:T(8,128)(2,1)S(1)} %get-tuple-element.249), channel_id=1, source_target_pairs={{0,8},{8,16},{16,24},{24,0},{1,9},{9,17},{17,25},{25,1},{2,10},{10... | collective-permute-start | bytes 294920 | tf_op jit(solution)/shard_map/ppermute | solution.py:869
  160.6 18.0 %collective-permute-start.27 = (bf16[3,4,64,64]{3,2,1,0:T(8,128)(2,1)S(1)}, bf16[3,4,64,64]{3,2,1,0:T(8,128)(2,1)S(1)}, u32[]{:S(2)}, u32[]{:S(2)}) collective-permute-start(bf16[3,4,64,64]{3,2,1,0:T(8,128)(2,1)S(1)} %get-tuple-element.248), channel_id=1, source_target_pairs={{0,16},{8,24},{16,0},{24,8},{1,17},{9,25},{17,1},{25,9},{2,18},{10... | collective-permute-start | bytes 294920 | tf_op jit(solution)/shard_map/ppermute | solution.py:869
  160.6 18.0 %collective-permute-start.28 = (bf16[3,4,64,64]{3,2,1,0:T(8,128)(2,1)S(1)}, bf16[3,4,64,64]{3,2,1,0:T(8,128)(2,1)S(1)}, u32[]{:S(2)}, u32[]{:S(2)}) collective-permute-start(bf16[3,4,64,64]{3,2,1,0:T(8,128)(2,1)S(1)} %get-tuple-element.247), channel_id=1, source_target_pairs={{0,24},{8,0},{16,8},{24,16},{1,25},{9,1},{17,9},{25,17},{2,26},{10... | collective-permute-start | bytes 294920 | tf_op jit(solution)/shard_map/ppermute | solution.py:869
  178.7 1.4 collective-permute-start.29
  179.0 34.4 %copy-start.17 = (s32[4]{0:T(128)S(1)}, s32[4]{0:T(128)}, u32[]{:S(2)}) copy-start(s32[4]{0:T(128)} %pad_add_fusion.1.block_of) | copy-start | bytes 52
  179.1 8.2 %collective-permute-start.41 = (bf16[2,4,32,256]{3,2,1,0:T(8,128)(2,1)S(1)}, bf16[2,4,32,256]{3,2,1,0:T(8,128)(2,1)S(1)}, u32[]{:S(2)}, u32[]{:S(2)}) collective-permute-start(bf16[2,4,32,256]{3,2,1,0:T(8,128)(2,1)S(1)} %get-tuple-element.213), channel_id=1, source_target_pairs={{0,4},{4,0},{1,5},{5,1},{2,6},{6,2},{3,7},{7,3},{8,12},{12,8},{9,1... | collective-permute-start | bytes 393224 | tf_op jit(solution)/shard_map/ppermute | solution.py:873
  180.1 14.9 %collective-permute-start.30 = (bf16[512,256]{1,0:T(8,128)(2,1)S(1)}, bf16[512,256]{1,0:T(8,128)(2,1)S(1)}, u32[]{:S(2)}, u32[]{:S(2)}) collective-permute-start(bf16[512,256]{1,0:T(8,128)(2,1)S(1)} %bitcast.155), channel_id=1, source_target_pairs={{0,16},{8,24},{16,0},{24,8},{1,17},{9,25},{17,1},{25,9},{2,18},{10... | collective-permute-start | bytes 786440 | tf_op jit(solution)/shard_map/ppermute | solution.py:869
  180.9 16.7 %collective-permute-start.33 = (bf16[512,256]{1,0:T(8,128)(2,1)S(1)}, bf16[512,256]{1,0:T(8,128)(2,1)S(1)}, u32[]{:S(2)}, u32[]{:S(2)}) collective-permute-start(bf16[512,256]{1,0:T(8,128)(2,1)S(1)} %bitcast.156), channel_id=1, source_target_pairs={{8,0},{16,8},{24,16},{9,1},{17,9},{25,17},{10,2},{18,10},{26,18},{... | collective-permute-start | bytes 786440 | tf_op jit(solution)/shard_map/ppermute | solution.py:892
  182.2 31.2 %collective-permute-start.32 = (bf16[512,256]{1,0:T(8,128)(2,1)S(1)}, bf16[512,256]{1,0:T(8,128)(2,1)S(1)}, u32[]{:S(2)}, u32[]{:S(2)}) collective-permute-start(bf16[512,256]{1,0:T(8,128)(2,1)S(1)} %bitcast.157), channel_id=1, source_target_pairs={{0,8},{8,16},{16,24},{1,9},{9,17},{17,25},{2,10},{10,18},{18,26},{... | collective-permute-start | bytes 786440 | tf_op jit(solution)/shard_map/ppermute | solution.py:891
  195.0 16.9 %collective-permute-start.42 = (bf16[512,256]{1,0:T(8,128)(2,1)S(1)}, bf16[512,256]{1,0:T(8,128)(2,1)S(1)}, u32[]{:S(2)}, u32[]{:S(2)}) collective-permute-start(bf16[512,256]{1,0:T(8,128)(2,1)S(1)} %bitcast.151), channel_id=1, source_target_pairs={{0,16},{8,24},{16,0},{24,8},{1,17},{9,25},{17,1},{25,9},{2,18},{10... | collective-permute-start | bytes 786440 | tf_op jit(solution)/shard_map/ppermute | solution.py:869
  195.0 18.4 %collective-permute-start.31 = (bf16[512,256]{1,0:T(8,128)(2,1)S(1)}, bf16[512,256]{1,0:T(8,128)(2,1)S(1)}, u32[]{:S(2)}, u32[]{:S(2)}) collective-permute-start(bf16[512,256]{1,0:T(8,128)(2,1)S(1)} %collective-permute-done.30.h2), channel_id=1, source_target_pairs={{8,0},{16,24},{9,1},{17,25},{10,2},{18,26},{11,3},{19,27},{12,4},{... | collective-permute-start | bytes 786440 | tf_op jit(solution)/shard_map/ppermute | solution.py:897
  196.4 22.3 %collective-permute-start.45 = (bf16[512,256]{1,0:T(8,128)(2,1)S(1)}, bf16[512,256]{1,0:T(8,128)(2,1)S(1)}, u32[]{:S(2)}, u32[]{:S(2)}) collective-permute-start(bf16[512,256]{1,0:T(8,128)(2,1)S(1)} %bitcast.152), channel_id=1, source_target_pairs={{8,0},{16,8},{24,16},{9,1},{17,9},{25,17},{10,2},{18,10},{26,18},{... | collective-permute-start | bytes 786440 | tf_op jit(solution)/shard_map/ppermute | solution.py:892
  197.7 21.5 %collective-permute-start.44 = (bf16[512,256]{1,0:T(8,128)(2,1)S(1)}, bf16[512,256]{1,0:T(8,128)(2,1)S(1)}, u32[]{:S(2)}, u32[]{:S(2)}) collective-permute-start(bf16[512,256]{1,0:T(8,128)(2,1)S(1)} %bitcast.153), channel_id=1, source_target_pairs={{0,8},{8,16},{16,24},{1,9},{9,17},{17,25},{2,10},{10,18},{18,26},{... | collective-permute-start | bytes 786440 | tf_op jit(solution)/shard_map/ppermute | solution.py:891
  211.9 10.1 %collective-permute-start.43 = (bf16[512,256]{1,0:T(8,128)(2,1)S(1)}, bf16[512,256]{1,0:T(8,128)(2,1)S(1)}, u32[]{:S(2)}, u32[]{:S(2)}) collective-permute-start(bf16[512,256]{1,0:T(8,128)(2,1)S(1)} %collective-permute-done.42.h2), channel_id=1, source_target_pairs={{8,0},{16,24},{9,1},{17,25},{10,2},{18,26},{11,3},{19,27},{12,4},{... | collective-permute-start | bytes 786440 | tf_op jit(solution)/shard_map/ppermute | solution.py:897
  215.6 11.5 %collective-permute-start.37 = (bf16[4,32,1024]{2,1,0:T(8,128)(2,1)S(1)}, bf16[4,32,1024]{2,1,0:T(8,128)(2,1)S(1)}, u32[]{:S(2)}, u32[]{:S(2)}) collective-permute-start(bf16[4,32,1024]{2,1,0:T(8,128)(2,1)S(1)} %get-tuple-element.211), channel_id=1, source_target_pairs={{0,3},{1,2},{2,1},{3,0},{4,7},{5,6},{6,5},{7,4},{8,11},{9,10},{10,... | collective-permute-start | bytes 786440 | tf_op jit(solution)/shard_map/ppermute | solution.py:1164
  217.1 14.4 %collective-permute-start.36 = (bf16[4,32,1024]{2,1,0:T(8,128)(2,1)S(1)}, bf16[4,32,1024]{2,1,0:T(8,128)(2,1)S(1)}, u32[]{:S(2)}, u32[]{:S(2)}) collective-permute-start(bf16[4,32,1024]{2,1,0:T(8,128)(2,1)S(1)} %get-tuple-element.210), channel_id=1, source_target_pairs={{0,2},{2,0},{1,3},{3,1},{4,6},{6,4},{5,7},{7,5},{8,10},{10,8},{9,1... | collective-permute-start | bytes 786440 | tf_op jit(solution)/shard_map/ppermute | solution.py:881
  218.6 12.9 %collective-permute-start.35 = (bf16[4,32,1024]{2,1,0:T(8,128)(2,1)S(1)}, bf16[4,32,1024]{2,1,0:T(8,128)(2,1)S(1)}, u32[]{:S(2)}, u32[]{:S(2)}) collective-permute-start(bf16[4,32,1024]{2,1,0:T(8,128)(2,1)S(1)} %get-tuple-element.209), channel_id=1, source_target_pairs={{0,1},{1,0},{2,3},{3,2},{4,5},{5,4},{6,7},{7,6},{8,9},{9,8},{10,11... | collective-permute-start | bytes 786440 | tf_op jit(solution)/shard_map/ppermute | solution.py:877
  224.1 13.0 %collective-permute-start.48 = (bf16[4,32,1024]{2,1,0:T(8,128)(2,1)S(1)}, bf16[4,32,1024]{2,1,0:T(8,128)(2,1)S(1)}, u32[]{:S(2)}, u32[]{:S(2)}) collective-permute-start(bf16[4,32,1024]{2,1,0:T(8,128)(2,1)S(1)} %get-tuple-element.218), channel_id=1, source_target_pairs={{0,3},{1,2},{2,1},{3,0},{4,7},{5,6},{6,5},{7,4},{8,11},{9,10},{10,... | collective-permute-start | bytes 786440 | tf_op jit(solution)/shard_map/ppermute | solution.py:1164
  225.6 16.0 %collective-permute-start.47 = (bf16[4,32,1024]{2,1,0:T(8,128)(2,1)S(1)}, bf16[4,32,1024]{2,1,0:T(8,128)(2,1)S(1)}, u32[]{:S(2)}, u32[]{:S(2)}) collective-permute-start(bf16[4,32,1024]{2,1,0:T(8,128)(2,1)S(1)} %get-tuple-element.217), channel_id=1, source_target_pairs={{0,2},{2,0},{1,3},{3,1},{4,6},{6,4},{5,7},{7,5},{8,10},{10,8},{9,1... | collective-permute-start | bytes 786440 | tf_op jit(solution)/shard_map/ppermute | solution.py:881
  227.1 14.5 %collective-permute-start.46 = (bf16[4,32,1024]{2,1,0:T(8,128)(2,1)S(1)}, bf16[4,32,1024]{2,1,0:T(8,128)(2,1)S(1)}, u32[]{:S(2)}, u32[]{:S(2)}) collective-permute-start(bf16[4,32,1024]{2,1,0:T(8,128)(2,1)S(1)} %get-tuple-element.216), channel_id=1, source_target_pairs={{0,1},{1,0},{2,3},{3,2},{4,5},{5,4},{6,7},{7,6},{8,9},{9,8},{10,11... | collective-permute-start | bytes 786440 | tf_op jit(solution)/shard_map/ppermute | solution.py:877
  231.7 12.8 %collective-permute-start.38 = (bf16[32,1024]{1,0:T(8,128)(2,1)S(1)}, bf16[32,1024]{1,0:T(8,128)(2,1)S(1)}, u32[]{:S(2)}, u32[]{:S(2)}) collective-permute-start(bf16[32,1024]{1,0:T(8,128)(2,1)S(1)} %get-tuple-element.261), channel_id=1, source_target_pairs={{0,8},{8,16},{16,24},{24,0},{1,9},{9,17},{17,25},{25,1},{2,10},{10... | collective-permute-start | bytes 196616 | tf_op jit(solution)/shard_map/ppermute | solution.py:869
  234.5 14.9 %collective-permute-start.39 = (bf16[32,1024]{1,0:T(8,128)(2,1)S(1)}, bf16[32,1024]{1,0:T(8,128)(2,1)S(1)}, u32[]{:S(2)}, u32[]{:S(2)}) collective-permute-start(bf16[32,1024]{1,0:T(8,128)(2,1)S(1)} %get-tuple-element.260), channel_id=1, source_target_pairs={{0,16},{8,24},{16,0},{24,8},{1,17},{9,25},{17,1},{25,9},{2,18},{10... | collective-permute-start | bytes 196616 | tf_op jit(solution)/shard_map/ppermute | solution.py:869
  237.1 12.2 %collective-permute-start.40 = (bf16[32,1024]{1,0:T(8,128)(2,1)S(1)}, bf16[32,1024]{1,0:T(8,128)(2,1)S(1)}, u32[]{:S(2)}, u32[]{:S(2)}) collective-permute-start(bf16[32,1024]{1,0:T(8,128)(2,1)S(1)} %get-tuple-element.259), channel_id=1, source_target_pairs={{0,24},{8,0},{16,8},{24,16},{1,25},{9,1},{17,9},{25,17},{2,26},{10... | collective-permute-start | bytes 196616 | tf_op jit(solution)/shard_map/ppermute | solution.py:869
  241.8 7.5 %collective-permute-start.49 = (bf16[32,1024]{1,0:T(8,128)(2,1)S(1)}, bf16[32,1024]{1,0:T(8,128)(2,1)S(1)}, u32[]{:S(2)}, u32[]{:S(2)}) collective-permute-start(bf16[32,1024]{1,0:T(8,128)(2,1)S(1)} %get-tuple-element.255), channel_id=1, source_target_pairs={{0,8},{8,16},{16,24},{24,0},{1,9},{9,17},{17,25},{25,1},{2,10},{10... | collective-permute-start | bytes 196616 | tf_op jit(solution)/shard_map/ppermute | solution.py:869
  244.3 6.6 %collective-permute-start.50 = (bf16[32,1024]{1,0:T(8,128)(2,1)S(1)}, bf16[32,1024]{1,0:T(8,128)(2,1)S(1)}, u32[]{:S(2)}, u32[]{:S(2)}) collective-permute-start(bf16[32,1024]{1,0:T(8,128)(2,1)S(1)} %get-tuple-element.254), channel_id=1, source_target_pairs={{0,16},{8,24},{16,0},{24,8},{1,17},{9,25},{17,1},{25,9},{2,18},{10... | collective-permute-start | bytes 196616 | tf_op jit(solution)/shard_map/ppermute | solution.py:869
  244.5 6.4 %collective-permute-start.51 = (bf16[32,1024]{1,0:T(8,128)(2,1)S(1)}, bf16[32,1024]{1,0:T(8,128)(2,1)S(1)}, u32[]{:S(2)}, u32[]{:S(2)}) collective-permute-start(bf16[32,1024]{1,0:T(8,128)(2,1)S(1)} %get-tuple-element.253), channel_id=1, source_target_pairs={{0,24},{8,0},{16,8},{24,16},{1,25},{9,1},{17,9},{25,17},{2,26},{10... | collective-permute-start | bytes 196616 | tf_op jit(solution)/shard_map/ppermute | solution.py:869
  (53 other events, 254.3 us)
